TPU v7x, 32 devices: a whole 2x2x4 slice. The times are simulated.
32 devices in a mesh: gy: 4 (over y, x), gx: 8 (over z, core).
Axes of the slice: x: 2, y: 2, z: 4, core: 2. Of those that a mesh axis runs over, the one named last changes fastest.
Arguments:
- pixels: bfloat16 [6, 32, 64, 1536], P(None, 'gy', 'gx'), may hold values from -6 to 6
- pad_mask: int32 [6, 32, 64], P(None, 'gy', 'gx'), may hold values 0 or 1
- timestamps: int32 [5, 6], replicated, may hold values from 0 to 1999
- scene_dates: int32 [5], replicated, may hold values from 1 to 6, as said below
- scene_map: int32 [4, 8], replicated, may hold values from 0 to 4, as said below
- blend_weight: int32 [48, 96], P('gy', 'gx'), may hold values from 1 to 3
- cotangent: bfloat16 [6, 32, 64, 1536], P(None, 'gy', 'gx'), may hold values from -6 to 6
- patch_w: bfloat16 [1536, 768], P('gx'), may hold values from -0.15625 to 0.15625
- norm1_gain: bfloat16 [768], P('gx'), may hold values from 0.099609375 to 1.8984375
- norm1_bias: bfloat16 [768], P('gx'), may hold values from -2 to 2
- qkv_w: bfloat16 [768, 2304], P('gx'), may hold values from -0.3125 to 0.3125
- proj_w: bfloat16 [768, 768], P('gx'), may hold values from -1.25 to 1.25
- norm2_gain: bfloat16 [768], P('gx'), may hold values from 0.099609375 to 1.8984375
- norm2_bias: bfloat16 [768], P('gx'), may hold values from -2 to 2
- fc1_w: bfloat16 [768, 3072], P('gx'), may hold values from -0.21875 to 0.21875
- fc1_b: bfloat16 [3072], P('gx'), may hold values from -3 to 3
- fc2_w: bfloat16 [3072, 768], P('gx'), may hold values from -0.109375 to 0.109375
- dec_w: bfloat16 [768, 512], P('gx'), may hold values from -0.21875 to 0.21875
- head_w: bfloat16 [512, 1536], P('gx'), may hold values from -0.25 to 0.25
Outputs:
- recon: bfloat16 [6, 32, 64, 1536], P(None, 'gy', 'gx')
- pixel_grad: float32 [6, 32, 64, 1536], P(None, 'gy', 'gx')
- grad_patch_w: float32 [1536, 768], P('gx')
- grad_norm1_gain: float32 [768], P('gx')
- grad_norm1_bias: float32 [768], P('gx')
- grad_qkv_w: float32 [768, 2304], P('gx')
- grad_proj_w: float32 [768, 768], P('gx')
- grad_norm2_gain: float32 [768], P('gx')
- grad_norm2_bias: float32 [768], P('gx')
- grad_fc1_w: float32 [768, 3072], P('gx')
- grad_fc1_b: float32 [3072], P('gx')
- grad_fc2_w: float32 [3072, 768], P('gx')
- grad_dec_w: float32 [768, 512], P('gx')
- grad_head_w: float32 [512, 1536], P('gx')
Inputs may be any that keep to these rules, and one draw needn't show every extreme that they name: `scene_dates`: dates of each scene; scene 0 has all 6. `scene_map`: scene number of each tile; scene 0 holds a whole tile row and a whole tile column.
All inputs are finite; a program needn't handle non-finite values. No bound on the sum of `pad_mask` on one device may be relied on, other than what follows from the above.
Results may differ from a plain program's by a relative error of at most 0.02.
Values may be sent and summed in bfloat16 or wider, within the bound.
No kernel may reach another device: no remote copies, remote signals or barrier semaphores. Data moves between devices by JAX's collectives and lax.ppermute only.
A program may use at most 256 MiB of HBM per device.

v0:
```python
import jax
import jax.numpy as jnp
import numpy as np
from jax import lax
from jax.sharding import PartitionSpec as P

HEADS = 12
MARGIN = 2


norm_eps = 1e-06


def from_behind(block, axis, distance):
    devices = range(lax.axis_size(axis))
    route = [(i - distance, i) for i in devices if i - distance in devices]
    return lax.ppermute(block, axis, route)


def with_halo(block, sides, width):
    for axis, dim in sides:
        count = lax.axis_size(axis)
        forward = [(i, i + 1) for i in range(count - 1)]
        backward = [(target, source) for source, target in forward]
        low = lax.ppermute(
            lax.slice_in_dim(block, block.shape[dim] - width, None, axis=dim), axis, forward
        )
        high = lax.ppermute(lax.slice_in_dim(block, 0, width, axis=dim), axis, backward)
        block = jnp.concatenate([low, block, high], axis=dim)
    return block


def matmul(left, right):
    return jnp.dot(left, right, preferred_element_type=jnp.float32)


def layer_norm(hidden, gain_vec, shift_vec):
    center = jnp.mean(hidden, axis=-1, keepdims=True)
    centered = hidden - center
    spread = jnp.mean(centered * centered, axis=-1, keepdims=True)
    return centered * lax.rsqrt(spread + norm_eps) * gain_vec + shift_vec


def gelu_exact(values):
    return jax.nn.gelu(values, approximate=False)


def sincos(places, span_width):
    half_width = span_width // 2
    omega = 1.0 / 10000.0 ** (jnp.arange(half_width, dtype=jnp.float32) / half_width)
    angles = places[:, None] * omega[None, :]
    return jnp.concatenate([jnp.sin(angles), jnp.cos(angles)], axis=1)


def position_table(tile_row, tile_col, stamps, tile_side, model_width):
    side_width = model_width // 16 * 6
    time_width = model_width - 2 * side_width
    extent = tile_side + 2 * MARGIN
    num_dates = stamps.shape[0]
    offsets = jnp.arange(extent, dtype=jnp.int32) - MARGIN
    row_places = (tile_row * tile_side + offsets).astype(jnp.float32)
    col_places = (tile_col * tile_side + offsets).astype(jnp.float32)
    time_part = sincos(stamps.astype(jnp.float32), time_width)[:, None, None, :]
    row_part = sincos(row_places, side_width)[None, :, None, :]
    col_part = sincos(col_places, side_width)[None, None, :, :]
    full_shape = (num_dates, extent, extent)
    table = jnp.concatenate(
        [
            jnp.broadcast_to(time_part, full_shape + (time_width,)),
            jnp.broadcast_to(row_part, full_shape + (side_width,)),
            jnp.broadcast_to(col_part, full_shape + (side_width,)),
        ],
        axis=-1,
    )
    return table.reshape(num_dates * extent * extent, model_width)


def fold_back(extended):
    col_count = extended.shape[-2]
    left_rim = extended[..., :, :MARGIN, :]
    right_rim = extended[..., :, col_count - MARGIN :, :]
    from_east = from_behind(left_rim.astype(jnp.bfloat16), "gx", -1).astype(left_rim.dtype)
    from_west = from_behind(right_rim.astype(jnp.bfloat16), "gx", 1).astype(right_rim.dtype)
    inner = extended[..., :, MARGIN : col_count - MARGIN, :]
    inner_cols = col_count - 2 * MARGIN
    inner = jnp.concatenate(
        [
            inner[..., :, :MARGIN, :] + from_west,
            inner[..., :, MARGIN : inner_cols - MARGIN, :],
            inner[..., :, inner_cols - MARGIN :, :] + from_east,
        ],
        axis=-2,
    )
    row_count = inner.shape[-3]
    top_rim = inner[..., :MARGIN, :, :]
    bottom_rim = inner[..., row_count - MARGIN :, :, :]
    from_south = from_behind(top_rim.astype(jnp.bfloat16), "gy", -1).astype(top_rim.dtype)
    from_north = from_behind(bottom_rim.astype(jnp.bfloat16), "gy", 1).astype(bottom_rim.dtype)
    core = inner[..., MARGIN : row_count - MARGIN, :, :]
    core_rows = row_count - 2 * MARGIN
    return jnp.concatenate(
        [
            core[..., :MARGIN, :, :] + from_north,
            core[..., MARGIN : core_rows - MARGIN, :, :],
            core[..., core_rows - MARGIN :, :, :] + from_south,
        ],
        axis=-3,
    )


def on_device(
    pixels,
    pad_mask,
    timestamps,
    scene_dates,
    scene_map,
    blend_weight,
    cotangent,
    patch_w,
    norm1_gain,
    norm1_bias,
    qkv_w,
    proj_w,
    norm2_gain,
    norm2_bias,
    fc1_w,
    fc1_b,
    fc2_w,
    dec_w,
    head_w,
):
    num_dates = pixels.shape[0]
    tile_side = pixels.shape[1]
    pixel_width = pixels.shape[3]
    extent = tile_side + 2 * MARGIN
    token_count = num_dates * extent * extent
    (
        full_patch,
        full_gain1,
        full_shift1,
        full_qkv,
        full_proj,
        full_gain2,
        full_shift2,
        full_fc1,
        full_fc1_b,
        full_fc2,
        full_dec,
        full_head,
    ) = (
        lax.all_gather(patch_w, "gx", axis=0, tiled=True),
        lax.all_gather(norm1_gain, "gx", axis=0, tiled=True),
        lax.all_gather(norm1_bias, "gx", axis=0, tiled=True),
        lax.all_gather(qkv_w, "gx", axis=0, tiled=True),
        lax.all_gather(proj_w, "gx", axis=0, tiled=True),
        lax.all_gather(norm2_gain, "gx", axis=0, tiled=True),
        lax.all_gather(norm2_bias, "gx", axis=0, tiled=True),
        lax.all_gather(fc1_w, "gx", axis=0, tiled=True),
        lax.all_gather(fc1_b, "gx", axis=0, tiled=True),
        lax.all_gather(fc2_w, "gx", axis=0, tiled=True),
        lax.all_gather(dec_w, "gx", axis=0, tiled=True),
        lax.all_gather(head_w, "gx", axis=0, tiled=True),
    )
    model_width = full_patch.shape[1]
    head_dim = model_width // HEADS
    scale = float(head_dim) ** (-0.5)
    hidden_half = full_fc1.shape[1] // 2
    gain1 = full_gain1.astype(jnp.float32)
    shift1 = full_shift1.astype(jnp.float32)
    gain2 = full_gain2.astype(jnp.float32)
    shift2 = full_shift2.astype(jnp.float32)
    bias_fc1 = full_fc1_b.astype(jnp.float32)
    tile_row = lax.axis_index("gy")
    tile_col = lax.axis_index("gx")
    framed_map = jnp.pad(scene_map, 1, constant_values=-1)
    nearby = lax.dynamic_slice(framed_map, (tile_row, tile_col), (3, 3))
    own_scene = nearby[1, 1]
    bands = np.array([0] * MARGIN + [1] * tile_side + [2] * MARGIN)
    same_ext = (nearby == own_scene)[bands][:, bands]
    own_dates = scene_dates[own_scene]
    stamps = timestamps[own_scene]
    date_ok = jnp.arange(num_dates, dtype=jnp.int32) < own_dates
    key_ok = (date_ok[:, None, None] & same_ext[None, :, :]).reshape(token_count)
    weight_ext = blend_weight.astype(jnp.float32) * same_ext.astype(jnp.float32)
    valid = pad_mask.astype(jnp.float32) * date_ok.astype(jnp.float32)[:, None, None]
    denom = fold_back(weight_ext[None, :, :, None])[0, :, :, 0]
    masked = pixels * pad_mask.astype(jnp.bfloat16)[..., None]
    ext_pixels = with_halo(masked, (("gy", 1), ("gx", 2)), MARGIN)
    ext_rows = ext_pixels.reshape(token_count, pixel_width)
    position = position_table(tile_row, tile_col, stamps, tile_side, model_width)
    trunk0 = matmul(ext_rows, full_patch) + position
    normed1 = layer_norm(trunk0, gain1, shift1).astype(jnp.bfloat16)
    qkv_heads = (
        matmul(normed1, full_qkv)
        .astype(jnp.bfloat16)
        .reshape(token_count, 3, HEADS, head_dim)
        .transpose(1, 2, 0, 3)
    )
    query_heads = qkv_heads[0]
    key_heads = qkv_heads[1]
    value_heads = qkv_heads[2]

    def head_forward(head_item):
        query_h, key_h, value_h = head_item
        scores = matmul(query_h, key_h.T) * scale
        scores = jnp.where(key_ok[None, :], scores, -1000000000.0)
        row_top = jnp.max(scores, axis=-1, keepdims=True)
        raw_weights = jnp.exp(scores - row_top)
        row_total = jnp.sum(raw_weights, axis=-1, keepdims=True)
        probs = (raw_weights / row_total).astype(jnp.bfloat16)
        return (matmul(probs, value_h), (row_top + jnp.log(row_total))[:, 0])

    head_outs, log_totals = lax.map(head_forward, (query_heads, key_heads, value_heads))
    attended = head_outs.transpose(1, 0, 2).reshape(token_count, model_width).astype(jnp.bfloat16)
    trunk1 = trunk0 + matmul(attended, full_proj)
    normed2 = layer_norm(trunk1, gain2, shift2).astype(jnp.bfloat16)
    pre_halves = []
    act_halves = []
    mlp_out = jnp.zeros((token_count, model_width), jnp.float32)
    for half_idx in range(2):
        lower = half_idx * hidden_half
        pre_part = (
            matmul(normed2, full_fc1[:, lower : lower + hidden_half])
            + bias_fc1[lower : lower + hidden_half]
        )
        act_part = gelu_exact(pre_part).astype(jnp.bfloat16)
        mlp_out = mlp_out + matmul(act_part, full_fc2[lower : lower + hidden_half, :])
        pre_halves.append(pre_part)
        act_halves.append(act_part)
    trunk2_low = (trunk1 + mlp_out).astype(jnp.bfloat16)
    decoded = matmul(trunk2_low, full_dec).astype(jnp.bfloat16)
    pred = matmul(decoded, full_head)
    weighted = pred.reshape(num_dates, extent, extent, pixel_width) * weight_ext[None, :, :, None]
    numer = fold_back(weighted)
    recon = (valid[..., None] * numer / denom[None, :, :, None]).astype(jnp.bfloat16)
    grad_owned = valid[..., None] * (cotangent.astype(jnp.float32) / denom[None, :, :, None])
    grad_ext = with_halo(grad_owned, (("gy", 1), ("gx", 2)), MARGIN)
    dpred = (
        (grad_ext * weight_ext[None, :, :, None])
        .reshape(token_count, pixel_width)
        .astype(jnp.bfloat16)
    )
    grad_head = matmul(decoded.T, dpred)
    ddecoded = matmul(dpred, full_head.T).astype(jnp.bfloat16)
    grad_dec = matmul(trunk2_low.T, ddecoded)
    dtrunk2 = matmul(ddecoded, full_dec.T)
    dmlp = dtrunk2.astype(jnp.bfloat16)
    dnormed2 = jnp.zeros((token_count, model_width), jnp.float32)
    fc1_parts = []
    fc1_b_parts = []
    fc2_parts = []
    for half_idx in range(2):
        lower = half_idx * hidden_half
        dact = matmul(dmlp, full_fc2[lower : lower + hidden_half, :].T)
        fc2_parts.append(matmul(act_halves[half_idx].T, dmlp))
        _, gelu_back = jax.vjp(gelu_exact, pre_halves[half_idx])
        dpre = gelu_back(dact)[0].astype(jnp.bfloat16)
        fc1_b_parts.append(jnp.sum(dpre.astype(jnp.float32), axis=0))
        fc1_parts.append(matmul(normed2.T, dpre))
        dnormed2 = dnormed2 + matmul(dpre, full_fc1[:, lower : lower + hidden_half].T)
    grad_fc1 = jnp.concatenate(fc1_parts, axis=1)
    grad_fc1_b = jnp.concatenate(fc1_b_parts, axis=0)
    grad_fc2 = jnp.concatenate(fc2_parts, axis=0)
    _, norm2_back = jax.vjp(layer_norm, trunk1, gain2, shift2)
    dtrunk1_part, grad_gain2, grad_shift2 = norm2_back(dnormed2)
    dtrunk1 = dtrunk2 + dtrunk1_part
    dattn = dtrunk1.astype(jnp.bfloat16)
    grad_proj = matmul(attended.T, dattn)
    dout_heads = (
        matmul(dattn, full_proj.T)
        .astype(jnp.bfloat16)
        .reshape(token_count, HEADS, head_dim)
        .transpose(1, 0, 2)
    )

    def head_backward(head_item):
        query_h, key_h, value_h, dout_h, log_total = head_item
        scores = matmul(query_h, key_h.T) * scale
        scores = jnp.where(key_ok[None, :], scores, -1000000000.0)
        probs = jnp.exp(scores - log_total[:, None])
        dvalue = matmul(probs.astype(jnp.bfloat16).T, dout_h)
        dprobs = matmul(dout_h, value_h.T)
        dscores = (probs * (dprobs - jnp.sum(dprobs * probs, axis=-1, keepdims=True))).astype(
            jnp.bfloat16
        )
        dquery = matmul(dscores, key_h) * scale
        dkey = matmul(dscores.T, query_h) * scale
        return (dquery.astype(jnp.bfloat16), dkey.astype(jnp.bfloat16), dvalue.astype(jnp.bfloat16))

    dquery_heads, dkey_heads, dvalue_heads = lax.map(
        head_backward, (query_heads, key_heads, value_heads, dout_heads, log_totals)
    )
    dqkv = (
        jnp.stack([dquery_heads, dkey_heads, dvalue_heads])
        .transpose(2, 0, 1, 3)
        .reshape(token_count, 3 * model_width)
    )
    grad_qkv = matmul(normed1.T, dqkv)
    dnormed1 = matmul(dqkv, full_qkv.T)
    _, norm1_back = jax.vjp(layer_norm, trunk0, gain1, shift1)
    dtrunk0_part, grad_gain1, grad_shift1 = norm1_back(dnormed1)
    dembed = (dtrunk1 + dtrunk0_part).astype(jnp.bfloat16)
    grad_patch = matmul(ext_rows.T, dembed)
    dext = matmul(dembed, full_patch.T).reshape(num_dates, extent, extent, pixel_width)
    pixel_grad = fold_back(dext) * pad_mask.astype(jnp.float32)[..., None]
    shares = (
        lax.psum_scatter(
            grad_patch.astype(jnp.bfloat16), "gx", scatter_dimension=0, tiled=True
        ).astype(jnp.float32),
        lax.psum_scatter(
            grad_gain1.astype(jnp.bfloat16), "gx", scatter_dimension=0, tiled=True
        ).astype(jnp.float32),
        lax.psum_scatter(
            grad_shift1.astype(jnp.bfloat16), "gx", scatter_dimension=0, tiled=True
        ).astype(jnp.float32),
        lax.psum_scatter(
            grad_qkv.astype(jnp.bfloat16), "gx", scatter_dimension=0, tiled=True
        ).astype(jnp.float32),
        lax.psum_scatter(
            grad_proj.astype(jnp.bfloat16), "gx", scatter_dimension=0, tiled=True
        ).astype(jnp.float32),
        lax.psum_scatter(
            grad_gain2.astype(jnp.bfloat16), "gx", scatter_dimension=0, tiled=True
        ).astype(jnp.float32),
        lax.psum_scatter(
            grad_shift2.astype(jnp.bfloat16), "gx", scatter_dimension=0, tiled=True
        ).astype(jnp.float32),
        lax.psum_scatter(
            grad_fc1.astype(jnp.bfloat16), "gx", scatter_dimension=0, tiled=True
        ).astype(jnp.float32),
        lax.psum_scatter(
            grad_fc1_b.astype(jnp.bfloat16), "gx", scatter_dimension=0, tiled=True
        ).astype(jnp.float32),
        lax.psum_scatter(
            grad_fc2.astype(jnp.bfloat16), "gx", scatter_dimension=0, tiled=True
        ).astype(jnp.float32),
        lax.psum_scatter(
            grad_dec.astype(jnp.bfloat16), "gx", scatter_dimension=0, tiled=True
        ).astype(jnp.float32),
        lax.psum_scatter(
            grad_head.astype(jnp.bfloat16), "gx", scatter_dimension=0, tiled=True
        ).astype(jnp.float32),
    )
    summed = tuple(
        (
            lax.psum(shares[0].astype(jnp.bfloat16), "gy").astype(jnp.float32),
            lax.psum(shares[1].astype(jnp.bfloat16), "gy").astype(jnp.float32),
            lax.psum(shares[2].astype(jnp.bfloat16), "gy").astype(jnp.float32),
            lax.psum(shares[3].astype(jnp.bfloat16), "gy").astype(jnp.float32),
            lax.psum(shares[4].astype(jnp.bfloat16), "gy").astype(jnp.float32),
            lax.psum(shares[5].astype(jnp.bfloat16), "gy").astype(jnp.float32),
            lax.psum(shares[6].astype(jnp.bfloat16), "gy").astype(jnp.float32),
            lax.psum(shares[7].astype(jnp.bfloat16), "gy").astype(jnp.float32),
            lax.psum(shares[8].astype(jnp.bfloat16), "gy").astype(jnp.float32),
            lax.psum(shares[9].astype(jnp.bfloat16), "gy").astype(jnp.float32),
            lax.psum(shares[10].astype(jnp.bfloat16), "gy").astype(jnp.float32),
            lax.psum(shares[11].astype(jnp.bfloat16), "gy").astype(jnp.float32),
        )
    )
    return (
        recon,
        pixel_grad,
        summed[0],
        summed[1],
        summed[2],
        summed[3],
        summed[4],
        summed[5],
        summed[6],
        summed[7],
        summed[8],
        summed[9],
        summed[10],
        summed[11],
    )


def solution(mesh):
    in_specs = (
        P(None, "gy", "gx", None),
        P(None, "gy", "gx"),
        P(),
        P(),
        P(),
        P("gy", "gx"),
        P(None, "gy", "gx", None),
        P("gx", None),
        P("gx"),
        P("gx"),
        P("gx", None),
        P("gx", None),
        P("gx"),
        P("gx"),
        P("gx", None),
        P("gx"),
        P("gx", None),
        P("gx", None),
        P("gx", None),
    )
    out_specs = (
        P(None, "gy", "gx", None),
        P(None, "gy", "gx", None),
        P("gx", None),
        P("gx"),
        P("gx"),
        P("gx", None),
        P("gx", None),
        P("gx"),
        P("gx"),
        P("gx", None),
        P("gx"),
        P("gx", None),
        P("gx", None),
        P("gx", None),
    )
    return jax.shard_map(
        on_device, mesh=mesh, in_specs=in_specs, out_specs=out_specs, check_vma=False
    )
```

profile of v0, /device:TPU:0, one launch (start us, length us, event | category | flops | bytes accessed | tf_op | source)
XLA Modules:
  0.0 899.8 jit_solution(4665247724924200417)
XLA Ops:
  22.7 4.9 collective-permute-start
  34.6 3.0 pad_maximum_fusion.5
  37.6 4.4 reshape.192
  44.2 18.9 %all-reduce.11 = (bf16[768]{0:T(1024)(128)(2,1)S(1)}, bf16[768]{0:T(1024)(128)(2,1)S(1)}, bf16[768]{0:T(1024)(128)(2,1)S(1)}, bf16[768]{0:T(1024)(128)(2,1)S(1)}) all-reduce(bf16[768]{0:T(1024)(128)(2,1)S(1)} %dynamic-update-slice.1, bf16[768]{0:T(1024)(128)(2,1)S(1)} %dynamic-update-slice, ...), channel_id=1, replica_groups=mesh['gy'=4,'gx'=8] {'gx'}, use_global_device_ids=true, to_apply=%add.2 | all-reduce | flops 3072 | bytes 12288
  63.3 12.9 %all-gather = bf16[8,1,384]{2,1,0:T(2,128)(2,1)S(1)} all-gather(bf16[1,1,384]{2,1,0:T(2,128)(2,1)S(1)} %reshape.226), channel_id=1, replica_groups=mesh['gy'=4,'gx'=8] {'gx'}, dimensions={0}, use_global_device_ids=true | all-gather | bytes 6912 | tf_op jit(solution)/shard_map/all_gather | solution.py:159
  76.4 18.9 %all_gather.46 = bf16[768,512]{1,0:T(8,128)(2,1)} all-gather(bf16[96,512]{1,0:T(8,128)(2,1)S(1)} %copy-done.31), channel_id=1, replica_groups=mesh['gy'=4,'gx'=8] {'gx'}, dimensions={0}, use_global_device_ids=true | all-gather | bytes 884736 | tf_op jit(solution)/shard_map/all_gather | solution.py:161
  97.4 3.1 collective-permute-start.2
  101.3 5.0 collective-permute-start.10
  108.5 3.9 pad_maximum_fusion.4
  112.4 5.3 reshape.191
  117.6 5.7 fusion.119
  123.8 7.7 convolution_convert_fusion
  131.6 6.4 copy.159
  137.9 4.4 slice_bitcast_fusion
  142.3 2.9 copy.161
  145.2 3.9 copy.162
  149.1 3.9 copy.163
  153.0 77.0 %while.28 = (s32[]{:T(128)}, bf16[12,864,64]{1,2,0:T(8,128)(2,1)}, f32[12,864]{1,0:T(8,128)}, bf16[12,864,64]{2,1,0:T(8,128)(2,1)S(1)}, bf16[12,864,64]{2,1,0:T(...) while((s32[]{:T(128)}, bf16[12,864,64]{1,2,0:T(8,128)(2,1)}, ...), condition=%wide.region_5.6_spmd.clone, body=%wide.region_2.5_spmd.clone.sunk | while | flops 200060928 | bytes 9900007 | solution.py:213
  231.5 3.9 fusion.120
  237.7 17.7 %multiply_convert_fusion.2 = (bf16[864,1536]{1,0:T(8,128)(2,1)}, f32[864,1536]{1,0:T(8,128)}, f32[864,1536]{1,0:T(8,128)}) fusion(f32[1536]{0:T(1024)S(1)} %reshape.238, bf16[864,768]{1,0:T(8,128)(2,1)} %add_convert_fusion.4, bf16[768,3072]{1,0:T(8,128)(2,1)} %all-gather.14.cloned.1.call-done), kind=kOutput, calls=%fused_computation.71 | convolution fusion | flops 2126020608 | bytes 16963584 | tf_op jit(solution)/shard_map/dot_general | solution.py:34
  255.5 14.9 %multiply_convert_fusion.3 = (bf16[864,1536]{1,0:T(8,128)(2,1)}, f32[864,1536]{1,0:T(8,128)}, f32[864,1536]{1,0:T(8,128)}) fusion(f32[1536]{0:T(1024)S(1)} %reshape.237, bf16[864,768]{1,0:T(8,128)(2,1)S(1)} %copy-done.17, bf16[768,3072]{1,0:T(8,128)(2,1)S(1)} %copy-done.64), kind=kOutput, calls=%fused_computation.84 | convolution fusion | flops 2126020608 | bytes 16965632 | tf_op jit(solution)/shard_map/dot_general | solution.py:34
  270.4 4.8 fusion.73
  279.5 5.5 fusion.124
  285.1 7.1 reshape.194
  292.2 7.6 fusion.106
  300.5 11.8 %collective-permute-start.4 = (bf16[6,12,2,1536]{3,1,2,0:T(8,128)(2,1)S(1)}, bf16[6,12,2,1536]{3,1,2,0:T(8,128)(2,1)S(1)}, u32[]{:S(2)}, u32[]{:S(2)}) collective-permute-start(bf16[6,12,2,1536]{3,1,2,0:T(8,128)(2,1)S(1)} %copy.167), channel_id=1, source_target_pairs={{0,1},{1,2},{2,3},{3,4},{4,5},{5,6},{6,7},{8,9},{9,10},{10,11},{11... | collective-permute-start | bytes 1327112 | tf_op jit(solution)/shard_map/ppermute | solution.py:17
  317.4 4.3 slice_add_fusion.3
  322.9 3.7 collective-permute-start.6
  330.8 5.1 collective-permute-done.7
  339.1 4.6 collective-permute-start.12
  343.7 6.5 collective-permute-done.13
  356.4 13.3 %collective-permute-start.14 = (f32[6,12,2,1536]{3,1,2,0:T(8,128)}, f32[6,12,2,1536]{3,1,2,0:T(8,128)}, u32[]{:S(2)}, u32[]{:S(2)}) collective-permute-start(f32[6,12,2,1536]{3,1,2,0:T(8,128)} %copy.172), channel_id=1, source_target_pairs={{0,1},{1,2},{2,3},{3,4},{4,5},{5,6},{6,7},{8,9},{9,10},{10,11},{11... | collective-permute-start | bytes 2654216 | tf_op jit(solution)/shard_map/ppermute | solution.py:25
  373.9 3.6 pad_maximum_fusion
  377.6 7.1 concatenate.68
  384.6 4.6 convolution_convert_fusion.10
  393.5 7.7 fusion.122
  401.2 4.9 fusion.77
  406.2 7.4 fusion.123
  413.7 3.3 multiply_reduce_fusion.1
  422.7 3.6 convolution_convert_fusion.8
  428.1 6.0 convolution_convert_fusion.7
  434.2 113.4 %while.29 = (s32[]{:T(128)}, bf16[12,864,64]{1,2,0:T(8,128)(2,1)S(1)}, bf16[12,864,64]{1,2,0:T(8,128)(2,1)}, bf16[12,864,64]{1,2,0:T(8,128)(2,1)}, bf16[12,864,6...) while((s32[]{:T(128)}, ...), condition=%wide.region_12.13_spmd.clone, body=%wide.region_10.12_spmd.clone.sunk | while | flops 484752384 | bytes 24376856 | solution.py:290
  548.6 2.6 pad_maximum_fusion.3
  553.7 4.7 multiply_reduce_fusion.2
  562.4 3.9 convolution_convert_fusion.6
  566.4 8.2 convolution_convert_fusion.1
  575.9 5.0 convolution_convert_fusion.4
  580.9 2.9 convolution_convert_fusion.5
  583.8 2.7 pad_maximum_fusion.1
  587.8 4.6 convolution_convert_fusion.2
  592.4 2.9 convolution_convert_fusion.3
  599.1 6.3 fusion.125
  605.4 6.9 reshape.197
  612.3 5.9 copy.192
  619.1 20.6 %collective-permute-start.16 = (bf16[6,12,2,1536]{3,1,2,0:T(8,128)(2,1)}, bf16[6,12,2,1536]{3,1,2,0:T(8,128)(2,1)S(1)}, u32[]{:S(2)}, u32[]{:S(2)}) collective-permute-start(bf16[6,12,2,1536]{3,1,2,0:T(8,128)(2,1)} %get-tuple-element.405), channel_id=1, source_target_pairs={{0,1},{1,2},{2,3},{3,4},{4,5},{5,6},{6,7},{8,9},{9,10},{10,11},{11... | collective-permute-start | bytes 1327112 | tf_op jit(solution)/shard_map/ppermute | solution.py:17
  642.3 9.0 %copy.183 = f32[6,12,12,1536]{3,1,2,0:T(8,128)} copy(f32[6,12,12,1536]{3,2,1,0:T(8,128)} %reshape.197) | data formatting | bytes 10616832 | tf_op jit(solution)/shard_map/reshape | solution.py:304
  653.8 33.3 %all-reduce.10 = (bf16[768]{0:T(1024)(128)(2,1)S(1)}, bf16[768]{0:T(1024)(128)(2,1)}, bf16[768]{0:T(1024)(128)(2,1)}, bf16[768]{0:T(1024)(128)(2,1)}, bf16[3072]{0:T(1024)(128)(2,1)}) all-reduce(bf16[768]{0:T(1024)(128)(2,1)} %get-tuple-element.315, ...), channel_id=3, replica_groups=mesh['gy'=4,'gx'=8] {'gx'}, use_global_device_ids=true, to_apply=%region_18.19.clone | all-reduce | flops 6144 | bytes 24576
  691.2 20.8 %all-reduce.12 = (bf16[96]{0:T(256)(128)(2,1)}, bf16[96]{0:T(256)(128)(2,1)}, bf16[96]{0:T(256)(128)(2,1)}, bf16[96]{0:T(256)(128)(2,1)}, bf16[384]{0:T(512)(128)(2,1)S(1)}) all-reduce(bf16[96]{0:T(256)(128)(2,1)S(1)} %dynamic-slice.5, bf16[96]{0:T(256)(128)(2,1)S(1)} %dynamic-slice.7, ...), channel_id=1, replica_groups=mesh['gy'=4,'gx'=8] {'gy'}, use_global_device_ids=true, to_apply=%region_19.20 | all-reduce | flops 768 | bytes 3072 | tf_op jit(solution)/shard_map/psum | solution.py:347
  717.3 23.0 %reduce-scatter.14.cloned.1.call-done = bf16[96,3072]{1,0:T(8,128)(2,1)} async-done(((bf16[768,3072]{1,0:T(8,128)(2,1)}), bf16[96,3072]{1,0:T(8,128)(2,1)}) %reduce-scatter.14.cloned.1.call-update) | async-done | bytes 589840 | tf_op jit(solution)/shard_map/reduce_scatter | solution.py:328
  740.3 55.5 %reduce-scatter.16.cloned.1.call-done = bf16[384,768]{1,0:T(8,128)(2,1)} async-done(((bf16[3072,768]{1,0:T(8,128)(2,1)}), bf16[384,768]{1,0:T(8,128)(2,1)}) %reduce-scatter.16.cloned.1.call-update) | async-done | bytes 589840 | tf_op jit(solution)/shard_map/reduce_scatter | solution.py:334
  800.5 3.4 collective-permute-start.18
  806.5 8.8 collective-permute-done.18
  815.2 14.1 %collective-permute-done.19 = bf16[6,2,8,1536]{3,2,1,0:T(8,128)(2,1)S(1)} collective-permute-done((bf16[6,2,8,1536]{3,2,1,0:T(8,128)(2,1)S(1)}, bf16[6,2,8,1536]{3,2,1,0:T(8,128)(2,1)S(1)}, u32[]{:S(2)}, u32[]{:S(2)}) %collective-permute-start.19) | collective-permute-done | bytes 294944 | tf_op jit(solution)/shard_map/ppermute | solution.py:17
  831.1 52.5 %all-reduce.16.cloned.1.call-done = (bf16[192,768]{1,0:T(8,128)(2,1)}, bf16[96,2304]{1,0:T(8,128)(2,1)}, bf16[96,768]{1,0:T(8,128)(2,1)}, bf16[96,3072]{1,0:T(8,...) async-done(((bf16[192,768]{1,0:T(8,128)(2,1)}, bf16[96,2304]{1,0:T(8,128)(2,1)}, bf16[96,768]{1,0:T(8,128)(2,1)}, ...) | async-done | bytes 2359312 | tf_op jit(solution)/shard_map/psum | solution.py:346
  (574 shorter events, 307.7 us)
Async XLA Ops:
  7.2 14.0 %copy-start.23 = (bf16[6,8,8,1536]{3,2,1,0:T(8,128)(2,1)S(1)}, bf16[6,8,8,1536]{3,2,1,0:T(8,128)(2,1)}, u32[]{:S(2)}) copy-start(bf16[6,8,8,1536]{3,2,1,0:T(8,128)(2,1)} %param.26) | copy-start | bytes 3538948
  7.2 110.4 %all-gather.8.cloned.1.call-start = ((), (), s32[]{:S(2)}) async-start(), calls=%async_computation.7 | async-start | bytes 2654208 | tf_op jit(solution)/shard_map/all_gather | solution.py:151
  7.9 115.9 %all-gather.10.cloned.1.call-start = ((), (), s32[]{:S(2)}) async-start(), calls=%async_computation.8 | async-start | bytes 3981312 | tf_op jit(solution)/shard_map/all_gather | solution.py:154
  8.7 21.0 %copy-start.67 = (s32[5]{0:T(128)S(1)}, s32[5]{0:T(128)}, u32[]{:S(2)}) copy-start(s32[5]{0:T(128)} %param.29) | copy-start | bytes 64
  8.7 23.6 %copy-start.32 = (s32[6,8,8]{2,1,0:T(8,128)S(1)}, s32[6,8,8]{2,1,0:T(8,128)}, u32[]{:S(2)}) copy-start(s32[6,8,8]{2,1,0:T(8,128)} %param.27) | copy-start | bytes 4612
  8.7 221.3 %all-gather.12.cloned.1.call-start = ((), (), s32[]{:S(2)}) async-start(), calls=%async_computation.9 | async-start | bytes 1327104 | tf_op jit(solution)/shard_map/all_gather | solution.py:155
  9.4 228.3 %all-gather.14.cloned.1.call-start = ((), (), s32[]{:S(2)}) async-start(), calls=%async_computation.10 | async-start | bytes 5308416 | tf_op jit(solution)/shard_map/all_gather | solution.py:158
  10.0 260.4 %all-gather.16.cloned.1.call-start = ((), (), s32[]{:S(2)}) async-start(), calls=%async_computation.11 | async-start | bytes 5308416 | tf_op jit(solution)/shard_map/all_gather | solution.py:160
  10.6 268.9 %all-gather.18.cloned.1.call-start = ((), (), s32[]{:S(2)}) async-start(), calls=%async_computation.12 | async-start | bytes 1769472 | tf_op jit(solution)/shard_map/all_gather | solution.py:162
  16.1 84.4 %collective-permute-start.8 = (bf16[1,12,2,1]{1,2,3,0:T(2,128)(2,1)S(1)}, bf16[1,12,2,1]{1,2,3,0:T(2,128)(2,1)S(1)}, u32[]{:S(2)}, u32[]{:S(2)}) collective-permute-start(bf16[1,12,2,1]{1,2,3,0:T(2,128)(2,1)S(1)} %get-tuple-element.431), channel_id=1, source_target_pairs={{0,1},{1,2},{2,3},{3,4},{4,5},{5,6},{6,7},{8,9},{9,10},{10,11},{11... | collective-permute-start | bytes 152 | tf_op jit(solution)/shard_map/ppermute | solution.py:17
  18.5 82.0 %collective-permute-start.9 = (bf16[1,12,2,1]{1,2,3,0:T(2,128)(2,1)S(1)}, bf16[1,12,2,1]{1,2,3,0:T(2,128)(2,1)S(1)}, u32[]{:S(2)}, u32[]{:S(2)}) collective-permute-start(bf16[1,12,2,1]{1,2,3,0:T(2,128)(2,1)S(1)} %get-tuple-element.432), channel_id=1, source_target_pairs={{1,0},{2,1},{3,2},{4,3},{5,4},{6,5},{7,6},{9,8},{10,9},{11,10},{12... | collective-permute-start | bytes 152 | tf_op jit(solution)/shard_map/ppermute | solution.py:17
  21.4 73.8 %collective-permute-start.1 = (bf16[6,2,8,1536]{3,2,1,0:T(8,128)(2,1)S(1)}, bf16[6,2,8,1536]{3,2,1,0:T(8,128)(2,1)S(1)}, u32[]{:S(2)}, u32[]{:S(2)}) collective-permute-start(bf16[6,2,8,1536]{3,2,1,0:T(8,128)(2,1)S(1)} %get-tuple-element.422), channel_id=1, source_target_pairs={{8,0},{16,8},{24,16},{9,1},{17,9},{25,17},{10,2},{18,10},{26,18},{... | collective-permute-start | bytes 884744 | tf_op jit(solution)/shard_map/ppermute | solution.py:28
  22.7 72.5 %collective-permute-start = (bf16[6,2,8,1536]{3,2,1,0:T(8,128)(2,1)S(1)}, bf16[6,2,8,1536]{3,2,1,0:T(8,128)(2,1)S(1)}, u32[]{:S(2)}, u32[]{:S(2)}) collective-permute-start(bf16[6,2,8,1536]{3,2,1,0:T(8,128)(2,1)S(1)} %get-tuple-element.421), channel_id=1, source_target_pairs={{0,8},{8,16},{16,24},{1,9},{9,17},{17,25},{2,10},{10,18},{18,26},{... | collective-permute-start | bytes 884744 | tf_op jit(solution)/shard_map/ppermute | solution.py:25
  27.6 689.6 %reduce-scatter.18.cloned.1.call-start = ((), (), s32[]{:S(2)}) async-start(), calls=%async_computation.18 | async-start | bytes 884736 | tf_op jit(solution)/shard_map/reduce_scatter | solution.py:337
  32.3 68.3 %copy-start.50 = (f32[1,12,4,1]{1,2,3,0:T(4,128)}, f32[1,12,4,1]{1,2,3,0:T(4,128)S(1)}, u32[]{:S(2)}) copy-start(f32[1,12,4,1]{1,2,3,0:T(4,128)S(1)} %slice.261) | copy-start | bytes 580
  37.6 25.7 %copy-start.63 = (bf16[384]{0:T(512)(128)(2,1)S(1)}, bf16[384]{0:T(512)(128)(2,1)}, u32[]{:S(2)}) copy-start(bf16[384]{0:T(512)(128)(2,1)} %param.41) | copy-start | bytes 2308
  37.6 38.8 %copy-start.31 = (bf16[96,512]{1,0:T(8,128)(2,1)S(1)}, bf16[96,512]{1,0:T(8,128)(2,1)}, u32[]{:S(2)}) copy-start(bf16[96,512]{1,0:T(8,128)(2,1)} %param.43) | copy-start | bytes 294916
  63.1 60.7 %copy-start.60 = (f32[768]{0:T(1024)}, f32[768]{0:T(1024)S(1)}, u32[]{:S(2)}) copy-start(f32[768]{0:T(1024)S(1)} %convert_element_type.287) | copy-start | bytes 9220
  63.2 60.7 %copy-start.52 = (f32[768]{0:T(1024)}, f32[768]{0:T(1024)S(1)}, u32[]{:S(2)}) copy-start(f32[768]{0:T(1024)S(1)} %convert_element_type.286) | copy-start | bytes 9220
  76.3 159.5 %copy-start.42 = (f32[768]{0:T(1024)}, f32[768]{0:T(1024)S(1)}, u32[]{:S(2)}) copy-start(f32[768]{0:T(1024)S(1)} %convert_element_type.293) | copy-start | bytes 9220
  96.1 11.4 %collective-permute-start.3 = (bf16[6,12,2,1536]{3,1,2,0:T(8,128)(2,1)S(1)}, bf16[6,12,2,1536]{3,1,2,0:T(8,128)(2,1)S(1)}, u32[]{:S(2)}, u32[]{:S(2)}) collective-permute-start(bf16[6,12,2,1536]{3,1,2,0:T(8,128)(2,1)S(1)} %copy.156), channel_id=1, source_target_pairs={{1,0},{2,1},{3,2},{4,3},{5,4},{6,5},{7,6},{9,8},{10,9},{11,10},{12... | collective-permute-start | bytes 1327112 | tf_op jit(solution)/shard_map/ppermute | solution.py:28
  97.4 10.5 %collective-permute-start.2 = (bf16[6,12,2,1536]{3,1,2,0:T(8,128)(2,1)S(1)}, bf16[6,12,2,1536]{3,1,2,0:T(8,128)(2,1)S(1)}, u32[]{:S(2)}, u32[]{:S(2)}) collective-permute-start(bf16[6,12,2,1536]{3,1,2,0:T(8,128)(2,1)S(1)} %copy.155), channel_id=1, source_target_pairs={{0,1},{1,2},{2,3},{3,4},{4,5},{5,6},{6,7},{8,9},{9,10},{10,11},{11... | collective-permute-start | bytes 1327112 | tf_op jit(solution)/shard_map/ppermute | solution.py:25
  100.6 11.8 %copy-start.56 = (f32[1,12,2,1]{1,2,3,0:T(2,128)}, f32[1,12,2,1]{1,2,3,0:T(2,128)S(1)}, u32[]{:S(2)}) copy-start(f32[1,12,2,1]{1,2,3,0:T(2,128)S(1)} %get-tuple-element.427) | copy-start | bytes 292
  100.6 11.8 %copy-start.58 = (f32[1,12,2,1]{1,2,3,0:T(2,128)}, f32[1,12,2,1]{1,2,3,0:T(2,128)S(1)}, u32[]{:S(2)}) copy-start(f32[1,12,2,1]{1,2,3,0:T(2,128)S(1)} %get-tuple-element.428) | copy-start | bytes 292
  101.3 212.6 %collective-permute-start.10 = (bf16[1,2,8,1]{1,2,3,0:T(8,128)(2,1)}, bf16[1,2,8,1]{1,2,3,0:T(8,128)(2,1)}, u32[]{:S(2)}, u32[]{:S(2)}) collective-permute-start(bf16[1,2,8,1]{1,2,3,0:T(8,128)(2,1)} %get-tuple-element.433), channel_id=1, source_target_pairs={{0,8},{8,16},{16,24},{1,9},{9,17},{17,25},{2,10},{10,18},{18,26},{... | collective-permute-start | bytes 104 | tf_op jit(solution)/shard_map/ppermute | solution.py:17
  106.2 207.6 %collective-permute-start.11 = (bf16[1,2,8,1]{1,2,3,0:T(8,128)(2,1)}, bf16[1,2,8,1]{1,2,3,0:T(8,128)(2,1)}, u32[]{:S(2)}, u32[]{:S(2)}) collective-permute-start(bf16[1,2,8,1]{1,2,3,0:T(8,128)(2,1)} %get-tuple-element.434), channel_id=1, source_target_pairs={{8,0},{16,8},{24,16},{9,1},{17,9},{25,17},{10,2},{18,10},{26,18},{... | collective-permute-start | bytes 104 | tf_op jit(solution)/shard_map/ppermute | solution.py:17
  123.3 8.2 copy-start.2
  123.3 8.2 copy-start.40
  123.8 7.8 copy-start.46
  123.8 7.8 copy-start.54
  235.4 39.9 %copy-start = (f32[864,768]{1,0:T(8,128)}, f32[864,768]{1,0:T(8,128)S(1)}, u32[]{:S(2)}) copy-start(f32[864,768]{1,0:T(8,128)S(1)} %get-tuple-element.448) | copy-start | bytes 7962628
  235.8 19.6 %copy-start.48 = (f32[864]{0:T(1024)}, f32[864]{0:T(1024)S(1)}, u32[]{:S(2)}) copy-start(f32[864]{0:T(1024)S(1)} %multiply_reduce_fusion.5) | copy-start | bytes 10372
  236.2 19.3 %copy-start.44 = (f32[864]{0:T(1024)}, f32[864]{0:T(1024)S(1)}, u32[]{:S(2)}) copy-start(f32[864]{0:T(1024)S(1)} %fusion.99) | copy-start | bytes 10372
  237.7 17.8 %copy-start.17 = (bf16[864,768]{1,0:T(8,128)(2,1)S(1)}, bf16[864,768]{1,0:T(8,128)(2,1)}, u32[]{:S(2)}) copy-start(bf16[864,768]{1,0:T(8,128)(2,1)} %add_convert_fusion.4) | copy-start | bytes 3981316
  237.7 17.8 %copy-start.64 = (bf16[768,3072]{1,0:T(8,128)(2,1)S(1)}, bf16[768,3072]{1,0:T(8,128)(2,1)}, u32[]{:S(2)}) copy-start(bf16[768,3072]{1,0:T(8,128)(2,1)} %all-gather.14.cloned.1.call-done) | copy-start | bytes 14155780
  299.8 14.0 %copy-start.51 = (f32[1,12,4,1]{1,2,3,0:T(4,128)S(1)}, f32[1,12,4,1]{1,2,3,0:T(4,128)}, u32[]{:S(2)}) copy-start(f32[1,12,4,1]{1,2,3,0:T(4,128)} %copy-done.50) | copy-start | bytes 580
  299.8 14.0 %copy-start.57 = (f32[1,12,2,1]{1,2,3,0:T(2,128)S(1)}, f32[1,12,2,1]{1,2,3,0:T(2,128)}, u32[]{:S(2)}) copy-start(f32[1,12,2,1]{1,2,3,0:T(2,128)} %copy-done.56) | copy-start | bytes 292
  299.8 14.0 %copy-start.59 = (f32[1,12,2,1]{1,2,3,0:T(2,128)S(1)}, f32[1,12,2,1]{1,2,3,0:T(2,128)}, u32[]{:S(2)}) copy-start(f32[1,12,2,1]{1,2,3,0:T(2,128)} %copy-done.58) | copy-start | bytes 292
  300.5 16.7 %collective-permute-start.4 = (bf16[6,12,2,1536]{3,1,2,0:T(8,128)(2,1)S(1)}, bf16[6,12,2,1536]{3,1,2,0:T(8,128)(2,1)S(1)}, u32[]{:S(2)}, u32[]{:S(2)}) collective-permute-start(bf16[6,12,2,1536]{3,1,2,0:T(8,128)(2,1)S(1)} %copy.167), channel_id=1, source_target_pairs={{0,1},{1,2},{2,3},{3,4},{4,5},{5,6},{6,7},{8,9},{9,10},{10,11},{11... | collective-permute-start | bytes 1327112 | tf_op jit(solution)/shard_map/ppermute | solution.py:17
  312.4 4.9 collective-permute-start.5
  322.9 7.9 collective-permute-start.6
  326.6 9.3 %collective-permute-start.7 = (bf16[6,2,8,1536]{3,2,1,0:T(8,128)(2,1)S(1)}, bf16[6,2,8,1536]{3,2,1,0:T(8,128)(2,1)S(1)}, u32[]{:S(2)}, u32[]{:S(2)}) collective-permute-start(bf16[6,2,8,1536]{3,2,1,0:T(8,128)(2,1)S(1)} %get-tuple-element.418), channel_id=1, source_target_pairs={{8,0},{16,8},{24,16},{9,1},{17,9},{25,17},{10,2},{18,10},{26,18},{... | collective-permute-start | bytes 884744 | tf_op jit(solution)/shard_map/ppermute | solution.py:17
  337.8 12.3 %collective-permute-start.13 = (f32[6,2,8,1536]{3,2,1,0:T(8,128)S(1)}, f32[6,2,8,1536]{3,2,1,0:T(8,128)S(1)}, u32[]{:S(2)}, u32[]{:S(2)}) collective-permute-start(f32[6,2,8,1536]{3,2,1,0:T(8,128)S(1)} %get-tuple-element.414), channel_id=1, source_target_pairs={{8,0},{16,8},{24,16},{9,1},{17,9},{25,17},{10,2},{18,10},{26,18},{... | collective-permute-start | bytes 1769480 | tf_op jit(solution)/shard_map/ppermute | solution.py:28
  339.1 12.8 %collective-permute-start.12 = (f32[6,2,8,1536]{3,2,1,0:T(8,128)S(1)}, f32[6,2,8,1536]{3,2,1,0:T(8,128)S(1)}, u32[]{:S(2)}, u32[]{:S(2)}) collective-permute-start(f32[6,2,8,1536]{3,2,1,0:T(8,128)S(1)} %get-tuple-element.413), channel_id=1, source_target_pairs={{0,8},{8,16},{16,24},{1,9},{9,17},{17,25},{2,10},{10,18},{18,26},{... | collective-permute-start | bytes 1769480 | tf_op jit(solution)/shard_map/ppermute | solution.py:25
  353.9 15.9 %collective-permute-start.15 = (f32[6,12,2,1536]{3,1,2,0:T(8,128)}, f32[6,12,2,1536]{3,1,2,0:T(8,128)}, u32[]{:S(2)}, u32[]{:S(2)}) collective-permute-start(f32[6,12,2,1536]{3,1,2,0:T(8,128)} %copy.173), channel_id=1, source_target_pairs={{1,0},{2,1},{3,2},{4,3},{5,4},{6,5},{7,6},{9,8},{10,9},{11,10},{12... | collective-permute-start | bytes 2654216 | tf_op jit(solution)/shard_map/ppermute | solution.py:28
  356.4 15.5 %collective-permute-start.14 = (f32[6,12,2,1536]{3,1,2,0:T(8,128)}, f32[6,12,2,1536]{3,1,2,0:T(8,128)}, u32[]{:S(2)}, u32[]{:S(2)}) collective-permute-start(f32[6,12,2,1536]{3,1,2,0:T(8,128)} %copy.172), channel_id=1, source_target_pairs={{0,1},{1,2},{2,3},{3,4},{4,5},{5,6},{6,7},{8,9},{9,10},{10,11},{11... | collective-permute-start | bytes 2654216 | tf_op jit(solution)/shard_map/ppermute | solution.py:25
  391.6 14.6 %copy-start.19 = (bf16[864,768]{1,0:T(8,128)(2,1)}, bf16[864,768]{1,0:T(8,128)(2,1)S(1)}, u32[]{:S(2)}) copy-start(bf16[864,768]{1,0:T(8,128)(2,1)S(1)} %get-tuple-element.451) | copy-start | bytes 3981316
  393.5 323.8 %reduce-scatter.12.cloned.1.call-start = ((), (), s32[]{:S(2)}) async-start(), calls=%async_computation.15 | async-start | bytes 1327104 | tf_op jit(solution)/shard_map/reduce_scatter | solution.py:319
  401.2 12.4 %slice-start = ((s8[4718592]{0:T(1024)(128)(4,1)}), s8[4194304]{0:T(1024)(128)(4,1)S(1)}, s32[]{:S(2)}) async-start(s8[4718592]{0:T(1024)(128)(4,1)} %bitcast.171), calls=%async_computation.21 | async-start | bytes 8388608
  406.1 7.5 copy-start.1
  406.2 7.5 copy-start.37
  406.2 7.5 copy-start.43
  406.2 7.5 copy-start.45
  422.6 294.7 %reduce-scatter.20.cloned.1.call-start = ((), (), s32[]{:S(2)}) async-start(), calls=%async_computation.19 | async-start | bytes 1769472 | tf_op jit(solution)/shard_map/reduce_scatter | solution.py:340
  434.1 283.2 %reduce-scatter.8.cloned.1.call-start = ((), (), s32[]{:S(2)}) async-start(), calls=%async_computation.13 | async-start | bytes 2654208 | tf_op jit(solution)/shard_map/reduce_scatter | solution.py:307
  566.4 150.9 %reduce-scatter.10.cloned.1.call-start = ((), (), s32[]{:S(2)}) async-start(), calls=%async_computation.14 | async-start | bytes 3981312 | tf_op jit(solution)/shard_map/reduce_scatter | solution.py:316
  574.6 165.7 %reduce-scatter.14.cloned.1.call-start = ((), (), s32[]{:S(2)}) async-start(), calls=%async_computation.16 | async-start | bytes 5308416 | tf_op jit(solution)/shard_map/reduce_scatter | solution.py:328
  586.5 209.3 %reduce-scatter.16.cloned.1.call-start = ((), (), s32[]{:S(2)}) async-start(), calls=%async_computation.17 | async-start | bytes 5308416 | tf_op jit(solution)/shard_map/reduce_scatter | solution.py:334
  597.8 285.8 %all-reduce.16.cloned.1.call-start = ((), (), s32[]{:S(2)}) async-start(), calls=%async_computation.20 | async-start | bytes 4718592 | tf_op jit(solution)/shard_map/psum | solution.py:346
  619.1 176.8 %collective-permute-start.16 = (bf16[6,12,2,1536]{3,1,2,0:T(8,128)(2,1)}, bf16[6,12,2,1536]{3,1,2,0:T(8,128)(2,1)S(1)}, u32[]{:S(2)}, u32[]{:S(2)}) collective-permute-start(bf16[6,12,2,1536]{3,1,2,0:T(8,128)(2,1)} %get-tuple-element.405), channel_id=1, source_target_pairs={{0,1},{1,2},{2,3},{3,4},{4,5},{5,6},{6,7},{8,9},{9,10},{10,11},{11... | collective-permute-start | bytes 1327112 | tf_op jit(solution)/shard_map/ppermute | solution.py:17
  639.7 156.2 %collective-permute-start.17 = (bf16[6,12,2,1536]{3,1,2,0:T(8,128)(2,1)S(1)}, bf16[6,12,2,1536]{3,1,2,0:T(8,128)(2,1)S(1)}, u32[]{:S(2)}, u32[]{:S(2)}) collective-permute-start(bf16[6,12,2,1536]{3,1,2,0:T(8,128)(2,1)S(1)} %get-tuple-element.406), channel_id=1, source_target_pairs={{1,0},{2,1},{3,2},{4,3},{5,4},{6,5},{7,6},{9,8},{10,9},{11,10},{12... | collective-permute-start | bytes 1327112 | tf_op jit(solution)/shard_map/ppermute | solution.py:17
  800.5 14.8 %collective-permute-start.18 = (bf16[6,2,8,1536]{3,2,1,0:T(8,128)(2,1)S(1)}, bf16[6,2,8,1536]{3,2,1,0:T(8,128)(2,1)S(1)}, u32[]{:S(2)}, u32[]{:S(2)}) collective-permute-start(bf16[6,2,8,1536]{3,2,1,0:T(8,128)(2,1)S(1)} %get-tuple-element.415), channel_id=1, source_target_pairs={{0,8},{8,16},{16,24},{1,9},{9,17},{17,25},{2,10},{10,18},{18,26},{... | collective-permute-start | bytes 884744 | tf_op jit(solution)/shard_map/ppermute | solution.py:17
  803.9 25.5 %collective-permute-start.19 = (bf16[6,2,8,1536]{3,2,1,0:T(8,128)(2,1)S(1)}, bf16[6,2,8,1536]{3,2,1,0:T(8,128)(2,1)S(1)}, u32[]{:S(2)}, u32[]{:S(2)}) collective-permute-start(bf16[6,2,8,1536]{3,2,1,0:T(8,128)(2,1)S(1)} %get-tuple-element.416), channel_id=1, source_target_pairs={{8,0},{16,8},{24,16},{9,1},{17,9},{25,17},{10,2},{18,10},{26,18},{... | collective-permute-start | bytes 884744 | tf_op jit(solution)/shard_map/ppermute | solution.py:17
  806.3 23.1 %copy-start.30 = (f32[6,8,8]{2,1,0:T(8,128)S(1)}, f32[6,8,8]{2,1,0:T(8,128)}, u32[]{:S(2)}) copy-start(f32[6,8,8]{2,1,0:T(8,128)} %get-tuple-element.425) | copy-start | bytes 4612
  (53 other events, 216.8 us)
Sparse Core Ops, SparseCore 0:
  9.7 34.3 all-gather.7
  45.7 45.1 all-gather.9
  92.5 26.2 all-gather.11
  120.3 50.4 all-gather.13
  172.3 50.5 all-gather.15
  224.4 23.8 all-gather.17
  393.6 61.6 reduce-scatter.17
  458.2 30.9 reduce-scatter.11
  491.7 32.6 reduce-scatter.19
  566.5 66.3 reduce-scatter.7
  635.3 49.8 reduce-scatter.9
  687.3 52.9 reduce-scatter.13
  742.6 53.1 reduce-scatter.15
  799.6 83.9 all-reduce.15
where the time goes:
time: 912 us; the launch traced here: 900 us
  matrix products  292 us (32%)
  waiting for transfers between devices  172 us (19%)
  local copies, waits for them, and re-layouts  140 us (15%)
  blocking collectives  105 us (12%)
  starting transfers between devices  86.1 us (9%)
  other arithmetic  83.4 us (9%)
  between operations  19.9 us (2%)
    dot_general x111, matrix products, matmul(): return jnp.dot(left, right, preferred_element_type=jnp.float32)  292 us
    reduce_scatter x1, waiting for transfers between devices, on_device(): lax.psum_scatter(grad_fc2.astype(jnp.bfloat16), 'gx', scatter_dimension=0...  55.5 us
    ppermute x12, starting transfers between devices, from_behind(): return lax.ppermute(block, axis, route)  54.5 us
    psum x1, waiting for transfers between devices, on_device(): lax.psum(shares[0].astype(jnp.bfloat16), 'gy').astype(jnp.float32)  52.5 us
    unnamed x2, blocking collectives  52.2 us
    unnamed x186, local copies, waits for them, and re-layouts  32.2 us
    ppermute x12, waiting for transfers between devices, from_behind(): return lax.ppermute(block, axis, route)  29.8 us
    ppermute x4, starting transfers between devices, with_halo(): lax.ppermute(lax.slice_in_dim(block, block.shape[dim] - width, None, axis...  25.8 us
  transfers between devices with their start and end apart: 34, of which 10 were waited for; matrix products, arithmetic and copies ran while one was open for 51% of the time, Pallas kernels for 0%

commit v1 on v0

v1 whole, which is shorter than its diff:
```python
import functools
import jax
import jax.numpy as jnp
import numpy as np
from jax import lax
from jax.experimental import pallas as pl
from jax.experimental.pallas import tpu as pltpu
from jax.sharding import PartitionSpec as P

HEADS = 12
MARGIN = 2
norm_eps = 1e-06
VMEM_BYTES = 56 * 1024 * 1024
f32, bf16 = jnp.float32, jnp.bfloat16


def params():
    return pltpu.CompilerParams(vmem_limit_bytes=VMEM_BYTES)


def cost(flops, nbytes):
    return pl.CostEstimate(flops=int(flops), bytes_accessed=int(nbytes), transcendentals=0)


def dot(a, b, ca=1, cb=0):
    return lax.dot_general(a, b, (((ca,), (cb,)), ((), ())), preferred_element_type=f32)


def whole(shape):
    return pl.BlockSpec(shape, lambda *_: (0,) * len(shape))


def rows(block, width):
    return pl.BlockSpec((block, width), lambda i: (i, 0))


def last_part(width):
    return pl.BlockSpec((1, width, width), lambda i: (3, 0, 0))


def norm_parts(hidden):
    center = jnp.mean(hidden, axis=-1, keepdims=True)
    centered = hidden - center
    spread = jnp.mean(centered * centered, axis=-1, keepdims=True)
    rstd = lax.rsqrt(spread + norm_eps)
    return centered * rstd, rstd


def token_block(tokens):
    for parts in (3, 2):
        if tokens % (16 * parts) == 0:
            return tokens // parts
    return tokens


def stacked(ref, depth):
    shares = ref.shape[0]
    return ref[:, : depth // shares, :].reshape(depth, ref.shape[2])


def embed_kernel(ext_ref, w_ref, pick_ref, table_ref, gain_ref, shift_ref, h0_ref, a_ref):
    hidden = dot(ext_ref[...], stacked(w_ref, ext_ref.shape[1])) + dot(pick_ref[...], table_ref[...])
    h0_ref[...] = hidden
    xhat, _ = norm_parts(hidden)
    a_ref[...] = (xhat * gain_ref[...] + shift_ref[...]).astype(bf16)


def embed(ext, patch_w, pick, table, gain, shift):
    tokens, depth = ext.shape
    width = patch_w.shape[2]
    tb = token_block(tokens)
    return pl.pallas_call(
        embed_kernel,
        grid=(tokens // tb,),
        in_specs=[rows(tb, depth), whole(patch_w.shape), rows(tb, pick.shape[1]),
                  whole(table.shape), whole(gain.shape), whole(shift.shape)],
        out_specs=[rows(tb, width), rows(tb, width)],
        out_shape=[jax.ShapeDtypeStruct((tokens, width), f32),
                   jax.ShapeDtypeStruct((tokens, width), bf16)],
        compiler_params=params(),
        cost_estimate=cost(2 * tokens * depth * width, tokens * depth * 2 + depth * width * 2 + tokens * width * 6),
        name="embed",
    )(ext, patch_w, pick, table, gain, shift)


def columns_kernel(a_ref, w_ref, o_ref):
    o_ref[...] = dot(a_ref[...], w_ref[0]).astype(o_ref.dtype)


def project(a, parts, count):
    tokens, width = a.shape
    half = width // 2
    return pl.pallas_call(
        columns_kernel,
        grid=(2 * count,),
        in_specs=[whole(a.shape), pl.BlockSpec((1, width, half), lambda i: (i // 2, 0, i % 2))],
        out_specs=pl.BlockSpec((tokens, half), lambda i: (0, i)),
        out_shape=jax.ShapeDtypeStruct((tokens, count * width), bf16),
        compiler_params=params(),
        cost_estimate=cost(2 * tokens * width * width * count, a.size * 2 + width * width * count * 2 + tokens * width * count * 2),
        name="project",
    )(a, parts)


def three_parts(value):
    first = value.astype(bf16)
    rest = value - first.astype(f32)
    second = rest.astype(bf16)
    third = (rest - second.astype(f32)).astype(bf16)
    return first, second, third


def in_lanes(parts, lane, tail):
    out = tail
    for spot, part in reversed(list(enumerate(parts))):
        out = jnp.where(lane == spot, part.astype(f32), out)
    return out.astype(bf16)


def attn_fwd_kernel(q_ref, k_ref, v_ref, kx_ref, o_ref, qx_ref, *, block, scale):
    tokens, pair = q_ref.shape
    half = pair // 2
    k_aug = jnp.concatenate([k_ref[...], kx_ref[...]], axis=1)
    v_aug = jnp.concatenate([v_ref[...], jnp.ones((tokens, pair), bf16)], axis=1)
    lane = lax.broadcasted_iota(jnp.int32, (block, pair), 1)
    for start in range(0, tokens, block):
        q_blk = q_ref[start : start + block, :].astype(f32) * scale
        outs = []
        for j in range(2):
            mine = (lane >= half) if j else (lane < half)
            q_aug = jnp.concatenate(
                [jnp.where(mine, q_blk, 0.0).astype(bf16),
                 jnp.where(lane == 3, 1.0, 0.0).astype(bf16)], axis=1)
            s = dot(q_aug, k_aug, 1, 1)
            top = jnp.max(s, axis=1, keepdims=True)
            p = jnp.exp(s - top).astype(bf16)
            mixed = dot(p, v_aug)
            total = mixed[:, pair:]
            outs.append(mixed[:, :pair] / total)
            lse = jnp.log(total) + top
            qx_ref[j, start : start + block, :] = in_lanes(
                three_parts(-lse), lane, jnp.where(lane == 3, 1.0, 0.0))
        o_ref[start : start + block, :] = jnp.where(lane < half, outs[0], outs[1]).astype(bf16)


def attn_fwd(qkv, kx, scale):
    tokens = qkv.shape[0]
    width = qkv.shape[1] // 3
    pairs = HEADS // 2
    pw = width // pairs
    spec = lambda part: pl.BlockSpec((tokens, pw), lambda h, part=part: (0, part * pairs + h))
    return pl.pallas_call(
        functools.partial(attn_fwd_kernel, block=token_block(tokens), scale=scale),
        grid=(pairs,),
        in_specs=[spec(0), spec(1), spec(2), whole(kx.shape)],
        out_specs=[pl.BlockSpec((tokens, pw), lambda h: (0, h)),
                   pl.BlockSpec((2, tokens, pw), lambda h: (h, 0, 0))],
        out_shape=[jax.ShapeDtypeStruct((tokens, width), bf16),
                   jax.ShapeDtypeStruct((HEADS, tokens, pw), bf16)],
        compiler_params=params(),
        cost_estimate=cost(2 * 4 * HEADS * tokens * tokens * 256, qkv.size * 2 + tokens * width * 2),
        name="attn_fwd",
    )(qkv, qkv, qkv, kx)


def attn_bwd_kernel(q_ref, k_ref, v_ref, do_ref, o_ref, qx_ref, kx_ref, d_ref, *, block, scale):
    tokens, pair = q_ref.shape
    half = pair // 2
    lane = lax.broadcasted_iota(jnp.int32, (tokens, pair), 1)
    q_all = q_ref[...].astype(f32) * scale
    do_all = do_ref[...].astype(f32)
    prod = do_all * o_ref[...].astype(f32)
    kx = kx_ref[...]
    dq = [None, None]
    dk = [None] * (tokens // block)
    dv = [None] * (tokens // block)
    for j in range(2):
        mine = (lane >= half) if j else (lane < half)
        q_j = jnp.where(mine, q_all, 0.0).astype(bf16)
        do_j = jnp.where(mine, do_all, 0.0).astype(bf16)
        delta = jnp.sum(jnp.where(mine, prod, 0.0), axis=1, keepdims=True)
        dox = in_lanes(three_parts(-delta), lane, jnp.zeros_like(prod))
        q_aug = jnp.concatenate([q_j, qx_ref[j]], axis=1)
        do_aug = jnp.concatenate([do_j, dox], axis=1)
        for b in range(tokens // block):
            at = slice(b * block, (b + 1) * block)
            k_blk = k_ref[at, :]
            sT = dot(jnp.concatenate([k_blk, kx[at]], axis=1), q_aug, 1, 1)
            pT = jnp.exp(sT)
            dpT = dot(jnp.concatenate([v_ref[at, :], kx[at]], axis=1), do_aug, 1, 1)
            dsT = (pT * dpT).astype(bf16)
            dv_b = dot(pT.astype(bf16), do_j)
            dk_b = dot(dsT, q_j)
            dq_b = dot(dsT, k_blk, 0, 0)
            dv[b] = dv_b if dv[b] is None else dv[b] + dv_b
            dk[b] = dk_b if dk[b] is None else dk[b] + dk_b
            dq[j] = dq_b if dq[j] is None else dq[j] + dq_b
    for b in range(tokens // block):
        at = slice(b * block, (b + 1) * block)
        d_ref[1, at, :] = dk[b].astype(bf16)
        d_ref[2, at, :] = dv[b].astype(bf16)
    d_ref[0] = (jnp.where(lane < half, dq[0], dq[1]) * scale).astype(bf16)


def attn_bwd(qkv, do, o, qx, kx, scale):
    tokens = qkv.shape[0]
    width = qkv.shape[1] // 3
    pairs = HEADS // 2
    pw = width // pairs
    spec = lambda part: pl.BlockSpec((tokens, pw), lambda h, part=part: (0, part * pairs + h))
    one = pl.BlockSpec((tokens, pw), lambda h: (0, h))
    return pl.pallas_call(
        functools.partial(attn_bwd_kernel, block=token_block(tokens), scale=scale),
        grid=(pairs,),
        in_specs=[spec(0), spec(1), spec(2), one, one,
                  pl.BlockSpec((2, tokens, pw), lambda h: (h, 0, 0)), whole(kx.shape)],
        out_specs=pl.BlockSpec((3, tokens, pw), lambda h: (0, 0, h)),
        out_shape=jax.ShapeDtypeStruct((3, tokens, width), bf16),
        compiler_params=params(),
        cost_estimate=cost(2 * 5 * HEADS * tokens * tokens * 256, qkv.size * 2 + tokens * width * 10),
        name="attn_bwd",
    )(qkv, qkv, qkv, do, o, qx, kx)


def proj_kernel(o_ref, w_ref, h0_ref, gain_ref, shift_ref, h1_ref, c_ref):
    hidden = h0_ref[...] + dot(o_ref[...], w_ref[0])
    h1_ref[...] = hidden
    xhat, _ = norm_parts(hidden)
    c_ref[...] = (xhat * gain_ref[...] + shift_ref[...]).astype(bf16)


def proj_norm(o, proj_w, h0, gain, shift):
    tokens, width = o.shape
    tb = token_block(tokens)
    return pl.pallas_call(
        proj_kernel,
        grid=(tokens // tb,),
        in_specs=[rows(tb, width), last_part(width), rows(tb, width), whole(gain.shape), whole(shift.shape)],
        out_specs=[rows(tb, width), rows(tb, width)],
        out_shape=[jax.ShapeDtypeStruct((tokens, width), f32),
                   jax.ShapeDtypeStruct((tokens, width), bf16)],
        compiler_params=params(),
        cost_estimate=cost(2 * tokens * width * width, tokens * width * 12 + width * width * 2),
        name="proj_norm",
    )(o, proj_w, h0, gain, shift)


def mlp_fwd_kernel(c_ref, fc1_ref, b_ref, fc2_ref, h1_ref, u_ref, g_ref, h2_ref, acc_ref):
    step = pl.program_id(0)
    pre = dot(c_ref[...], fc1_ref[0]) + b_ref[...]
    cdf = 0.5 * (1.0 + lax.erf(pre * np.float32(0.5 ** 0.5)))
    act = (pre * cdf).astype(bf16)
    u_ref[...] = act
    g_ref[...] = (cdf + pre * jnp.exp(-0.5 * pre * pre) * np.float32((2 * np.pi) ** -0.5)).astype(bf16)
    part = dot(act, fc2_ref[...])

    @pl.when(step == 0)
    def _():
        acc_ref[...] = h1_ref[...] + part

    @pl.when(step > 0)
    def _():
        acc_ref[...] += part

    @pl.when(step == pl.num_programs(0) - 1)
    def _():
        h2_ref[...] = acc_ref[...].astype(bf16)


def mlp_fwd(c, fc1, bias, fc2, h1):
    tokens, width = c.shape
    parts, _, block = fc1.shape
    ff = parts * block
    cols = lambda n: pl.BlockSpec((n, block), lambda i: (0, i))
    return pl.pallas_call(
        mlp_fwd_kernel,
        grid=(ff // block,),
        in_specs=[whole(c.shape), pl.BlockSpec((1, width, block), lambda i: (i, 0, 0)), cols(1),
                  pl.BlockSpec((block, width), lambda i: (i, 0)), whole(h1.shape)],
        out_specs=[cols(tokens), cols(tokens), whole(c.shape)],
        out_shape=[jax.ShapeDtypeStruct((tokens, ff), bf16), jax.ShapeDtypeStruct((tokens, ff), bf16),
                   jax.ShapeDtypeStruct((tokens, width), bf16)],
        scratch_shapes=[pltpu.VMEM((tokens, width), f32)],
        compiler_params=params(),
        cost_estimate=cost(4 * tokens * width * ff, tokens * ff * 4 + width * ff * 4 + tokens * width * 8),
        name="mlp_fwd",
    )(c, fc1, bias, fc2, h1)


def split_rows(value, core, keep_ref, send_ref, chips):
    width = value.shape[1]
    value = value.astype(bf16).reshape(chips, 2, value.shape[0] // chips // 2, width)
    even, odd = value[:, 0], value[:, 1]

    @pl.when(core == 0)
    def _():
        keep_ref[...] = even
        send_ref[...] = odd

    @pl.when(core == 1)
    def _():
        keep_ref[...] = odd
        send_ref[...] = even


def mlp_bwd_kernel(pos_ref, dm_ref, c_ref, u_ref, g_ref, fc1_ref, fc2_ref, dc_ref, gb_ref, k1_ref, s1_ref, k2_ref, s2_ref, *, chips):
    step = pl.program_id(0)
    core = pos_ref[2]
    dm = dm_ref[...]
    df32 = dot(dm, fc2_ref[...], 1, 1) * g_ref[...].astype(f32)
    df = df32.astype(bf16)
    gb_ref[...] = jnp.sum(df.astype(f32), axis=0, keepdims=True)
    parts, rows_each = k2_ref.shape[0], k2_ref.shape[2]
    width = dm.shape[1]
    grad2 = dot(u_ref[...], dm, 0, 0).astype(bf16).reshape(2, parts, rows_each, width)
    split_two(grad2, core, k2_ref, s2_ref)
    split_rows(dot(c_ref[...], df, 0, 0), core, k1_ref.at[0], s1_ref.at[0], chips)
    part = dot(df, fc1_ref[0], 1, 1)

    @pl.when(step == 0)
    def _():
        dc_ref[...] = part

    @pl.when(step > 0)
    def _():
        dc_ref[...] += part


def split_two(pair, core, keep_ref, send_ref):
    @pl.when(core == 0)
    def _():
        keep_ref[:, 0] = pair[0]
        send_ref[:, 0] = pair[1]

    @pl.when(core == 1)
    def _():
        keep_ref[:, 0] = pair[1]
        send_ref[:, 0] = pair[0]


def mlp_bwd(pos, dm, c, u, g, fc1, fc2, chips):
    tokens, width = c.shape
    parts, _, block = fc1.shape
    ff = parts * block
    rows1, rows2 = width // chips // 2, ff // chips // 2 // parts
    cols = lambda n: pl.BlockSpec((n, block), lambda i, _: (0, i))
    by_part = pl.BlockSpec((1, chips, rows1, block), lambda i, _: (i, 0, 0, 0))
    by_chip = pl.BlockSpec((parts, 1, rows2, width), lambda i, _: (0, i, 0, 0))
    grad1 = jax.ShapeDtypeStruct((parts, chips, rows1, block), bf16)
    grad2 = jax.ShapeDtypeStruct((parts, chips, rows2, width), bf16)
    return pl.pallas_call(
        functools.partial(mlp_bwd_kernel, chips=chips),
        grid_spec=pltpu.PrefetchScalarGridSpec(
            num_scalar_prefetch=1,
            grid=(parts,),
            in_specs=[whole(dm.shape), whole(c.shape), cols(tokens), cols(tokens),
                      pl.BlockSpec((1, width, block), lambda i, _: (i, 0, 0)),
                      pl.BlockSpec((block, width), lambda i, _: (i, 0))],
            out_specs=[whole(c.shape), cols(1), by_part, by_part, by_chip, by_chip],
        ),
        out_shape=[jax.ShapeDtypeStruct((tokens, width), f32), jax.ShapeDtypeStruct((1, ff), f32),
                   grad1, grad1, grad2, grad2],
        compiler_params=params(),
        cost_estimate=cost(8 * tokens * width * ff, tokens * ff * 4 + width * ff * 8 + tokens * width * 8),
        name="mlp_bwd",
    )(pos, dm, c, u, g, fc1, fc2)


def qkvo_grad_kernel(pos_ref, a_ref, d_ref, o_ref, dattn_ref, keep_ref, send_ref, *, chips):
    part = pl.program_id(0)
    core = pos_ref[2]

    @pl.when(part < 3)
    def _():
        split_rows(dot(a_ref[...], d_ref[0], 0, 0), core, keep_ref.at[0], send_ref.at[0], chips)

    @pl.when(part == 3)
    def _():
        split_rows(dot(o_ref[...], dattn_ref[...], 0, 0), core, keep_ref.at[0], send_ref.at[0], chips)


def qkvo_grad(pos, a, dqkv, o, dattn, chips):
    tokens, width = a.shape
    each = width // chips // 2
    out = pl.BlockSpec((1, chips, each, width), lambda i, _: (i, 0, 0, 0))
    shape = jax.ShapeDtypeStruct((4, chips, each, width), bf16)
    return pl.pallas_call(
        functools.partial(qkvo_grad_kernel, chips=chips),
        grid_spec=pltpu.PrefetchScalarGridSpec(
            num_scalar_prefetch=1,
            grid=(4,),
            in_specs=[whole(a.shape), pl.BlockSpec((1, tokens, width), lambda i, _: (jnp.minimum(i, 2), 0, 0)),
                      whole(a.shape), whole(a.shape)],
            out_specs=[out, out],
        ),
        out_shape=[shape, shape],
        compiler_params=params(),
        cost_estimate=cost(8 * tokens * width * width, tokens * width * 12 + width * width * 8),
        name="qkvo_grad",
    )(pos, a, dqkv, o, dattn)


def patch_grad_kernel(ext_ref, demb_ref, small_ref, out_ref):
    shares, spare, width = small_ref.shape
    grad = dot(ext_ref[...], demb_ref[...], 0, 0).astype(bf16)
    each = grad.shape[0] // shares
    out_ref[:, :each, :] = grad.reshape(shares, each, width)
    out_ref[:, each:, :] = small_ref[...]


def patch_grad(ext, demb, small):
    tokens, depth = ext.shape
    shares, spare, width = small.shape
    steps = 4
    per = shares // steps
    each = depth // shares
    return pl.pallas_call(
        patch_grad_kernel,
        grid=(steps,),
        in_specs=[pl.BlockSpec((tokens, depth // steps), lambda i: (0, i)), whole(demb.shape),
                  pl.BlockSpec((per, spare, width), lambda i: (i, 0, 0))],
        out_specs=pl.BlockSpec((per, each + spare, width), lambda i: (i, 0, 0)),
        out_shape=jax.ShapeDtypeStruct((shares, each + spare, width), bf16),
        compiler_params=params(),
        cost_estimate=cost(2 * tokens * depth * width, ext.size * 2 + demb.size * 2 + depth * width * 2),
        name="patch_grad",
    )(ext, demb, small)


def pixel_grad_kernel(d_ref, w_ref, shown_ref, out_ref):
    out_ref[...] = dot(d_ref[...], stacked(w_ref, out_ref.shape[1]), 1, 1) * shown_ref[...]


def pixel_back(dmasked, patch, shown, depth):
    own, width = dmasked.shape
    tb = token_block(own)
    return pl.pallas_call(
        pixel_grad_kernel,
        grid=(own // tb,),
        in_specs=[rows(tb, width), whole(patch.shape), rows(tb, 1)],
        out_specs=rows(tb, depth),
        out_shape=jax.ShapeDtypeStruct((own, depth), f32),
        compiler_params=params(),
        cost_estimate=cost(2 * own * depth * width, own * depth * 4 + depth * width * 2),
        name="pixel_back",
    )(dmasked, patch, shown)


def place_kernel(pos_ref, *refs, kinds, groups):
    count = len(kinds)
    per = count + 3 * len(groups)
    outs = refs[2 * per :]
    z, g, core = pos_ref[0], pos_ref[1], pos_ref[2]

    def put(m, share, part, row, value):
        if kinds[m] == "wide":
            each = outs[m].shape[1] // 8
            outs[m][part, pl.ds(pl.multiple_of(share * each + row, 16), value.shape[0]), :] = value
        else:
            each = outs[m].shape[0] // 32
            start = (share * 4 + part) * each + row
            outs[m][pl.ds(pl.multiple_of(start, 16), value.shape[0]), :] = value

    for rel in range(2):
        cc = core ^ rel
        mine = refs[rel * per : (rel + 1) * per]
        for m in range(count):
            each = mine[m].shape[0] if kinds[m] == "wide" else mine[m].shape[0] // 4
            width = outs[m].shape[-1]
            for part in range(4):
                value = mine[m][:, part * width : (part + 1) * width] if kinds[m] == "wide" else mine[m][part * each : (part + 1) * each, :]
                put(m, z * 2 + cc, part, 0, value)
        for i, (m, row, height, first) in enumerate(groups):
            got, near, far = mine[count + 3 * i : count + 3 * i + 3]
            for k in range(3):
                share = ((z - k - 1) & 3) * 2 + cc
                for ref, base, turn in ((got, 0, 0), (near, 0, first), (far, 0, 3 ^ first), (far, 3, 3)):
                    put(m, share, g ^ turn, row, ref[base + k])


def place(pos, pieces, others, kinds, groups, shapes):
    args = (*pieces, *others)
    return pl.pallas_call(
        functools.partial(place_kernel, kinds=kinds, groups=groups),
        grid_spec=pltpu.PrefetchScalarGridSpec(
            num_scalar_prefetch=1,
            grid=(1,),
            in_specs=[whole(p.shape) for p in args],
            out_specs=[whole(s) for s in shapes],
        ),
        out_shape=[jax.ShapeDtypeStruct(s, bf16) for s in shapes],
        compiler_params=params(),
        cost_estimate=cost(0, 4 * sum(np.prod(s) for s in shapes)),
        name="place",
    )(pos, *args)


def norm_back(dnormed, hidden, gain):
    xhat, rstd = norm_parts(hidden)
    dxhat = dnormed * gain
    mean_d = jnp.mean(dxhat, axis=-1, keepdims=True)
    mean_dx = jnp.mean(dxhat * xhat, axis=-1, keepdims=True)
    grad = rstd * (dxhat - mean_d - xhat * mean_dx)
    return grad, jnp.sum(dnormed * xhat, axis=0, keepdims=True), jnp.sum(dnormed, axis=0, keepdims=True)


def sum_rows(step, ref, part):
    @pl.when(step == 0)
    def _():
        ref[...] = part

    @pl.when(step > 0)
    def _():
        ref[...] += part


def norm2_back_kernel(dc_ref, h1_ref, dh2_ref, gain_ref, w_ref, dh1_ref, da_ref, do_ref, gg_ref, gs_ref):
    step = pl.program_id(0)
    grad, ggain, gshift = norm_back(dc_ref[...], h1_ref[...], gain_ref[...])
    dh1 = dh2_ref[...] + grad
    dh1_ref[...] = dh1
    dattn = dh1.astype(bf16)
    da_ref[...] = dattn
    do_ref[...] = dot(dattn, w_ref[0], 1, 1).astype(bf16)
    sum_rows(step, gg_ref, ggain)
    sum_rows(step, gs_ref, gshift)


def norm2_back(dc, h1, dh2, gain, proj_w):
    tokens, width = dc.shape
    tb = token_block(tokens)
    blk = rows(tb, width)
    vec = whole((1, width))
    return pl.pallas_call(
        norm2_back_kernel,
        grid=(tokens // tb,),
        in_specs=[blk, blk, blk, vec, last_part(width)],
        out_specs=[blk, blk, blk, vec, vec],
        out_shape=[jax.ShapeDtypeStruct((tokens, width), f32), jax.ShapeDtypeStruct((tokens, width), bf16),
                   jax.ShapeDtypeStruct((tokens, width), bf16),
                   jax.ShapeDtypeStruct((1, width), f32), jax.ShapeDtypeStruct((1, width), f32)],
        compiler_params=params(),
        cost_estimate=cost(2 * tokens * width * width, tokens * width * 20 + width * width * 2),
        name="norm2_back",
    )(dc, h1, dh2, gain, proj_w)


def norm1_back_kernel(d_ref, w_ref, h0_ref, dh1_ref, gain_ref, de_ref, gg_ref, gs_ref):
    step = pl.program_id(0)
    da = dot(d_ref[0], w_ref[0], 1, 1) + dot(d_ref[1], w_ref[1], 1, 1) + dot(d_ref[2], w_ref[2], 1, 1)
    grad, ggain, gshift = norm_back(da, h0_ref[...], gain_ref[...])
    de_ref[...] = (dh1_ref[...] + grad).astype(bf16)
    sum_rows(step, gg_ref, ggain)
    sum_rows(step, gs_ref, gshift)


def norm1_back(dqkv, qkv_w, h0, dh1, gain):
    _, tokens, width = dqkv.shape
    tb = token_block(tokens)
    blk = rows(tb, width)
    vec = whole((1, width))
    return pl.pallas_call(
        norm1_back_kernel,
        grid=(tokens // tb,),
        in_specs=[pl.BlockSpec((3, tb, width), lambda i: (0, i, 0)), whole((3, width, width)), blk, blk, vec],
        out_specs=[blk, vec, vec],
        out_shape=[jax.ShapeDtypeStruct((tokens, width), bf16),
                   jax.ShapeDtypeStruct((1, width), f32), jax.ShapeDtypeStruct((1, width), f32)],
        compiler_params=params(),
        cost_estimate=cost(6 * tokens * width * width, tokens * width * 16 + width * width * 6),
        name="norm1_back",
    )(dqkv, qkv_w, h0, dh1, gain)


def part_slices(side):
    low, own, high = slice(0, MARGIN), slice(MARGIN, MARGIN + side), slice(MARGIN + side, 2 * MARGIN + side)
    return [(own, own), (own, low), (own, high), (low, own), (high, own),
            (low, low), (low, high), (high, low), (high, high)]


@functools.lru_cache(None)
def token_places(dates, side):
    extent = side + 2 * MARGIN
    grid = np.stack(np.meshgrid(np.arange(dates), np.arange(extent), np.arange(extent), indexing="ij"), -1)
    return np.concatenate([grid[:, r, c].reshape(-1, 3) for r, c in part_slices(side)])


@functools.lru_cache(None)
def halo_tables(dates, side):
    places = token_places(dates, side)
    extent = side + 2 * MARGIN
    own = dates * side * side
    edge = dates * side * MARGIN
    index = {tuple(p): i for i, p in enumerate(places)}

    def table(wanted, count):
        out = np.zeros((len(wanted), count), np.float32)
        out[np.arange(len(wanted)), [index[w] for w in wanted]] = 1
        return out

    def shifted(part, dr, dc):
        r, c = part_slices(side)[part]
        grid = np.stack(np.meshgrid(np.arange(dates), np.arange(extent)[r], np.arange(extent)[c], indexing="ij"), -1)
        return [(d, y + dr, x + dc) for d, y, x in grid.reshape(-1, 3)]

    first = table(shifted(1, 0, side) + shifted(2, 0, -side), own)
    north = shifted(3, side, 0) + shifted(5, side, 0) + shifted(6, side, 0)
    south = shifted(4, -side, 0) + shifted(7, -side, 0) + shifted(8, -side, 0)
    second = table(north + south, own + 2 * edge)
    return first, second


def chain(axis, step):
    count = lax.axis_size(axis)
    return [(i, i + step) for i in range(count) if 0 <= i + step < count]


def pick(table, values):
    return lax.dot(jnp.asarray(table, bf16), values, preferred_element_type=f32)


def give_margin(own, dates, side):
    first, second = halo_tables(dates, side)
    edge = dates * side * MARGIN
    corner = dates * MARGIN * MARGIN
    sent = pick(first, own).astype(bf16)
    left = lax.ppermute(sent[:edge], "gx", chain("gx", 1))
    right = lax.ppermute(sent[edge:], "gx", chain("gx", -1))
    middle = jnp.concatenate([own, left, right])
    sent = pick(second, middle).astype(bf16)
    upper = lax.ppermute(sent[: edge + 2 * corner], "gy", chain("gy", 1))
    lower = lax.ppermute(sent[edge + 2 * corner :], "gy", chain("gy", -1))
    return jnp.concatenate([middle, upper[:edge], lower[:edge], upper[edge:], lower[edge:]])


def take_margin(every, dates, side):
    first, second = halo_tables(dates, side)
    own = dates * side * side
    edge = dates * side * MARGIN
    corner = dates * MARGIN * MARGIN
    after = own + 2 * edge
    upper = jnp.concatenate([every[after : after + edge], every[after + 2 * edge : after + 2 * edge + 2 * corner]])
    lower = jnp.concatenate([every[after + edge : after + 2 * edge], every[after + 2 * edge + 2 * corner :]])
    below = lax.ppermute(upper, "gy", chain("gy", -1))
    above = lax.ppermute(lower, "gy", chain("gy", 1))
    middle = every[:after].astype(f32) + pick(second.T, jnp.concatenate([below, above]))
    sides = middle[own:].astype(bf16)
    east = lax.ppermute(sides[:edge], "gx", chain("gx", -1))
    west = lax.ppermute(sides[edge:], "gx", chain("gx", 1))
    return middle[:own] + pick(first.T, jnp.concatenate([east, west]))


def sincos(places, span_width):
    half_width = span_width // 2
    omega = 1.0 / 10000.0 ** (jnp.arange(half_width, dtype=f32) / half_width)
    angles = places[:, None] * omega[None, :]
    return jnp.concatenate([jnp.sin(angles), jnp.cos(angles)], axis=1)


def position_parts(tile_row, tile_col, stamps, side, width):
    side_width = width // 16 * 6
    time_width = width - 2 * side_width
    extent = side + 2 * MARGIN
    dates = stamps.shape[0]
    offsets = jnp.arange(extent, dtype=jnp.int32) - MARGIN
    table = jnp.concatenate([
        jnp.pad(sincos(stamps.astype(f32), time_width), ((0, 0), (0, 2 * side_width))),
        jnp.pad(sincos((tile_row * side + offsets).astype(f32), side_width), ((0, 0), (time_width, side_width))),
        jnp.pad(sincos((tile_col * side + offsets).astype(f32), side_width), ((0, 0), (time_width + side_width, 0))),
    ])
    places = token_places(dates, side)
    hot = np.zeros((len(places), dates + 2 * extent), np.float32)
    spots = np.arange(len(places))
    hot[spots, places[:, 0]] = 1
    hot[spots, dates + places[:, 1]] = 1
    hot[spots, dates + extent + places[:, 2]] = 1
    hot = np.concatenate([hot] * 3, axis=1)
    spare = -hot.shape[1] % 128
    hot = np.pad(hot, ((0, 0), (0, spare)))
    parts = jnp.concatenate(three_parts(table))
    return jnp.asarray(hot, bf16), jnp.pad(parts, ((0, spare), (0, 0)))


def dense(left, right, ca=1, cb=0):
    return lax.dot_general(left, right, (((ca,), (cb,)), ((), ())), preferred_element_type=f32)


def gather(shard):
    return lax.all_gather(shard, "gx", axis=0, tiled=True)


def swap(value, axis, bit):
    return lax.ppermute(value, axis, [(i, i ^ bit) for i in range(lax.axis_size(axis))])


def turn(value, step):
    count = lax.axis_size("gx")
    return lax.ppermute(value, "gx", [(i, (i + 2 * step) % count) for i in range(count)])


def after(value, *earlier):
    return lax.optimization_barrier((value, *earlier))[0]


def along_z(mine):
    return jnp.stack([turn(mine, k) for k in (1, 2, 3)])


def along_gy(got, first):
    near = swap(got, "gy", first)
    far = swap(jnp.concatenate([got, near]), "gy", 3 ^ first)
    return got, near, far


def core_swap(pieces):
    return tuple(swap(p, "gx", 1) for p in pieces)


def added(*values):
    return sum(v.astype(f32) for v in values).astype(bf16)


def at(value, index, axis=0):
    return lax.dynamic_index_in_dim(value, index, axis, keepdims=False)


def folded_gy(value):
    return value.reshape(2, 2, *value.shape[1:])


def near_sum(keep, got, first, g):
    keep, got = folded_gy(keep), folded_gy(got)
    dim, b = (1, g & 1) if first == 1 else (0, g >> 1)
    return added(at(keep, 1 - b, dim), at(got, 1 - b, dim)), added(at(keep, b, dim), at(got, b, dim))


def far_sum(keep, got, first, g):
    b = (g >> 1) if first == 1 else (g & 1)
    return added(at(keep, 1 - b), at(got, 1 - b)), (at(keep, b), at(got, b))


def along_z_sum(mine, z):
    came = [turn(at(mine, (z + k) % 4), k) for k in (1, 2, 3)]
    return at(mine, z), came


def four_parts(mine, first, g):
    pair = jnp.stack([mine, swap(mine, "gy", first)])
    every = jnp.concatenate([pair, swap(pair, "gy", 3 ^ first)])
    place_of = lambda rel: rel if first == 1 else (rel >> 1) | ((rel & 1) << 1)
    return [at(every, place_of(p ^ g)).astype(f32) for p in range(4)]


def gather_last(dec_w, head_w):
    rows_each, width = head_w.shape
    slabs = head_w.reshape(rows_each, -1, dec_w.shape[1]).transpose(1, 0, 2).reshape(-1, dec_w.shape[1])
    return lax.all_gather(jnp.concatenate([dec_w, slabs]), "gx", axis=0, tiled=False)


def gather_pieces(qkv_w, proj_w, fc1_w, fc2_w, ready):
    each, width = proj_w.shape
    half = each // 2
    row = lax.axis_index("gy")
    share_a = jnp.concatenate([qkv_w, proj_w], axis=1)
    got_a = along_z(lax.dynamic_slice_in_dim(share_a, row * width, width, axis=1))
    pieces_a = (share_a, *along_gy(got_a[:, :half], 1), *along_gy(got_a[:, half:], 2))
    mine_b = jnp.concatenate([lax.dynamic_slice_in_dim(fc1_w, row * width, width, axis=1),
                              lax.dynamic_slice_in_dim(fc2_w, row * each, each, axis=0)])
    got_b = along_z(after(mine_b, got_a, ready))
    pieces_b = (fc1_w, fc2_w, *along_gy(got_b[:, :each], 1), *along_gy(got_b[:, each:], 2))
    return (pieces_a, core_swap(pieces_a)), (pieces_b, core_swap(pieces_b))


def place_a(pos, pieces, others, ready):
    each = pieces[0].shape[0]
    half, width = each // 2, pieces[1].shape[-1]
    others = lax.optimization_barrier((*others, ready))[:-1]
    return place(pos, pieces, others, ("wide",), ((0, 0, half, 1), (0, half, half, 2)), [(4, width, width)])[0]


def place_b(pos, pieces, others, ready):
    each, width = pieces[0].shape[0], pieces[2].shape[-1]
    others = lax.optimization_barrier((*others, ready))[:-1]
    return place(pos, pieces, others, ("wide", "tall"), ((0, 0, each, 1), (1, 0, each, 2)),
                 [(4, width, width), (4 * width, width)])


def collect_all(keep, send, tall):
    both = jnp.stack([keep, send], axis=2)
    parts, chips, _, rows_each, width = both.shape
    if tall:
        grad = both.transpose(1, 2, 0, 3, 4).reshape(-1, width)
    else:
        grad = both.transpose(1, 2, 3, 0, 4).reshape(-1, parts * width)
    grad = lax.psum(scatter(grad), "gy").astype(f32)
    return jnp.split(grad, parts, axis=0 if tall else 1)


def over_gy(part):
    if lax.axis_size("gy") != 4:
        return lax.psum(part, "gy")
    part = added(part, swap(part, "gy", 1))
    return added(part, swap(part, "gy", 2))


def scatter(grad):
    return lax.psum_scatter(grad.astype(bf16), "gx", scatter_dimension=0, tiled=True)


def on_device(pixels, pad_mask, timestamps, scene_dates, scene_map, blend_weight, cotangent, patch_w, norm1_gain,
              norm1_bias, qkv_w, proj_w, norm2_gain, norm2_bias, fc1_w, fc1_b, fc2_w, dec_w, head_w):
    dates, side, _, pixel_width = pixels.shape
    own = dates * side * side
    extent = side + 2 * MARGIN
    places = token_places(dates, side)
    tokens = len(places)
    model_width = patch_w.shape[1]
    scale = float(model_width // HEADS) ** (-0.5)
    tile_row = lax.axis_index("gy")
    tile_col = lax.axis_index("gx")
    split = lax.axis_size("gx") == 8 and lax.axis_size("gy") == 4
    chip, core = (tile_col >> 1, tile_col & 1) if split else (0, 0)
    pos = jnp.stack([jnp.int32(chip), tile_row, jnp.int32(core)]).astype(jnp.int32)

    vectors = jnp.concatenate([norm1_gain, norm1_bias, norm2_gain, norm2_bias, fc1_b])
    each, spare = norm1_gain.shape[0], model_width - vectors.shape[0]
    vectors = jnp.broadcast_to(jnp.pad(vectors, (0, spare))[None, :], (8, model_width))
    masked = (pixels * pad_mask.astype(bf16)[..., None]).reshape(own, pixel_width)
    ext = give_margin(masked, dates, side)

    nearby = lax.dynamic_slice(jnp.pad(scene_map, 1, constant_values=-1), (tile_row, tile_col), (3, 3))
    own_scene = nearby[1, 1]
    bands = np.array([0] * MARGIN + [1] * side + [2] * MARGIN)
    same = (nearby == own_scene)[bands][:, bands].astype(f32)
    weight = blend_weight.astype(f32) * same
    own_dates = scene_dates[own_scene]
    stamps = timestamps[own_scene]
    date_ok = jnp.arange(dates, dtype=jnp.int32) < own_dates
    spot_hot = np.zeros((tokens, extent * extent), np.float32)
    spot_hot[np.arange(tokens), places[:, 1] * extent + places[:, 2]] = 1
    per_token = pick(spot_hot, jnp.stack([weight.reshape(-1), same.reshape(-1)], axis=1).astype(bf16))
    weight_tok = per_token[:, :1]
    seen = per_token[:, 1:] * (jnp.asarray(places[:, :1], jnp.int32) < own_dates).astype(f32)
    lane = np.arange(128)[None, :]
    kx = jnp.where(lane < 3, 1.0, jnp.where(lane == 3, (1.0 - seen) * -1e9, 0.0)).astype(bf16)
    shown = pad_mask.reshape(own, 1).astype(f32)
    valid = (pad_mask.astype(f32) * date_ok.astype(f32)[:, None, None]).reshape(own, 1)

    full_patch = lax.all_gather(jnp.concatenate([patch_w, vectors]), "gx", axis=0, tiled=False)
    if split:
        pieces_a, pieces_b = gather_pieces(qkv_w, proj_w, fc1_w, fc2_w, ext)
    else:
        parts_of = lambda m: m.reshape(model_width, 4, model_width).transpose(1, 0, 2)
        full_a = parts_of(jnp.concatenate([gather(qkv_w), gather(proj_w)], axis=1))
        full_fc1, full_fc2 = parts_of(gather(fc1_w)), gather(fc2_w)
    dec_rows, dec_width = dec_w.shape
    head_rows, slabs = head_w.shape[0], pixel_width // dec_width
    tops = gather_last(dec_w, after(head_w, full_patch))
    full_dec = tops[:, :dec_rows].reshape(-1, dec_width)
    full_head = tops[:, dec_rows:].reshape(-1, slabs, head_rows, dec_width).transpose(0, 2, 1, 3).reshape(-1, pixel_width)

    hot, table = position_parts(tile_row, tile_col, stamps, side, model_width)
    small = full_patch[:, patch_w.shape[0], :].astype(f32)
    gain1, shift1, gain2, shift2 = (small[:, i * each : (i + 1) * each].reshape(1, -1) for i in range(4))
    full_b = small[:, 4 * each : 4 * each + fc1_b.shape[0]].reshape(1, -1)

    h0, a = embed(ext, full_patch, hot, table, gain1, shift1)
    if split:
        full_a = place_a(pos, *pieces_a, a)
    qkv = project(a, full_a, 3)
    weight_tok = after(weight_tok, qkv)
    denom = take_margin(weight_tok.astype(bf16), dates, side)
    ratio = valid / denom
    gr = (cotangent.reshape(own, pixel_width).astype(f32) * ratio).astype(bf16)
    o, qx = attn_fwd(qkv, kx, scale)
    h1, c = proj_norm(o, full_a, h0, gain2, shift2)
    if split:
        full_fc1, full_fc2 = place_b(pos, *pieces_b, c)
    gz = dense(after(gr, c), full_head, 1, 1).astype(bf16)
    dz_every = give_margin(gz, dates, side)
    u, slope, h2r = mlp_fwd(c, full_fc1, full_b, full_fc2, h1)
    z = dense(h2r, full_dec).astype(bf16)
    folded = take_margin((z.astype(f32) * weight_tok).astype(bf16), dates, side).astype(bf16)
    recon = (dense(folded, full_head) * ratio).astype(bf16)

    grad_head = dense(folded, gr, 0, 0)
    dz = (dz_every.astype(f32) * weight_tok).astype(bf16)
    grad_dec = dense(h2r, dz, 0, 0)
    dh2 = dense(dz, full_dec, 1, 1)
    dm = dh2.astype(bf16)
    dc, grad_fc1_b, keep1, send1, keep2, send2 = mlp_bwd(pos, dm, c, u, slope, full_fc1, full_fc2, 4)
    g = tile_row
    if split:
        got1, got2 = swap(send1, "gx", 1), swap(send2, "gx", 1)
    dh1, dattn, do, grad_gain2, grad_shift2 = norm2_back(dc, h1, dh2, gain2, full_a)
    if split:
        got1, got2 = after(got1, do), after(got2, do)
        out1, keep1 = near_sum(keep1, got1, 1, g)
        out2, keep2 = near_sum(keep2, got2, 2, g)
        do, out1, out2 = lax.optimization_barrier((do, out1, out2))
        got1, got2 = swap(out1, "gy", 1), swap(out2, "gy", 2)
    dqkv = attn_bwd(qkv, do, o, qx, kx, scale)
    if split:
        got1, got2 = after(got1, dqkv), after(got2, dqkv)
        out1, keep1 = far_sum(keep1, got1, 1, g)
        out2, keep2 = far_sum(keep2, got2, 2, g)
        dqkv, out1, out2 = lax.optimization_barrier((dqkv, out1, out2))
        got1, got2 = swap(out1, "gy", 2), swap(out2, "gy", 1)
    keep3, send3 = qkvo_grad(pos, a, dqkv, o, dattn, 4)
    if split:
        got3 = swap(send3, "gx", 1)
        got1, got2 = after(got1, keep3), after(got2, keep3)
        mine1, came1 = along_z_sum(added(*keep1, got1), chip)
        mine2, came2 = along_z_sum(added(*keep2, got2), chip)
        got3 = after(got3, mine1, mine2)
        half = keep3.shape[2] // 2
        out3, keep3a = near_sum(keep3[:, :, :half], got3[:, :, :half], 1, g)
        out4, keep3b = near_sum(keep3[:, :, half:], got3[:, :, half:], 2, g)
        dqkv, out3, out4 = lax.optimization_barrier((dqkv, out3, out4))
        got3, got4 = swap(out3, "gy", 1), swap(out4, "gy", 2)
    demb, grad_gain1, grad_shift1 = norm1_back(dqkv, full_a, h0, dh1, gain1)
    if split:
        got3, got4 = after(got3, demb), after(got4, demb)
        out3, keep3a = far_sum(keep3a, got3, 1, g)
        out4, keep3b = far_sum(keep3b, got4, 2, g)
        demb, out3, out4 = lax.optimization_barrier((demb, out3, out4))
        got3, got4 = swap(out3, "gy", 2), swap(out4, "gy", 1)
    shares = lax.axis_size("gx")
    small = jnp.concatenate([v.reshape(shares, -1) for v in (grad_gain1, grad_shift1, grad_gain2, grad_shift2, grad_fc1_b)],
                            axis=1).astype(bf16)
    small = jnp.pad(small, ((0, 0), (0, spare)))
    grad_patch = patch_grad(ext, demb, jnp.broadcast_to(small[:, None, :], (shares, 8, model_width)))
    part_patch = lax.psum_scatter(grad_patch, "gx", scatter_dimension=0, tiled=False)
    if split:
        got3, got4 = after(got3, grad_patch), after(got4, grad_patch)
        mine3, came3 = along_z_sum(jnp.concatenate([added(*keep3a, got3), added(*keep3b, got4)], axis=1), chip)
        demb = after(demb, mine3)
        came1, came2 = [after(v, mine3) for v in came1], [after(v, mine3) for v in came2]
        sum1 = four_parts(added(mine1, *came1), 1, g)
        sum2 = four_parts(added(mine2, *came2), 2, g)
    dmasked = take_margin(demb, dates, side).astype(bf16)
    pixel_grad = pixel_back(dmasked, full_patch, shown, pixel_width)
    grad_head, grad_dec = scatter(grad_head), scatter(grad_dec)
    ends = over_gy(jnp.concatenate([grad_dec, grad_head.reshape(-1, dec_width)]))
    if split:
        came3 = [after(v, pixel_grad) for v in came3]
        sum3 = four_parts(added(mine3, *came3), 1, g)
    else:
        sum1, sum2, sum3 = collect_all(keep1, send1, False), collect_all(keep2, send2, True), collect_all(keep3, send3, False)
    last = over_gy(part_patch).astype(f32)
    small = last[patch_w.shape[0]]
    return (
        recon.reshape(pixels.shape),
        pixel_grad.reshape(pixels.shape),
        last[: patch_w.shape[0]],
        small[:each],
        small[each : 2 * each],
        jnp.concatenate(sum3[:3], axis=1),
        sum3[3],
        small[2 * each : 3 * each],
        small[3 * each : 4 * each],
        jnp.concatenate(sum1, axis=1),
        small[4 * each : 4 * each + fc1_b.shape[0]],
        jnp.concatenate(sum2, axis=0),
        ends[:dec_rows].astype(f32),
        ends[dec_rows:].reshape(head_rows, pixel_width).astype(f32),
    )


def solution(mesh):
    in_specs = (
        P(None, "gy", "gx", None),
        P(None, "gy", "gx"),
        P(),
        P(),
        P(),
        P("gy", "gx"),
        P(None, "gy", "gx", None),
        P("gx", None),
        P("gx"),
        P("gx"),
        P("gx", None),
        P("gx", None),
        P("gx"),
        P("gx"),
        P("gx", None),
        P("gx"),
        P("gx", None),
        P("gx", None),
        P("gx", None),
    )
    out_specs = (
        P(None, "gy", "gx", None),
        P(None, "gy", "gx", None),
        P("gx", None),
        P("gx"),
        P("gx"),
        P("gx", None),
        P("gx", None),
        P("gx"),
        P("gx"),
        P("gx", None),
        P("gx"),
        P("gx", None),
        P("gx", None),
        P("gx", None),
    )
    return jax.shard_map(
        on_device, mesh=mesh, in_specs=in_specs, out_specs=out_specs, check_vma=False
    )
```

time: 912 us -> 572 us (0.63)
  the two profiles are of different devices: /device:TPU:0 before, /device:TPU:8 now
where the time goes in v1:
time: 572 us; the launch traced here: 564 us
  Pallas kernels  179 us (31%)
  waiting for transfers between devices  157 us (27%)
  starting transfers between devices  107 us (19%)
  other arithmetic  42.1 us (7%)
  local copies, waits for them, and re-layouts  37.6 us (7%)
  matrix products  23.7 us (4%)
  between operations  18 us (3%)
    ppermute x44, waiting for transfers between devices, swap(): lax.ppermute(value, axis, [(i, i ^ bit) for i in range(lax.axis_size(axis...  64.7 us
    ppermute x15, waiting for transfers between devices, turn(): lax.ppermute(value, 'gx', [(i, (i + 2 * step) % count) for i in range(cou...  52.5 us
    ppermute x44, starting transfers between devices, swap(): lax.ppermute(value, axis, [(i, i ^ bit) for i in range(lax.axis_size(axis...  34.1 us
    pallas_call x1, Pallas kernels, attn_bwd(): pl.pallas_call(functools.partial(attn_bwd_kernel, block=token_block(token...  33.6 us
    pallas_call x1, Pallas kernels, mlp_bwd(): pl.pallas_call(functools.partial(mlp_bwd_kernel, chips=chips), grid_spec=...  32.6 us
    ppermute x15, starting transfers between devices, turn(): lax.ppermute(value, 'gx', [(i, (i + 2 * step) % count) for i in range(cou...  21.1 us
    pallas_call x1, Pallas kernels, attn_fwd(): pl.pallas_call(functools.partial(attn_fwd_kernel, block=token_block(token...  18.4 us
    convert_element_type x19, other arithmetic, added(): return sum((v.astype(f32) for v in values)).astype(bf16)  18 us
  transfers between devices with their start and end apart: 84, of which 36 were waited for; matrix products, arithmetic and copies ran while one was open for 14% of the time, Pallas kernels for 26%

profile of v1, /device:TPU:8, one launch (start us, length us, event | category | flops | bytes accessed | tf_op | source)
XLA Modules:
  0.0 563.7 jit_solution(17896584168122797541)
XLA Ops:
  10.0 2.6 collective-permute-start.5
  18.7 3.6 collective-permute-start.1
  46.5 3.4 collective-permute-start.2
  54.6 3.6 collective-permute-done.2
  59.0 10.7 %collective-permute-done.3 = bf16[144,1536]{1,0:T(8,128)(2,1)S(1)} collective-permute-done((bf16[144,1536]{1,0:T(8,128)(2,1)S(1)}, bf16[144,1536]{1,0:T(8,128)(2,1)S(1)}, u32[]{:S(2)}, u32[]{:S(2)}) %collective-permute-start.3) | collective-permute-done | bytes 442400 | tf_op jit(solution)/shard_map/ppermute | solution.py:632
  71.7 2.1 collective-permute-start.18
  74.5 2.0 collective-permute-start.20
  78.2 15.6 %collective-permute-done.18 = bf16[192,768]{1,0:T(8,128)(2,1)S(1)} collective-permute-done((bf16[192,768]{1,0:T(8,128)(2,1)S(1)}, bf16[192,768]{1,0:T(8,128)(2,1)S(1)}, u32[]{:S(2)}, u32[]{:S(2)}) %collective-permute-start.18) | collective-permute-done | bytes 294944 | tf_op jit(solution)/shard_map/ppermute | solution.py:698
  93.8 5.5 collective-permute-done.19
  100.4 2.1 collective-permute-start.9
  105.2 11.9 %collective-permute-done.9.refs_5_ = bf16[3,48,768]{2,1,0:T(8,128)(2,1)S(1)} collective-permute-done((bf16[3,48,768]{2,1,0:T(8,128)(2,1)S(1)}, bf16[3,48,768]{2,1,0:T(8,128)(2,1)S(1)}, u32[]{:S(2)}, u32[]{:S(2)}) %collective-permute-start.9) | collective-permute-done | bytes 221216 | tf_op jit(solution)/shard_map/ppermute | solution.py:693
  126.6 3.7 collective-permute-done.8.refs_3_
  133.9 6.8 %embed.1 = (f32[864,768]{1,0:T(8,128)}, bf16[864,768]{1,0:T(8,128)(2,1)}) custom-call(bf16[864,1536]{1,0:T(8,128)(2,1)} %slice_dynamic-update-slice_fusion.2.ext_ref, bf16[8,200,768]{2,1,0:T(8,128)(2,1)} %bitcast.264, bf16[864,128]{1,0:T(8,128)(2,1)} %constant.258.clone.pick_ref, bf16[128,768]{1,0:T(8,128)(2,1)} %fusion.45.table_ref, ...), custom_call_target="tpu_custom_call" | custom-call | flops 2038431744 | bytes 8994816 | tf_op jit(solution)/shard_map/embed/pallas_call | solution.py:72
  141.9 6.7 %collective-permute-done.24.refs_7_ = bf16[6,96,768]{2,1,0:T(8,128)(2,1)} collective-permute-done((bf16[6,96,768]{2,1,0:T(8,128)(2,1)}, bf16[6,96,768]{2,1,0:T(8,128)(2,1)}, u32[]{:S(2)}, u32[]{:S(2)}) %collective-permute-start.24) | collective-permute-done | bytes 884768 | tf_op jit(solution)/shard_map/ppermute | solution.py:693
  149.1 5.4 place.2.w_ref
  154.6 8.7 %project.1.q_ref.k_ref.v_ref = bf16[864,2304]{1,0:T(8,128)(2,1)} custom-call(bf16[864,768]{1,0:T(8,128)(2,1)} %get-tuple-element.93.a_ref, bf16[4,768,768]{2,1,0:T(8,128)(2,1)} %place.2.w_ref), custom_call_target="tpu_custom_call" | custom-call | flops 3057647616 | bytes 8847360 | tf_op jit(solution)/shard_map/project/pallas_call | solution.py:93
  164.7 18.4 %attn_fwd.1 = (bf16[864,768]{1,0:T(8,128)(2,1)}, bf16[12,864,128]{2,1,0:T(8,128)(2,1)}) custom-call(bf16[864,2304]{1,0:T(8,128)(2,1)} %project.1.q_ref.k_ref.v_ref, bf16[864,2304]{1,0:T(8,128)(2,1)} %project.1.q_ref.k_ref.v_ref, bf16[864,2304]{1,0:T(8,128)(2,1)} %project.1.q_ref.k_ref.v_ref, bf16[864,128]{1,0:T(8,128)(2,1)} %select_convert_fusion.kx_ref), custom_call_target="tpu_custom_call" | custom-call | flops 18345885696 | bytes 5308416 | tf_op jit(solution)/shard_map/attn_fwd/pallas_call | solution.py:152
  184.4 5.8 %proj_norm.1 = (f32[864,768]{1,0:T(8,128)}, bf16[864,768]{1,0:T(8,128)(2,1)}) custom-call(bf16[864,768]{1,0:T(8,128)(2,1)} %get-tuple-element.101.o_ref, bf16[4,768,768]{2,1,0:T(8,128)(2,1)} %place.2.w_ref, f32[864,768]{1,0:T(8,128)} %get-tuple-element.102.h0_ref, f32[1,768]{1,0:T(1,128)} %reshape.341.gain_ref, f32[1,768]{1,0:T(1,128)} %reshape.342.shift_ref), custom_call_target="tpu_custom_call" | custom-call | flops 1019215872 | bytes 9142272 | tf_op jit(solution)/shard_map/proj_norm/pallas_call | solution.py:235
  193.5 4.5 collective-permute-start.38
  198.8 8.8 %place.3 = (bf16[4,768,768]{2,1,0:T(8,128)(2,1)}, bf16[3072,768]{1,0:T(8,128)(2,1)}) custom-call(s32[3]{0:T(128)} %pad_add_fusion.pos_ref, bf16[96,3072]{1,0:T(8,128)(2,1)} %refs_0_.1, bf16[384,768]{1,0:T(8,128)(2,1)} %refs_1_.1, bf16[3,96,768]{2,1,0:T(8,128)(2,1)} %copy-done.1, bf16[3,96,768]{2,1,0:T(8,128)(2,1)} %copy-done.9, ...), custom_call_target="tpu_custom_call" | custom-call | bytes 18874368 | tf_op jit(solution)/shard_map/place/pallas_call | solution.py:483
  209.9 2.4 collective-permute-start.40
  212.3 17.4 %mlp_fwd.1 = (bf16[864,3072]{1,0:T(8,128)(2,1)}, bf16[864,3072]{1,0:T(8,128)(2,1)}, bf16[864,768]{1,0:T(8,128)(2,1)}) custom-call(bf16[864,768]{1,0:T(8,128)(2,1)} %get-tuple-element.103.c_ref, bf16[4,768,768]{2,1,0:T(8,128)(2,1)} %get-tuple-element.113.fc1_ref, f32[1,3072]{1,0:T(1,128)} %bitcast.294, bf16[3072,768]{1,0:T(8,128)(2,1)} %get-tuple-element.114.fc2_ref, ...), custom_call_target="tpu_custom_call" | custom-call | flops 8153726976 | bytes 25362432 | tf_op jit(solution)/shard_map/mlp_fwd/pallas_call | solution.py:275
  238.4 2.9 collective-permute-start.41
  241.2 2.8 collective-permute-start.42
  246.5 4.4 collective-permute-start.43
  252.3 2.8 collective-permute-done.43
  255.1 4.2 collective-permute-done.44
  259.3 2.8 fusion.93
  262.2 32.6 %mlp_bwd.1 = (f32[864,768]{1,0:T(8,128)}, f32[1,3072]{1,0:T(1,128)}, bf16[4,4,96,768]{3,2,1,0:T(8,128)(2,1)}, bf16[4,4,96,768]{3,2,1,0:T(8,128)(2,1)}, bf16[4,4,...) custom-call(s32[3]{0:T(128)} %pad_add_fusion.pos_ref, bf16[864,768]{1,0:T(8,128)(2,1)} %get-tuple-element.266.dm_ref, ...), custom_call_target="tpu_custom_call" | custom-call | flops 16307453952 | bytes 34799616 | tf_op jit(solution)/shard_map/mlp_bwd/pallas_call | solution.py:351
  296.6 4.7 collective-permute-start.34
  301.3 1.9 convolution_convert_fusion.3
  306.1 2.1 collective-permute-start.36
  309.1 3.6 collective-permute-start.35
  313.0 2.4 collective-permute-done.35
  315.6 2.2 convolution_convert_fusion
  318.1 8.9 %norm2_back.1 = (f32[864,768]{1,0:T(8,128)}, bf16[864,768]{1,0:T(8,128)(2,1)}, bf16[864,768]{1,0:T(8,128)(2,1)}, f32[1,768]{1,0:T(1,128)}, f32[1,768]{1,0:T(1,128)}) custom-call(f32[864,768]{1,0:T(8,128)} %get-tuple-element.122.dc_ref, f32[864,768]{1,0:T(8,128)} %get-tuple-element.115.h1_ref, f32[864,768]{1,0:T(8,128)} %get-tuple-element.267.dh2_ref, ...), custom_call_target="tpu_custom_call" | custom-call | flops 1019215872 | bytes 14450688 | tf_op jit(solution)/shard_map/norm2_back/pallas_call | solution.py:534
  327.0 2.7 fusion.10
  329.7 3.4 add_convert_fusion
  333.1 4.5 collective-permute-start.48
  339.2 33.6 %attn_bwd.1.d_ref = bf16[3,864,768]{2,1,0:T(8,128)(2,1)} custom-call(bf16[864,2304]{1,0:T(8,128)(2,1)} %project.1.q_ref.k_ref.v_ref, bf16[864,2304]{1,0:T(8,128)(2,1)} %project.1.q_ref.k_ref.v_ref, bf16[864,2304]{1,0:T(8,128)(2,1)} %project.1.q_ref.k_ref.v_ref, bf16[864,768]{1,0:T(8,128)(2,1)} %get-tuple-element.130.do_ref, ...), custom_call_target="tpu_custom_call" | custom-call | flops 22932357120 | bytes 10616832 | tf_op jit(solution)/shard_map/attn_bwd/pallas_call | solution.py:212
  374.9 11.0 %qkvo_grad.1 = (bf16[4,4,96,768]{3,2,1,0:T(8,128)(2,1)}, bf16[4,4,96,768]{3,2,1,0:T(8,128)(2,1)}) custom-call(s32[3]{0:T(128)} %pad_add_fusion.pos_ref, bf16[864,768]{1,0:T(8,128)(2,1)} %get-tuple-element.93.a_ref, bf16[3,864,768]{2,1,0:T(8,128)(2,1)} %attn_bwd.1.d_ref, bf16[864,768]{1,0:T(8,128)(2,1)} %get-tuple-element.101.o_ref, ...), custom_call_target="tpu_custom_call" | custom-call | flops 4076863488 | bytes 12681216 | tf_op jit(solution)/shard_map/qkvo_grad/pallas_call | solution.py:387
  391.4 3.4 fusion
  395.3 4.3 collective-permute-done.77
  400.1 16.0 %collective-permute-done.78 = bf16[288,512]{1,0:T(8,128)(2,1)S(1)} collective-permute-done((bf16[288,512]{1,0:T(8,128)(2,1)S(1)}, bf16[288,512]{1,0:T(8,128)(2,1)S(1)}, u32[]{:S(2)}, u32[]{:S(2)}) %collective-permute-start.78) | collective-permute-done | bytes 294944 | tf_op jit(solution)/shard_map/ppermute | solution.py:693
  424.5 8.8 %norm1_back.1 = (bf16[864,768]{1,0:T(8,128)(2,1)}, f32[1,768]{1,0:T(1,128)}, f32[1,768]{1,0:T(1,128)}) custom-call(bf16[3,864,768]{2,1,0:T(8,128)(2,1)} %attn_bwd.1.d_ref, bf16[4,768,768]{2,1,0:T(8,128)(2,1)} %place.2.w_ref, f32[864,768]{1,0:T(8,128)} %get-tuple-element.102.h0_ref, f32[864,768]{1,0:T(8,128)} %get-tuple-element.146.dh1_ref, ...), custom_call_target="tpu_custom_call" | custom-call | flops 3057647616 | bytes 14155776 | tf_op jit(solution)/shard_map/norm1_back/pallas_call | solution.py:562
  443.6 6.5 %patch_grad.1 = bf16[8,200,768]{2,1,0:T(8,128)(2,1)} custom-call(bf16[864,1536]{1,0:T(8,128)(2,1)} %slice_dynamic-update-slice_fusion.2.ext_ref, bf16[864,768]{1,0:T(8,128)(2,1)} %get-tuple-element.162.demb_ref, bf16[8,8,768]{2,1,0:T(8,128)(2,1)} %broadcast_in_dim.75.small_ref), custom_call_target="tpu_custom_call" | custom-call | flops 2038431744 | bytes 6340608 | tf_op jit(solution)/shard_map/patch_grad/pallas_call | solution.py:417
  453.0 2.1 collective-permute-start.73
  455.1 2.0 collective-permute-start.67
  457.1 2.6 collective-permute-start.68
  464.3 12.3 %collective-permute-done.73 = bf16[96,768]{1,0:T(8,128)(2,1)S(1)} collective-permute-done((bf16[96,768]{1,0:T(8,128)(2,1)}, bf16[96,768]{1,0:T(8,128)(2,1)S(1)}, u32[]{:S(2)}, u32[]{:S(2)}) %collective-permute-start.73) | collective-permute-done | bytes 147488 | tf_op jit(solution)/shard_map/ppermute | solution.py:698
  476.6 3.1 collective-permute-done.74
  479.9 8.3 %collective-permute-done.67 = bf16[96,768]{1,0:T(8,128)(2,1)S(1)} collective-permute-done((bf16[96,768]{1,0:T(8,128)(2,1)}, bf16[96,768]{1,0:T(8,128)(2,1)S(1)}, u32[]{:S(2)}, u32[]{:S(2)}) %collective-permute-start.67) | collective-permute-done | bytes 147488 | tf_op jit(solution)/shard_map/ppermute | solution.py:698
  488.1 4.0 collective-permute-done.68
  492.2 2.2 collective-permute-done.69
  499.6 2.1 collective-permute-start.63
  502.1 6.6 %collective-permute-done.56 = bf16[144,768]{1,0:T(8,128)(2,1)S(1)} collective-permute-done((bf16[144,768]{1,0:T(8,128)(2,1)S(1)}, bf16[144,768]{1,0:T(8,128)(2,1)S(1)}, u32[]{:S(2)}, u32[]{:S(2)}) %collective-permute-start.56) | collective-permute-done | bytes 221216 | tf_op jit(solution)/shard_map/ppermute | solution.py:644
  509.2 2.1 collective-permute-start.59
  511.7 4.1 collective-permute-done.59
  518.0 2.4 collective-permute-done.58
  521.5 5.9 %pixel_back.1 = f32[384,1536]{1,0:T(8,128)} custom-call(bf16[384,768]{1,0:T(8,128)(2,1)} %fusion.12.d_ref, bf16[8,200,768]{2,1,0:T(8,128)(2,1)} %bitcast.265, f32[384,1]{1,0:T(8,128)} %convert_element_type.733.shown_ref), custom_call_target="tpu_custom_call" | custom-call | flops 905969664 | bytes 4718592 | tf_op jit(solution)/shard_map/pixel_back/pallas_call | solution.py:437
  530.2 2.6 collective-permute-done.65
  532.8 2.6 collective-permute-start.66
  537.8 5.2 collective-permute-done.66
  547.1 7.6 %collective-permute-done.61 = bf16[200,768]{1,0:T(8,128)(2,1)S(1)} collective-permute-done((bf16[200,768]{1,0:T(8,128)(2,1)S(1)}, bf16[200,768]{1,0:T(8,128)(2,1)S(1)}, u32[]{:S(2)}, u32[]{:S(2)}) %collective-permute-start.61) | collective-permute-done | bytes 307232 | tf_op jit(solution)/shard_map/ppermute | solution.py:693
  (453 shorter events, 144.0 us)
Async XLA Ops:
  7.2 124.4 %all-gather.5.cloned.1.call-start = ((), (), s32[]{:S(2)}) async-start(), calls=%async_computation.6 | async-start | bytes 2764800 | tf_op jit(solution)/shard_map/all_gather | solution.py:849
  10.0 32.5 %collective-permute-start.5 = (bf16[96,768]{1,0:T(8,128)(2,1)}, bf16[96,768]{1,0:T(8,128)(2,1)}, u32[]{:S(2)}, u32[]{:S(2)}) collective-permute-start(bf16[96,768]{1,0:T(8,128)(2,1)} %constant_dynamic-slice_fusion.2), channel_id=1, source_target_pairs={{0,4},{1,5},{2,6},{3,7},{4,0},{5,1},{6,2},{7,3},{8,12},{9,13},{10,... | collective-permute-start | bytes 442376 | tf_op jit(solution)/shard_map/ppermute | solution.py:698
  12.6 29.9 %collective-permute-start.6 = (bf16[96,768]{1,0:T(8,128)(2,1)}, bf16[96,768]{1,0:T(8,128)(2,1)}, u32[]{:S(2)}, u32[]{:S(2)}) collective-permute-start(bf16[96,768]{1,0:T(8,128)(2,1)} %constant_dynamic-slice_fusion.2), channel_id=1, source_target_pairs={{0,6},{1,7},{2,0},{3,1},{4,2},{5,3},{6,4},{7,5},{8,14},{9,15},{10,... | collective-permute-start | bytes 442376 | tf_op jit(solution)/shard_map/ppermute | solution.py:698
  13.1 29.5 %collective-permute-start.4 = (bf16[96,768]{1,0:T(8,128)(2,1)}, bf16[96,768]{1,0:T(8,128)(2,1)}, u32[]{:S(2)}, u32[]{:S(2)}) collective-permute-start(bf16[96,768]{1,0:T(8,128)(2,1)} %constant_dynamic-slice_fusion.2), channel_id=1, source_target_pairs={{0,2},{1,3},{2,4},{3,5},{4,6},{5,7},{6,0},{7,1},{8,10},{9,11},{10,... | collective-permute-start | bytes 442376 | tf_op jit(solution)/shard_map/ppermute | solution.py:698
  16.8 26.8 %collective-permute-start = (bf16[96,1536]{1,0:T(8,128)(2,1)}, bf16[96,1536]{1,0:T(8,128)(2,1)}, u32[]{:S(2)}, u32[]{:S(2)}) collective-permute-start(bf16[96,1536]{1,0:T(8,128)(2,1)} %get-tuple-element.227), channel_id=1, source_target_pairs={{0,1},{1,2},{2,3},{3,4},{4,5},{5,6},{6,7},{8,9},{9,10},{10,11},{11... | collective-permute-start | bytes 884744 | tf_op jit(solution)/shard_map/ppermute | solution.py:627
  18.7 26.3 %collective-permute-start.1 = (bf16[96,1536]{1,0:T(8,128)(2,1)}, bf16[96,1536]{1,0:T(8,128)(2,1)}, u32[]{:S(2)}, u32[]{:S(2)}) collective-permute-start(bf16[96,1536]{1,0:T(8,128)(2,1)} %get-tuple-element.226), channel_id=1, source_target_pairs={{1,0},{2,1},{3,2},{4,3},{5,4},{6,5},{7,6},{9,8},{10,9},{11,10},{12... | collective-permute-start | bytes 884744 | tf_op jit(solution)/shard_map/ppermute | solution.py:628
  23.3 207.0 %all-gather.7.cloned.1.call-start = ((), (), s32[]{:S(2)}) async-start(), calls=%async_computation.7 | async-start | bytes 2654208 | tf_op jit(solution)/shard_map/all_gather | solution.py:757
  46.5 11.7 %collective-permute-start.2 = (bf16[144,1536]{1,0:T(8,128)(2,1)S(1)}, bf16[144,1536]{1,0:T(8,128)(2,1)S(1)}, u32[]{:S(2)}, u32[]{:S(2)}) collective-permute-start(bf16[144,1536]{1,0:T(8,128)(2,1)S(1)} %get-tuple-element.195), channel_id=1, source_target_pairs={{0,8},{8,16},{16,24},{1,9},{9,17},{17,25},{2,10},{10,18},{18,26},{... | collective-permute-start | bytes 1327112 | tf_op jit(solution)/shard_map/ppermute | solution.py:631
  49.9 19.7 %collective-permute-start.3 = (bf16[144,1536]{1,0:T(8,128)(2,1)S(1)}, bf16[144,1536]{1,0:T(8,128)(2,1)S(1)}, u32[]{:S(2)}, u32[]{:S(2)}) collective-permute-start(bf16[144,1536]{1,0:T(8,128)(2,1)S(1)} %get-tuple-element.194), channel_id=1, source_target_pairs={{8,0},{16,8},{24,16},{9,1},{17,9},{25,17},{10,2},{18,10},{26,18},{... | collective-permute-start | bytes 1327112 | tf_op jit(solution)/shard_map/ppermute | solution.py:632
  71.7 22.1 %collective-permute-start.18 = (bf16[192,768]{1,0:T(8,128)(2,1)S(1)}, bf16[192,768]{1,0:T(8,128)(2,1)S(1)}, u32[]{:S(2)}, u32[]{:S(2)}) collective-permute-start(bf16[192,768]{1,0:T(8,128)(2,1)S(1)} %pad_maximum_fusion.10), channel_id=1, source_target_pairs={{0,2},{1,3},{2,4},{3,5},{4,6},{5,7},{6,0},{7,1},{8,10},{9,11},{10,... | collective-permute-start | bytes 884744 | tf_op jit(solution)/shard_map/ppermute | solution.py:698
  73.8 25.5 %collective-permute-start.19 = (bf16[192,768]{1,0:T(8,128)(2,1)S(1)}, bf16[192,768]{1,0:T(8,128)(2,1)S(1)}, u32[]{:S(2)}, u32[]{:S(2)}) collective-permute-start(bf16[192,768]{1,0:T(8,128)(2,1)S(1)} %pad_maximum_fusion.10), channel_id=1, source_target_pairs={{0,4},{1,5},{2,6},{3,7},{4,0},{5,1},{6,2},{7,3},{8,12},{9,13},{10,... | collective-permute-start | bytes 884744 | tf_op jit(solution)/shard_map/ppermute | solution.py:698
  74.5 25.5 %collective-permute-start.20 = (bf16[192,768]{1,0:T(8,128)(2,1)S(1)}, bf16[192,768]{1,0:T(8,128)(2,1)S(1)}, u32[]{:S(2)}, u32[]{:S(2)}) collective-permute-start(bf16[192,768]{1,0:T(8,128)(2,1)S(1)} %pad_maximum_fusion.10), channel_id=1, source_target_pairs={{0,6},{1,7},{2,0},{3,1},{4,2},{5,3},{6,4},{7,5},{8,14},{9,15},{10,... | collective-permute-start | bytes 884744 | tf_op jit(solution)/shard_map/ppermute | solution.py:698
  76.6 28.0 %collective-permute-start.7 = (bf16[3,48,768]{2,1,0:T(8,128)(2,1)S(1)}, bf16[3,48,768]{2,1,0:T(8,128)(2,1)S(1)}, u32[]{:S(2)}, u32[]{:S(2)}) collective-permute-start(bf16[3,48,768]{2,1,0:T(8,128)(2,1)S(1)} %get-tuple-element.229.refs_1_), channel_id=1, source_target_pairs={{0,8},{8,0},{16,24},{24,16},{1,9},{9,1},{17,25},{25,17},{2,10},{10... | collective-permute-start | bytes 663560 | tf_op jit(solution)/shard_map/ppermute | solution.py:693
  100.3 17.9 %collective-permute-start.23 = (bf16[3,96,768]{2,1,0:T(8,128)(2,1)S(1)}, bf16[3,96,768]{2,1,0:T(8,128)(2,1)S(1)}, u32[]{:S(2)}, u32[]{:S(2)}) collective-permute-start(bf16[3,96,768]{2,1,0:T(8,128)(2,1)S(1)} %get-tuple-element.192.refs_5_), channel_id=1, source_target_pairs={{0,16},{8,24},{16,0},{24,8},{1,17},{9,25},{17,1},{25,9},{2,18},{10... | collective-permute-start | bytes 1327112 | tf_op jit(solution)/shard_map/ppermute | solution.py:693
  100.4 16.7 %collective-permute-start.9 = (bf16[3,48,768]{2,1,0:T(8,128)(2,1)S(1)}, bf16[3,48,768]{2,1,0:T(8,128)(2,1)S(1)}, u32[]{:S(2)}, u32[]{:S(2)}) collective-permute-start(bf16[3,48,768]{2,1,0:T(8,128)(2,1)S(1)} %get-tuple-element.228.refs_4_), channel_id=1, source_target_pairs={{0,16},{8,24},{16,0},{24,8},{1,17},{9,25},{17,1},{25,9},{2,18},{10... | collective-permute-start | bytes 663560 | tf_op jit(solution)/shard_map/ppermute | solution.py:693
  102.4 18.2 %collective-permute-start.21 = (bf16[3,96,768]{2,1,0:T(8,128)(2,1)S(1)}, bf16[3,96,768]{2,1,0:T(8,128)(2,1)S(1)}, u32[]{:S(2)}, u32[]{:S(2)}) collective-permute-start(bf16[3,96,768]{2,1,0:T(8,128)(2,1)S(1)} %get-tuple-element.193.refs_2_), channel_id=1, source_target_pairs={{0,8},{8,0},{16,24},{24,16},{1,9},{9,1},{17,25},{25,17},{2,10},{10... | collective-permute-start | bytes 1327112 | tf_op jit(solution)/shard_map/ppermute | solution.py:693
  104.6 17.1 %collective-permute-start.12 = (bf16[3,48,768]{2,1,0:T(8,128)(2,1)S(1)}, bf16[3,48,768]{2,1,0:T(8,128)(2,1)S(1)}, u32[]{:S(2)}, u32[]{:S(2)}) collective-permute-start(bf16[3,48,768]{2,1,0:T(8,128)(2,1)S(1)} %get-tuple-element.229.refs_1_), channel_id=1, source_target_pairs={{0,1},{1,0},{2,3},{3,2},{4,5},{5,4},{6,7},{7,6},{8,9},{9,8},{10,11... | collective-permute-start | bytes 663560 | tf_op jit(solution)/shard_map/ppermute | solution.py:693
  104.6 17.6 %collective-permute-start.15 = (bf16[3,48,768]{2,1,0:T(8,128)(2,1)S(1)}, bf16[3,48,768]{2,1,0:T(8,128)(2,1)S(1)}, u32[]{:S(2)}, u32[]{:S(2)}) collective-permute-start(bf16[3,48,768]{2,1,0:T(8,128)(2,1)S(1)} %get-tuple-element.228.refs_4_), channel_id=1, source_target_pairs={{0,1},{1,0},{2,3},{3,2},{4,5},{5,4},{6,7},{7,6},{8,9},{9,8},{10,11... | collective-permute-start | bytes 663560 | tf_op jit(solution)/shard_map/ppermute | solution.py:693
  117.1 13.2 %collective-permute-start.8 = (bf16[6,48,768]{2,1,0:T(8,128)(2,1)S(1)}, bf16[6,48,768]{2,1,0:T(8,128)(2,1)}, u32[]{:S(2)}, u32[]{:S(2)}) collective-permute-start(bf16[6,48,768]{2,1,0:T(8,128)(2,1)S(1)} %pad_maximum_fusion.7), channel_id=1, source_target_pairs={{0,16},{8,24},{16,0},{24,8},{1,17},{9,25},{17,1},{25,9},{2,18},{10... | collective-permute-start | bytes 1327112 | tf_op jit(solution)/shard_map/ppermute | solution.py:693
  118.2 13.4 %collective-permute-start.10 = (bf16[6,48,768]{2,1,0:T(8,128)(2,1)}, bf16[6,48,768]{2,1,0:T(8,128)(2,1)}, u32[]{:S(2)}, u32[]{:S(2)}) collective-permute-start(bf16[6,48,768]{2,1,0:T(8,128)(2,1)} %pad_maximum_fusion.8), channel_id=1, source_target_pairs={{0,8},{8,0},{16,24},{24,16},{1,9},{9,1},{17,25},{25,17},{2,10},{10... | collective-permute-start | bytes 1327112 | tf_op jit(solution)/shard_map/ppermute | solution.py:693
  121.7 26.9 %collective-permute-start.24 = (bf16[6,96,768]{2,1,0:T(8,128)(2,1)}, bf16[6,96,768]{2,1,0:T(8,128)(2,1)}, u32[]{:S(2)}, u32[]{:S(2)}) collective-permute-start(bf16[6,96,768]{2,1,0:T(8,128)(2,1)} %pad_maximum_fusion.2), channel_id=1, source_target_pairs={{0,8},{8,0},{16,24},{24,16},{1,9},{9,1},{17,25},{25,17},{2,10},{10... | collective-permute-start | bytes 2654216 | tf_op jit(solution)/shard_map/ppermute | solution.py:693
  122.4 26.2 %collective-permute-start.22 = (bf16[6,96,768]{2,1,0:T(8,128)(2,1)}, bf16[6,96,768]{2,1,0:T(8,128)(2,1)}, u32[]{:S(2)}, u32[]{:S(2)}) collective-permute-start(bf16[6,96,768]{2,1,0:T(8,128)(2,1)} %pad_maximum_fusion.1), channel_id=1, source_target_pairs={{0,16},{8,24},{16,0},{24,8},{1,17},{9,25},{17,1},{25,9},{2,18},{10... | collective-permute-start | bytes 2654216 | tf_op jit(solution)/shard_map/ppermute | solution.py:693
  126.4 14.4 %collective-permute-start.11 = (bf16[96,3072]{1,0:T(8,128)(2,1)S(1)}, bf16[96,3072]{1,0:T(8,128)(2,1)}, u32[]{:S(2)}, u32[]{:S(2)}) collective-permute-start(bf16[96,3072]{1,0:T(8,128)(2,1)S(1)} %constant_dynamic-update-slice_fusion.3.refs_0_), channel_id=1, source_target_pairs={{0,1},{1,0},{2,3},{3,2},{4,5},{5,4},{6,7},{7,6},{8,9},{9,8},{10,11... | collective-permute-start | bytes 1769480 | tf_op jit(solution)/shard_map/ppermute | solution.py:693
  130.3 11.1 %collective-permute-start.14 = (bf16[6,48,768]{2,1,0:T(8,128)(2,1)}, bf16[6,48,768]{2,1,0:T(8,128)(2,1)}, u32[]{:S(2)}, u32[]{:S(2)}) collective-permute-start(bf16[6,48,768]{2,1,0:T(8,128)(2,1)} %collective-permute-done.8.refs_3_), channel_id=1, source_target_pairs={{0,1},{1,0},{2,3},{3,2},{4,5},{5,4},{6,7},{7,6},{8,9},{9,8},{10,11... | collective-permute-start | bytes 1327112 | tf_op jit(solution)/shard_map/ppermute | solution.py:693
  140.8 49.5 %collective-permute-start.25 = (bf16[96,3072]{1,0:T(8,128)(2,1)S(1)}, bf16[96,3072]{1,0:T(8,128)(2,1)}, u32[]{:S(2)}, u32[]{:S(2)}) collective-permute-start(bf16[96,3072]{1,0:T(8,128)(2,1)S(1)} %copy-done.21), channel_id=1, source_target_pairs={{0,1},{1,0},{2,3},{3,2},{4,5},{5,4},{6,7},{7,6},{8,9},{9,8},{10,11... | collective-permute-start | bytes 1769480 | tf_op jit(solution)/shard_map/ppermute | solution.py:693
  141.3 49.0 %collective-permute-start.26 = (bf16[384,768]{1,0:T(8,128)(2,1)S(1)}, bf16[384,768]{1,0:T(8,128)(2,1)}, u32[]{:S(2)}, u32[]{:S(2)}) collective-permute-start(bf16[384,768]{1,0:T(8,128)(2,1)S(1)} %copy-done.22), channel_id=1, source_target_pairs={{0,1},{1,0},{2,3},{3,2},{4,5},{5,4},{6,7},{7,6},{8,9},{9,8},{10,11... | collective-permute-start | bytes 1769480 | tf_op jit(solution)/shard_map/ppermute | solution.py:693
  141.4 49.4 %collective-permute-start.27 = (bf16[3,96,768]{2,1,0:T(8,128)(2,1)S(1)}, bf16[3,96,768]{2,1,0:T(8,128)(2,1)}, u32[]{:S(2)}, u32[]{:S(2)}) collective-permute-start(bf16[3,96,768]{2,1,0:T(8,128)(2,1)S(1)} %get-tuple-element.193.refs_2_), channel_id=1, source_target_pairs={{0,1},{1,0},{2,3},{3,2},{4,5},{5,4},{6,7},{7,6},{8,9},{9,8},{10,11... | collective-permute-start | bytes 1327112 | tf_op jit(solution)/shard_map/ppermute | solution.py:693
  148.6 49.5 %collective-permute-start.32 = (bf16[6,96,768]{2,1,0:T(8,128)(2,1)}, bf16[6,96,768]{2,1,0:T(8,128)(2,1)}, u32[]{:S(2)}, u32[]{:S(2)}) collective-permute-start(bf16[6,96,768]{2,1,0:T(8,128)(2,1)} %collective-permute-done.24.refs_7_), channel_id=1, source_target_pairs={{0,1},{1,0},{2,3},{3,2},{4,5},{5,4},{6,7},{7,6},{8,9},{9,8},{10,11... | collective-permute-start | bytes 2654216 | tf_op jit(solution)/shard_map/ppermute | solution.py:693
  148.6 49.5 %collective-permute-start.29 = (bf16[6,96,768]{2,1,0:T(8,128)(2,1)}, bf16[6,96,768]{2,1,0:T(8,128)(2,1)}, u32[]{:S(2)}, u32[]{:S(2)}) collective-permute-start(bf16[6,96,768]{2,1,0:T(8,128)(2,1)} %collective-permute-done.22.refs_4_), channel_id=1, source_target_pairs={{0,1},{1,0},{2,3},{3,2},{4,5},{5,4},{6,7},{7,6},{8,9},{9,8},{10,11... | collective-permute-start | bytes 2654216 | tf_op jit(solution)/shard_map/ppermute | solution.py:693
  164.2 223.5 %reduce-scatter.6.cloned.1.call-start = ((), (), s32[]{:S(2)}) async-start(), calls=%async_computation.4 | async-start | bytes 884736 | tf_op jit(solution)/shard_map/reduce_scatter | solution.py:807
  192.2 15.4 %collective-permute-start.37 = (bf16[144,1]{0,1:T(2,128)(2,1)S(1)}, bf16[144,1]{0,1:T(2,128)(2,1)S(1)}, u32[]{:S(2)}, u32[]{:S(2)}) collective-permute-start(bf16[144,1]{0,1:T(2,128)(2,1)S(1)} %pad_maximum_fusion.23), channel_id=1, source_target_pairs={{8,0},{16,8},{24,16},{9,1},{17,9},{25,17},{10,2},{18,10},{26,18},{... | collective-permute-start | bytes 872 | tf_op jit(solution)/shard_map/ppermute | solution.py:644
  193.5 14.1 %collective-permute-start.38 = (bf16[144,1]{0,1:T(2,128)(2,1)S(1)}, bf16[144,1]{0,1:T(2,128)(2,1)S(1)}, u32[]{:S(2)}, u32[]{:S(2)}) collective-permute-start(bf16[144,1]{0,1:T(2,128)(2,1)S(1)} %pad_maximum_fusion.24), channel_id=1, source_target_pairs={{0,8},{8,16},{16,24},{1,9},{9,17},{17,25},{2,10},{10,18},{18,26},{... | collective-permute-start | bytes 872 | tf_op jit(solution)/shard_map/ppermute | solution.py:645
  207.9 21.8 %collective-permute-start.39 = (bf16[96,1]{0,1:T(2,128)(2,1)S(1)}, bf16[96,1]{0,1:T(2,128)(2,1)S(1)}, u32[]{:S(2)}, u32[]{:S(2)}) collective-permute-start(bf16[96,1]{0,1:T(2,128)(2,1)S(1)} %get-tuple-element.250), channel_id=1, source_target_pairs={{1,0},{2,1},{3,2},{4,3},{5,4},{6,5},{7,6},{9,8},{10,9},{11,10},{12... | collective-permute-start | bytes 584 | tf_op jit(solution)/shard_map/ppermute | solution.py:648
  209.9 19.9 %collective-permute-start.40 = (bf16[96,1]{0,1:T(2,128)(2,1)S(1)}, bf16[96,1]{0,1:T(2,128)(2,1)S(1)}, u32[]{:S(2)}, u32[]{:S(2)}) collective-permute-start(bf16[96,1]{0,1:T(2,128)(2,1)S(1)} %get-tuple-element.251), channel_id=1, source_target_pairs={{0,1},{1,2},{2,3},{3,4},{4,5},{5,6},{6,7},{8,9},{9,10},{10,11},{11... | collective-permute-start | bytes 584 | tf_op jit(solution)/shard_map/ppermute | solution.py:649
  294.7 32.2 %collective-permute-start.46 = (bf16[4,4,96,768]{3,2,1,0:T(8,128)(2,1)}, bf16[4,4,96,768]{3,2,1,0:T(8,128)(2,1)}, u32[]{:S(2)}, u32[]{:S(2)}) collective-permute-start(bf16[4,4,96,768]{3,2,1,0:T(8,128)(2,1)} %get-tuple-element.128), channel_id=1, source_target_pairs={{0,1},{1,0},{2,3},{3,2},{4,5},{5,4},{6,7},{7,6},{8,9},{9,8},{10,11... | collective-permute-start | bytes 7077896 | tf_op jit(solution)/shard_map/ppermute | solution.py:693
  294.8 32.2 %collective-permute-start.45 = (bf16[4,4,96,768]{3,2,1,0:T(8,128)(2,1)}, bf16[4,4,96,768]{3,2,1,0:T(8,128)(2,1)}, u32[]{:S(2)}, u32[]{:S(2)}) collective-permute-start(bf16[4,4,96,768]{3,2,1,0:T(8,128)(2,1)} %get-tuple-element.125), channel_id=1, source_target_pairs={{0,1},{1,0},{2,3},{3,2},{4,5},{5,4},{6,7},{7,6},{8,9},{9,8},{10,11... | collective-permute-start | bytes 7077896 | tf_op jit(solution)/shard_map/ppermute | solution.py:693
  303.3 85.3 %reduce-scatter.8.cloned.1.call-start = ((), (), s32[]{:S(2)}) async-start(), calls=%async_computation.5 | async-start | bytes 1769472 | tf_op jit(solution)/shard_map/reduce_scatter | solution.py:807
  317.8 217.7 %reduce-scatter.4.cloned.1.call-start = ((), (), s32[]{:S(2)}) async-start(), calls=%async_computation.3 | async-start | bytes 2764800 | tf_op jit(solution)/shard_map/reduce_scatter | solution.py:933
  333.1 39.7 %collective-permute-start.48 = (bf16[2,4,96,768]{3,2,1,0:T(8,128)(2,1)}, bf16[2,4,96,768]{3,2,1,0:T(8,128)(2,1)S(1)}, u32[]{:S(2)}, u32[]{:S(2)}) collective-permute-start(bf16[2,4,96,768]{3,2,1,0:T(8,128)(2,1)} %get-tuple-element.134), channel_id=1, source_target_pairs={{0,16},{8,24},{16,0},{24,8},{1,17},{9,25},{17,1},{25,9},{2,18},{10... | collective-permute-start | bytes 3538952 | tf_op jit(solution)/shard_map/ppermute | solution.py:693
  339.1 33.7 %collective-permute-start.47 = (bf16[2,4,96,768]{3,2,1,0:T(8,128)(2,1)}, bf16[2,4,96,768]{3,2,1,0:T(8,128)(2,1)S(1)}, u32[]{:S(2)}, u32[]{:S(2)}) collective-permute-start(bf16[2,4,96,768]{3,2,1,0:T(8,128)(2,1)} %fusion.10), channel_id=1, source_target_pairs={{0,8},{8,0},{16,24},{24,16},{1,9},{9,1},{17,25},{25,17},{2,10},{10... | collective-permute-start | bytes 3538952 | tf_op jit(solution)/shard_map/ppermute | solution.py:693
  385.9 32.6 %collective-permute-start.49 = (bf16[4,4,96,768]{3,2,1,0:T(8,128)(2,1)}, bf16[4,4,96,768]{3,2,1,0:T(8,128)(2,1)}, u32[]{:S(2)}, u32[]{:S(2)}) collective-permute-start(bf16[4,4,96,768]{3,2,1,0:T(8,128)(2,1)} %get-tuple-element.139), channel_id=1, source_target_pairs={{0,1},{1,0},{2,3},{3,2},{4,5},{5,4},{6,7},{7,6},{8,9},{9,8},{10,11... | collective-permute-start | bytes 7077896 | tf_op jit(solution)/shard_map/ppermute | solution.py:693
  389.7 9.9 %collective-permute-start.77 = (bf16[288,512]{1,0:T(8,128)(2,1)S(1)}, bf16[288,512]{1,0:T(8,128)(2,1)S(1)}, u32[]{:S(2)}, u32[]{:S(2)}) collective-permute-start(bf16[288,512]{1,0:T(8,128)(2,1)S(1)} %constant_dynamic-update-slice_fusion.8), channel_id=1, source_target_pairs={{0,8},{8,0},{16,24},{24,16},{1,9},{9,1},{17,25},{25,17},{2,10},{10... | collective-permute-start | bytes 884744 | tf_op jit(solution)/shard_map/ppermute | solution.py:693
  394.7 21.5 %collective-permute-start.51 = (bf16[4,96,768]{2,1,0:T(8,128)(2,1)S(1)}, bf16[4,96,768]{2,1,0:T(8,128)(2,1)S(1)}, u32[]{:S(2)}, u32[]{:S(2)}) collective-permute-start(bf16[4,96,768]{2,1,0:T(8,128)(2,1)S(1)} %copy-done.28), channel_id=1, source_target_pairs={{0,8},{8,0},{16,24},{24,16},{1,9},{9,1},{17,25},{25,17},{2,10},{10... | collective-permute-start | bytes 1769480 | tf_op jit(solution)/shard_map/ppermute | solution.py:693
  395.1 21.1 %collective-permute-start.50 = (bf16[4,96,768]{2,1,0:T(8,128)(2,1)S(1)}, bf16[4,96,768]{2,1,0:T(8,128)(2,1)S(1)}, u32[]{:S(2)}, u32[]{:S(2)}) collective-permute-start(bf16[4,96,768]{2,1,0:T(8,128)(2,1)S(1)} %copy-done.27), channel_id=1, source_target_pairs={{0,16},{8,24},{16,0},{24,8},{1,17},{9,25},{17,1},{25,9},{2,18},{10... | collective-permute-start | bytes 1769480 | tf_op jit(solution)/shard_map/ppermute | solution.py:693
  399.7 16.5 %collective-permute-start.78 = (bf16[288,512]{1,0:T(8,128)(2,1)S(1)}, bf16[288,512]{1,0:T(8,128)(2,1)S(1)}, u32[]{:S(2)}, u32[]{:S(2)}) collective-permute-start(bf16[288,512]{1,0:T(8,128)(2,1)S(1)} %add_convert_fusion.11), channel_id=1, source_target_pairs={{0,16},{8,24},{16,0},{24,8},{1,17},{9,25},{17,1},{25,9},{2,18},{10... | collective-permute-start | bytes 884744 | tf_op jit(solution)/shard_map/ppermute | solution.py:693
  422.6 14.1 %collective-permute-start.53 = (bf16[2,4,48,768]{3,2,1,0:T(8,128)(2,1)}, bf16[2,4,48,768]{3,2,1,0:T(8,128)(2,1)}, u32[]{:S(2)}, u32[]{:S(2)}) collective-permute-start(bf16[2,4,48,768]{3,2,1,0:T(8,128)(2,1)} %get-tuple-element.150), channel_id=1, source_target_pairs={{0,16},{8,24},{16,0},{24,8},{1,17},{9,25},{17,1},{25,9},{2,18},{10... | collective-permute-start | bytes 1769480 | tf_op jit(solution)/shard_map/ppermute | solution.py:693
  422.9 14.0 %collective-permute-start.52 = (bf16[2,4,48,768]{3,2,1,0:T(8,128)(2,1)}, bf16[2,4,48,768]{3,2,1,0:T(8,128)(2,1)}, u32[]{:S(2)}, u32[]{:S(2)}) collective-permute-start(bf16[2,4,48,768]{3,2,1,0:T(8,128)(2,1)} %get-tuple-element.148), channel_id=1, source_target_pairs={{0,8},{8,0},{16,24},{24,16},{1,9},{9,1},{17,25},{25,17},{2,10},{10... | collective-permute-start | bytes 1769480 | tf_op jit(solution)/shard_map/ppermute | solution.py:693
  439.6 15.5 %collective-permute-start.55 = (bf16[4,48,768]{2,1,0:T(8,128)(2,1)}, bf16[4,48,768]{2,1,0:T(8,128)(2,1)}, u32[]{:S(2)}, u32[]{:S(2)}) collective-permute-start(bf16[4,48,768]{2,1,0:T(8,128)(2,1)} %fusion.43), channel_id=1, source_target_pairs={{0,8},{8,0},{16,24},{24,16},{1,9},{9,1},{17,25},{25,17},{2,10},{10... | collective-permute-start | bytes 884744 | tf_op jit(solution)/shard_map/ppermute | solution.py:693
  441.2 15.9 %collective-permute-start.54 = (bf16[4,48,768]{2,1,0:T(8,128)(2,1)S(1)}, bf16[4,48,768]{2,1,0:T(8,128)(2,1)}, u32[]{:S(2)}, u32[]{:S(2)}) collective-permute-start(bf16[4,48,768]{2,1,0:T(8,128)(2,1)S(1)} %fusion.42), channel_id=1, source_target_pairs={{0,16},{8,24},{16,0},{24,8},{1,17},{9,25},{17,1},{25,9},{2,18},{10... | collective-permute-start | bytes 884744 | tf_op jit(solution)/shard_map/ppermute | solution.py:693
  451.6 11.3 %collective-permute-start.72 = (bf16[96,768]{1,0:T(8,128)(2,1)}, bf16[96,768]{1,0:T(8,128)(2,1)S(1)}, u32[]{:S(2)}, u32[]{:S(2)}) collective-permute-start(bf16[96,768]{1,0:T(8,128)(2,1)} %get-tuple-element.204), channel_id=1, source_target_pairs={{0,2},{1,3},{2,4},{3,5},{4,6},{5,7},{6,0},{7,1},{8,10},{9,11},{10,... | collective-permute-start | bytes 442376 | tf_op jit(solution)/shard_map/ppermute | solution.py:698
  453.0 23.7 %collective-permute-start.73 = (bf16[96,768]{1,0:T(8,128)(2,1)}, bf16[96,768]{1,0:T(8,128)(2,1)S(1)}, u32[]{:S(2)}, u32[]{:S(2)}) collective-permute-start(bf16[96,768]{1,0:T(8,128)(2,1)} %get-tuple-element.206), channel_id=1, source_target_pairs={{0,4},{1,5},{2,6},{3,7},{4,0},{5,1},{6,2},{7,3},{8,12},{9,13},{10,... | collective-permute-start | bytes 442376 | tf_op jit(solution)/shard_map/ppermute | solution.py:698
  455.1 24.6 %collective-permute-start.74 = (bf16[96,768]{1,0:T(8,128)(2,1)}, bf16[96,768]{1,0:T(8,128)(2,1)S(1)}, u32[]{:S(2)}, u32[]{:S(2)}) collective-permute-start(bf16[96,768]{1,0:T(8,128)(2,1)} %get-tuple-element.205), channel_id=1, source_target_pairs={{0,6},{1,7},{2,0},{3,1},{4,2},{5,3},{6,4},{7,5},{8,14},{9,15},{10,... | collective-permute-start | bytes 442376 | tf_op jit(solution)/shard_map/ppermute | solution.py:698
  455.1 33.0 %collective-permute-start.67 = (bf16[96,768]{1,0:T(8,128)(2,1)}, bf16[96,768]{1,0:T(8,128)(2,1)S(1)}, u32[]{:S(2)}, u32[]{:S(2)}) collective-permute-start(bf16[96,768]{1,0:T(8,128)(2,1)} %get-tuple-element.212), channel_id=1, source_target_pairs={{0,2},{1,3},{2,4},{3,5},{4,6},{5,7},{6,0},{7,1},{8,10},{9,11},{10,... | collective-permute-start | bytes 442376 | tf_op jit(solution)/shard_map/ppermute | solution.py:698
  457.1 35.0 %collective-permute-start.68 = (bf16[96,768]{1,0:T(8,128)(2,1)S(1)}, bf16[96,768]{1,0:T(8,128)(2,1)S(1)}, u32[]{:S(2)}, u32[]{:S(2)}) collective-permute-start(bf16[96,768]{1,0:T(8,128)(2,1)S(1)} %get-tuple-element.214), channel_id=1, source_target_pairs={{0,4},{1,5},{2,6},{3,7},{4,0},{5,1},{6,2},{7,3},{8,12},{9,13},{10,... | collective-permute-start | bytes 442376 | tf_op jit(solution)/shard_map/ppermute | solution.py:698
  462.9 31.5 %collective-permute-start.69 = (bf16[96,768]{1,0:T(8,128)(2,1)S(1)}, bf16[96,768]{1,0:T(8,128)(2,1)S(1)}, u32[]{:S(2)}, u32[]{:S(2)}) collective-permute-start(bf16[96,768]{1,0:T(8,128)(2,1)S(1)} %get-tuple-element.213), channel_id=1, source_target_pairs={{0,6},{1,7},{2,0},{3,1},{4,2},{5,3},{6,4},{7,5},{8,14},{9,15},{10,... | collective-permute-start | bytes 442376 | tf_op jit(solution)/shard_map/ppermute | solution.py:698
  479.8 29.4 %collective-permute-start.75 = (bf16[96,768]{1,0:T(8,128)(2,1)S(1)}, bf16[96,768]{1,0:T(8,128)(2,1)S(1)}, u32[]{:S(2)}, u32[]{:S(2)}) collective-permute-start(bf16[96,768]{1,0:T(8,128)(2,1)S(1)} %add_convert_fusion.12), channel_id=1, source_target_pairs={{0,16},{8,24},{16,0},{24,8},{1,17},{9,25},{17,1},{25,9},{2,18},{10... | collective-permute-start | bytes 442376 | tf_op jit(solution)/shard_map/ppermute | solution.py:693
  496.3 15.0 %collective-permute-start.70 = (bf16[96,768]{1,0:T(8,128)(2,1)S(1)}, bf16[96,768]{1,0:T(8,128)(2,1)S(1)}, u32[]{:S(2)}, u32[]{:S(2)}) collective-permute-start(bf16[96,768]{1,0:T(8,128)(2,1)S(1)} %add_convert_fusion.13), channel_id=1, source_target_pairs={{0,8},{8,0},{16,24},{24,16},{1,9},{9,1},{17,25},{25,17},{2,10},{10... | collective-permute-start | bytes 442376 | tf_op jit(solution)/shard_map/ppermute | solution.py:693
  497.9 10.8 %collective-permute-start.56 = (bf16[144,768]{1,0:T(8,128)(2,1)S(1)}, bf16[144,768]{1,0:T(8,128)(2,1)S(1)}, u32[]{:S(2)}, u32[]{:S(2)}) collective-permute-start(bf16[144,768]{1,0:T(8,128)(2,1)S(1)} %pad_maximum_fusion.15), channel_id=1, source_target_pairs={{8,0},{16,8},{24,16},{9,1},{17,9},{25,17},{10,2},{18,10},{26,18},{... | collective-permute-start | bytes 663560 | tf_op jit(solution)/shard_map/ppermute | solution.py:644
  499.4 28.0 %collective-permute-start.62 = (bf16[96,768]{1,0:T(8,128)(2,1)S(1)}, bf16[96,768]{1,0:T(8,128)(2,1)S(1)}, u32[]{:S(2)}, u32[]{:S(2)}) collective-permute-start(bf16[96,768]{1,0:T(8,128)(2,1)S(1)} %get-tuple-element.220), channel_id=1, source_target_pairs={{0,2},{1,3},{2,4},{3,5},{4,6},{5,7},{6,0},{7,1},{8,10},{9,11},{10,... | collective-permute-start | bytes 442376 | tf_op jit(solution)/shard_map/ppermute | solution.py:698
  499.6 27.7 %collective-permute-start.63 = (bf16[96,768]{1,0:T(8,128)(2,1)S(1)}, bf16[96,768]{1,0:T(8,128)(2,1)S(1)}, u32[]{:S(2)}, u32[]{:S(2)}) collective-permute-start(bf16[96,768]{1,0:T(8,128)(2,1)S(1)} %get-tuple-element.222), channel_id=1, source_target_pairs={{0,4},{1,5},{2,6},{3,7},{4,0},{5,1},{6,2},{7,3},{8,12},{9,13},{10,... | collective-permute-start | bytes 442376 | tf_op jit(solution)/shard_map/ppermute | solution.py:698
  508.8 18.6 %collective-permute-start.64 = (bf16[96,768]{1,0:T(8,128)(2,1)S(1)}, bf16[96,768]{1,0:T(8,128)(2,1)S(1)}, u32[]{:S(2)}, u32[]{:S(2)}) collective-permute-start(bf16[96,768]{1,0:T(8,128)(2,1)S(1)} %get-tuple-element.223), channel_id=1, source_target_pairs={{0,6},{1,7},{2,0},{3,1},{4,2},{5,3},{6,4},{7,5},{8,14},{9,15},{10,... | collective-permute-start | bytes 442376 | tf_op jit(solution)/shard_map/ppermute | solution.py:698
  511.3 24.0 %collective-permute-start.76 = (bf16[2,96,768]{2,1,0:T(8,128)(2,1)S(1)}, bf16[2,96,768]{2,1,0:T(8,128)(2,1)S(1)}, u32[]{:S(2)}, u32[]{:S(2)}) collective-permute-start(bf16[2,96,768]{2,1,0:T(8,128)(2,1)S(1)} %pad_maximum_fusion.14), channel_id=1, source_target_pairs={{0,8},{8,0},{16,24},{24,16},{1,9},{9,1},{17,25},{25,17},{2,10},{10... | collective-permute-start | bytes 884744 | tf_op jit(solution)/shard_map/ppermute | solution.py:693
  532.8 10.3 %collective-permute-start.66 = (bf16[2,96,768]{2,1,0:T(8,128)(2,1)S(1)}, bf16[2,96,768]{2,1,0:T(8,128)(2,1)S(1)}, u32[]{:S(2)}, u32[]{:S(2)}) collective-permute-start(bf16[2,96,768]{2,1,0:T(8,128)(2,1)S(1)} %pad_maximum_fusion.12), channel_id=1, source_target_pairs={{0,16},{8,24},{16,0},{24,8},{1,17},{9,25},{17,1},{25,9},{2,18},{10... | collective-permute-start | bytes 884744 | tf_op jit(solution)/shard_map/ppermute | solution.py:693
  535.5 10.0 %collective-permute-start.60 = (bf16[200,768]{1,0:T(8,128)(2,1)}, bf16[200,768]{1,0:T(8,128)(2,1)S(1)}, u32[]{:S(2)}, u32[]{:S(2)}) collective-permute-start(bf16[200,768]{1,0:T(8,128)(2,1)} %bitcast.288), channel_id=1, source_target_pairs={{0,8},{8,0},{16,24},{24,16},{1,9},{9,1},{17,25},{25,17},{2,10},{10... | collective-permute-start | bytes 921608 | tf_op jit(solution)/shard_map/ppermute | solution.py:693
  (92 other events, 1048.9 us)
Sparse Core Ops, SparseCore 0:
  23.4 32.6 all-gather.4
  164.3 30.8 all-gather.6
  303.4 27.2 reduce-scatter.5
  333.0 32.4 reduce-scatter.7
  450.2 58.6 reduce-scatter.3

commit v2 on v1

v2 whole, which is shorter than its diff:
```python
import functools
import jax
import jax.numpy as jnp
import numpy as np
from jax import lax
from jax.experimental import pallas as pl
from jax.experimental.pallas import tpu as pltpu
from jax.sharding import PartitionSpec as P

HEADS = 12
MARGIN = 2
norm_eps = 1e-06
VMEM_BYTES = 56 * 1024 * 1024
f32, bf16 = jnp.float32, jnp.bfloat16


def params():
    return pltpu.CompilerParams(vmem_limit_bytes=VMEM_BYTES)


def cost(flops, nbytes):
    return pl.CostEstimate(flops=int(flops), bytes_accessed=int(nbytes), transcendentals=0)


def dot(a, b, ca=1, cb=0):
    return lax.dot_general(a, b, (((ca,), (cb,)), ((), ())), preferred_element_type=f32)


def whole(shape):
    return pl.BlockSpec(shape, lambda *_: (0,) * len(shape))


def rows(block, width):
    return pl.BlockSpec((block, width), lambda i: (i, 0))


def columns_part(gathered, width, index):
    shares, each, _ = gathered.shape
    return pl.BlockSpec((shares, each, width), lambda i: (0, 0, index(i)))


def last_part(gathered, width):
    return columns_part(gathered, width, lambda i: 3)


def patch_part(gathered, depth):
    shares, _, width = gathered.shape
    return pl.BlockSpec((shares, depth // shares, width), lambda i: (0, 0, 0))


def square(ref):
    return ref[...].reshape(-1, ref.shape[-1])


def norm_parts(hidden):
    center = jnp.mean(hidden, axis=-1, keepdims=True)
    centered = hidden - center
    spread = jnp.mean(centered * centered, axis=-1, keepdims=True)
    rstd = lax.rsqrt(spread + norm_eps)
    return centered * rstd, rstd


def token_block(tokens):
    for parts in (3, 2):
        if tokens % (16 * parts) == 0:
            return tokens // parts
    return tokens


def embed_kernel(own_ref, left_ref, right_ref, upper_ref, lower_ref, w_ref, pick_ref, table_ref, vec_ref, ext_ref, h0_ref, a_ref, *, pieces):
    refs = (own_ref, left_ref, right_ref, upper_ref, lower_ref)
    for step, held in enumerate(pieces):
        @pl.when(pl.program_id(0) == step)
        def _(held=held):
            spot = 0
            for i, start, count in held:
                ext_ref[spot : spot + count, :] = refs[i][start : start + count, :]
                spot += count
    hidden = dot(ext_ref[...], square(w_ref)) + dot(pick_ref[...], table_ref[...])
    h0_ref[...] = hidden
    xhat, _ = norm_parts(hidden)
    a_ref[...] = (xhat * vec_ref[0:1, :] + vec_ref[1:2, :]).astype(bf16)


def embed(strips, gathered, pick, table, vec):
    tokens = pick.shape[0]
    depth = strips[0].shape[1]
    width = gathered.shape[2]
    tb = token_block(tokens)
    sizes = [strips[0].shape[0]] + [s.shape[0] - 16 for s in strips[1:]]
    pieces, room = [[]], tb
    for i, size in enumerate(sizes):
        start = 0
        while start < size:
            if room == 0:
                pieces.append([])
                room = tb
            count = min(size - start, room)
            pieces[-1].append((i, start, count))
            start, room = start + count, room - count
    return pl.pallas_call(
        functools.partial(embed_kernel, pieces=pieces),
        grid=(tokens // tb,),
        in_specs=[whole(s.shape) for s in strips] + [patch_part(gathered, depth), rows(tb, pick.shape[1]),
                  whole(table.shape), whole(vec.shape)],
        out_specs=[rows(tb, depth), rows(tb, width), rows(tb, width)],
        out_shape=[jax.ShapeDtypeStruct((tokens, depth), bf16), jax.ShapeDtypeStruct((tokens, width), f32),
                   jax.ShapeDtypeStruct((tokens, width), bf16)],
        compiler_params=params(),
        cost_estimate=cost(2 * tokens * depth * width, tokens * depth * 4 + depth * width * 2 + tokens * width * 6),
        name="embed",
    )(*strips, gathered, pick, table, vec)


def columns_kernel(a_ref, w_ref, o_ref):
    o_ref[...] = dot(a_ref[...], square(w_ref)).astype(o_ref.dtype)


def project(a, gathered, count):
    tokens, width = a.shape
    half = width // 2
    return pl.pallas_call(
        columns_kernel,
        grid=(2 * count,),
        in_specs=[whole(a.shape), columns_part(gathered, half, lambda i: i)],
        out_specs=pl.BlockSpec((tokens, half), lambda i: (0, i)),
        out_shape=jax.ShapeDtypeStruct((tokens, count * width), bf16),
        compiler_params=params(),
        cost_estimate=cost(2 * tokens * width * width * count, a.size * 2 + width * width * count * 2 + tokens * width * count * 2),
        name="project",
    )(a, gathered)


def three_parts(value):
    first = value.astype(bf16)
    rest = value - first.astype(f32)
    second = rest.astype(bf16)
    third = (rest - second.astype(f32)).astype(bf16)
    return first, second, third


def in_lanes(parts, lane, tail):
    out = tail
    for spot, part in reversed(list(enumerate(parts))):
        out = jnp.where(lane == spot, part.astype(f32), out)
    return out.astype(bf16)


def attn_fwd_kernel(q_ref, k_ref, v_ref, kx_ref, o_ref, qx_ref, *, block, scale):
    tokens, pair = q_ref.shape
    half = pair // 2
    k_aug = jnp.concatenate([k_ref[...], kx_ref[...]], axis=1)
    v_aug = jnp.concatenate([v_ref[...], jnp.ones((tokens, pair), bf16)], axis=1)
    lane = lax.broadcasted_iota(jnp.int32, (block, pair), 1)
    for start in range(0, tokens, block):
        q_blk = q_ref[start : start + block, :].astype(f32) * scale
        outs = []
        for j in range(2):
            mine = (lane >= half) if j else (lane < half)
            q_aug = jnp.concatenate(
                [jnp.where(mine, q_blk, 0.0).astype(bf16),
                 jnp.where(lane == 3, 1.0, 0.0).astype(bf16)], axis=1)
            s = dot(q_aug, k_aug, 1, 1)
            top = jnp.max(s, axis=1, keepdims=True)
            p = jnp.exp(s - top).astype(bf16)
            mixed = dot(p, v_aug)
            total = mixed[:, pair:]
            outs.append(mixed[:, :pair] / total)
            lse = jnp.log(total) + top
            qx_ref[j, start : start + block, :] = in_lanes(
                three_parts(-lse), lane, jnp.where(lane == 3, 1.0, 0.0))
        o_ref[start : start + block, :] = jnp.where(lane < half, outs[0], outs[1]).astype(bf16)


def attn_fwd(qkv, kx, scale):
    tokens = qkv.shape[0]
    width = qkv.shape[1] // 3
    pairs = HEADS // 2
    pw = width // pairs
    spec = lambda part: pl.BlockSpec((tokens, pw), lambda h, part=part: (0, part * pairs + h))
    return pl.pallas_call(
        functools.partial(attn_fwd_kernel, block=token_block(tokens), scale=scale),
        grid=(pairs,),
        in_specs=[spec(0), spec(1), spec(2), whole(kx.shape)],
        out_specs=[pl.BlockSpec((tokens, pw), lambda h: (0, h)),
                   pl.BlockSpec((2, tokens, pw), lambda h: (h, 0, 0))],
        out_shape=[jax.ShapeDtypeStruct((tokens, width), bf16),
                   jax.ShapeDtypeStruct((HEADS, tokens, pw), bf16)],
        compiler_params=params(),
        cost_estimate=cost(2 * 4 * HEADS * tokens * tokens * 256, qkv.size * 2 + tokens * width * 2),
        name="attn_fwd",
    )(qkv, qkv, qkv, kx)


def attn_bwd_kernel(q_ref, k_ref, v_ref, do_ref, o_ref, qx_ref, kx_ref, d_ref, *, block, scale):
    tokens, pair = q_ref.shape
    half = pair // 2
    lane = lax.broadcasted_iota(jnp.int32, (tokens, pair), 1)
    q_all = q_ref[...].astype(f32) * scale
    do_all = do_ref[...].astype(f32)
    prod = do_all * o_ref[...].astype(f32)
    kx = kx_ref[...]
    dq = [None, None]
    dk = [None] * (tokens // block)
    dv = [None] * (tokens // block)
    for j in range(2):
        mine = (lane >= half) if j else (lane < half)
        q_j = jnp.where(mine, q_all, 0.0).astype(bf16)
        do_j = jnp.where(mine, do_all, 0.0).astype(bf16)
        delta = jnp.sum(jnp.where(mine, prod, 0.0), axis=1, keepdims=True)
        dox = in_lanes(three_parts(-delta), lane, jnp.zeros_like(prod))
        q_aug = jnp.concatenate([q_j, qx_ref[j]], axis=1)
        do_aug = jnp.concatenate([do_j, dox], axis=1)
        for b in range(tokens // block):
            at = slice(b * block, (b + 1) * block)
            k_blk = k_ref[at, :]
            sT = dot(jnp.concatenate([k_blk, kx[at]], axis=1), q_aug, 1, 1)
            pT = jnp.exp(sT)
            dpT = dot(jnp.concatenate([v_ref[at, :], kx[at]], axis=1), do_aug, 1, 1)
            dsT = (pT * dpT).astype(bf16)
            dv_b = dot(pT.astype(bf16), do_j)
            dk_b = dot(dsT, q_j)
            dq_b = dot(dsT, k_blk, 0, 0)
            dv[b] = dv_b if dv[b] is None else dv[b] + dv_b
            dk[b] = dk_b if dk[b] is None else dk[b] + dk_b
            dq[j] = dq_b if dq[j] is None else dq[j] + dq_b
    for b in range(tokens // block):
        at = slice(b * block, (b + 1) * block)
        d_ref[1, at, :] = dk[b].astype(bf16)
        d_ref[2, at, :] = dv[b].astype(bf16)
    d_ref[0] = (jnp.where(lane < half, dq[0], dq[1]) * scale).astype(bf16)


def attn_bwd(qkv, do, o, qx, kx, scale):
    tokens = qkv.shape[0]
    width = qkv.shape[1] // 3
    pairs = HEADS // 2
    pw = width // pairs
    spec = lambda part: pl.BlockSpec((tokens, pw), lambda h, part=part: (0, part * pairs + h))
    one = pl.BlockSpec((tokens, pw), lambda h: (0, h))
    return pl.pallas_call(
        functools.partial(attn_bwd_kernel, block=token_block(tokens), scale=scale),
        grid=(pairs,),
        in_specs=[spec(0), spec(1), spec(2), one, one,
                  pl.BlockSpec((2, tokens, pw), lambda h: (h, 0, 0)), whole(kx.shape)],
        out_specs=pl.BlockSpec((3, tokens, pw), lambda h: (0, 0, h)),
        out_shape=jax.ShapeDtypeStruct((3, tokens, width), bf16),
        compiler_params=params(),
        cost_estimate=cost(2 * 5 * HEADS * tokens * tokens * 256, qkv.size * 2 + tokens * width * 10),
        name="attn_bwd",
    )(qkv, qkv, qkv, do, o, qx, kx)


def proj_kernel(o_ref, w_ref, h0_ref, vec_ref, h1_ref, c_ref):
    hidden = h0_ref[...] + dot(o_ref[...], square(w_ref))
    h1_ref[...] = hidden
    xhat, _ = norm_parts(hidden)
    c_ref[...] = (xhat * vec_ref[2:3, :] + vec_ref[3:4, :]).astype(bf16)


def proj_norm(o, proj_w, h0, vec):
    tokens, width = o.shape
    tb = token_block(tokens)
    return pl.pallas_call(
        proj_kernel,
        grid=(tokens // tb,),
        in_specs=[rows(tb, width), last_part(proj_w, width), rows(tb, width), whole(vec.shape)],
        out_specs=[rows(tb, width), rows(tb, width)],
        out_shape=[jax.ShapeDtypeStruct((tokens, width), f32),
                   jax.ShapeDtypeStruct((tokens, width), bf16)],
        compiler_params=params(),
        cost_estimate=cost(2 * tokens * width * width, tokens * width * 12 + width * width * 2),
        name="proj_norm",
    )(o, proj_w, h0, vec)


def mlp_weight_specs(gathered, width):
    shares, parts, _, _ = gathered.shape
    each = width // shares
    return [pl.BlockSpec((shares, 1, each, width), lambda i, *_: (0, i, 0, 0)),
            pl.BlockSpec((shares // parts, parts, each, width), lambda i, *_: (i, 0, 1, 0))]


def mlp_fwd_kernel(c_ref, fc1_ref, b_ref, fc2_ref, h1_ref, u_ref, g_ref, h2_ref, acc_ref):
    step = pl.program_id(0)
    pre = dot(c_ref[...], square(fc1_ref)) + b_ref[...]
    cdf = 0.5 * (1.0 + lax.erf(pre * np.float32(0.5 ** 0.5)))
    act = (pre * cdf).astype(bf16)
    u_ref[...] = act
    g_ref[...] = (cdf + pre * jnp.exp(-0.5 * pre * pre) * np.float32((2 * np.pi) ** -0.5)).astype(bf16)
    part = dot(act, square(fc2_ref))

    @pl.when(step == 0)
    def _():
        acc_ref[...] = h1_ref[...] + part

    @pl.when(step > 0)
    def _():
        acc_ref[...] += part

    @pl.when(step == pl.num_programs(0) - 1)
    def _():
        h2_ref[...] = acc_ref[...].astype(bf16)


def mlp_fwd(c, gathered, bias, h1):
    tokens, width = c.shape
    parts, block = gathered.shape[1], width
    ff = parts * block
    fc1_spec, fc2_spec = mlp_weight_specs(gathered, width)
    cols = lambda n: pl.BlockSpec((n, block), lambda i: (0, i))
    return pl.pallas_call(
        mlp_fwd_kernel,
        grid=(ff // block,),
        in_specs=[whole(c.shape), fc1_spec, cols(1), fc2_spec, whole(h1.shape)],
        out_specs=[cols(tokens), cols(tokens), whole(c.shape)],
        out_shape=[jax.ShapeDtypeStruct((tokens, ff), bf16), jax.ShapeDtypeStruct((tokens, ff), bf16),
                   jax.ShapeDtypeStruct((tokens, width), bf16)],
        scratch_shapes=[pltpu.VMEM((tokens, width), f32)],
        compiler_params=params(),
        cost_estimate=cost(4 * tokens * width * ff, tokens * ff * 4 + width * ff * 4 + tokens * width * 8),
        name="mlp_fwd",
    )(c, gathered, bias, gathered, h1)


def split_rows(value, core, keep_ref, send_ref, chips):
    width = value.shape[1]
    value = value.astype(bf16).reshape(chips, 2, value.shape[0] // chips // 2, width)
    even, odd = value[:, 0], value[:, 1]

    @pl.when(core == 0)
    def _():
        keep_ref[...] = even
        send_ref[...] = odd

    @pl.when(core == 1)
    def _():
        keep_ref[...] = odd
        send_ref[...] = even


def mlp_bwd_kernel(pos_ref, dm_ref, c_ref, u_ref, g_ref, fc1_ref, fc2_ref, dc_ref, gb_ref, k1_ref, s1_ref, k2_ref, s2_ref, *, chips):
    step = pl.program_id(0)
    core = pos_ref[2]
    dm = dm_ref[...]
    df32 = dot(dm, square(fc2_ref), 1, 1) * g_ref[...].astype(f32)
    df = df32.astype(bf16)
    gb_ref[...] = jnp.sum(df.astype(f32), axis=0, keepdims=True)
    parts, rows_each = k2_ref.shape[0], k2_ref.shape[2]
    width = dm.shape[1]
    grad2 = dot(u_ref[...], dm, 0, 0).astype(bf16).reshape(2, parts, rows_each, width)
    split_two(grad2, core, k2_ref, s2_ref)
    split_rows(dot(c_ref[...], df, 0, 0), core, k1_ref.at[0], s1_ref.at[0], chips)
    part = dot(df, square(fc1_ref), 1, 1)

    @pl.when(step == 0)
    def _():
        dc_ref[...] = part

    @pl.when(step > 0)
    def _():
        dc_ref[...] += part


def split_two(pair, core, keep_ref, send_ref):
    @pl.when(core == 0)
    def _():
        keep_ref[:, 0] = pair[0]
        send_ref[:, 0] = pair[1]

    @pl.when(core == 1)
    def _():
        keep_ref[:, 0] = pair[1]
        send_ref[:, 0] = pair[0]


def mlp_bwd(pos, dm, c, u, g, gathered, chips):
    tokens, width = c.shape
    parts, block = gathered.shape[1], width
    ff = parts * block
    rows1, rows2 = width // chips // 2, ff // chips // 2 // parts
    cols = lambda n: pl.BlockSpec((n, block), lambda i, _: (0, i))
    by_part = pl.BlockSpec((1, chips, rows1, block), lambda i, _: (i, 0, 0, 0))
    by_chip = pl.BlockSpec((parts, 1, rows2, width), lambda i, _: (0, i, 0, 0))
    grad1 = jax.ShapeDtypeStruct((parts, chips, rows1, block), bf16)
    grad2 = jax.ShapeDtypeStruct((parts, chips, rows2, width), bf16)
    return pl.pallas_call(
        functools.partial(mlp_bwd_kernel, chips=chips),
        grid_spec=pltpu.PrefetchScalarGridSpec(
            num_scalar_prefetch=1,
            grid=(parts,),
            in_specs=[whole(dm.shape), whole(c.shape), cols(tokens), cols(tokens), *mlp_weight_specs(gathered, width)],
            out_specs=[whole(c.shape), cols(1), by_part, by_part, by_chip, by_chip],
        ),
        out_shape=[jax.ShapeDtypeStruct((tokens, width), f32), jax.ShapeDtypeStruct((1, ff), f32),
                   grad1, grad1, grad2, grad2],
        compiler_params=params(),
        cost_estimate=cost(8 * tokens * width * ff, tokens * ff * 4 + width * ff * 8 + tokens * width * 8),
        name="mlp_bwd",
    )(pos, dm, c, u, g, gathered, gathered)


def qkvo_grad_kernel(pos_ref, a_ref, d_ref, o_ref, dattn_ref, keep_ref, send_ref, *, chips):
    part = pl.program_id(0)
    core = pos_ref[2]

    @pl.when(part < 3)
    def _():
        split_rows(dot(a_ref[...], d_ref[0], 0, 0), core, keep_ref.at[0], send_ref.at[0], chips)

    @pl.when(part == 3)
    def _():
        split_rows(dot(o_ref[...], dattn_ref[...], 0, 0), core, keep_ref.at[0], send_ref.at[0], chips)


def qkvo_grad(pos, a, dqkv, o, dattn, chips):
    tokens, width = a.shape
    each = width // chips // 2
    out = pl.BlockSpec((1, chips, each, width), lambda i, _: (i, 0, 0, 0))
    shape = jax.ShapeDtypeStruct((4, chips, each, width), bf16)
    return pl.pallas_call(
        functools.partial(qkvo_grad_kernel, chips=chips),
        grid_spec=pltpu.PrefetchScalarGridSpec(
            num_scalar_prefetch=1,
            grid=(4,),
            in_specs=[whole(a.shape), pl.BlockSpec((1, tokens, width), lambda i, _: (jnp.minimum(i, 2), 0, 0)),
                      whole(a.shape), whole(a.shape)],
            out_specs=[out, out],
        ),
        out_shape=[shape, shape],
        compiler_params=params(),
        cost_estimate=cost(8 * tokens * width * width, tokens * width * 12 + width * width * 8),
        name="qkvo_grad",
    )(pos, a, dqkv, o, dattn)


def patch_grad_kernel(pos_ref, ext_ref, demb_ref, bias_ref, *refs):
    core = pos_ref[2]
    *vector_refs, keep_ref, send_ref = refs
    parts, _, each, width = keep_ref.shape
    grad = dot(ext_ref[...], demb_ref[...], 0, 0).astype(bf16)
    depth = grad.shape[0] // 2 // parts
    spare = each - depth
    grad = grad.reshape(2, parts, depth, width)
    small = [ref[...] for ref in vector_refs]
    small += [bias_ref[:, i * width : (i + 1) * width] for i in range(bias_ref.shape[1] // width)]
    row = lax.broadcasted_iota(jnp.int32, (spare, width), 0)
    block = jnp.zeros((spare, width), f32)
    for i, value in enumerate(small):
        block = jnp.where(row == i, value, block)
    block = block.astype(bf16)

    def put(ref, value):
        ref[:, 0, :depth, :] = value
        for part in range(parts):
            ref[part, 0, depth:, :] = block

    @pl.when(core == 0)
    def _():
        put(keep_ref, grad[0])
        put(send_ref, grad[1])

    @pl.when(core == 1)
    def _():
        put(keep_ref, grad[1])
        put(send_ref, grad[0])


def patch_grad(pos, ext, demb, bias, vectors, parts, chips):
    tokens, depth = ext.shape
    width = demb.shape[1]
    each = depth // (2 * chips) // parts + 16
    out = pl.BlockSpec((parts, 1, each, width), lambda i, _: (0, i, 0, 0))
    shape = jax.ShapeDtypeStruct((parts, chips, each, width), bf16)
    return pl.pallas_call(
        patch_grad_kernel,
        grid_spec=pltpu.PrefetchScalarGridSpec(
            num_scalar_prefetch=1,
            grid=(chips,),
            in_specs=[pl.BlockSpec((tokens, depth // chips), lambda i, _: (0, i)), whole(demb.shape), whole(bias.shape)]
            + [whole(v.shape) for v in vectors],
            out_specs=[out, out],
        ),
        out_shape=[shape, shape],
        compiler_params=params(),
        cost_estimate=cost(2 * tokens * depth * width, ext.size * 2 + demb.size * 2 + depth * width * 2),
        name="patch_grad",
    )(pos, ext, demb, bias, *vectors)


def pixel_grad_kernel(d_ref, w_ref, shown_ref, out_ref):
    out_ref[...] = dot(d_ref[...], square(w_ref), 1, 1) * shown_ref[...]


def pixel_back(dmasked, patch, shown, depth):
    own, width = dmasked.shape
    tb = token_block(own)
    return pl.pallas_call(
        pixel_grad_kernel,
        grid=(own // tb,),
        in_specs=[rows(tb, width), patch_part(patch, depth), rows(tb, 1)],
        out_specs=rows(tb, depth),
        out_shape=jax.ShapeDtypeStruct((own, depth), f32),
        compiler_params=params(),
        cost_estimate=cost(2 * own * depth * width, own * depth * 4 + depth * width * 2),
        name="pixel_back",
    )(dmasked, patch, shown)


def place_kernel(pos_ref, *refs):
    out_ref = refs[-1]
    z, g, core = pos_ref[0], pos_ref[1], pos_ref[2]
    width = out_ref.shape[3]
    for rel in range(2):
        cc = core ^ rel
        fc1_ref, fc2_ref, *moved = refs[rel * 6 : (rel + 1) * 6]
        each = fc1_ref.shape[0]
        for part in range(4):
            out_ref[z * 2 + cc, part, :each, :] = fc1_ref[:, part * width : (part + 1) * width]
            out_ref[z * 2 + cc, part, each:, :] = fc2_ref[part * each : (part + 1) * each, :]
        for turn in range(4):
            for k in range(3):
                out_ref[((z - k - 1) & 3) * 2 + cc, g ^ turn] = moved[turn][k]


def place(pos, pieces, others):
    args = (*pieces, *others)
    each, width = pieces[0].shape[0], pieces[1].shape[1]
    shape = (8, 4, 2 * each, width)
    return pl.pallas_call(
        place_kernel,
        grid_spec=pltpu.PrefetchScalarGridSpec(
            num_scalar_prefetch=1,
            grid=(1,),
            in_specs=[whole(p.shape) for p in args],
            out_specs=whole(shape),
        ),
        out_shape=jax.ShapeDtypeStruct(shape, bf16),
        compiler_params=params(),
        cost_estimate=cost(0, 4 * np.prod(shape)),
        name="place",
    )(pos, *args)


def norm_back(dnormed, hidden, gain):
    xhat, rstd = norm_parts(hidden)
    dxhat = dnormed * gain
    mean_d = jnp.mean(dxhat, axis=-1, keepdims=True)
    mean_dx = jnp.mean(dxhat * xhat, axis=-1, keepdims=True)
    grad = rstd * (dxhat - mean_d - xhat * mean_dx)
    return grad, jnp.sum(dnormed * xhat, axis=0, keepdims=True), jnp.sum(dnormed, axis=0, keepdims=True)


def sum_rows(step, ref, part):
    @pl.when(step == 0)
    def _():
        ref[...] = part

    @pl.when(step > 0)
    def _():
        ref[...] += part


def norm2_back_kernel(dc_ref, h1_ref, dh2_ref, gain_ref, w_ref, dh1_ref, da_ref, do_ref, gg_ref, gs_ref):
    step = pl.program_id(0)
    grad, ggain, gshift = norm_back(dc_ref[...], h1_ref[...], gain_ref[2:3, :])
    dh1 = dh2_ref[...] + grad
    dh1_ref[...] = dh1
    dattn = dh1.astype(bf16)
    da_ref[...] = dattn
    do_ref[...] = dot(dattn, square(w_ref), 1, 1).astype(bf16)
    sum_rows(step, gg_ref, ggain)
    sum_rows(step, gs_ref, gshift)


def norm2_back(dc, h1, dh2, gain, proj_w):
    tokens, width = dc.shape
    tb = token_block(tokens)
    blk = rows(tb, width)
    vec = whole((1, width))
    return pl.pallas_call(
        norm2_back_kernel,
        grid=(tokens // tb,),
        in_specs=[blk, blk, blk, whole(gain.shape), last_part(proj_w, width)],
        out_specs=[blk, blk, blk, vec, vec],
        out_shape=[jax.ShapeDtypeStruct((tokens, width), f32), jax.ShapeDtypeStruct((tokens, width), bf16),
                   jax.ShapeDtypeStruct((tokens, width), bf16),
                   jax.ShapeDtypeStruct((1, width), f32), jax.ShapeDtypeStruct((1, width), f32)],
        compiler_params=params(),
        cost_estimate=cost(2 * tokens * width * width, tokens * width * 20 + width * width * 2),
        name="norm2_back",
    )(dc, h1, dh2, gain, proj_w)


def norm1_back_kernel(d_ref, w_ref, h0_ref, dh1_ref, gain_ref, de_ref, gg_ref, gs_ref):
    step = pl.program_id(0)
    width = h0_ref.shape[1]
    da = sum(dot(d_ref[p], w_ref[:, :, p * width : (p + 1) * width].reshape(width, width), 1, 1) for p in range(3))
    grad, ggain, gshift = norm_back(da, h0_ref[...], gain_ref[0:1, :])
    de_ref[...] = (dh1_ref[...] + grad).astype(bf16)
    sum_rows(step, gg_ref, ggain)
    sum_rows(step, gs_ref, gshift)


def norm1_back(dqkv, qkv_w, h0, dh1, gain):
    tokens, width = h0.shape
    tb = token_block(tokens)
    blk = rows(tb, width)
    vec = whole((1, width))
    return pl.pallas_call(
        norm1_back_kernel,
        grid=(tokens // tb,),
        in_specs=[pl.BlockSpec((3, tb, width), lambda i: (0, i, 0)), columns_part(qkv_w, 3 * width, lambda i: 0), blk, blk, whole(gain.shape)],
        out_specs=[blk, vec, vec],
        out_shape=[jax.ShapeDtypeStruct((tokens, width), bf16),
                   jax.ShapeDtypeStruct((1, width), f32), jax.ShapeDtypeStruct((1, width), f32)],
        compiler_params=params(),
        cost_estimate=cost(6 * tokens * width * width, tokens * width * 16 + width * width * 6),
        name="norm1_back",
    )(dqkv, qkv_w, h0, dh1, gain)


def part_slices(side):
    low, own, high = slice(0, MARGIN), slice(MARGIN, MARGIN + side), slice(MARGIN + side, 2 * MARGIN + side)
    return [(own, own), (own, low), (own, high), (low, own), (low, low), (low, high),
            (high, own), (high, low), (high, high)]


@functools.lru_cache(None)
def token_places(dates, side):
    extent = side + 2 * MARGIN
    grid = np.stack(np.meshgrid(np.arange(dates), np.arange(extent), np.arange(extent), indexing="ij"), -1)
    return np.concatenate([grid[:, r, c].reshape(-1, 3) for r, c in part_slices(side)])


@functools.lru_cache(None)
def halo_tables(dates, side):
    places = token_places(dates, side)
    extent = side + 2 * MARGIN
    own = dates * side * side
    edge = dates * side * MARGIN
    index = {tuple(p): i for i, p in enumerate(places)}

    def table(wanted, count):
        out = np.zeros((len(wanted), count), np.float32)
        out[np.arange(len(wanted)), [index[w] for w in wanted]] = 1
        return out

    def shifted(part, dr, dc):
        r, c = part_slices(side)[part]
        grid = np.stack(np.meshgrid(np.arange(dates), np.arange(extent)[r], np.arange(extent)[c], indexing="ij"), -1)
        return [(d, y + dr, x + dc) for d, y, x in grid.reshape(-1, 3)]

    first = table(shifted(1, 0, side) + shifted(2, 0, -side), own)
    north = shifted(3, side, 0) + shifted(4, side, 0) + shifted(5, side, 0)
    south = shifted(6, -side, 0) + shifted(7, -side, 0) + shifted(8, -side, 0)
    second = table(north + south, own + 2 * edge)
    return first, second


def chain(axis, step):
    count = lax.axis_size(axis)
    return [(i, i + step) for i in range(count) if 0 <= i + step < count]


def pick(table, values):
    return lax.dot(jnp.asarray(table, bf16), values, preferred_element_type=f32)


def to_neighbours(low, high, axis):
    return lax.ppermute(low, axis, chain(axis, -1)), lax.ppermute(high, axis, chain(axis, 1))


def margin_first(own, dates, side):
    first, _ = halo_tables(dates, side)
    edge = dates * side * MARGIN
    sent = pick(first, own).astype(bf16)
    return sent[edge:], sent[:edge]


def margin_second(own, right, left, dates, side):
    _, second = halo_tables(dates, side)
    both = dates * side * MARGIN + 2 * dates * MARGIN * MARGIN
    middle = jnp.concatenate([own, left, right])
    sent = pick(second, middle).astype(bf16)
    return middle, sent[both:], sent[:both]


def give_margin_and_sum(own, dates, side, weight, *ready):
    first, second = halo_tables(dates, side)
    edge = dates * side * MARGIN
    corner = dates * MARGIN * MARGIN
    width = own.shape[1]

    def with_rows(strip, values):
        values = values.reshape(1, -1).astype(bf16)
        return jnp.concatenate([strip, jnp.pad(values, ((0, 15), (0, width - values.shape[1])))])

    def values_of(strip, *shape):
        return strip[-16, : np.prod(shape)].reshape(shape).astype(f32)

    sent = pick(first, own).astype(bf16)
    right, left = to_neighbours(with_rows(sent[edge:], weight[:, :MARGIN]), with_rows(sent[:edge], weight[:, -MARGIN:]), "gx")
    right, left, *_ = tied(right, left, *ready)
    extent = side + 2 * MARGIN
    total = weight[:, MARGIN:-MARGIN]
    total = total + jnp.pad(values_of(left, extent, MARGIN), ((0, 0), (0, side - MARGIN)))
    total = total + jnp.pad(values_of(right, extent, MARGIN), ((0, 0), (side - MARGIN, 0)))
    middle = jnp.concatenate([own, left[:edge], right[:edge]])
    sent = pick(second, middle).astype(bf16)
    lower, upper = to_neighbours(with_rows(sent[edge + 2 * corner :], total[:MARGIN]),
                                 with_rows(sent[: edge + 2 * corner], total[-MARGIN:]), "gy")
    total = total[MARGIN:-MARGIN]
    total = total + jnp.pad(values_of(upper, MARGIN, side), ((0, side - MARGIN), (0, 0)))
    total = total + jnp.pad(values_of(lower, MARGIN, side), ((side - MARGIN, 0), (0, 0)))
    return (own, left, right, upper, lower), total


def fold_first(every, dates, side):
    edge = dates * side * MARGIN
    middle = dates * side * side + 2 * edge
    both = edge + 2 * dates * MARGIN * MARGIN
    return every[middle : middle + both], every[middle + both :]


def fold_second(every, below, above, dates, side):
    _, second = halo_tables(dates, side)
    own = dates * side * side
    edge = dates * side * MARGIN
    middle = every[: own + 2 * edge].astype(f32) + pick(second.T, jnp.concatenate([below, above]))
    sides = middle[own:].astype(bf16)
    return middle[:own], sides[:edge], sides[edge:]


def fold_third(part, east, west, dates, side):
    first, _ = halo_tables(dates, side)
    return (part + pick(first.T, jnp.concatenate([east, west]))).astype(bf16)


def sincos(places, span_width):
    half_width = span_width // 2
    omega = 1.0 / 10000.0 ** (jnp.arange(half_width, dtype=f32) / half_width)
    angles = places[:, None] * omega[None, :]
    return jnp.concatenate([jnp.sin(angles), jnp.cos(angles)], axis=1)


def position_parts(tile_row, tile_col, stamps, side, width):
    side_width = width // 16 * 6
    time_width = width - 2 * side_width
    extent = side + 2 * MARGIN
    dates = stamps.shape[0]
    offsets = jnp.arange(extent, dtype=jnp.int32) - MARGIN
    table = jnp.concatenate([
        jnp.pad(sincos(stamps.astype(f32), time_width), ((0, 0), (0, 2 * side_width))),
        jnp.pad(sincos((tile_row * side + offsets).astype(f32), side_width), ((0, 0), (time_width, side_width))),
        jnp.pad(sincos((tile_col * side + offsets).astype(f32), side_width), ((0, 0), (time_width + side_width, 0))),
    ])
    places = token_places(dates, side)
    hot = np.zeros((len(places), dates + 2 * extent), np.float32)
    spots = np.arange(len(places))
    hot[spots, places[:, 0]] = 1
    hot[spots, dates + places[:, 1]] = 1
    hot[spots, dates + extent + places[:, 2]] = 1
    hot = np.concatenate([hot] * 3, axis=1)
    spare = -hot.shape[1] % 128
    hot = np.pad(hot, ((0, 0), (0, spare)))
    parts = jnp.concatenate(three_parts(table))
    return jnp.asarray(hot, bf16), jnp.pad(parts, ((0, spare), (0, 0)))


def dense(left, right, ca=1, cb=0):
    return lax.dot_general(left, right, (((ca,), (cb,)), ((), ())), preferred_element_type=f32)


def gather(shard):
    return lax.all_gather(shard, "gx", axis=0, tiled=True)


def swap(value, axis, bit):
    return lax.ppermute(value, axis, [(i, i ^ bit) for i in range(lax.axis_size(axis))])


def turn(value, step):
    count = lax.axis_size("gx")
    return lax.ppermute(value, "gx", [(i, (i + 2 * step) % count) for i in range(count)])


def after(value, *earlier):
    return lax.optimization_barrier((value, *earlier))[0]


def along_z(mine):
    return jnp.stack([turn(mine, k) for k in (1, 2, 3)])


def tied(*values):
    return lax.optimization_barrier(values)


def along_gy(got):
    return got, swap(got, "gy", 1), swap(got, "gy", 2), swap(got, "gy", 3)


def core_swap(pieces):
    return tuple(swap(p, "gx", 1) for p in pieces)


def added(*values):
    return sum(v.astype(f32) for v in values).astype(bf16)


def at(value, index, axis=0):
    return lax.dynamic_index_in_dim(value, index, axis, keepdims=False)


def folded_gy(value):
    return value.reshape(2, 2, *value.shape[1:])


def near_sum(keep, got, first, g):
    keep, got = folded_gy(keep), folded_gy(got)
    dim, b = (1, g & 1) if first == 1 else (0, g >> 1)
    return added(at(keep, 1 - b, dim), at(got, 1 - b, dim)), added(at(keep, b, dim), at(got, b, dim))


def far_sum(keep, got, first, g):
    b = (g >> 1) if first == 1 else (g & 1)
    return added(at(keep, 1 - b), at(got, 1 - b)), (at(keep, b), at(got, b))


def to_each(keep, got, g):
    return [added(at(keep, g ^ m), at(got, g ^ m)) for m in (1, 2, 3)], (at(keep, g), at(got, g))


def swap_each(values):
    return [swap(v, "gy", m) for v, m in zip(values, (1, 2, 3))]


def along_z_sum(mine, z):
    came = [turn(at(mine, (z + k) % 4), k) for k in (1, 2, 3)]
    return at(mine, z), came


def side_by_side(value):
    half = value.shape[1] // 2
    return jnp.concatenate([value[:, :half], value[:, half:]], axis=2)


def stacked_again(value):
    half = value.shape[1] // 2
    return jnp.concatenate([value[:, :half], value[:, half:]])


def to_all_gy(mine):
    return [mine] + [swap(mine, "gy", m) for m in (1, 2, 3)]


def in_order(every, g):
    every = jnp.stack(every)
    return [at(every, p ^ g) for p in range(4)]


def gather_apart(shard):
    return lax.all_gather(shard, "gx", axis=0, tiled=False)


def collect_all(keep, send, tall):
    both = jnp.stack([keep, send], axis=2)
    parts, chips, _, rows_each, width = both.shape
    if tall:
        grad = both.transpose(1, 2, 0, 3, 4).reshape(-1, width)
    else:
        grad = both.transpose(1, 2, 3, 0, 4).reshape(-1, parts * width)
    grad = lax.psum(scatter(grad), "gy").astype(f32)
    return jnp.split(grad, parts, axis=0 if tall else 1)


def scatter(grad):
    return lax.psum_scatter(grad.astype(bf16), "gx", scatter_dimension=0, tiled=True)


def on_device(pixels, pad_mask, timestamps, scene_dates, scene_map, blend_weight, cotangent, patch_w, norm1_gain,
              norm1_bias, qkv_w, proj_w, norm2_gain, norm2_bias, fc1_w, fc1_b, fc2_w, dec_w, head_w):
    dates, side, _, pixel_width = pixels.shape
    own = dates * side * side
    extent = side + 2 * MARGIN
    places = token_places(dates, side)
    tokens = len(places)
    model_width = patch_w.shape[1]
    scale = float(model_width // HEADS) ** (-0.5)
    tile_row = lax.axis_index("gy")
    tile_col = lax.axis_index("gx")
    split = lax.axis_size("gx") == 8 and lax.axis_size("gy") == 4
    chip, core = (tile_col >> 1, tile_col & 1) if split else (0, 0)
    pos = jnp.stack([jnp.int32(chip), tile_row, jnp.int32(core)]).astype(jnp.int32)

    nearby = lax.dynamic_slice(jnp.pad(scene_map, 1, constant_values=-1), (tile_row, tile_col), (3, 3))
    own_scene = nearby[1, 1]
    bands = np.array([0] * MARGIN + [1] * side + [2] * MARGIN)
    same = (nearby == own_scene)[bands][:, bands].astype(f32)
    weight = blend_weight.astype(f32) * same
    masked = (pixels * pad_mask.astype(bf16)[..., None]).reshape(own, pixel_width)
    each = norm1_gain.shape[0]
    vectors = jnp.concatenate([jnp.stack([norm1_gain, norm1_bias, norm2_gain, norm2_bias]), fc1_b.reshape(-1, each)])
    vectors = jnp.pad(vectors, ((0, 16 - vectors.shape[0]), (0, model_width - each)))
    dec_rows, dec_width = dec_w.shape
    head_rows, slabs = head_w.shape[0], pixel_width // dec_width
    share_p = jnp.concatenate([patch_w, vectors])
    share_a = jnp.concatenate([qkv_w, proj_w], axis=1)
    slabs_of = head_w.reshape(head_rows, slabs, dec_width).transpose(1, 0, 2).reshape(-1, dec_width)
    share_d = jnp.concatenate([dec_w, slabs_of])
    front_p = gather_apart(share_p)
    masked, share_a = tied(masked, share_a)
    front_a = gather_apart(share_a)
    quarter = patch_w.shape[0] // 4
    if split:
        row = tile_row
        mine_b = jnp.concatenate([lax.dynamic_slice_in_dim(fc1_w, row * model_width, model_width, axis=1),
                                  lax.dynamic_slice_in_dim(fc2_w, row * each, each, axis=0)])
        got_b = along_z(mine_b)
        strips, denom = give_margin_and_sum(masked, dates, side, weight, got_b)
    else:
        strips, denom = give_margin_and_sum(masked, dates, side, weight)
    tops = gather_apart(after(share_d, *strips[1:], front_p))
    full_dec = tops[:, :dec_rows].reshape(-1, dec_width)
    full_head = tops[:, dec_rows:].reshape(-1, slabs, head_rows, dec_width).transpose(0, 2, 1, 3).reshape(-1, pixel_width)
    small = front_p[:, patch_w.shape[0] :]
    if split:
        got_b = after(got_b, *strips[1:])
        pieces_b = (fc1_w, fc2_w, *along_gy(got_b))
        strips = tied(*strips, got_b)[:-1]
    else:
        parts_of = lambda m: m.reshape(8, model_width // 8, 4, model_width).transpose(0, 2, 1, 3)
        quarters_of = lambda m: m.reshape(8, 4, -1, model_width)
        full_mlp = jnp.concatenate([parts_of(gather(fc1_w)), quarters_of(gather(fc2_w))], axis=2)
    own_dates = scene_dates[own_scene]
    stamps = timestamps[own_scene]
    date_ok = jnp.arange(dates, dtype=jnp.int32) < own_dates
    spot_hot = np.zeros((tokens, extent * extent), np.float32)
    spot_hot[np.arange(tokens), places[:, 1] * extent + places[:, 2]] = 1
    per_token = pick(spot_hot, jnp.stack([weight.reshape(-1), same.reshape(-1)], axis=1).astype(bf16))
    weight_tok = per_token[:, :1]
    seen = per_token[:, 1:] * (jnp.asarray(places[:, :1], jnp.int32) < own_dates).astype(f32)
    lane = np.arange(128)[None, :]
    kx = jnp.where(lane < 3, 1.0, jnp.where(lane == 3, (1.0 - seen) * -1e9, 0.0)).astype(bf16)
    denom = jnp.broadcast_to(denom[None], (dates, side, side)).reshape(own, 1)

    hot, table = position_parts(tile_row, tile_col, stamps, side, model_width)
    small = small[:, :8, :each].astype(f32)
    vec = small[:, :4].transpose(1, 0, 2).reshape(4, -1)
    full_b = small[:, 4:].reshape(1, -1)

    shown = pad_mask.reshape(own, 1).astype(f32)
    valid = (pad_mask.astype(f32) * date_ok.astype(f32)[:, None, None]).reshape(own, 1)
    ratio = valid / denom
    gr = (cotangent.reshape(own, pixel_width).astype(f32) * ratio).astype(bf16)
    ext, h0, a = embed(strips, front_p, hot, table, vec)
    qkv = project(a, front_a, 3)
    if split:
        qkv, *pieces_b = tied(qkv, *pieces_b)
        others_b = core_swap(pieces_b)
    o, qx = attn_fwd(qkv, kx, scale)
    if split:
        o, *others_b = tied(o, *others_b)
    h1, c = proj_norm(o, front_a, h0, vec)
    gz = dense(after(gr, c), full_head, 1, 1).astype(bf16)
    west, east = margin_first(gz, dates, side)
    c, west, east = tied(c, west, east)
    right, left = to_neighbours(west, east, "gx")
    if split:
        full_mlp = place(pos, pieces_b, (*others_b[:-1], after(others_b[-1], c)))
        full_mlp, right, left = tied(full_mlp, right, left)
    middle, north, south = margin_second(gz, right, left, dates, side)
    full_mlp, north, south = tied(full_mlp, north, south)
    lower, upper = to_neighbours(north, south, "gy")
    u, slope, h2r = mlp_fwd(c, full_mlp, full_b, h1)
    z = dense(h2r, full_dec).astype(bf16)
    every = (z.astype(f32) * weight_tok).astype(bf16)
    north, south = fold_first(every, dates, side)
    below, above = to_neighbours(north, south, "gy")

    lower, upper, north, south = tied(lower, upper, north, south)
    dz_every = jnp.concatenate([middle, upper, lower])
    dz = (dz_every.astype(f32) * weight_tok).astype(bf16)
    dh2 = dense(dz, full_dec, 1, 1)
    dm, north, south = tied(dh2.astype(bf16), north, south)
    dc, grad_fc1_b, keep1, send1, keep2, send2 = mlp_bwd(pos, dm, c, u, slope, full_mlp, 4)
    g = tile_row
    if split:
        got1, got2 = swap(send1, "gx", 1), swap(send2, "gx", 1)
    below, above, dc = tied(below, above, dc)
    folded, west, east = fold_second(every, below, above, dates, side)
    grad_dec = dense(h2r, dz, 0, 0)
    dc, west, east, grad_dec = tied(dc, west, east, grad_dec)
    right, left = to_neighbours(west, east, "gx")
    dh1, dattn, do, grad_gain2, grad_shift2 = norm2_back(dc, h1, dh2, vec, front_a)
    if split:
        got1, got2 = after(got1, do), after(got2, do)
        out1, keep1 = near_sum(keep1, got1, 1, g)
        out2, keep2 = near_sum(keep2, got2, 2, g)
        do, out1, out2 = tied(do, out1, out2)
        got1, got2 = swap(out1, "gy", 1), swap(out2, "gy", 2)
    right, left, do = tied(right, left, do)
    folded = fold_third(folded, right, left, dates, side)
    grad_head = dense(folded, gr, 0, 0)
    do, grad_head, grad_dec = tied(do, grad_head.astype(bf16), grad_dec)
    grad_head, grad_dec = scatter(grad_head), scatter(grad_dec)
    dqkv = attn_bwd(qkv, do, o, qx, kx, scale)
    if split:
        got1, got2 = after(got1, dqkv), after(got2, dqkv)
        out1, keep1 = far_sum(keep1, got1, 1, g)
        out2, keep2 = far_sum(keep2, got2, 2, g)
        dqkv, out1, out2 = tied(dqkv, out1, out2)
        got1, got2 = swap(out1, "gy", 2), swap(out2, "gy", 1)
    keep3, send3 = qkvo_grad(pos, a, dqkv, o, dattn, 4)
    ends = jnp.concatenate([after(grad_dec, keep3), after(grad_head, keep3).reshape(-1, dec_width)])
    if split:
        got3 = swap(send3, "gx", 1)
        got1, got2 = after(got1, keep3), after(got2, keep3)
        mine1, came1 = along_z_sum(jnp.concatenate([added(*keep1, got1), added(*keep2, got2)], axis=1), chip)
        dqkv, mine1, ends = tied(dqkv, mine1, ends)
        ends_near = swap(ends, "gy", 1)
    demb, grad_gain1, grad_shift1 = norm1_back(dqkv, front_a, h0, dh1, vec)
    vectors = (grad_gain1, grad_shift1, grad_gain2, grad_shift2)
    north, south = fold_first(demb, dates, side)
    if split:
        got3, ends_near = after(got3, demb), after(ends_near, demb)
        outs3, keep3 = to_each(keep3, got3, g)
        ends = added(ends, ends_near)
        demb, north, south, ends, *outs3 = tied(demb, north, south, ends, *outs3)
    below, above = to_neighbours(north, south, "gy")
    if split:
        got3 = swap_each(outs3)
        keep4, send4 = patch_grad(pos, ext, demb, grad_fc1_b, vectors, 4, 4)
        got4 = swap(send4, "gx", 1)
        below, above = after(below, keep4), after(above, keep4)
    part, west, east = fold_second(demb, below, above, dates, side)
    right, left = to_neighbours(west, east, "gx")
    if split:
        got4 = after(got4, west, east)
        outs4, keep4 = to_each(keep4, got4, g)
        came1 = [after(v, *outs4) for v in came1]
        done1 = added(mine1, *came1)
        right, left, done1, *outs4 = tied(right, left, done1, *outs4)
        got4 = swap_each(outs4)
        dmasked = fold_third(part, right, left, dates, side)
        pixel_grad = pixel_back(dmasked, front_p, shown, pixel_width)
        every1 = to_all_gy(after(done1, dmasked))
        got3 = [after(v, pixel_grad) for v in got3]
        mine3 = added(*keep3, *got3)
        got4 = [after(v, mine3) for v in got4]
        mine4, came4 = along_z_sum(jnp.concatenate([mine3, added(*keep4, *got4)], axis=1), chip)
        folded, mine4, ends = tied(folded, mine4, ends)
        ends_far = swap(ends, "gy", 2)
        recon = (dense(folded, full_head) * ratio).astype(bf16)
        came4 = [after(v, recon) for v in came4]
        done4 = added(mine4, *came4)
        every1 = tied(*every1, done4)[:-1]
        every4 = to_all_gy(done4)
        every1 = in_order(every1, g)
        sum1 = jnp.concatenate([v[:each] for v in every1], axis=1).astype(f32)
        sum2 = jnp.concatenate([v[each:] for v in every1], axis=0).astype(f32)
        ends = ends.astype(f32) + ends_far.astype(f32)
        every4 = tied(*every4, sum1, sum2, ends)[:-3]
        every4 = in_order(every4, g)
        sum1, sum2 = jnp.split(sum1, 4, axis=1), jnp.split(sum2, 4, axis=0)
        sum3 = [v[:each] for v in every4]
        grad_patch = jnp.concatenate([v[each : each + quarter] for v in every4])
        small = every4[0][each + quarter :]
    else:
        recon = (dense(folded, full_head) * ratio).astype(bf16)
        dmasked = fold_third(part, right, left, dates, side)
        sum1, sum2 = collect_all(keep1, send1, False), collect_all(keep2, send2, True)
        sum3 = collect_all(keep3, send3, False)
        pixel_grad = pixel_back(dmasked, front_p, shown, pixel_width)
        grad_patch = lax.psum(scatter(dense(ext, demb, 0, 0)), "gy")
        small = lax.psum(jnp.concatenate([*vectors, grad_fc1_b.reshape(-1, model_width)]), ("gy", "gx"))
        ends = lax.psum(ends, "gy")
    small = small.astype(f32)
    mine_of = lambda value, count: lax.dynamic_slice_in_dim(value.reshape(-1), tile_col * count, count)
    grad_bias = mine_of(small[4 : 4 + full_b.shape[1] // model_width], fc1_b.shape[0])
    return (
        recon.reshape(pixels.shape),
        pixel_grad.reshape(pixels.shape),
        grad_patch.astype(f32),
        mine_of(small[0], each),
        mine_of(small[1], each),
        jnp.concatenate(sum3[:3], axis=1).astype(f32),
        sum3[3].astype(f32),
        mine_of(small[2], each),
        mine_of(small[3], each),
        jnp.concatenate(sum1, axis=1).astype(f32),
        grad_bias,
        jnp.concatenate(sum2, axis=0).astype(f32),
        ends[:dec_rows].astype(f32),
        ends[dec_rows:].reshape(head_rows, pixel_width).astype(f32),
    )


def solution(mesh):
    in_specs = (
        P(None, "gy", "gx", None),
        P(None, "gy", "gx"),
        P(),
        P(),
        P(),
        P("gy", "gx"),
        P(None, "gy", "gx", None),
        P("gx", None),
        P("gx"),
        P("gx"),
        P("gx", None),
        P("gx", None),
        P("gx"),
        P("gx"),
        P("gx", None),
        P("gx"),
        P("gx", None),
        P("gx", None),
        P("gx", None),
    )
    out_specs = (
        P(None, "gy", "gx", None),
        P(None, "gy", "gx", None),
        P("gx", None),
        P("gx"),
        P("gx"),
        P("gx", None),
        P("gx", None),
        P("gx"),
        P("gx"),
        P("gx", None),
        P("gx"),
        P("gx", None),
        P("gx", None),
        P("gx", None),
    )
    return jax.shard_map(
        on_device, mesh=mesh, in_specs=in_specs, out_specs=out_specs, check_vma=False
    )
```

time: 572 us -> 521 us (0.911)
  the two profiles are of different devices: /device:TPU:8 before, /device:TPU:0 now
where the time goes in v2:
time: 521 us; the launch traced here: 515 us
  Pallas kernels  175 us (34%)
  waiting for transfers between devices  116 us (22%)
  starting transfers between devices  105 us (20%)
  other arithmetic  44.9 us (9%)
  local copies, waits for them, and re-layouts  30.6 us (6%)
  matrix products  26.8 us (5%)
  between operations  17.2 us (3%)
    ppermute x31, starting transfers between devices, swap(): lax.ppermute(value, axis, [(i, i ^ bit) for i in range(lax.axis_size(axis...  49.2 us
    ppermute x9, waiting for transfers between devices, turn(): lax.ppermute(value, 'gx', [(i, (i + 2 * step) % count) for i in range(cou...  42.5 us
    ppermute x31, waiting for transfers between devices, swap(): lax.ppermute(value, axis, [(i, i ^ bit) for i in range(lax.axis_size(axis...  36.4 us
    pallas_call x1, Pallas kernels, attn_bwd(): pl.pallas_call(functools.partial(attn_bwd_kernel, block=token_block(token...  33.6 us
    ppermute x8, starting transfers between devices, to_neighbours(): lax.ppermute(high, axis, chain(axis, 1))  33.1 us
    pallas_call x1, Pallas kernels, mlp_bwd(): pl.pallas_call(functools.partial(mlp_bwd_kernel, chips=chips), grid_spec=...  31.8 us
    all_gather x3, waiting for transfers between devices, gather_apart(): return lax.all_gather(shard, 'gx', axis=0, tiled=False)  27.1 us
    convert_element_type x13, other arithmetic, added(): return sum((v.astype(f32) for v in values)).astype(bf16)  20.1 us
  transfers between devices with their start and end apart: 61, of which 20 were waited for; matrix products, arithmetic and copies ran while one was open for 14% of the time, Pallas kernels for 22%

profile of v2, /device:TPU:0, one launch (start us, length us, event | category | flops | bytes accessed | tf_op | source)
XLA Modules:
  0.0 514.8 jit_solution(16409129215836458095)
XLA Ops:
  8.9 1.7 fusion.52
  12.0 1.8 pad_maximum_fusion.3
  16.3 3.0 collective-permute-start.2
  19.3 2.6 collective-permute-start.3
  27.5 2.0 collective-permute-start.1
  37.2 18.2 %collective-permute-done.3 = bf16[192,768]{1,0:T(8,128)(2,1)} collective-permute-done((bf16[192,768]{1,0:T(8,128)(2,1)}, bf16[192,768]{1,0:T(8,128)(2,1)}, u32[]{:S(2)}, u32[]{:S(2)}) %collective-permute-start.3) | collective-permute-done | bytes 294944 | tf_op jit(solution)/shard_map/ppermute | solution.py:785
  63.2 5.3 %collective-permute-start.5 = (bf16[160,1536]{1,0:T(8,128)(2,1)S(1)}, bf16[160,1536]{1,0:T(8,128)(2,1)}, u32[]{:S(2)}, u32[]{:S(2)}) collective-permute-start(bf16[160,1536]{1,0:T(8,128)(2,1)S(1)} %fusion.40), channel_id=1, source_target_pairs={{0,8},{8,16},{16,24},{1,9},{9,17},{17,25},{2,10},{10,18},{18,26},{... | collective-permute-start | bytes 1474568 | tf_op jit(solution)/shard_map/ppermute | solution.py:671
  75.9 6.1 %collective-permute-start.7 = (bf16[3,192,768]{2,1,0:T(8,128)(2,1)S(1)}, bf16[3,192,768]{2,1,0:T(8,128)(2,1)S(1)}, u32[]{:S(2)}, u32[]{:S(2)}) collective-permute-start(bf16[3,192,768]{2,1,0:T(8,128)(2,1)S(1)} %pad_maximum_fusion.2.refs_2_), channel_id=1, source_target_pairs={{0,8},{8,0},{16,24},{24,16},{1,9},{9,1},{17,25},{25,17},{2,10},{10... | collective-permute-start | bytes 2654216 | tf_op jit(solution)/shard_map/ppermute | solution.py:780
  81.9 3.8 collective-permute-start.8
  89.1 7.7 %embed.1 = (bf16[864,1536]{1,0:T(8,128)(2,1)}, f32[864,768]{1,0:T(8,128)}, bf16[864,768]{1,0:T(8,128)(2,1)}) custom-call(bf16[384,1536]{1,0:T(8,128)(2,1)} %bitcast.234, bf16[112,1536]{1,0:T(8,128)(2,1)} %collective-permute-done.1.left_ref, bf16[112,1536]{1,0:T(8,128)(2,1)} %collective-permute-done.right_ref, ...), custom_call_target="tpu_custom_call" | custom-call | flops 2038431744 | bytes 11649024 | tf_op jit(solution)/shard_map/embed/pallas_call | solution.py:101
  96.7 26.0 %all-gather.9.cloned.1.call-done = bf16[768,3072]{1,0:T(8,128)(2,1)} async-done(((bf16[96,3072]{1,0:T(8,128)(2,1)}), bf16[768,3072]{1,0:T(8,128)(2,1)}) %all-gather.9.cloned.1.call-update) | async-done | bytes 4718608 | tf_op jit(solution)/shard_map/all_gather | solution.py:864
  122.8 8.7 %project.1.q_ref.k_ref.v_ref = bf16[864,2304]{1,0:T(8,128)(2,1)} custom-call(bf16[864,768]{1,0:T(8,128)(2,1)} %get-tuple-element.161.a_ref, bf16[8,96,3072]{2,1,0:T(8,128)(2,1)} %bitcast.228), custom_call_target="tpu_custom_call" | custom-call | flops 3057647616 | bytes 8847360 | tf_op jit(solution)/shard_map/project/pallas_call | solution.py:122
  136.1 18.4 %attn_fwd.1 = (bf16[864,768]{1,0:T(8,128)(2,1)}, bf16[12,864,128]{2,1,0:T(8,128)(2,1)}) custom-call(bf16[864,2304]{1,0:T(8,128)(2,1)} %project.1.q_ref.k_ref.v_ref, bf16[864,2304]{1,0:T(8,128)(2,1)} %project.1.q_ref.k_ref.v_ref, bf16[864,2304]{1,0:T(8,128)(2,1)} %project.1.q_ref.k_ref.v_ref, bf16[864,128]{1,0:T(8,128)(2,1)} %select_convert_fusion.kx_ref), custom_call_target="tpu_custom_call" | custom-call | flops 18345885696 | bytes 5308416 | tf_op jit(solution)/shard_map/attn_fwd/pallas_call | solution.py:181
  155.5 1.5 slice.369
  160.1 6.6 %proj_norm.1 = (f32[864,768]{1,0:T(8,128)}, bf16[864,768]{1,0:T(8,128)(2,1)}) custom-call(bf16[864,768]{1,0:T(8,128)(2,1)} %get-tuple-element.171.o_ref, bf16[8,96,3072]{2,1,0:T(8,128)(2,1)} %bitcast.229, f32[864,768]{1,0:T(8,128)} %get-tuple-element.172.h0_ref, f32[4,768]{1,0:T(4,128)} %reshape.337.vec_ref.gain_ref), custom_call_target="tpu_custom_call" | custom-call | flops 1019215872 | bytes 9142272 | tf_op jit(solution)/shard_map/proj_norm/pallas_call | solution.py:264
  169.3 3.5 collective-permute-start.17
  173.1 8.8 %place.1.fc1_ref.fc2_ref = bf16[8,4,192,768]{3,2,1,0:T(8,128)(2,1)} custom-call(s32[3]{0:T(128)} %pad_add_fusion.pos_ref, bf16[96,3072]{1,0:T(8,128)(2,1)} %refs_0_, bf16[384,768]{1,0:T(8,128)(2,1)} %refs_1_, bf16[3,192,768]{2,1,0:T(8,128)(2,1)} %copy-done.1, bf16[3,192,768]{2,1,0:T(8,128)(2,1)} %copy-done.25, ...), custom_call_target="tpu_custom_call" | custom-call | bytes 18874368 | tf_op jit(solution)/shard_map/place/pallas_call | solution.py:530
  182.4 17.5 %mlp_fwd.1 = (bf16[864,3072]{1,0:T(8,128)(2,1)}, bf16[864,3072]{1,0:T(8,128)(2,1)}, bf16[864,768]{1,0:T(8,128)(2,1)}) custom-call(bf16[864,768]{1,0:T(8,128)(2,1)} %get-tuple-element.176.c_ref, bf16[8,4,192,768]{3,2,1,0:T(8,128)(2,1)} %place.1.fc1_ref.fc2_ref, f32[1,3072]{1,0:T(1,128)} %reshape.342.b_ref, bf16[8,4,192,768]{3,2,1,0:T(8,128)(2,1)} %place.1.fc1_ref.fc2_ref, ...), custom_call_target="tpu_custom_call" | custom-call | flops 8153726976 | bytes 25362432 | tf_op jit(solution)/shard_map/mlp_fwd/pallas_call | solution.py:312
  199.9 2.2 multiply_convert_fusion.1
  204.2 4.6 collective-permute-start.21
  211.4 2.8 fusion.105
  214.3 31.8 %mlp_bwd.1 = (f32[864,768]{1,0:T(8,128)}, f32[1,3072]{1,0:T(1,128)}, bf16[4,4,96,768]{3,2,1,0:T(8,128)(2,1)}, bf16[4,4,96,768]{3,2,1,0:T(8,128)(2,1)}, bf16[4,4,...) custom-call(s32[3]{0:T(128)} %pad_add_fusion.pos_ref, bf16[864,768]{1,0:T(8,128)(2,1)} %get-tuple-element.370.dm_ref, ...), custom_call_target="tpu_custom_call" | custom-call | flops 16307453952 | bytes 34799616 | tf_op jit(solution)/shard_map/mlp_bwd/pallas_call | solution.py:387
  246.1 9.8 %collective-permute-start.25 = (bf16[4,4,96,768]{3,2,1,0:T(8,128)(2,1)}, bf16[4,4,96,768]{3,2,1,0:T(8,128)(2,1)}, u32[]{:S(2)}, u32[]{:S(2)}) collective-permute-start(bf16[4,4,96,768]{3,2,1,0:T(8,128)(2,1)} %get-tuple-element.210), channel_id=1, source_target_pairs={{0,1},{1,0},{2,3},{3,2},{4,5},{5,4},{6,7},{7,6},{8,9},{9,8},{10,11... | collective-permute-start | bytes 7077896 | tf_op jit(solution)/shard_map/ppermute | solution.py:780
  257.2 5.6 %collective-permute-start.19 = (bf16[144,512]{1,0:T(8,128)(2,1)}, bf16[144,512]{1,0:T(8,128)(2,1)}, u32[]{:S(2)}, u32[]{:S(2)}) collective-permute-start(bf16[144,512]{1,0:T(8,128)(2,1)} %get-tuple-element.334), channel_id=1, source_target_pairs={{0,8},{8,16},{16,24},{1,9},{9,17},{17,25},{2,10},{10,18},{18,26},{... | collective-permute-start | bytes 442376 | tf_op jit(solution)/shard_map/ppermute | solution.py:671
  262.8 2.2 collective-permute-done.18
  267.5 2.4 fusion.106
  270.5 1.9 fusion.48
  273.7 3.7 collective-permute-start.23
  277.4 8.8 %norm2_back.1 = (f32[864,768]{1,0:T(8,128)}, bf16[864,768]{1,0:T(8,128)(2,1)}, bf16[864,768]{1,0:T(8,128)(2,1)}, f32[1,768]{1,0:T(1,128)}, f32[1,768]{1,0:T(1,128)}) custom-call(f32[864,768]{1,0:T(8,128)} %get-tuple-element.204.dc_ref, f32[864,768]{1,0:T(8,128)} %get-tuple-element.190.h1_ref, f32[864,768]{1,0:T(8,128)} %get-tuple-element.371.dh2_ref, ...), custom_call_target="tpu_custom_call" | custom-call | flops 1019215872 | bytes 14450688 | tf_op jit(solution)/shard_map/norm2_back/pallas_call | solution.py:581
  287.7 3.5 add_convert_fusion
  291.2 1.7 add_convert_fusion.1
  296.0 2.2 convolution_convert_fusion
  298.4 5.1 collective-permute-start.27
  303.5 1.5 collective-permute-start.26
  305.0 33.6 %attn_bwd.1.d_ref = bf16[3,864,768]{2,1,0:T(8,128)(2,1)} custom-call(bf16[864,2304]{1,0:T(8,128)(2,1)} %project.1.q_ref.k_ref.v_ref, bf16[864,2304]{1,0:T(8,128)(2,1)} %project.1.q_ref.k_ref.v_ref, bf16[864,2304]{1,0:T(8,128)(2,1)} %project.1.q_ref.k_ref.v_ref, bf16[864,768]{1,0:T(8,128)(2,1)} %get-tuple-element.217.do_ref, ...), custom_call_target="tpu_custom_call" | custom-call | flops 22932357120 | bytes 10616832 | tf_op jit(solution)/shard_map/attn_bwd/pallas_call | solution.py:241
  338.6 2.0 fusion.39
  341.6 10.7 %qkvo_grad.1 = (bf16[4,4,96,768]{3,2,1,0:T(8,128)(2,1)}, bf16[4,4,96,768]{3,2,1,0:T(8,128)(2,1)}) custom-call(s32[3]{0:T(128)} %pad_add_fusion.pos_ref, bf16[864,768]{1,0:T(8,128)(2,1)} %get-tuple-element.161.a_ref, bf16[3,864,768]{2,1,0:T(8,128)(2,1)} %attn_bwd.1.d_ref, bf16[864,768]{1,0:T(8,128)(2,1)} %get-tuple-element.171.o_ref, ...), custom_call_target="tpu_custom_call" | custom-call | flops 4076863488 | bytes 12681216 | tf_op jit(solution)/shard_map/qkvo_grad/pallas_call | solution.py:421
  352.3 1.8 collective-permute-start.28
  354.9 14.7 %collective-permute-done.30 = bf16[4,96,768]{2,1,0:T(8,128)(2,1)} collective-permute-done((bf16[4,96,768]{2,1,0:T(8,128)(2,1)}, bf16[4,96,768]{2,1,0:T(8,128)(2,1)}, u32[]{:S(2)}, u32[]{:S(2)}) %collective-permute-start.30) | collective-permute-done | bytes 589856 | tf_op jit(solution)/shard_map/ppermute | solution.py:780
  374.6 1.6 collective-permute-start.31
  376.2 8.9 %norm1_back.1 = (bf16[864,768]{1,0:T(8,128)(2,1)}, f32[1,768]{1,0:T(1,128)}, f32[1,768]{1,0:T(1,128)}) custom-call(bf16[3,864,768]{2,1,0:T(8,128)(2,1)} %attn_bwd.1.d_ref, bf16[8,96,3072]{2,1,0:T(8,128)(2,1)} %bitcast.231, f32[864,768]{1,0:T(8,128)} %get-tuple-element.172.h0_ref, f32[864,768]{1,0:T(8,128)} %get-tuple-element.236.dh1_ref, ...), custom_call_target="tpu_custom_call" | custom-call | flops 3057647616 | bytes 14155776 | tf_op jit(solution)/shard_map/norm1_back/pallas_call | solution.py:610
  385.1 1.8 fusion.92
  387.1 2.8 fusion.37
  389.9 7.5 %patch_grad.1 = (bf16[4,4,64,768]{3,2,1,0:T(8,128)(2,1)}, bf16[4,4,64,768]{3,2,1,0:T(8,128)(2,1)}) custom-call(s32[3]{0:T(128)} %pad_add_fusion.pos_ref, bf16[864,1536]{1,0:T(8,128)(2,1)} %get-tuple-element.244.ext_ref, bf16[864,768]{1,0:T(8,128)(2,1)} %get-tuple-element.242.demb_ref, f32[1,3072]{1,0:T(1,128)} %get-tuple-element.245.bias_ref, ...), custom_call_target="tpu_custom_call" | custom-call | flops 2038431744 | bytes 6340608 | tf_op jit(solution)/shard_map/patch_grad/pallas_call | solution.py:475
  398.7 5.4 %collective-permute-start.34 = (bf16[144,768]{1,0:T(8,128)(2,1)}, bf16[144,768]{1,0:T(8,128)(2,1)}, u32[]{:S(2)}, u32[]{:S(2)}) collective-permute-start(bf16[144,768]{1,0:T(8,128)(2,1)} %get-tuple-element.252), channel_id=1, source_target_pairs={{0,8},{8,16},{16,24},{1,9},{9,17},{17,25},{2,10},{10,18},{18,26},{... | collective-permute-start | bytes 663560 | tf_op jit(solution)/shard_map/ppermute | solution.py:671
  408.9 2.8 collective-permute-start.32
  414.5 2.5 collective-permute-start.41
  417.0 2.4 fusion.44
  420.4 8.2 %collective-permute-done.39 = bf16[192,768]{1,0:T(8,128)(2,1)S(1)} collective-permute-done((bf16[192,768]{1,0:T(8,128)(2,1)}, bf16[192,768]{1,0:T(8,128)(2,1)S(1)}, u32[]{:S(2)}, u32[]{:S(2)}) %collective-permute-start.39) | collective-permute-done | bytes 294944 | tf_op jit(solution)/shard_map/ppermute | solution.py:785
  429.9 3.0 collective-permute-start.36
  434.9 2.8 collective-permute-start.45
  438.9 5.7 %pixel_back.1 = f32[384,1536]{1,0:T(8,128)} custom-call(bf16[384,768]{1,0:T(8,128)(2,1)} %fusion.12.d_ref, bf16[8,208,768]{2,1,0:T(8,128)(2,1)} %bitcast.241, f32[384,1]{1,0:T(8,128)} %convert_element_type.705.shown_ref), custom_call_target="tpu_custom_call" | custom-call | flops 905969664 | bytes 4718592 | tf_op jit(solution)/shard_map/pixel_back/pallas_call | solution.py:498
  446.0 2.0 fusion.23
  448.0 11.8 %collective-permute-done.44 = bf16[4,64,768]{2,1,0:T(8,128)(2,1)} collective-permute-done((bf16[4,64,768]{2,1,0:T(8,128)(2,1)}, bf16[4,64,768]{2,1,0:T(8,128)(2,1)}, u32[]{:S(2)}, u32[]{:S(2)}) %collective-permute-start.44) | collective-permute-done | bytes 393248 | tf_op jit(solution)/shard_map/ppermute | solution.py:780
  459.8 1.6 fusion.31
  463.8 1.5 collective-permute-start.52
  465.3 1.7 collective-permute-start.53
  468.0 5.2 %collective-permute-done.46 = bf16[160,768]{1,0:T(8,128)(2,1)S(1)} collective-permute-done((bf16[160,768]{1,0:T(8,128)(2,1)}, bf16[160,768]{1,0:T(8,128)(2,1)S(1)}, u32[]{:S(2)}, u32[]{:S(2)}) %collective-permute-start.46) | collective-permute-done | bytes 245792 | tf_op jit(solution)/shard_map/ppermute | solution.py:785
  473.2 1.8 fusion
  475.0 7.8 %collective-permute-done.47 = bf16[160,768]{1,0:T(8,128)(2,1)S(1)} collective-permute-done((bf16[160,768]{1,0:T(8,128)(2,1)}, bf16[160,768]{1,0:T(8,128)(2,1)S(1)}, u32[]{:S(2)}, u32[]{:S(2)}) %collective-permute-start.47) | collective-permute-done | bytes 245792 | tf_op jit(solution)/shard_map/ppermute | solution.py:785
  483.2 3.1 collective-permute-done.48
  487.2 1.6 collective-permute-start.50
  492.4 5.6 %collective-permute-done.55 = bf16[288,512]{1,0:T(8,128)(2,1)S(1)} collective-permute-done((bf16[288,512]{1,0:T(8,128)(2,1)S(1)}, bf16[288,512]{1,0:T(8,128)(2,1)S(1)}, u32[]{:S(2)}, u32[]{:S(2)}) %collective-permute-start.55) | collective-permute-done | bytes 294944 | tf_op jit(solution)/shard_map/ppermute | solution.py:780
  499.7 2.5 collective-permute-done.50
  (343 shorter events, 100.2 us)
Async XLA Ops:
  7.2 66.9 %all-gather.7.cloned.1.call-start = ((), (), s32[]{:S(2)}) async-start(), calls=%async_computation.4 | async-start | bytes 2875392 | tf_op jit(solution)/shard_map/all_gather | solution.py:864
  10.6 112.2 %all-gather.9.cloned.1.call-start = ((), (), s32[]{:S(2)}) async-start(), calls=%async_computation.5 | async-start | bytes 5308416 | tf_op jit(solution)/shard_map/all_gather | solution.py:864
  14.0 22.0 %copy-start = (bf16[6,8,8,1536]{3,2,1,0:T(8,128)(2,1)}, bf16[6,8,8,1536]{3,2,1,0:T(8,128)(2,1)S(1)}, u32[]{:S(2)}) copy-start(bf16[6,8,8,1536]{3,2,1,0:T(8,128)(2,1)S(1)} %broadcast_multiply_fusion) | copy-start | bytes 3538948
  14.1 141.4 %all-gather.11.cloned.1.call-start = ((), (), s32[]{:S(2)}) async-start(), calls=%async_computation.6 | async-start | bytes 2654208 | tf_op jit(solution)/shard_map/all_gather | solution.py:864
  16.3 21.0 %collective-permute-start.2 = (bf16[192,768]{1,0:T(8,128)(2,1)}, bf16[192,768]{1,0:T(8,128)(2,1)}, u32[]{:S(2)}, u32[]{:S(2)}) collective-permute-start(bf16[192,768]{1,0:T(8,128)(2,1)} %pad_maximum_fusion.4), channel_id=1, source_target_pairs={{0,2},{1,3},{2,4},{3,5},{4,6},{5,7},{6,0},{7,1},{8,10},{9,11},{10,... | collective-permute-start | bytes 884744 | tf_op jit(solution)/shard_map/ppermute | solution.py:785
  19.3 36.1 %collective-permute-start.3 = (bf16[192,768]{1,0:T(8,128)(2,1)}, bf16[192,768]{1,0:T(8,128)(2,1)}, u32[]{:S(2)}, u32[]{:S(2)}) collective-permute-start(bf16[192,768]{1,0:T(8,128)(2,1)} %pad_maximum_fusion.4), channel_id=1, source_target_pairs={{0,4},{1,5},{2,6},{3,7},{4,0},{5,1},{6,2},{7,3},{8,12},{9,13},{10,... | collective-permute-start | bytes 884744 | tf_op jit(solution)/shard_map/ppermute | solution.py:785
  21.9 33.5 %collective-permute-start.4 = (bf16[192,768]{1,0:T(8,128)(2,1)}, bf16[192,768]{1,0:T(8,128)(2,1)}, u32[]{:S(2)}, u32[]{:S(2)}) collective-permute-start(bf16[192,768]{1,0:T(8,128)(2,1)} %pad_maximum_fusion.4), channel_id=1, source_target_pairs={{0,6},{1,7},{2,0},{3,1},{4,2},{5,3},{6,4},{7,5},{8,14},{9,15},{10,... | collective-permute-start | bytes 884744 | tf_op jit(solution)/shard_map/ppermute | solution.py:785
  27.5 29.2 %collective-permute-start.1 = (bf16[112,1536]{1,0:T(8,128)(2,1)}, bf16[112,1536]{1,0:T(8,128)(2,1)}, u32[]{:S(2)}, u32[]{:S(2)}) collective-permute-start(bf16[112,1536]{1,0:T(8,128)(2,1)} %fusion.51), channel_id=1, source_target_pairs={{0,1},{1,2},{2,3},{3,4},{4,5},{5,6},{6,7},{8,9},{9,10},{10,11},{11... | collective-permute-start | bytes 1032200 | tf_op jit(solution)/shard_map/ppermute | solution.py:671
  30.5 26.2 %collective-permute-start = (bf16[112,1536]{1,0:T(8,128)(2,1)}, bf16[112,1536]{1,0:T(8,128)(2,1)}, u32[]{:S(2)}, u32[]{:S(2)}) collective-permute-start(bf16[112,1536]{1,0:T(8,128)(2,1)} %fusion.50), channel_id=1, source_target_pairs={{1,0},{2,1},{3,2},{4,3},{5,4},{6,5},{7,6},{9,8},{10,9},{11,10},{12... | collective-permute-start | bytes 1032200 | tf_op jit(solution)/shard_map/ppermute | solution.py:671
  56.7 29.1 %copy-start.1 = (bf16[3,192,768]{2,1,0:T(8,128)(2,1)}, bf16[3,192,768]{2,1,0:T(8,128)(2,1)S(1)}, u32[]{:S(2)}) copy-start(bf16[3,192,768]{2,1,0:T(8,128)(2,1)S(1)} %pad_maximum_fusion.2.refs_2_) | copy-start | bytes 2654212
  61.6 11.1 %collective-permute-start.6 = (bf16[160,1536]{1,0:T(8,128)(2,1)S(1)}, bf16[160,1536]{1,0:T(8,128)(2,1)}, u32[]{:S(2)}, u32[]{:S(2)}) collective-permute-start(bf16[160,1536]{1,0:T(8,128)(2,1)S(1)} %fusion.41), channel_id=1, source_target_pairs={{8,0},{16,8},{24,16},{9,1},{17,9},{25,17},{10,2},{18,10},{26,18},{... | collective-permute-start | bytes 1474568 | tf_op jit(solution)/shard_map/ppermute | solution.py:671
  63.2 10.9 %collective-permute-start.5 = (bf16[160,1536]{1,0:T(8,128)(2,1)S(1)}, bf16[160,1536]{1,0:T(8,128)(2,1)}, u32[]{:S(2)}, u32[]{:S(2)}) collective-permute-start(bf16[160,1536]{1,0:T(8,128)(2,1)S(1)} %fusion.40), channel_id=1, source_target_pairs={{0,8},{8,16},{16,24},{1,9},{9,17},{17,25},{2,10},{10,18},{18,26},{... | collective-permute-start | bytes 1474568 | tf_op jit(solution)/shard_map/ppermute | solution.py:671
  74.2 280.7 %reduce-scatter.3.cloned.1.call-start = ((), (), s32[]{:S(2)}) async-start(), calls=%async_computation.2 | async-start | bytes 884736 | tf_op jit(solution)/shard_map/reduce_scatter | solution.py:879
  75.9 55.6 %collective-permute-start.7 = (bf16[3,192,768]{2,1,0:T(8,128)(2,1)S(1)}, bf16[3,192,768]{2,1,0:T(8,128)(2,1)S(1)}, u32[]{:S(2)}, u32[]{:S(2)}) collective-permute-start(bf16[3,192,768]{2,1,0:T(8,128)(2,1)S(1)} %pad_maximum_fusion.2.refs_2_), channel_id=1, source_target_pairs={{0,8},{8,0},{16,24},{24,16},{1,9},{9,1},{17,25},{25,17},{2,10},{10... | collective-permute-start | bytes 2654216 | tf_op jit(solution)/shard_map/ppermute | solution.py:780
  81.9 49.5 %collective-permute-start.8 = (bf16[3,192,768]{2,1,0:T(8,128)(2,1)S(1)}, bf16[3,192,768]{2,1,0:T(8,128)(2,1)}, u32[]{:S(2)}, u32[]{:S(2)}) collective-permute-start(bf16[3,192,768]{2,1,0:T(8,128)(2,1)S(1)} %pad_maximum_fusion.2.refs_2_), channel_id=1, source_target_pairs={{0,16},{8,24},{16,0},{24,8},{1,17},{9,25},{17,1},{25,9},{2,18},{10... | collective-permute-start | bytes 2654216 | tf_op jit(solution)/shard_map/ppermute | solution.py:780
  85.7 45.7 %collective-permute-start.9 = (bf16[3,192,768]{2,1,0:T(8,128)(2,1)S(1)}, bf16[3,192,768]{2,1,0:T(8,128)(2,1)}, u32[]{:S(2)}, u32[]{:S(2)}) collective-permute-start(bf16[3,192,768]{2,1,0:T(8,128)(2,1)S(1)} %pad_maximum_fusion.2.refs_2_), channel_id=1, source_target_pairs={{0,24},{8,16},{16,8},{24,0},{1,25},{9,17},{17,9},{25,1},{2,26},{10... | collective-permute-start | bytes 2654216 | tf_op jit(solution)/shard_map/ppermute | solution.py:780
  131.5 4.3 collective-permute-start.10
  134.8 25.3 %collective-permute-start.12 = (bf16[3,192,768]{2,1,0:T(8,128)(2,1)S(1)}, bf16[3,192,768]{2,1,0:T(8,128)(2,1)S(1)}, u32[]{:S(2)}, u32[]{:S(2)}) collective-permute-start(bf16[3,192,768]{2,1,0:T(8,128)(2,1)S(1)} %copy-done.2), channel_id=1, source_target_pairs={{0,1},{1,0},{2,3},{3,2},{4,5},{5,4},{6,7},{7,6},{8,9},{9,8},{10,11... | collective-permute-start | bytes 2654216 | tf_op jit(solution)/shard_map/ppermute | solution.py:780
  135.0 25.1 %collective-permute-start.13 = (bf16[3,192,768]{2,1,0:T(8,128)(2,1)}, bf16[3,192,768]{2,1,0:T(8,128)(2,1)}, u32[]{:S(2)}, u32[]{:S(2)}) collective-permute-start(bf16[3,192,768]{2,1,0:T(8,128)(2,1)} %copy-done.25), channel_id=1, source_target_pairs={{0,1},{1,0},{2,3},{3,2},{4,5},{5,4},{6,7},{7,6},{8,9},{9,8},{10,11... | collective-permute-start | bytes 2654216 | tf_op jit(solution)/shard_map/ppermute | solution.py:780
  135.3 24.8 %collective-permute-start.14 = (bf16[3,192,768]{2,1,0:T(8,128)(2,1)}, bf16[3,192,768]{2,1,0:T(8,128)(2,1)}, u32[]{:S(2)}, u32[]{:S(2)}) collective-permute-start(bf16[3,192,768]{2,1,0:T(8,128)(2,1)} %collective-permute-done.8.refs_4_), channel_id=1, source_target_pairs={{0,1},{1,0},{2,3},{3,2},{4,5},{5,4},{6,7},{7,6},{8,9},{9,8},{10,11... | collective-permute-start | bytes 2654216 | tf_op jit(solution)/shard_map/ppermute | solution.py:780
  135.5 24.6 %collective-permute-start.15 = (bf16[3,192,768]{2,1,0:T(8,128)(2,1)}, bf16[3,192,768]{2,1,0:T(8,128)(2,1)}, u32[]{:S(2)}, u32[]{:S(2)}) collective-permute-start(bf16[3,192,768]{2,1,0:T(8,128)(2,1)} %collective-permute-done.9.refs_5_), channel_id=1, source_target_pairs={{0,1},{1,0},{2,3},{3,2},{4,5},{5,4},{6,7},{7,6},{8,9},{9,8},{10,11... | collective-permute-start | bytes 2654216 | tf_op jit(solution)/shard_map/ppermute | solution.py:780
  135.8 24.3 %collective-permute-start.11 = (bf16[384,768]{1,0:T(8,128)(2,1)}, bf16[384,768]{1,0:T(8,128)(2,1)}, u32[]{:S(2)}, u32[]{:S(2)}) collective-permute-start(bf16[384,768]{1,0:T(8,128)(2,1)} %refs_1_), channel_id=1, source_target_pairs={{0,1},{1,0},{2,3},{3,2},{4,5},{5,4},{6,7},{7,6},{8,9},{9,8},{10,11... | collective-permute-start | bytes 1769480 | tf_op jit(solution)/shard_map/ppermute | solution.py:780
  168.0 14.0 %collective-permute-start.16 = (bf16[96,512]{1,0:T(8,128)(2,1)S(1)}, bf16[96,512]{1,0:T(8,128)(2,1)S(1)}, u32[]{:S(2)}, u32[]{:S(2)}) collective-permute-start(bf16[96,512]{1,0:T(8,128)(2,1)S(1)} %get-tuple-element.184), channel_id=1, source_target_pairs={{1,0},{2,1},{3,2},{4,3},{5,4},{6,5},{7,6},{9,8},{10,9},{11,10},{12... | collective-permute-start | bytes 294920 | tf_op jit(solution)/shard_map/ppermute | solution.py:671
  169.3 12.7 %collective-permute-start.17 = (bf16[96,512]{1,0:T(8,128)(2,1)S(1)}, bf16[96,512]{1,0:T(8,128)(2,1)S(1)}, u32[]{:S(2)}, u32[]{:S(2)}) collective-permute-start(bf16[96,512]{1,0:T(8,128)(2,1)S(1)} %get-tuple-element.185), channel_id=1, source_target_pairs={{0,1},{1,2},{2,3},{3,4},{4,5},{5,6},{6,7},{8,9},{9,10},{10,11},{11... | collective-permute-start | bytes 294920 | tf_op jit(solution)/shard_map/ppermute | solution.py:671
  202.9 7.0 %collective-permute-start.20 = (bf16[144,512]{1,0:T(8,128)(2,1)S(1)}, bf16[144,512]{1,0:T(8,128)(2,1)S(1)}, u32[]{:S(2)}, u32[]{:S(2)}) collective-permute-start(bf16[144,512]{1,0:T(8,128)(2,1)S(1)} %get-tuple-element.192), channel_id=1, source_target_pairs={{8,0},{16,8},{24,16},{9,1},{17,9},{25,17},{10,2},{18,10},{26,18},{... | collective-permute-start | bytes 442376 | tf_op jit(solution)/shard_map/ppermute | solution.py:671
  204.2 7.2 %collective-permute-start.21 = (bf16[144,512]{1,0:T(8,128)(2,1)S(1)}, bf16[144,512]{1,0:T(8,128)(2,1)S(1)}, u32[]{:S(2)}, u32[]{:S(2)}) collective-permute-start(bf16[144,512]{1,0:T(8,128)(2,1)S(1)} %get-tuple-element.193), channel_id=1, source_target_pairs={{0,8},{8,16},{16,24},{1,9},{9,17},{17,25},{2,10},{10,18},{18,26},{... | collective-permute-start | bytes 442376 | tf_op jit(solution)/shard_map/ppermute | solution.py:671
  246.1 40.2 %collective-permute-start.25 = (bf16[4,4,96,768]{3,2,1,0:T(8,128)(2,1)}, bf16[4,4,96,768]{3,2,1,0:T(8,128)(2,1)}, u32[]{:S(2)}, u32[]{:S(2)}) collective-permute-start(bf16[4,4,96,768]{3,2,1,0:T(8,128)(2,1)} %get-tuple-element.210), channel_id=1, source_target_pairs={{0,1},{1,0},{2,3},{3,2},{4,5},{5,4},{6,7},{7,6},{8,9},{9,8},{10,11... | collective-permute-start | bytes 7077896 | tf_op jit(solution)/shard_map/ppermute | solution.py:780
  255.8 30.4 %collective-permute-start.24 = (bf16[4,4,96,768]{3,2,1,0:T(8,128)(2,1)}, bf16[4,4,96,768]{3,2,1,0:T(8,128)(2,1)S(1)}, u32[]{:S(2)}, u32[]{:S(2)}) collective-permute-start(bf16[4,4,96,768]{3,2,1,0:T(8,128)(2,1)} %get-tuple-element.207), channel_id=1, source_target_pairs={{0,1},{1,0},{2,3},{3,2},{4,5},{5,4},{6,7},{7,6},{8,9},{9,8},{10,11... | collective-permute-start | bytes 7077896 | tf_op jit(solution)/shard_map/ppermute | solution.py:780
  255.9 9.0 %collective-permute-start.18 = (bf16[144,512]{1,0:T(8,128)(2,1)}, bf16[144,512]{1,0:T(8,128)(2,1)}, u32[]{:S(2)}, u32[]{:S(2)}) collective-permute-start(bf16[144,512]{1,0:T(8,128)(2,1)} %get-tuple-element.335), channel_id=1, source_target_pairs={{8,0},{16,8},{24,16},{9,1},{17,9},{25,17},{10,2},{18,10},{26,18},{... | collective-permute-start | bytes 442376 | tf_op jit(solution)/shard_map/ppermute | solution.py:671
  257.2 8.9 %collective-permute-start.19 = (bf16[144,512]{1,0:T(8,128)(2,1)}, bf16[144,512]{1,0:T(8,128)(2,1)}, u32[]{:S(2)}, u32[]{:S(2)}) collective-permute-start(bf16[144,512]{1,0:T(8,128)(2,1)} %get-tuple-element.334), channel_id=1, source_target_pairs={{0,8},{8,16},{16,24},{1,9},{9,17},{17,25},{2,10},{10,18},{18,26},{... | collective-permute-start | bytes 442376 | tf_op jit(solution)/shard_map/ppermute | solution.py:671
  272.5 20.5 %collective-permute-start.22 = (bf16[96,512]{1,0:T(8,128)(2,1)}, bf16[96,512]{1,0:T(8,128)(2,1)}, u32[]{:S(2)}, u32[]{:S(2)}) collective-permute-start(bf16[96,512]{1,0:T(8,128)(2,1)} %get-tuple-element.202), channel_id=1, source_target_pairs={{1,0},{2,1},{3,2},{4,3},{5,4},{6,5},{7,6},{9,8},{10,9},{11,10},{12... | collective-permute-start | bytes 294920 | tf_op jit(solution)/shard_map/ppermute | solution.py:671
  273.7 19.2 %collective-permute-start.23 = (bf16[96,512]{1,0:T(8,128)(2,1)}, bf16[96,512]{1,0:T(8,128)(2,1)}, u32[]{:S(2)}, u32[]{:S(2)}) collective-permute-start(bf16[96,512]{1,0:T(8,128)(2,1)} %get-tuple-element.203), channel_id=1, source_target_pairs={{0,1},{1,2},{2,3},{3,4},{4,5},{5,6},{6,7},{8,9},{9,10},{10,11},{11... | collective-permute-start | bytes 294920 | tf_op jit(solution)/shard_map/ppermute | solution.py:671
  298.2 75.3 %reduce-scatter.5.cloned.1.call-start = ((), (), s32[]{:S(2)}) async-start(), calls=%async_computation.3 | async-start | bytes 1769472 | tf_op jit(solution)/shard_map/reduce_scatter | solution.py:879
  298.4 40.1 %collective-permute-start.27 = (bf16[2,4,96,768]{3,2,1,0:T(8,128)(2,1)}, bf16[2,4,96,768]{3,2,1,0:T(8,128)(2,1)}, u32[]{:S(2)}, u32[]{:S(2)}) collective-permute-start(bf16[2,4,96,768]{3,2,1,0:T(8,128)(2,1)} %get-tuple-element.221), channel_id=1, source_target_pairs={{0,16},{8,24},{16,0},{24,8},{1,17},{9,25},{17,1},{25,9},{2,18},{10... | collective-permute-start | bytes 3538952 | tf_op jit(solution)/shard_map/ppermute | solution.py:780
  303.5 35.1 %collective-permute-start.26 = (bf16[2,4,96,768]{3,2,1,0:T(8,128)(2,1)}, bf16[2,4,96,768]{3,2,1,0:T(8,128)(2,1)S(1)}, u32[]{:S(2)}, u32[]{:S(2)}) collective-permute-start(bf16[2,4,96,768]{3,2,1,0:T(8,128)(2,1)} %get-tuple-element.219), channel_id=1, source_target_pairs={{0,8},{8,0},{16,24},{24,16},{1,9},{9,1},{17,25},{25,17},{2,10},{10... | collective-permute-start | bytes 3538952 | tf_op jit(solution)/shard_map/ppermute | solution.py:780
  352.3 34.8 %collective-permute-start.28 = (bf16[4,4,96,768]{3,2,1,0:T(8,128)(2,1)}, bf16[4,4,96,768]{3,2,1,0:T(8,128)(2,1)}, u32[]{:S(2)}, u32[]{:S(2)}) collective-permute-start(bf16[4,4,96,768]{3,2,1,0:T(8,128)(2,1)} %get-tuple-element.226), channel_id=1, source_target_pairs={{0,1},{1,0},{2,3},{3,2},{4,5},{5,4},{6,7},{7,6},{8,9},{9,8},{10,11... | collective-permute-start | bytes 7077896 | tf_op jit(solution)/shard_map/ppermute | solution.py:780
  354.1 15.6 %collective-permute-start.30 = (bf16[4,96,768]{2,1,0:T(8,128)(2,1)}, bf16[4,96,768]{2,1,0:T(8,128)(2,1)}, u32[]{:S(2)}, u32[]{:S(2)}) collective-permute-start(bf16[4,96,768]{2,1,0:T(8,128)(2,1)} %fusion.39), channel_id=1, source_target_pairs={{0,8},{8,0},{16,24},{24,16},{1,9},{9,1},{17,25},{25,17},{2,10},{10... | collective-permute-start | bytes 1769480 | tf_op jit(solution)/shard_map/ppermute | solution.py:780
  354.6 15.3 %collective-permute-start.29 = (bf16[4,96,768]{2,1,0:T(8,128)(2,1)}, bf16[4,96,768]{2,1,0:T(8,128)(2,1)}, u32[]{:S(2)}, u32[]{:S(2)}) collective-permute-start(bf16[4,96,768]{2,1,0:T(8,128)(2,1)} %fusion.38), channel_id=1, source_target_pairs={{0,16},{8,24},{16,0},{24,8},{1,17},{9,25},{17,1},{25,9},{2,18},{10... | collective-permute-start | bytes 1769480 | tf_op jit(solution)/shard_map/ppermute | solution.py:780
  374.6 12.3 %collective-permute-start.31 = (bf16[288,512]{1,0:T(8,128)(2,1)S(1)}, bf16[288,512]{1,0:T(8,128)(2,1)S(1)}, u32[]{:S(2)}, u32[]{:S(2)}) collective-permute-start(bf16[288,512]{1,0:T(8,128)(2,1)S(1)} %pad_maximum_fusion.6), channel_id=1, source_target_pairs={{0,8},{8,0},{16,24},{24,16},{1,9},{9,1},{17,25},{25,17},{2,10},{10... | collective-permute-start | bytes 884744 | tf_op jit(solution)/shard_map/ppermute | solution.py:780
  389.9 21.8 %copy-start.15 = (bf16[576,144]{1,0:T(8,128)(2,1)S(1)}, bf16[576,144]{1,0:T(8,128)(2,1)}, u32[]{:S(2)}) copy-start(bf16[576,144]{1,0:T(8,128)(2,1)} %constant.280) | copy-start | bytes 497668
  397.4 17.1 %collective-permute-start.38 = (bf16[4,4,64,768]{3,2,1,0:T(8,128)(2,1)}, bf16[4,4,64,768]{3,2,1,0:T(8,128)(2,1)}, u32[]{:S(2)}, u32[]{:S(2)}) collective-permute-start(bf16[4,4,64,768]{3,2,1,0:T(8,128)(2,1)} %get-tuple-element.255), channel_id=1, source_target_pairs={{0,1},{1,0},{2,3},{3,2},{4,5},{5,4},{6,7},{7,6},{8,9},{9,8},{10,11... | collective-permute-start | bytes 4718600 | tf_op jit(solution)/shard_map/ppermute | solution.py:780
  397.4 10.4 %collective-permute-start.33 = (bf16[144,768]{1,0:T(8,128)(2,1)}, bf16[144,768]{1,0:T(8,128)(2,1)}, u32[]{:S(2)}, u32[]{:S(2)}) collective-permute-start(bf16[144,768]{1,0:T(8,128)(2,1)} %get-tuple-element.243), channel_id=1, source_target_pairs={{8,0},{16,8},{24,16},{9,1},{17,9},{25,17},{10,2},{18,10},{26,18},{... | collective-permute-start | bytes 663560 | tf_op jit(solution)/shard_map/ppermute | solution.py:671
  398.7 10.2 %collective-permute-start.34 = (bf16[144,768]{1,0:T(8,128)(2,1)}, bf16[144,768]{1,0:T(8,128)(2,1)}, u32[]{:S(2)}, u32[]{:S(2)}) collective-permute-start(bf16[144,768]{1,0:T(8,128)(2,1)} %get-tuple-element.252), channel_id=1, source_target_pairs={{0,8},{8,16},{16,24},{1,9},{9,17},{17,25},{2,10},{10,18},{18,26},{... | collective-permute-start | bytes 663560 | tf_op jit(solution)/shard_map/ppermute | solution.py:671
  404.9 14.5 %collective-permute-start.37 = (bf16[192,768]{1,0:T(8,128)(2,1)}, bf16[192,768]{1,0:T(8,128)(2,1)S(1)}, u32[]{:S(2)}, u32[]{:S(2)}) collective-permute-start(bf16[192,768]{1,0:T(8,128)(2,1)} %get-tuple-element.316), channel_id=1, source_target_pairs={{0,2},{1,3},{2,4},{3,5},{4,6},{5,7},{6,0},{7,1},{8,10},{9,11},{10,... | collective-permute-start | bytes 884744 | tf_op jit(solution)/shard_map/ppermute | solution.py:785
  406.4 22.2 %collective-permute-start.39 = (bf16[192,768]{1,0:T(8,128)(2,1)}, bf16[192,768]{1,0:T(8,128)(2,1)S(1)}, u32[]{:S(2)}, u32[]{:S(2)}) collective-permute-start(bf16[192,768]{1,0:T(8,128)(2,1)} %get-tuple-element.318), channel_id=1, source_target_pairs={{0,4},{1,5},{2,6},{3,7},{4,0},{5,1},{6,2},{7,3},{8,12},{9,13},{10,... | collective-permute-start | bytes 884744 | tf_op jit(solution)/shard_map/ppermute | solution.py:785
  407.8 22.0 %collective-permute-start.40 = (bf16[192,768]{1,0:T(8,128)(2,1)}, bf16[192,768]{1,0:T(8,128)(2,1)S(1)}, u32[]{:S(2)}, u32[]{:S(2)}) collective-permute-start(bf16[192,768]{1,0:T(8,128)(2,1)} %get-tuple-element.319), channel_id=1, source_target_pairs={{0,6},{1,7},{2,0},{3,1},{4,2},{5,3},{6,4},{7,5},{8,14},{9,15},{10,... | collective-permute-start | bytes 884744 | tf_op jit(solution)/shard_map/ppermute | solution.py:785
  408.9 26.1 %collective-permute-start.32 = (bf16[4,96,768]{2,1,0:T(8,128)(2,1)}, bf16[4,96,768]{2,1,0:T(8,128)(2,1)}, u32[]{:S(2)}, u32[]{:S(2)}) collective-permute-start(bf16[4,96,768]{2,1,0:T(8,128)(2,1)} %get-tuple-element.241), channel_id=1, source_target_pairs={{0,8},{8,0},{16,24},{24,16},{1,9},{9,1},{17,25},{25,17},{2,10},{10... | collective-permute-start | bytes 1769480 | tf_op jit(solution)/shard_map/ppermute | solution.py:780
  414.5 31.5 %collective-permute-start.41 = (bf16[4,96,768]{2,1,0:T(8,128)(2,1)}, bf16[4,96,768]{2,1,0:T(8,128)(2,1)}, u32[]{:S(2)}, u32[]{:S(2)}) collective-permute-start(bf16[4,96,768]{2,1,0:T(8,128)(2,1)} %get-tuple-element.263), channel_id=1, source_target_pairs={{0,16},{8,24},{16,0},{24,8},{1,17},{9,25},{17,1},{25,9},{2,18},{10... | collective-permute-start | bytes 1769480 | tf_op jit(solution)/shard_map/ppermute | solution.py:780
  419.4 26.6 %collective-permute-start.42 = (bf16[4,96,768]{2,1,0:T(8,128)(2,1)}, bf16[4,96,768]{2,1,0:T(8,128)(2,1)}, u32[]{:S(2)}, u32[]{:S(2)}) collective-permute-start(bf16[4,96,768]{2,1,0:T(8,128)(2,1)} %get-tuple-element.265), channel_id=1, source_target_pairs={{0,24},{8,16},{16,8},{24,0},{1,25},{9,17},{17,9},{25,1},{2,26},{10... | collective-permute-start | bytes 1769480 | tf_op jit(solution)/shard_map/ppermute | solution.py:780
  428.6 4.5 collective-permute-start.35
  429.9 4.0 collective-permute-start.36
  433.9 14.1 %collective-permute-start.43 = (bf16[4,64,768]{2,1,0:T(8,128)(2,1)}, bf16[4,64,768]{2,1,0:T(8,128)(2,1)}, u32[]{:S(2)}, u32[]{:S(2)}) collective-permute-start(bf16[4,64,768]{2,1,0:T(8,128)(2,1)} %get-tuple-element.267), channel_id=1, source_target_pairs={{0,8},{8,0},{16,24},{24,16},{1,9},{9,1},{17,25},{25,17},{2,10},{10... | collective-permute-start | bytes 1179656 | tf_op jit(solution)/shard_map/ppermute | solution.py:780
  434.6 25.1 %collective-permute-start.44 = (bf16[4,64,768]{2,1,0:T(8,128)(2,1)}, bf16[4,64,768]{2,1,0:T(8,128)(2,1)}, u32[]{:S(2)}, u32[]{:S(2)}) collective-permute-start(bf16[4,64,768]{2,1,0:T(8,128)(2,1)} %get-tuple-element.269), channel_id=1, source_target_pairs={{0,16},{8,24},{16,0},{24,8},{1,17},{9,25},{17,1},{25,9},{2,18},{10... | collective-permute-start | bytes 1179656 | tf_op jit(solution)/shard_map/ppermute | solution.py:780
  434.9 24.8 %collective-permute-start.45 = (bf16[4,64,768]{2,1,0:T(8,128)(2,1)}, bf16[4,64,768]{2,1,0:T(8,128)(2,1)}, u32[]{:S(2)}, u32[]{:S(2)}) collective-permute-start(bf16[4,64,768]{2,1,0:T(8,128)(2,1)} %get-tuple-element.271), channel_id=1, source_target_pairs={{0,24},{8,16},{16,8},{24,0},{1,25},{9,17},{17,9},{25,1},{2,26},{10... | collective-permute-start | bytes 1179656 | tf_op jit(solution)/shard_map/ppermute | solution.py:780
  462.3 10.9 %collective-permute-start.46 = (bf16[160,768]{1,0:T(8,128)(2,1)}, bf16[160,768]{1,0:T(8,128)(2,1)S(1)}, u32[]{:S(2)}, u32[]{:S(2)}) collective-permute-start(bf16[160,768]{1,0:T(8,128)(2,1)} %get-tuple-element.328), channel_id=1, source_target_pairs={{0,2},{1,3},{2,4},{3,5},{4,6},{5,7},{6,0},{7,1},{8,10},{9,11},{10,... | collective-permute-start | bytes 737288 | tf_op jit(solution)/shard_map/ppermute | solution.py:785
  463.8 23.4 %collective-permute-start.52 = (bf16[192,768]{1,0:T(8,128)(2,1)S(1)}, bf16[192,768]{1,0:T(8,128)(2,1)S(1)}, u32[]{:S(2)}, u32[]{:S(2)}) collective-permute-start(bf16[192,768]{1,0:T(8,128)(2,1)S(1)} %add_convert_fusion.10), channel_id=1, source_target_pairs={{0,8},{8,0},{16,24},{24,16},{1,9},{9,1},{17,25},{25,17},{2,10},{10... | collective-permute-start | bytes 884744 | tf_op jit(solution)/shard_map/ppermute | solution.py:780
  465.3 23.5 %collective-permute-start.53 = (bf16[192,768]{1,0:T(8,128)(2,1)S(1)}, bf16[192,768]{1,0:T(8,128)(2,1)S(1)}, u32[]{:S(2)}, u32[]{:S(2)}) collective-permute-start(bf16[192,768]{1,0:T(8,128)(2,1)S(1)} %add_convert_fusion.10), channel_id=1, source_target_pairs={{0,16},{8,24},{16,0},{24,8},{1,17},{9,25},{17,1},{25,9},{2,18},{10... | collective-permute-start | bytes 884744 | tf_op jit(solution)/shard_map/ppermute | solution.py:780
  467.0 22.9 %collective-permute-start.54 = (bf16[192,768]{1,0:T(8,128)(2,1)S(1)}, bf16[192,768]{1,0:T(8,128)(2,1)S(1)}, u32[]{:S(2)}, u32[]{:S(2)}) collective-permute-start(bf16[192,768]{1,0:T(8,128)(2,1)S(1)} %add_convert_fusion.10), channel_id=1, source_target_pairs={{0,24},{8,16},{16,8},{24,0},{1,25},{9,17},{17,9},{25,1},{2,26},{10... | collective-permute-start | bytes 884744 | tf_op jit(solution)/shard_map/ppermute | solution.py:780
  467.2 15.6 %collective-permute-start.47 = (bf16[160,768]{1,0:T(8,128)(2,1)}, bf16[160,768]{1,0:T(8,128)(2,1)S(1)}, u32[]{:S(2)}, u32[]{:S(2)}) collective-permute-start(bf16[160,768]{1,0:T(8,128)(2,1)} %get-tuple-element.330), channel_id=1, source_target_pairs={{0,4},{1,5},{2,6},{3,7},{4,0},{5,1},{6,2},{7,3},{8,12},{9,13},{10,... | collective-permute-start | bytes 737288 | tf_op jit(solution)/shard_map/ppermute | solution.py:785
  473.2 13.0 %collective-permute-start.48 = (bf16[160,768]{1,0:T(8,128)(2,1)}, bf16[160,768]{1,0:T(8,128)(2,1)S(1)}, u32[]{:S(2)}, u32[]{:S(2)}) collective-permute-start(bf16[160,768]{1,0:T(8,128)(2,1)} %get-tuple-element.331), channel_id=1, source_target_pairs={{0,6},{1,7},{2,0},{3,1},{4,2},{5,3},{6,4},{7,5},{8,14},{9,15},{10,... | collective-permute-start | bytes 737288 | tf_op jit(solution)/shard_map/ppermute | solution.py:785
  482.9 15.2 %collective-permute-start.55 = (bf16[288,512]{1,0:T(8,128)(2,1)S(1)}, bf16[288,512]{1,0:T(8,128)(2,1)S(1)}, u32[]{:S(2)}, u32[]{:S(2)}) collective-permute-start(bf16[288,512]{1,0:T(8,128)(2,1)S(1)} %add_convert_fusion.11), channel_id=1, source_target_pairs={{0,16},{8,24},{16,0},{24,8},{1,17},{9,25},{17,1},{25,9},{2,18},{10... | collective-permute-start | bytes 884744 | tf_op jit(solution)/shard_map/ppermute | solution.py:780
  486.4 13.3 %collective-permute-start.49 = (bf16[160,768]{1,0:T(8,128)(2,1)S(1)}, bf16[160,768]{1,0:T(8,128)(2,1)S(1)}, u32[]{:S(2)}, u32[]{:S(2)}) collective-permute-start(bf16[160,768]{1,0:T(8,128)(2,1)S(1)} %add_convert_fusion.12), channel_id=1, source_target_pairs={{0,8},{8,0},{16,24},{24,16},{1,9},{9,1},{17,25},{25,17},{2,10},{10... | collective-permute-start | bytes 737288 | tf_op jit(solution)/shard_map/ppermute | solution.py:780
  487.2 15.1 %collective-permute-start.50 = (bf16[160,768]{1,0:T(8,128)(2,1)S(1)}, bf16[160,768]{1,0:T(8,128)(2,1)S(1)}, u32[]{:S(2)}, u32[]{:S(2)}) collective-permute-start(bf16[160,768]{1,0:T(8,128)(2,1)S(1)} %add_convert_fusion.12), channel_id=1, source_target_pairs={{0,16},{8,24},{16,0},{24,8},{1,17},{9,25},{17,1},{25,9},{2,18},{10... | collective-permute-start | bytes 737288 | tf_op jit(solution)/shard_map/ppermute | solution.py:780
  488.8 13.4 %collective-permute-start.51 = (bf16[160,768]{1,0:T(8,128)(2,1)S(1)}, bf16[160,768]{1,0:T(8,128)(2,1)S(1)}, u32[]{:S(2)}, u32[]{:S(2)}) collective-permute-start(bf16[160,768]{1,0:T(8,128)(2,1)S(1)} %add_convert_fusion.12), channel_id=1, source_target_pairs={{0,24},{8,16},{16,8},{24,0},{1,25},{9,17},{17,9},{25,1},{2,26},{10... | collective-permute-start | bytes 737288 | tf_op jit(solution)/shard_map/ppermute | solution.py:780
  (51 other events, 376.5 us)
Sparse Core Ops, SparseCore 0:
  10.7 56.6 all-gather.6
  69.6 53.1 all-gather.8
  125.0 30.4 all-gather.10
  298.3 35.3 reduce-scatter.2
  336.0 32.2 reduce-scatter.4

commit v3 on v2

--- a/solution.py
+++ b/solution.py
@@ -34,13 +34,9 @@
     return pl.BlockSpec((block, width), lambda i: (i, 0))
 
 
-def columns_part(gathered, width, index):
-    shares, each, _ = gathered.shape
-    return pl.BlockSpec((shares, each, width), lambda i: (0, 0, index(i)))
-
-
 def last_part(gathered, width):
-    return columns_part(gathered, width, lambda i: 3)
+    shares = gathered.shape[0]
+    return pl.BlockSpec((shares, 1, width // shares, width), lambda i: (0, 3, 0, 0))
 
 
 def patch_part(gathered, depth):
@@ -122,7 +118,7 @@
     return pl.pallas_call(
         columns_kernel,
         grid=(2 * count,),
-        in_specs=[whole(a.shape), columns_part(gathered, half, lambda i: i)],
+        in_specs=[whole(a.shape), pl.BlockSpec((gathered.shape[0], 1, width // gathered.shape[0], half), lambda i: (0, i // 2, 0, i % 2))],
         out_specs=pl.BlockSpec((tokens, half), lambda i: (0, i)),
         out_shape=jax.ShapeDtypeStruct((tokens, count * width), bf16),
         compiler_params=params(),
@@ -507,28 +503,32 @@
     )(dmasked, patch, shown)
 
 
-def place_kernel(pos_ref, *refs):
+def place_kernel(pos_ref, *refs, kinds):
     out_ref = refs[-1]
     z, g, core = pos_ref[0], pos_ref[1], pos_ref[2]
     width = out_ref.shape[3]
+    count = len(kinds)
+    each = out_ref.shape[2] // count
     for rel in range(2):
         cc = core ^ rel
-        fc1_ref, fc2_ref, *moved = refs[rel * 6 : (rel + 1) * 6]
-        each = fc1_ref.shape[0]
-        for part in range(4):
-            out_ref[z * 2 + cc, part, :each, :] = fc1_ref[:, part * width : (part + 1) * width]
-            out_ref[z * 2 + cc, part, each:, :] = fc2_ref[part * each : (part + 1) * each, :]
+        mine = refs[rel * (count + 4) : (rel + 1) * (count + 4)]
+        for m, kind in enumerate(kinds):
+            for part in range(4):
+                if kind == "wide":
+                    value = mine[m][:, part * width : (part + 1) * width]
+                else:
+                    value = mine[m][part * each : (part + 1) * each, :]
+                out_ref[z * 2 + cc, part, m * each : (m + 1) * each, :] = value
         for turn in range(4):
             for k in range(3):
-                out_ref[((z - k - 1) & 3) * 2 + cc, g ^ turn] = moved[turn][k]
-
-
-def place(pos, pieces, others):
+                out_ref[((z - k - 1) & 3) * 2 + cc, g ^ turn] = mine[count + turn][k]
+
+
+def place(pos, pieces, others, kinds):
     args = (*pieces, *others)
-    each, width = pieces[0].shape[0], pieces[1].shape[1]
-    shape = (8, 4, 2 * each, width)
-    return pl.pallas_call(
-        place_kernel,
+    shape = (8, 4, pieces[-1].shape[1], pieces[-1].shape[2])
+    return pl.pallas_call(
+        functools.partial(place_kernel, kinds=kinds),
         grid_spec=pltpu.PrefetchScalarGridSpec(
             num_scalar_prefetch=1,
             grid=(1,),
@@ -595,7 +595,7 @@
 def norm1_back_kernel(d_ref, w_ref, h0_ref, dh1_ref, gain_ref, de_ref, gg_ref, gs_ref):
     step = pl.program_id(0)
     width = h0_ref.shape[1]
-    da = sum(dot(d_ref[p], w_ref[:, :, p * width : (p + 1) * width].reshape(width, width), 1, 1) for p in range(3))
+    da = sum(dot(d_ref[p], w_ref[:, p].reshape(width, width), 1, 1) for p in range(3))
     grad, ggain, gshift = norm_back(da, h0_ref[...], gain_ref[0:1, :])
     de_ref[...] = (dh1_ref[...] + grad).astype(bf16)
     sum_rows(step, gg_ref, ggain)
@@ -610,7 +610,7 @@
     return pl.pallas_call(
         norm1_back_kernel,
         grid=(tokens // tb,),
-        in_specs=[pl.BlockSpec((3, tb, width), lambda i: (0, i, 0)), columns_part(qkv_w, 3 * width, lambda i: 0), blk, blk, whole(gain.shape)],
+        in_specs=[pl.BlockSpec((3, tb, width), lambda i: (0, i, 0)), pl.BlockSpec((qkv_w.shape[0], 3, width // qkv_w.shape[0], width), lambda i: (0, 0, 0, 0)), blk, blk, whole(gain.shape)],
         out_specs=[blk, vec, vec],
         out_shape=[jax.ShapeDtypeStruct((tokens, width), bf16),
                    jax.ShapeDtypeStruct((1, width), f32), jax.ShapeDtypeStruct((1, width), f32)],
@@ -836,6 +836,12 @@
     return [swap(v, "gy", m) for v, m in zip(values, (1, 2, 3))]
 
 
+def scatter_z(mine):
+    count = lax.axis_size("gx")
+    groups = [list(range(core, count, 2)) for core in range(2)]
+    return lax.psum_scatter(mine, "gx", scatter_dimension=0, axis_index_groups=groups, tiled=False)
+
+
 def along_z_sum(mine, z):
     came = [turn(at(mine, (z + k) % 4), k) for k in (1, 2, 3)]
     return at(mine, z), came
@@ -910,29 +916,27 @@
     slabs_of = head_w.reshape(head_rows, slabs, dec_width).transpose(1, 0, 2).reshape(-1, dec_width)
     share_d = jnp.concatenate([dec_w, slabs_of])
     front_p = gather_apart(share_p)
-    masked, share_a = tied(masked, share_a)
-    front_a = gather_apart(share_a)
     quarter = patch_w.shape[0] // 4
+    parts_of = lambda m: m.reshape(8, model_width // 8, 4, model_width).transpose(0, 2, 1, 3)
     if split:
         row = tile_row
+        got_a = along_z(lax.dynamic_slice_in_dim(share_a, row * model_width, model_width, axis=1))
         mine_b = jnp.concatenate([lax.dynamic_slice_in_dim(fc1_w, row * model_width, model_width, axis=1),
                                   lax.dynamic_slice_in_dim(fc2_w, row * each, each, axis=0)])
-        got_b = along_z(mine_b)
-        strips, denom = give_margin_and_sum(masked, dates, side, weight, got_b)
+        strips, denom = give_margin_and_sum(masked, dates, side, weight, got_a)
+        got_b = along_z(after(mine_b, front_p, *strips[1:]))
+        pieces_a = (share_a, *along_gy(got_a))
+        others_a = core_swap(pieces_a)
+        share_d = after(share_d, got_b, *pieces_a)
     else:
         strips, denom = give_margin_and_sum(masked, dates, side, weight)
-    tops = gather_apart(after(share_d, *strips[1:], front_p))
+        front_a = parts_of(jnp.concatenate([gather(qkv_w), gather(proj_w)], axis=1))
+        quarters_of = lambda m: m.reshape(8, 4, -1, model_width)
+        full_mlp = jnp.concatenate([parts_of(gather(fc1_w)), quarters_of(gather(fc2_w))], axis=2)
+    tops = gather_apart(share_d)
     full_dec = tops[:, :dec_rows].reshape(-1, dec_width)
     full_head = tops[:, dec_rows:].reshape(-1, slabs, head_rows, dec_width).transpose(0, 2, 1, 3).reshape(-1, pixel_width)
     small = front_p[:, patch_w.shape[0] :]
-    if split:
-        got_b = after(got_b, *strips[1:])
-        pieces_b = (fc1_w, fc2_w, *along_gy(got_b))
-        strips = tied(*strips, got_b)[:-1]
-    else:
-        parts_of = lambda m: m.reshape(8, model_width // 8, 4, model_width).transpose(0, 2, 1, 3)
-        quarters_of = lambda m: m.reshape(8, 4, -1, model_width)
-        full_mlp = jnp.concatenate([parts_of(gather(fc1_w)), quarters_of(gather(fc2_w))], axis=2)
     own_dates = scene_dates[own_scene]
     stamps = timestamps[own_scene]
     date_ok = jnp.arange(dates, dtype=jnp.int32) < own_dates
@@ -955,20 +959,22 @@
     ratio = valid / denom
     gr = (cotangent.reshape(own, pixel_width).astype(f32) * ratio).astype(bf16)
     ext, h0, a = embed(strips, front_p, hot, table, vec)
+    if split:
+        front_a = place(pos, pieces_a, (*others_a[:-1], after(others_a[-1], a)), ("wide",))
+        a, got_b = tied(a, got_b)
+        pieces_b = (fc1_w, fc2_w, *along_gy(got_b))
     qkv = project(a, front_a, 3)
-    if split:
-        qkv, *pieces_b = tied(qkv, *pieces_b)
-        others_b = core_swap(pieces_b)
     o, qx = attn_fwd(qkv, kx, scale)
     if split:
-        o, *others_b = tied(o, *others_b)
+        o, *pieces_b = tied(o, *pieces_b)
+        others_b = core_swap(pieces_b)
     h1, c = proj_norm(o, front_a, h0, vec)
     gz = dense(after(gr, c), full_head, 1, 1).astype(bf16)
     west, east = margin_first(gz, dates, side)
     c, west, east = tied(c, west, east)
     right, left = to_neighbours(west, east, "gx")
     if split:
-        full_mlp = place(pos, pieces_b, (*others_b[:-1], after(others_b[-1], c)))
+        full_mlp = place(pos, pieces_b, (*others_b[:-1], after(others_b[-1], c)), ("wide", "tall"))
         full_mlp, right, left = tied(full_mlp, right, left)
     middle, north, south = margin_second(gz, right, left, dates, side)
     full_mlp, north, south = tied(full_mlp, north, south)
@@ -988,24 +994,26 @@
     g = tile_row
     if split:
         got1, got2 = swap(send1, "gx", 1), swap(send2, "gx", 1)
-    below, above, dc = tied(below, above, dc)
+    grad_dec = dense(h2r, dz, 0, 0)
+    dc, grad_dec = tied(dc, grad_dec.astype(bf16))
+    grad_dec = scatter(grad_dec)
+    dh1, dattn, do, grad_gain2, grad_shift2 = norm2_back(dc, h1, dh2, vec, front_a)
+    below, above, do = tied(below, above, do)
     folded, west, east = fold_second(every, below, above, dates, side)
-    grad_dec = dense(h2r, dz, 0, 0)
-    dc, west, east, grad_dec = tied(dc, west, east, grad_dec)
+    do, west, east = tied(do, west, east)
     right, left = to_neighbours(west, east, "gx")
-    dh1, dattn, do, grad_gain2, grad_shift2 = norm2_back(dc, h1, dh2, vec, front_a)
     if split:
         got1, got2 = after(got1, do), after(got2, do)
         out1, keep1 = near_sum(keep1, got1, 1, g)
         out2, keep2 = near_sum(keep2, got2, 2, g)
         do, out1, out2 = tied(do, out1, out2)
         got1, got2 = swap(out1, "gy", 1), swap(out2, "gy", 2)
-    right, left, do = tied(right, left, do)
+    dqkv = attn_bwd(qkv, do, o, qx, kx, scale)
+    right, left = after(right, dqkv), after(left, dqkv)
     folded = fold_third(folded, right, left, dates, side)
     grad_head = dense(folded, gr, 0, 0)
-    do, grad_head, grad_dec = tied(do, grad_head.astype(bf16), grad_dec)
-    grad_head, grad_dec = scatter(grad_head), scatter(grad_dec)
-    dqkv = attn_bwd(qkv, do, o, qx, kx, scale)
+    dqkv, grad_head = tied(dqkv, grad_head.astype(bf16))
+    grad_head = scatter(grad_head)
     if split:
         got1, got2 = after(got1, dqkv), after(got2, dqkv)
         out1, keep1 = far_sum(keep1, got1, 1, g)
@@ -1013,54 +1021,49 @@
         dqkv, out1, out2 = tied(dqkv, out1, out2)
         got1, got2 = swap(out1, "gy", 2), swap(out2, "gy", 1)
     keep3, send3 = qkvo_grad(pos, a, dqkv, o, dattn, 4)
-    ends = jnp.concatenate([after(grad_dec, keep3), after(grad_head, keep3).reshape(-1, dec_width)])
     if split:
         got3 = swap(send3, "gx", 1)
-        got1, got2 = after(got1, keep3), after(got2, keep3)
-        mine1, came1 = along_z_sum(jnp.concatenate([added(*keep1, got1), added(*keep2, got2)], axis=1), chip)
-        dqkv, mine1, ends = tied(dqkv, mine1, ends)
-        ends_near = swap(ends, "gy", 1)
     demb, grad_gain1, grad_shift1 = norm1_back(dqkv, front_a, h0, dh1, vec)
     vectors = (grad_gain1, grad_shift1, grad_gain2, grad_shift2)
     north, south = fold_first(demb, dates, side)
+    ends = jnp.concatenate([after(grad_dec, demb), after(grad_head, demb).reshape(-1, dec_width)])
     if split:
-        got3, ends_near = after(got3, demb), after(ends_near, demb)
+        got3, got1, got2 = after(got3, demb), after(got1, demb), after(got2, demb)
         outs3, keep3 = to_each(keep3, got3, g)
-        ends = added(ends, ends_near)
-        demb, north, south, ends, *outs3 = tied(demb, north, south, ends, *outs3)
+        mine1 = jnp.concatenate([added(*keep1, got1), added(*keep2, got2)], axis=1)
+        demb, mine1 = tied(demb, mine1)
+        done1 = scatter_z(mine1)
+        demb, north, south, *outs3 = tied(demb, north, south, *outs3)
     below, above = to_neighbours(north, south, "gy")
     if split:
         got3 = swap_each(outs3)
         keep4, send4 = patch_grad(pos, ext, demb, grad_fc1_b, vectors, 4, 4)
         got4 = swap(send4, "gx", 1)
-        below, above = after(below, keep4), after(above, keep4)
+        got3 = [after(v, keep4) for v in got3]
+        mine3 = added(*keep3, *got3)
+        below, above, got4 = after(below, mine3), after(above, mine3), after(got4, mine3)
     part, west, east = fold_second(demb, below, above, dates, side)
     right, left = to_neighbours(west, east, "gx")
     if split:
-        got4 = after(got4, west, east)
         outs4, keep4 = to_each(keep4, got4, g)
-        came1 = [after(v, *outs4) for v in came1]
-        done1 = added(mine1, *came1)
-        right, left, done1, *outs4 = tied(right, left, done1, *outs4)
+        right, left, *outs4 = tied(right, left, *outs4)
         got4 = swap_each(outs4)
         dmasked = fold_third(part, right, left, dates, side)
+        dmasked, done1 = tied(dmasked, done1)
+        every1 = to_all_gy(jnp.concatenate([done1, ends.reshape(-1, model_width)]))
         pixel_grad = pixel_back(dmasked, front_p, shown, pixel_width)
-        every1 = to_all_gy(after(done1, dmasked))
-        got3 = [after(v, pixel_grad) for v in got3]
-        mine3 = added(*keep3, *got3)
-        got4 = [after(v, mine3) for v in got4]
+        got4 = [after(v, pixel_grad) for v in got4]
         mine4, came4 = along_z_sum(jnp.concatenate([mine3, added(*keep4, *got4)], axis=1), chip)
-        folded, mine4, ends = tied(folded, mine4, ends)
-        ends_far = swap(ends, "gy", 2)
+        folded, mine4 = tied(folded, mine4)
         recon = (dense(folded, full_head) * ratio).astype(bf16)
         came4 = [after(v, recon) for v in came4]
         done4 = added(mine4, *came4)
         every1 = tied(*every1, done4)[:-1]
         every4 = to_all_gy(done4)
-        every1 = in_order(every1, g)
+        ends = added(*[v[2 * each :] for v in every1]).astype(f32).reshape(-1, dec_width)
+        every1 = in_order([v[: 2 * each] for v in every1], g)
         sum1 = jnp.concatenate([v[:each] for v in every1], axis=1).astype(f32)
         sum2 = jnp.concatenate([v[each:] for v in every1], axis=0).astype(f32)
-        ends = ends.astype(f32) + ends_far.astype(f32)
         every4 = tied(*every4, sum1, sum2, ends)[:-3]
         every4 = in_order(every4, g)
         sum1, sum2 = jnp.split(sum1, 4, axis=1), jnp.split(sum2, 4, axis=0)

time: 521 us -> 502 us (0.964)
  waiting for transfers between devices: 116 us -> 85.1 us
  local copies, waits for them, and re-layouts: 30.6 us -> 37.8 us
    all_gather x3 -> x2, waiting for transfers between devices: 27.1 us -> 2.45 us  [gather_apart(): return lax.all_gather(shard, 'gx', axis=0, tiled=False)]
    ppermute x9, waiting for transfers between devices: 42.5 us -> 25.7 us  [turn(): lax.ppermute(value, 'gx', [(i, (i + 2 * step) % count) for i in range(cou...]
    ppermute x31 -> x37, waiting for transfers between devices: 36.4 us -> 45.2 us  [swap(): lax.ppermute(value, axis, [(i, i ^ bit) for i in range(lax.axis_size(axis...]
    pallas_call x1 -> x2, Pallas kernels: 8.83 us -> 14.1 us  [place(): pl.pallas_call(functools.partial(place_kernel, kinds=kinds), grid_spec=pl...]
    ppermute x31 -> x37, starting transfers between devices: 49.2 us -> 46 us  [swap(): lax.ppermute(value, axis, [(i, i ^ bit) for i in range(lax.axis_size(axis...]
    convert_element_type x13 -> x11, other arithmetic: 20.1 us -> 21.9 us  [added(): return sum((v.astype(f32) for v in values)).astype(bf16)]
  transfers between devices with their start and end apart: 61 -> 67, of which waited for: 20 -> 22; matrix products, arithmetic and copies ran while one was open for 14% -> 18% of each run, Pallas kernels for 22% -> 26%
where the time goes in v3:
time: 502 us; the launch traced here: 496 us
  Pallas kernels  179 us (36%)
  starting transfers between devices  101 us (20%)
  waiting for transfers between devices  85.1 us (17%)
  other arithmetic  47.8 us (10%)
  local copies, waits for them, and re-layouts  37.8 us (8%)
  matrix products  27.2 us (5%)
  between operations  17.7 us (4%)
    ppermute x37, starting transfers between devices, swap(): lax.ppermute(value, axis, [(i, i ^ bit) for i in range(lax.axis_size(axis...  46 us
    ppermute x37, waiting for transfers between devices, swap(): lax.ppermute(value, axis, [(i, i ^ bit) for i in range(lax.axis_size(axis...  45.2 us
    pallas_call x1, Pallas kernels, attn_bwd(): pl.pallas_call(functools.partial(attn_bwd_kernel, block=token_block(token...  33.6 us
    pallas_call x1, Pallas kernels, mlp_bwd(): pl.pallas_call(functools.partial(mlp_bwd_kernel, chips=chips), grid_spec=...  31.8 us
    ppermute x8, starting transfers between devices, to_neighbours(): lax.ppermute(high, axis, chain(axis, 1))  31.1 us
    ppermute x9, waiting for transfers between devices, turn(): lax.ppermute(value, 'gx', [(i, (i + 2 * step) % count) for i in range(cou...  25.7 us
    convert_element_type x11, other arithmetic, added(): return sum((v.astype(f32) for v in values)).astype(bf16)  21.9 us
    pallas_call x1, Pallas kernels, attn_fwd(): pl.pallas_call(functools.partial(attn_fwd_kernel, block=token_block(token...  18.5 us
  transfers between devices with their start and end apart: 67, of which 22 were waited for; matrix products, arithmetic and copies ran while one was open for 18% of the time, Pallas kernels for 26%

profile of v3, /device:TPU:0, one launch (start us, length us, event | category | flops | bytes accessed | tf_op | source)
XLA Modules:
  0.0 495.9 jit_solution(6674625970374833456)
XLA Ops:
  10.1 3.0 collective-permute-start.2
  13.1 2.6 collective-permute-start.3
  22.9 2.0 collective-permute-start.1
  35.7 1.9 pad_maximum_fusion.4.refs_1_
  43.6 5.5 %collective-permute-start.5 = (bf16[160,1536]{1,0:T(8,128)(2,1)S(1)}, bf16[160,1536]{1,0:T(8,128)(2,1)}, u32[]{:S(2)}, u32[]{:S(2)}) collective-permute-start(bf16[160,1536]{1,0:T(8,128)(2,1)S(1)} %fusion.40), channel_id=1, source_target_pairs={{0,8},{8,16},{16,24},{1,9},{9,17},{17,25},{2,10},{10,18},{18,26},{... | collective-permute-start | bytes 1474568 | tf_op jit(solution)/shard_map/ppermute | solution.py:671
  52.5 5.3 %collective-permute-done.6.lower_ref = bf16[160,1536]{1,0:T(8,128)(2,1)} collective-permute-done((bf16[160,1536]{1,0:T(8,128)(2,1)S(1)}, bf16[160,1536]{1,0:T(8,128)(2,1)}, u32[]{:S(2)}, u32[]{:S(2)}) %collective-permute-start.6) | collective-permute-done | bytes 491552 | tf_op jit(solution)/shard_map/ppermute | solution.py:671
  57.9 1.9 collective-permute-done.5.upper_ref
  59.8 2.4 all-gather.5.cloned.1.call-done
  64.5 5.8 %collective-permute-start.10 = (bf16[3,96,768]{2,1,0:T(8,128)(2,1)}, bf16[3,96,768]{2,1,0:T(8,128)(2,1)S(1)}, u32[]{:S(2)}, u32[]{:S(2)}) collective-permute-start(bf16[3,96,768]{2,1,0:T(8,128)(2,1)} %pad_maximum_fusion.4.refs_1_), channel_id=1, source_target_pairs={{0,8},{8,0},{16,24},{24,16},{1,9},{9,1},{17,25},{25,17},{2,10},{10... | collective-permute-start | bytes 1327112 | tf_op jit(solution)/shard_map/ppermute | solution.py:780
  70.3 3.5 collective-permute-start.11
  74.8 1.8 collective-permute-start.9
  79.5 10.3 %collective-permute-done.8 = bf16[192,768]{1,0:T(8,128)(2,1)S(1)} collective-permute-done((bf16[192,768]{1,0:T(8,128)(2,1)}, bf16[192,768]{1,0:T(8,128)(2,1)S(1)}, u32[]{:S(2)}, u32[]{:S(2)}) %collective-permute-start.8) | collective-permute-done | bytes 294944 | tf_op jit(solution)/shard_map/ppermute | solution.py:785
  98.8 7.7 %embed.1 = (bf16[864,1536]{1,0:T(8,128)(2,1)}, f32[864,768]{1,0:T(8,128)}, bf16[864,768]{1,0:T(8,128)(2,1)}) custom-call(bf16[384,1536]{1,0:T(8,128)(2,1)} %bitcast.229, bf16[112,1536]{1,0:T(8,128)(2,1)} %collective-permute-done.1.left_ref, bf16[112,1536]{1,0:T(8,128)(2,1)} %collective-permute-done.right_ref, ...), custom_call_target="tpu_custom_call" | custom-call | flops 2038431744 | bytes 11649024 | tf_op jit(solution)/shard_map/embed/pallas_call | solution.py:97
  107.3 5.4 %place.2.w_ref = bf16[8,4,96,768]{3,2,1,0:T(8,128)(2,1)} custom-call(s32[3]{0:T(128)} %pad_add_fusion.pos_ref, bf16[96,3072]{1,0:T(8,128)(2,1)} %copy-done.3, bf16[3,96,768]{2,1,0:T(8,128)(2,1)} %pad_maximum_fusion.4.refs_1_, bf16[3,96,768]{2,1,0:T(8,128)(2,1)} %copy-done.33, bf16[3,96,768]{2,1,0:T(8,128)(2,1)} %collective-permute-done.11.refs_3_, ...), custom_call_target="tpu_custom_call" | custom-call | bytes 9437184 | tf_op jit(solution)/shard_map/place/pallas_call | solution.py:530
  112.7 3.2 collective-permute-start.18
  116.0 3.1 collective-permute-start.19
  119.1 8.6 %project.1.q_ref.k_ref.v_ref = bf16[864,2304]{1,0:T(8,128)(2,1)} custom-call(bf16[864,768]{1,0:T(8,128)(2,1)} %get-tuple-element.137.a_ref, bf16[8,4,96,768]{3,2,1,0:T(8,128)(2,1)} %place.2.w_ref), custom_call_target="tpu_custom_call" | custom-call | flops 3057647616 | bytes 8847360 | tf_op jit(solution)/shard_map/project/pallas_call | solution.py:118
  127.7 18.5 %attn_fwd.1 = (bf16[864,768]{1,0:T(8,128)(2,1)}, bf16[12,864,128]{2,1,0:T(8,128)(2,1)}) custom-call(bf16[864,2304]{1,0:T(8,128)(2,1)} %project.1.q_ref.k_ref.v_ref, bf16[864,2304]{1,0:T(8,128)(2,1)} %project.1.q_ref.k_ref.v_ref, bf16[864,2304]{1,0:T(8,128)(2,1)} %project.1.q_ref.k_ref.v_ref, bf16[864,128]{1,0:T(8,128)(2,1)} %select_convert_fusion.kx_ref), custom_call_target="tpu_custom_call" | custom-call | flops 18345885696 | bytes 5308416 | tf_op jit(solution)/shard_map/attn_fwd/pallas_call | solution.py:177
  146.2 11.4 %collective-permute-done.19.refs_4_ = bf16[3,192,768]{2,1,0:T(8,128)(2,1)} collective-permute-done((bf16[3,192,768]{2,1,0:T(8,128)(2,1)S(1)}, bf16[3,192,768]{2,1,0:T(8,128)(2,1)}, u32[]{:S(2)}, u32[]{:S(2)}) %collective-permute-start.19) | collective-permute-done | bytes 884768 | tf_op jit(solution)/shard_map/ppermute | solution.py:780
  159.3 5.8 %proj_norm.1 = (f32[864,768]{1,0:T(8,128)}, bf16[864,768]{1,0:T(8,128)(2,1)}) custom-call(bf16[864,768]{1,0:T(8,128)(2,1)} %get-tuple-element.141.o_ref, bf16[8,4,96,768]{3,2,1,0:T(8,128)(2,1)} %place.2.w_ref, f32[864,768]{1,0:T(8,128)} %get-tuple-element.142.h0_ref, f32[4,768]{1,0:T(4,128)} %reshape.344.vec_ref.gain_ref), custom_call_target="tpu_custom_call" | custom-call | flops 1019215872 | bytes 9142272 | tf_op jit(solution)/shard_map/proj_norm/pallas_call | solution.py:260
  172.9 3.2 collective-permute-start.28
  177.7 8.6 %place.3.fc1_ref.fc2_ref = bf16[8,4,192,768]{3,2,1,0:T(8,128)(2,1)} custom-call(s32[3]{0:T(128)} %pad_add_fusion.pos_ref, bf16[96,3072]{1,0:T(8,128)(2,1)} %refs_0_, bf16[384,768]{1,0:T(8,128)(2,1)} %refs_1_, bf16[3,192,768]{2,1,0:T(8,128)(2,1)} %copy-done.1, bf16[3,192,768]{2,1,0:T(8,128)(2,1)} %collective-permute-done.18.refs_3_, ...), custom_call_target="tpu_custom_call" | custom-call | bytes 18874368 | tf_op jit(solution)/shard_map/place/pallas_call | solution.py:530
  187.5 17.5 %mlp_fwd.1 = (bf16[864,3072]{1,0:T(8,128)(2,1)}, bf16[864,3072]{1,0:T(8,128)(2,1)}, bf16[864,768]{1,0:T(8,128)(2,1)}) custom-call(bf16[864,768]{1,0:T(8,128)(2,1)} %get-tuple-element.146.c_ref, bf16[8,4,192,768]{3,2,1,0:T(8,128)(2,1)} %place.3.fc1_ref.fc2_ref, f32[1,3072]{1,0:T(1,128)} %reshape.349.b_ref, bf16[8,4,192,768]{3,2,1,0:T(8,128)(2,1)} %place.3.fc1_ref.fc2_ref, ...), custom_call_target="tpu_custom_call" | custom-call | flops 8153726976 | bytes 25362432 | tf_op jit(solution)/shard_map/mlp_fwd/pallas_call | solution.py:308
  205.0 2.2 multiply_convert_fusion.1
  209.3 4.6 collective-permute-start.32
  216.5 2.8 fusion.97
  219.3 31.8 %mlp_bwd.1 = (f32[864,768]{1,0:T(8,128)}, f32[1,3072]{1,0:T(1,128)}, bf16[4,4,96,768]{3,2,1,0:T(8,128)(2,1)}, bf16[4,4,96,768]{3,2,1,0:T(8,128)(2,1)}, bf16[4,4,...) custom-call(s32[3]{0:T(128)} %pad_add_fusion.pos_ref, bf16[864,768]{1,0:T(8,128)(2,1)} %get-tuple-element.328.dm_ref, ...), custom_call_target="tpu_custom_call" | custom-call | flops 16307453952 | bytes 34799616 | tf_op jit(solution)/shard_map/mlp_bwd/pallas_call | solution.py:383
  251.1 3.6 collective-permute-start.35
  256.1 5.7 %collective-permute-start.30 = (bf16[144,512]{1,0:T(8,128)(2,1)}, bf16[144,512]{1,0:T(8,128)(2,1)}, u32[]{:S(2)}, u32[]{:S(2)}) collective-permute-start(bf16[144,512]{1,0:T(8,128)(2,1)} %get-tuple-element.292), channel_id=1, source_target_pairs={{0,8},{8,16},{16,24},{1,9},{9,17},{17,25},{2,10},{10,18},{18,26},{... | collective-permute-start | bytes 442376 | tf_op jit(solution)/shard_map/ppermute | solution.py:671
  261.8 3.5 convolution_convert_fusion.3
  265.4 8.5 %norm2_back.1 = (f32[864,768]{1,0:T(8,128)}, bf16[864,768]{1,0:T(8,128)(2,1)}, bf16[864,768]{1,0:T(8,128)(2,1)}, f32[1,768]{1,0:T(1,128)}, f32[1,768]{1,0:T(1,128)}) custom-call(f32[864,768]{1,0:T(8,128)} %get-tuple-element.169.dc_ref, f32[864,768]{1,0:T(8,128)} %get-tuple-element.160.h1_ref, f32[864,768]{1,0:T(8,128)} %get-tuple-element.329.dh2_ref, ...), custom_call_target="tpu_custom_call" | custom-call | flops 1019215872 | bytes 14450688 | tf_op jit(solution)/shard_map/norm2_back/pallas_call | solution.py:581
  275.2 2.2 fusion.98
  279.4 3.7 collective-permute-start.36
  284.6 4.2 add_convert_fusion
  290.5 3.6 collective-permute-start.38
  294.1 33.6 %attn_bwd.1.d_ref = bf16[3,864,768]{2,1,0:T(8,128)(2,1)} custom-call(bf16[864,2304]{1,0:T(8,128)(2,1)} %project.1.q_ref.k_ref.v_ref, bf16[864,2304]{1,0:T(8,128)(2,1)} %project.1.q_ref.k_ref.v_ref, bf16[864,2304]{1,0:T(8,128)(2,1)} %project.1.q_ref.k_ref.v_ref, bf16[864,768]{1,0:T(8,128)(2,1)} %get-tuple-element.182.do_ref, ...), custom_call_target="tpu_custom_call" | custom-call | flops 22932357120 | bytes 10616832 | tf_op jit(solution)/shard_map/attn_bwd/pallas_call | solution.py:237
  330.8 2.2 convolution_convert_fusion
  333.3 2.0 fusion.39
  335.4 2.0 fusion.38
  337.4 10.9 %qkvo_grad.1 = (bf16[4,4,96,768]{3,2,1,0:T(8,128)(2,1)}, bf16[4,4,96,768]{3,2,1,0:T(8,128)(2,1)}) custom-call(s32[3]{0:T(128)} %pad_add_fusion.pos_ref, bf16[864,768]{1,0:T(8,128)(2,1)} %get-tuple-element.137.a_ref, bf16[3,864,768]{2,1,0:T(8,128)(2,1)} %attn_bwd.1.d_ref, bf16[864,768]{1,0:T(8,128)(2,1)} %get-tuple-element.141.o_ref, ...), custom_call_target="tpu_custom_call" | custom-call | flops 4076863488 | bytes 12681216 | tf_op jit(solution)/shard_map/qkvo_grad/pallas_call | solution.py:417
  348.2 2.2 collective-permute-start.39
  352.5 8.8 %norm1_back.1 = (bf16[864,768]{1,0:T(8,128)(2,1)}, f32[1,768]{1,0:T(1,128)}, f32[1,768]{1,0:T(1,128)}) custom-call(bf16[3,864,768]{2,1,0:T(8,128)(2,1)} %attn_bwd.1.d_ref, bf16[8,4,96,768]{3,2,1,0:T(8,128)(2,1)} %place.2.w_ref, f32[864,768]{1,0:T(8,128)} %get-tuple-element.142.h0_ref, f32[864,768]{1,0:T(8,128)} %get-tuple-element.196.dh1_ref, ...), custom_call_target="tpu_custom_call" | custom-call | flops 3057647616 | bytes 14155776 | tf_op jit(solution)/shard_map/norm1_back/pallas_call | solution.py:610
  361.3 1.8 fusion.84
  363.2 2.7 collective-permute-done.40
  370.9 2.9 fusion.37
  377.3 7.5 %patch_grad.1 = (bf16[4,4,64,768]{3,2,1,0:T(8,128)(2,1)}, bf16[4,4,64,768]{3,2,1,0:T(8,128)(2,1)}) custom-call(s32[3]{0:T(128)} %pad_add_fusion.pos_ref, bf16[864,1536]{1,0:T(8,128)(2,1)} %get-tuple-element.205.ext_ref, bf16[864,768]{1,0:T(8,128)(2,1)} %get-tuple-element.206.demb_ref, f32[1,3072]{1,0:T(1,128)} %get-tuple-element.207.bias_ref, ...), custom_call_target="tpu_custom_call" | custom-call | flops 2038431744 | bytes 6340608 | tf_op jit(solution)/shard_map/patch_grad/pallas_call | solution.py:471
  388.0 2.4 collective-permute-done.42
  390.4 3.4 collective-permute-start.47
  393.8 7.0 %collective-permute-done.43 = bf16[4,96,768]{2,1,0:T(8,128)(2,1)} collective-permute-done((bf16[4,96,768]{2,1,0:T(8,128)(2,1)}, bf16[4,96,768]{2,1,0:T(8,128)(2,1)}, u32[]{:S(2)}, u32[]{:S(2)}) %collective-permute-start.43) | collective-permute-done | bytes 589856 | tf_op jit(solution)/shard_map/ppermute | solution.py:780
  400.8 3.1 collective-permute-done.44
  403.9 2.0 fusion.23
  405.9 1.8 collective-permute-done.46
  409.8 3.0 collective-permute-start.49
  413.1 2.8 fusion.44
  415.9 2.6 collective-permute-start.50
  418.5 3.2 collective-permute-start.51
  423.2 5.7 %pixel_back.1 = f32[384,1536]{1,0:T(8,128)} custom-call(bf16[384,768]{1,0:T(8,128)(2,1)} %fusion.12.d_ref, bf16[8,208,768]{2,1,0:T(8,128)(2,1)} %bitcast.236, f32[384,1]{1,0:T(8,128)} %convert_element_type.689.shown_ref), custom_call_target="tpu_custom_call" | custom-call | flops 905969664 | bytes 4718592 | tf_op jit(solution)/shard_map/pixel_back/pallas_call | solution.py:494
  428.9 11.0 %collective-permute-done.51 = bf16[4,64,768]{2,1,0:T(8,128)(2,1)} collective-permute-done((bf16[4,64,768]{2,1,0:T(8,128)(2,1)}, bf16[4,64,768]{2,1,0:T(8,128)(2,1)}, u32[]{:S(2)}, u32[]{:S(2)}) %collective-permute-start.51) | collective-permute-done | bytes 393248 | tf_op jit(solution)/shard_map/ppermute | solution.py:780
  442.6 1.8 collective-permute-start.53
  448.1 5.4 %collective-permute-done.53 = bf16[160,768]{1,0:T(8,128)(2,1)S(1)} collective-permute-done((bf16[160,768]{1,0:T(8,128)(2,1)}, bf16[160,768]{1,0:T(8,128)(2,1)S(1)}, u32[]{:S(2)}, u32[]{:S(2)}) %collective-permute-start.53) | collective-permute-done | bytes 245792 | tf_op jit(solution)/shard_map/ppermute | solution.py:785
  453.8 1.8 fusion
  455.6 7.7 %collective-permute-done.54 = bf16[160,768]{1,0:T(8,128)(2,1)S(1)} collective-permute-done((bf16[160,768]{1,0:T(8,128)(2,1)}, bf16[160,768]{1,0:T(8,128)(2,1)S(1)}, u32[]{:S(2)}, u32[]{:S(2)}) %collective-permute-start.54) | collective-permute-done | bytes 245792 | tf_op jit(solution)/shard_map/ppermute | solution.py:785
  463.4 2.2 collective-permute-done.55
  469.4 5.3 %collective-permute-done.61 = bf16[384,768]{1,0:T(8,128)(2,1)} collective-permute-done((bf16[384,768]{1,0:T(8,128)(2,1)S(1)}, bf16[384,768]{1,0:T(8,128)(2,1)}, u32[]{:S(2)}, u32[]{:S(2)}) %collective-permute-start.61) | collective-permute-done | bytes 589856 | tf_op jit(solution)/shard_map/ppermute | solution.py:780
  (389 shorter events, 113.4 us)
Async XLA Ops:
  7.2 55.0 %all-gather.5.cloned.1.call-start = ((), (), s32[]{:S(2)}) async-start(), calls=%async_computation.6 | async-start | bytes 2875392 | tf_op jit(solution)/shard_map/all_gather | solution.py:870
  10.1 25.6 %collective-permute-start.2 = (bf16[96,768]{1,0:T(8,128)(2,1)}, bf16[96,768]{1,0:T(8,128)(2,1)}, u32[]{:S(2)}, u32[]{:S(2)}) collective-permute-start(bf16[96,768]{1,0:T(8,128)(2,1)} %constant_dynamic-slice_fusion.7), channel_id=1, source_target_pairs={{0,2},{1,3},{2,4},{3,5},{4,6},{5,7},{6,0},{7,1},{8,10},{9,11},{10,... | collective-permute-start | bytes 442376 | tf_op jit(solution)/shard_map/ppermute | solution.py:785
  13.1 22.6 %collective-permute-start.3 = (bf16[96,768]{1,0:T(8,128)(2,1)}, bf16[96,768]{1,0:T(8,128)(2,1)}, u32[]{:S(2)}, u32[]{:S(2)}) collective-permute-start(bf16[96,768]{1,0:T(8,128)(2,1)} %constant_dynamic-slice_fusion.7), channel_id=1, source_target_pairs={{0,4},{1,5},{2,6},{3,7},{4,0},{5,1},{6,2},{7,3},{8,12},{9,13},{10,... | collective-permute-start | bytes 442376 | tf_op jit(solution)/shard_map/ppermute | solution.py:785
  15.7 20.0 %collective-permute-start.4 = (bf16[96,768]{1,0:T(8,128)(2,1)}, bf16[96,768]{1,0:T(8,128)(2,1)}, u32[]{:S(2)}, u32[]{:S(2)}) collective-permute-start(bf16[96,768]{1,0:T(8,128)(2,1)} %constant_dynamic-slice_fusion.7), channel_id=1, source_target_pairs={{0,6},{1,7},{2,0},{3,1},{4,2},{5,3},{6,4},{7,5},{8,14},{9,15},{10,... | collective-permute-start | bytes 442376 | tf_op jit(solution)/shard_map/ppermute | solution.py:785
  22.9 14.7 %collective-permute-start.1 = (bf16[112,1536]{1,0:T(8,128)(2,1)}, bf16[112,1536]{1,0:T(8,128)(2,1)}, u32[]{:S(2)}, u32[]{:S(2)}) collective-permute-start(bf16[112,1536]{1,0:T(8,128)(2,1)} %fusion.50), channel_id=1, source_target_pairs={{0,1},{1,2},{2,3},{3,4},{4,5},{5,6},{6,7},{8,9},{9,10},{10,11},{11... | collective-permute-start | bytes 1032200 | tf_op jit(solution)/shard_map/ppermute | solution.py:671
  25.9 11.7 %collective-permute-start = (bf16[112,1536]{1,0:T(8,128)(2,1)}, bf16[112,1536]{1,0:T(8,128)(2,1)}, u32[]{:S(2)}, u32[]{:S(2)}) collective-permute-start(bf16[112,1536]{1,0:T(8,128)(2,1)} %fusion.49), channel_id=1, source_target_pairs={{1,0},{2,1},{3,2},{4,3},{5,4},{6,5},{7,6},{9,8},{10,9},{11,10},{12... | collective-permute-start | bytes 1032200 | tf_op jit(solution)/shard_map/ppermute | solution.py:671
  28.1 138.0 %all-gather.7.cloned.1.call-start = ((), (), s32[]{:S(2)}) async-start(), calls=%async_computation.7 | async-start | bytes 2654208 | tf_op jit(solution)/shard_map/all_gather | solution.py:870
  41.9 16.0 %collective-permute-start.6 = (bf16[160,1536]{1,0:T(8,128)(2,1)S(1)}, bf16[160,1536]{1,0:T(8,128)(2,1)}, u32[]{:S(2)}, u32[]{:S(2)}) collective-permute-start(bf16[160,1536]{1,0:T(8,128)(2,1)S(1)} %fusion.41), channel_id=1, source_target_pairs={{8,0},{16,8},{24,16},{9,1},{17,9},{25,17},{10,2},{18,10},{26,18},{... | collective-permute-start | bytes 1474568 | tf_op jit(solution)/shard_map/ppermute | solution.py:671
  43.6 16.2 %collective-permute-start.5 = (bf16[160,1536]{1,0:T(8,128)(2,1)S(1)}, bf16[160,1536]{1,0:T(8,128)(2,1)}, u32[]{:S(2)}, u32[]{:S(2)}) collective-permute-start(bf16[160,1536]{1,0:T(8,128)(2,1)S(1)} %fusion.40), channel_id=1, source_target_pairs={{0,8},{8,16},{16,24},{1,9},{9,17},{17,25},{2,10},{10,18},{18,26},{... | collective-permute-start | bytes 1474568 | tf_op jit(solution)/shard_map/ppermute | solution.py:671
  62.2 12.6 %collective-permute-start.7 = (bf16[192,768]{1,0:T(8,128)(2,1)}, bf16[192,768]{1,0:T(8,128)(2,1)S(1)}, u32[]{:S(2)}, u32[]{:S(2)}) collective-permute-start(bf16[192,768]{1,0:T(8,128)(2,1)} %pad_maximum_fusion.5), channel_id=1, source_target_pairs={{0,2},{1,3},{2,4},{3,5},{4,6},{5,7},{6,0},{7,1},{8,10},{9,11},{10,... | collective-permute-start | bytes 884744 | tf_op jit(solution)/shard_map/ppermute | solution.py:785
  64.5 27.2 %collective-permute-start.10 = (bf16[3,96,768]{2,1,0:T(8,128)(2,1)}, bf16[3,96,768]{2,1,0:T(8,128)(2,1)S(1)}, u32[]{:S(2)}, u32[]{:S(2)}) collective-permute-start(bf16[3,96,768]{2,1,0:T(8,128)(2,1)} %pad_maximum_fusion.4.refs_1_), channel_id=1, source_target_pairs={{0,8},{8,0},{16,24},{24,16},{1,9},{9,1},{17,25},{25,17},{2,10},{10... | collective-permute-start | bytes 1327112 | tf_op jit(solution)/shard_map/ppermute | solution.py:780
  70.3 21.7 %collective-permute-start.11 = (bf16[3,96,768]{2,1,0:T(8,128)(2,1)}, bf16[3,96,768]{2,1,0:T(8,128)(2,1)}, u32[]{:S(2)}, u32[]{:S(2)}) collective-permute-start(bf16[3,96,768]{2,1,0:T(8,128)(2,1)} %pad_maximum_fusion.4.refs_1_), channel_id=1, source_target_pairs={{0,16},{8,24},{16,0},{24,8},{1,17},{9,25},{17,1},{25,9},{2,18},{10... | collective-permute-start | bytes 1327112 | tf_op jit(solution)/shard_map/ppermute | solution.py:780
  73.8 19.0 %collective-permute-start.12 = (bf16[3,96,768]{2,1,0:T(8,128)(2,1)}, bf16[3,96,768]{2,1,0:T(8,128)(2,1)}, u32[]{:S(2)}, u32[]{:S(2)}) collective-permute-start(bf16[3,96,768]{2,1,0:T(8,128)(2,1)} %pad_maximum_fusion.4.refs_1_), channel_id=1, source_target_pairs={{0,24},{8,16},{16,8},{24,0},{1,25},{9,17},{17,9},{25,1},{2,26},{10... | collective-permute-start | bytes 1327112 | tf_op jit(solution)/shard_map/ppermute | solution.py:780
  73.8 16.0 %collective-permute-start.8 = (bf16[192,768]{1,0:T(8,128)(2,1)}, bf16[192,768]{1,0:T(8,128)(2,1)S(1)}, u32[]{:S(2)}, u32[]{:S(2)}) collective-permute-start(bf16[192,768]{1,0:T(8,128)(2,1)} %pad_maximum_fusion.5), channel_id=1, source_target_pairs={{0,4},{1,5},{2,6},{3,7},{4,0},{5,1},{6,2},{7,3},{8,12},{9,13},{10,... | collective-permute-start | bytes 884744 | tf_op jit(solution)/shard_map/ppermute | solution.py:785
  74.8 15.0 %collective-permute-start.9 = (bf16[192,768]{1,0:T(8,128)(2,1)}, bf16[192,768]{1,0:T(8,128)(2,1)S(1)}, u32[]{:S(2)}, u32[]{:S(2)}) collective-permute-start(bf16[192,768]{1,0:T(8,128)(2,1)} %pad_maximum_fusion.5), channel_id=1, source_target_pairs={{0,6},{1,7},{2,0},{3,1},{4,2},{5,3},{6,4},{7,5},{8,14},{9,15},{10,... | collective-permute-start | bytes 884744 | tf_op jit(solution)/shard_map/ppermute | solution.py:785
  89.8 16.7 %collective-permute-start.13 = (bf16[96,3072]{1,0:T(8,128)(2,1)S(1)}, bf16[96,3072]{1,0:T(8,128)(2,1)S(1)}, u32[]{:S(2)}, u32[]{:S(2)}) collective-permute-start(bf16[96,3072]{1,0:T(8,128)(2,1)S(1)} %constant_dynamic-update-slice_fusion.refs_0_), channel_id=1, source_target_pairs={{0,1},{1,0},{2,3},{3,2},{4,5},{5,4},{6,7},{7,6},{8,9},{9,8},{10,11... | collective-permute-start | bytes 1769480 | tf_op jit(solution)/shard_map/ppermute | solution.py:780
  92.8 292.8 %reduce-scatter.6.cloned.1.call-start = ((), (), s32[]{:S(2)}) async-start(), calls=%async_computation.4 | async-start | bytes 884736 | tf_op jit(solution)/shard_map/reduce_scatter | solution.py:885
  94.3 12.2 %collective-permute-start.14 = (bf16[3,96,768]{2,1,0:T(8,128)(2,1)}, bf16[3,96,768]{2,1,0:T(8,128)(2,1)}, u32[]{:S(2)}, u32[]{:S(2)}) collective-permute-start(bf16[3,96,768]{2,1,0:T(8,128)(2,1)} %pad_maximum_fusion.4.refs_1_), channel_id=1, source_target_pairs={{0,1},{1,0},{2,3},{3,2},{4,5},{5,4},{6,7},{7,6},{8,9},{9,8},{10,11... | collective-permute-start | bytes 1327112 | tf_op jit(solution)/shard_map/ppermute | solution.py:780
  94.3 12.2 %collective-permute-start.17 = (bf16[3,96,768]{2,1,0:T(8,128)(2,1)}, bf16[3,96,768]{2,1,0:T(8,128)(2,1)}, u32[]{:S(2)}, u32[]{:S(2)}) collective-permute-start(bf16[3,96,768]{2,1,0:T(8,128)(2,1)} %collective-permute-done.12.refs_4_), channel_id=1, source_target_pairs={{0,1},{1,0},{2,3},{3,2},{4,5},{5,4},{6,7},{7,6},{8,9},{9,8},{10,11... | collective-permute-start | bytes 1327112 | tf_op jit(solution)/shard_map/ppermute | solution.py:780
  94.8 11.7 %collective-permute-start.15 = (bf16[3,96,768]{2,1,0:T(8,128)(2,1)S(1)}, bf16[3,96,768]{2,1,0:T(8,128)(2,1)}, u32[]{:S(2)}, u32[]{:S(2)}) collective-permute-start(bf16[3,96,768]{2,1,0:T(8,128)(2,1)S(1)} %collective-permute-done.10.refs_2_), channel_id=1, source_target_pairs={{0,1},{1,0},{2,3},{3,2},{4,5},{5,4},{6,7},{7,6},{8,9},{9,8},{10,11... | collective-permute-start | bytes 1327112 | tf_op jit(solution)/shard_map/ppermute | solution.py:780
  94.8 11.7 %collective-permute-start.16 = (bf16[3,96,768]{2,1,0:T(8,128)(2,1)}, bf16[3,96,768]{2,1,0:T(8,128)(2,1)}, u32[]{:S(2)}, u32[]{:S(2)}) collective-permute-start(bf16[3,96,768]{2,1,0:T(8,128)(2,1)} %collective-permute-done.11.refs_3_), channel_id=1, source_target_pairs={{0,1},{1,0},{2,3},{3,2},{4,5},{5,4},{6,7},{7,6},{8,9},{9,8},{10,11... | collective-permute-start | bytes 1327112 | tf_op jit(solution)/shard_map/ppermute | solution.py:780
  112.7 33.5 %collective-permute-start.18 = (bf16[3,192,768]{2,1,0:T(8,128)(2,1)S(1)}, bf16[3,192,768]{2,1,0:T(8,128)(2,1)}, u32[]{:S(2)}, u32[]{:S(2)}) collective-permute-start(bf16[3,192,768]{2,1,0:T(8,128)(2,1)S(1)} %pad_maximum_fusion.3.refs_2_), channel_id=1, source_target_pairs={{0,8},{8,0},{16,24},{24,16},{1,9},{9,1},{17,25},{25,17},{2,10},{10... | collective-permute-start | bytes 2654216 | tf_op jit(solution)/shard_map/ppermute | solution.py:780
  116.0 41.7 %collective-permute-start.19 = (bf16[3,192,768]{2,1,0:T(8,128)(2,1)S(1)}, bf16[3,192,768]{2,1,0:T(8,128)(2,1)}, u32[]{:S(2)}, u32[]{:S(2)}) collective-permute-start(bf16[3,192,768]{2,1,0:T(8,128)(2,1)S(1)} %pad_maximum_fusion.3.refs_2_), channel_id=1, source_target_pairs={{0,16},{8,24},{16,0},{24,8},{1,17},{9,25},{17,1},{25,9},{2,18},{10... | collective-permute-start | bytes 2654216 | tf_op jit(solution)/shard_map/ppermute | solution.py:780
  119.1 38.6 %collective-permute-start.20 = (bf16[3,192,768]{2,1,0:T(8,128)(2,1)S(1)}, bf16[3,192,768]{2,1,0:T(8,128)(2,1)S(1)}, u32[]{:S(2)}, u32[]{:S(2)}) collective-permute-start(bf16[3,192,768]{2,1,0:T(8,128)(2,1)S(1)} %pad_maximum_fusion.3.refs_2_), channel_id=1, source_target_pairs={{0,24},{8,16},{16,8},{24,0},{1,25},{9,17},{17,9},{25,1},{2,26},{10... | collective-permute-start | bytes 2654216 | tf_op jit(solution)/shard_map/ppermute | solution.py:780
  157.7 11.8 %collective-permute-start.21 = (bf16[96,3072]{1,0:T(8,128)(2,1)S(1)}, bf16[96,3072]{1,0:T(8,128)(2,1)}, u32[]{:S(2)}, u32[]{:S(2)}) collective-permute-start(bf16[96,3072]{1,0:T(8,128)(2,1)S(1)} %copy-done.19), channel_id=1, source_target_pairs={{0,1},{1,0},{2,3},{3,2},{4,5},{5,4},{6,7},{7,6},{8,9},{9,8},{10,11... | collective-permute-start | bytes 1769480 | tf_op jit(solution)/shard_map/ppermute | solution.py:780
  159.3 13.6 %collective-permute-start.26 = (bf16[3,192,768]{2,1,0:T(8,128)(2,1)}, bf16[3,192,768]{2,1,0:T(8,128)(2,1)}, u32[]{:S(2)}, u32[]{:S(2)}) collective-permute-start(bf16[3,192,768]{2,1,0:T(8,128)(2,1)} %copy-done.25), channel_id=1, source_target_pairs={{0,1},{1,0},{2,3},{3,2},{4,5},{5,4},{6,7},{7,6},{8,9},{9,8},{10,11... | collective-permute-start | bytes 2654216 | tf_op jit(solution)/shard_map/ppermute | solution.py:780
  165.1 12.6 %collective-permute-start.23 = (bf16[3,192,768]{2,1,0:T(8,128)(2,1)S(1)}, bf16[3,192,768]{2,1,0:T(8,128)(2,1)}, u32[]{:S(2)}, u32[]{:S(2)}) collective-permute-start(bf16[3,192,768]{2,1,0:T(8,128)(2,1)S(1)} %pad_maximum_fusion.3.refs_2_), channel_id=1, source_target_pairs={{0,1},{1,0},{2,3},{3,2},{4,5},{5,4},{6,7},{7,6},{8,9},{9,8},{10,11... | collective-permute-start | bytes 2654216 | tf_op jit(solution)/shard_map/ppermute | solution.py:780
  165.6 12.1 %collective-permute-start.24 = (bf16[3,192,768]{2,1,0:T(8,128)(2,1)}, bf16[3,192,768]{2,1,0:T(8,128)(2,1)}, u32[]{:S(2)}, u32[]{:S(2)}) collective-permute-start(bf16[3,192,768]{2,1,0:T(8,128)(2,1)} %collective-permute-done.18.refs_3_), channel_id=1, source_target_pairs={{0,1},{1,0},{2,3},{3,2},{4,5},{5,4},{6,7},{7,6},{8,9},{9,8},{10,11... | collective-permute-start | bytes 2654216 | tf_op jit(solution)/shard_map/ppermute | solution.py:780
  165.7 12.0 %collective-permute-start.25 = (bf16[3,192,768]{2,1,0:T(8,128)(2,1)}, bf16[3,192,768]{2,1,0:T(8,128)(2,1)}, u32[]{:S(2)}, u32[]{:S(2)}) collective-permute-start(bf16[3,192,768]{2,1,0:T(8,128)(2,1)} %collective-permute-done.19.refs_4_), channel_id=1, source_target_pairs={{0,1},{1,0},{2,3},{3,2},{4,5},{5,4},{6,7},{7,6},{8,9},{9,8},{10,11... | collective-permute-start | bytes 2654216 | tf_op jit(solution)/shard_map/ppermute | solution.py:780
  171.6 14.7 %collective-permute-start.27 = (bf16[96,512]{1,0:T(8,128)(2,1)S(1)}, bf16[96,512]{1,0:T(8,128)(2,1)S(1)}, u32[]{:S(2)}, u32[]{:S(2)}) collective-permute-start(bf16[96,512]{1,0:T(8,128)(2,1)S(1)} %get-tuple-element.154), channel_id=1, source_target_pairs={{1,0},{2,1},{3,2},{4,3},{5,4},{6,5},{7,6},{9,8},{10,9},{11,10},{12... | collective-permute-start | bytes 294920 | tf_op jit(solution)/shard_map/ppermute | solution.py:671
  172.9 13.4 %collective-permute-start.28 = (bf16[96,512]{1,0:T(8,128)(2,1)S(1)}, bf16[96,512]{1,0:T(8,128)(2,1)S(1)}, u32[]{:S(2)}, u32[]{:S(2)}) collective-permute-start(bf16[96,512]{1,0:T(8,128)(2,1)S(1)} %get-tuple-element.155), channel_id=1, source_target_pairs={{0,1},{1,2},{2,3},{3,4},{4,5},{5,6},{6,7},{8,9},{9,10},{10,11},{11... | collective-permute-start | bytes 294920 | tf_op jit(solution)/shard_map/ppermute | solution.py:671
  209.3 7.2 %collective-permute-start.32 = (bf16[144,512]{1,0:T(8,128)(2,1)S(1)}, bf16[144,512]{1,0:T(8,128)(2,1)S(1)}, u32[]{:S(2)}, u32[]{:S(2)}) collective-permute-start(bf16[144,512]{1,0:T(8,128)(2,1)S(1)} %get-tuple-element.163), channel_id=1, source_target_pairs={{0,8},{8,16},{16,24},{1,9},{9,17},{17,25},{2,10},{10,18},{18,26},{... | collective-permute-start | bytes 442376 | tf_op jit(solution)/shard_map/ppermute | solution.py:671
  251.1 32.0 %collective-permute-start.35 = (bf16[4,4,96,768]{3,2,1,0:T(8,128)(2,1)}, bf16[4,4,96,768]{3,2,1,0:T(8,128)(2,1)}, u32[]{:S(2)}, u32[]{:S(2)}) collective-permute-start(bf16[4,4,96,768]{3,2,1,0:T(8,128)(2,1)} %get-tuple-element.180), channel_id=1, source_target_pairs={{0,1},{1,0},{2,3},{3,2},{4,5},{5,4},{6,7},{7,6},{8,9},{9,8},{10,11... | collective-permute-start | bytes 7077896 | tf_op jit(solution)/shard_map/ppermute | solution.py:780
  254.7 28.5 %collective-permute-start.34 = (bf16[4,4,96,768]{3,2,1,0:T(8,128)(2,1)}, bf16[4,4,96,768]{3,2,1,0:T(8,128)(2,1)S(1)}, u32[]{:S(2)}, u32[]{:S(2)}) collective-permute-start(bf16[4,4,96,768]{3,2,1,0:T(8,128)(2,1)} %get-tuple-element.177), channel_id=1, source_target_pairs={{0,1},{1,0},{2,3},{3,2},{4,5},{5,4},{6,7},{7,6},{8,9},{9,8},{10,11... | collective-permute-start | bytes 7077896 | tf_op jit(solution)/shard_map/ppermute | solution.py:780
  254.8 19.1 %collective-permute-start.29 = (bf16[144,512]{1,0:T(8,128)(2,1)}, bf16[144,512]{1,0:T(8,128)(2,1)}, u32[]{:S(2)}, u32[]{:S(2)}) collective-permute-start(bf16[144,512]{1,0:T(8,128)(2,1)} %get-tuple-element.293), channel_id=1, source_target_pairs={{8,0},{16,8},{24,16},{9,1},{17,9},{25,17},{10,2},{18,10},{26,18},{... | collective-permute-start | bytes 442376 | tf_op jit(solution)/shard_map/ppermute | solution.py:671
  256.1 17.8 %collective-permute-start.30 = (bf16[144,512]{1,0:T(8,128)(2,1)}, bf16[144,512]{1,0:T(8,128)(2,1)}, u32[]{:S(2)}, u32[]{:S(2)}) collective-permute-start(bf16[144,512]{1,0:T(8,128)(2,1)} %get-tuple-element.292), channel_id=1, source_target_pairs={{0,8},{8,16},{16,24},{1,9},{9,17},{17,25},{2,10},{10,18},{18,26},{... | collective-permute-start | bytes 442376 | tf_op jit(solution)/shard_map/ppermute | solution.py:671
  278.1 49.6 %collective-permute-start.33 = (bf16[96,512]{1,0:T(8,128)(2,1)}, bf16[96,512]{1,0:T(8,128)(2,1)}, u32[]{:S(2)}, u32[]{:S(2)}) collective-permute-start(bf16[96,512]{1,0:T(8,128)(2,1)} %get-tuple-element.174), channel_id=1, source_target_pairs={{1,0},{2,1},{3,2},{4,3},{5,4},{6,5},{7,6},{9,8},{10,9},{11,10},{12... | collective-permute-start | bytes 294920 | tf_op jit(solution)/shard_map/ppermute | solution.py:671
  279.4 48.3 %collective-permute-start.36 = (bf16[96,512]{1,0:T(8,128)(2,1)}, bf16[96,512]{1,0:T(8,128)(2,1)}, u32[]{:S(2)}, u32[]{:S(2)}) collective-permute-start(bf16[96,512]{1,0:T(8,128)(2,1)} %get-tuple-element.185), channel_id=1, source_target_pairs={{0,1},{1,2},{2,3},{3,4},{4,5},{5,6},{6,7},{8,9},{9,10},{10,11},{11... | collective-permute-start | bytes 294920 | tf_op jit(solution)/shard_map/ppermute | solution.py:671
  283.1 102.5 %reduce-scatter.8.cloned.1.call-start = ((), (), s32[]{:S(2)}) async-start(), calls=%async_computation.5 | async-start | bytes 1769472 | tf_op jit(solution)/shard_map/reduce_scatter | solution.py:885
  290.5 42.8 %collective-permute-start.38 = (bf16[2,4,96,768]{3,2,1,0:T(8,128)(2,1)}, bf16[2,4,96,768]{3,2,1,0:T(8,128)(2,1)}, u32[]{:S(2)}, u32[]{:S(2)}) collective-permute-start(bf16[2,4,96,768]{3,2,1,0:T(8,128)(2,1)} %get-tuple-element.190), channel_id=1, source_target_pairs={{0,16},{8,24},{16,0},{24,8},{1,17},{9,25},{17,1},{25,9},{2,18},{10... | collective-permute-start | bytes 3538952 | tf_op jit(solution)/shard_map/ppermute | solution.py:780
  294.1 41.2 %collective-permute-start.37 = (bf16[2,4,96,768]{3,2,1,0:T(8,128)(2,1)}, bf16[2,4,96,768]{3,2,1,0:T(8,128)(2,1)}, u32[]{:S(2)}, u32[]{:S(2)}) collective-permute-start(bf16[2,4,96,768]{3,2,1,0:T(8,128)(2,1)} %get-tuple-element.188), channel_id=1, source_target_pairs={{0,8},{8,0},{16,24},{24,16},{1,9},{9,1},{17,25},{25,17},{2,10},{10... | collective-permute-start | bytes 3538952 | tf_op jit(solution)/shard_map/ppermute | solution.py:780
  333.0 90.1 %reduce-scatter.4.cloned.1.call-start = ((), (), s32[]{:S(2)}) async-start(), calls=%async_computation.3 | async-start | bytes 1474560 | tf_op jit(solution)/shard_map/reduce_scatter | solution.py:842
  348.2 21.7 %collective-permute-start.39 = (bf16[4,4,96,768]{3,2,1,0:T(8,128)(2,1)}, bf16[4,4,96,768]{3,2,1,0:T(8,128)(2,1)}, u32[]{:S(2)}, u32[]{:S(2)}) collective-permute-start(bf16[4,4,96,768]{3,2,1,0:T(8,128)(2,1)} %get-tuple-element.195), channel_id=1, source_target_pairs={{0,1},{1,0},{2,3},{3,2},{4,5},{5,4},{6,7},{7,6},{8,9},{9,8},{10,11... | collective-permute-start | bytes 7077896 | tf_op jit(solution)/shard_map/ppermute | solution.py:780
  350.5 15.4 %collective-permute-start.40 = (bf16[4,96,768]{2,1,0:T(8,128)(2,1)}, bf16[4,96,768]{2,1,0:T(8,128)(2,1)S(1)}, u32[]{:S(2)}, u32[]{:S(2)}) collective-permute-start(bf16[4,96,768]{2,1,0:T(8,128)(2,1)} %fusion.38), channel_id=1, source_target_pairs={{0,16},{8,24},{16,0},{24,8},{1,17},{9,25},{17,1},{25,9},{2,18},{10... | collective-permute-start | bytes 1769480 | tf_op jit(solution)/shard_map/ppermute | solution.py:780
  351.1 15.2 %collective-permute-start.41 = (bf16[4,96,768]{2,1,0:T(8,128)(2,1)}, bf16[4,96,768]{2,1,0:T(8,128)(2,1)S(1)}, u32[]{:S(2)}, u32[]{:S(2)}) collective-permute-start(bf16[4,96,768]{2,1,0:T(8,128)(2,1)} %fusion.39), channel_id=1, source_target_pairs={{0,8},{8,0},{16,24},{24,16},{1,9},{9,1},{17,25},{25,17},{2,10},{10... | collective-permute-start | bytes 1769480 | tf_op jit(solution)/shard_map/ppermute | solution.py:780
  373.8 16.6 %collective-permute-start.42 = (bf16[4,96,768]{2,1,0:T(8,128)(2,1)}, bf16[4,96,768]{2,1,0:T(8,128)(2,1)}, u32[]{:S(2)}, u32[]{:S(2)}) collective-permute-start(bf16[4,96,768]{2,1,0:T(8,128)(2,1)} %get-tuple-element.204), channel_id=1, source_target_pairs={{0,8},{8,0},{16,24},{24,16},{1,9},{9,1},{17,25},{25,17},{2,10},{10... | collective-permute-start | bytes 1769480 | tf_op jit(solution)/shard_map/ppermute | solution.py:780
  375.3 25.5 %collective-permute-start.43 = (bf16[4,96,768]{2,1,0:T(8,128)(2,1)}, bf16[4,96,768]{2,1,0:T(8,128)(2,1)}, u32[]{:S(2)}, u32[]{:S(2)}) collective-permute-start(bf16[4,96,768]{2,1,0:T(8,128)(2,1)} %get-tuple-element.214), channel_id=1, source_target_pairs={{0,16},{8,24},{16,0},{24,8},{1,17},{9,25},{17,1},{25,9},{2,18},{10... | collective-permute-start | bytes 1769480 | tf_op jit(solution)/shard_map/ppermute | solution.py:780
  377.0 27.0 %collective-permute-start.44 = (bf16[4,96,768]{2,1,0:T(8,128)(2,1)S(1)}, bf16[4,96,768]{2,1,0:T(8,128)(2,1)}, u32[]{:S(2)}, u32[]{:S(2)}) collective-permute-start(bf16[4,96,768]{2,1,0:T(8,128)(2,1)S(1)} %get-tuple-element.216), channel_id=1, source_target_pairs={{0,24},{8,16},{16,8},{24,0},{1,25},{9,17},{17,9},{25,1},{2,26},{10... | collective-permute-start | bytes 1769480 | tf_op jit(solution)/shard_map/ppermute | solution.py:780
  384.8 28.3 %collective-permute-start.45 = (bf16[4,4,64,768]{3,2,1,0:T(8,128)(2,1)}, bf16[4,4,64,768]{3,2,1,0:T(8,128)(2,1)}, u32[]{:S(2)}, u32[]{:S(2)}) collective-permute-start(bf16[4,4,64,768]{3,2,1,0:T(8,128)(2,1)} %get-tuple-element.218), channel_id=1, source_target_pairs={{0,1},{1,0},{2,3},{3,2},{4,5},{5,4},{6,7},{7,6},{8,9},{9,8},{10,11... | collective-permute-start | bytes 4718600 | tf_op jit(solution)/shard_map/ppermute | solution.py:780
  386.7 21.0 %collective-permute-start.46 = (bf16[144,768]{1,0:T(8,128)(2,1)}, bf16[144,768]{1,0:T(8,128)(2,1)S(1)}, u32[]{:S(2)}, u32[]{:S(2)}) collective-permute-start(bf16[144,768]{1,0:T(8,128)(2,1)} %get-tuple-element.220), channel_id=1, source_target_pairs={{8,0},{16,8},{24,16},{9,1},{17,9},{25,17},{10,2},{18,10},{26,18},{... | collective-permute-start | bytes 663560 | tf_op jit(solution)/shard_map/ppermute | solution.py:671
  390.4 17.3 %collective-permute-start.47 = (bf16[144,768]{1,0:T(8,128)(2,1)S(1)}, bf16[144,768]{1,0:T(8,128)(2,1)S(1)}, u32[]{:S(2)}, u32[]{:S(2)}) collective-permute-start(bf16[144,768]{1,0:T(8,128)(2,1)S(1)} %copy-done.46), channel_id=1, source_target_pairs={{0,8},{8,16},{16,24},{1,9},{9,17},{17,25},{2,10},{10,18},{18,26},{... | collective-permute-start | bytes 663560 | tf_op jit(solution)/shard_map/ppermute | solution.py:671
  408.5 7.4 %collective-permute-start.48 = (bf16[96,768]{1,0:T(8,128)(2,1)S(1)}, bf16[96,768]{1,0:T(8,128)(2,1)S(1)}, u32[]{:S(2)}, u32[]{:S(2)}) collective-permute-start(bf16[96,768]{1,0:T(8,128)(2,1)S(1)} %get-tuple-element.291), channel_id=1, source_target_pairs={{1,0},{2,1},{3,2},{4,3},{5,4},{6,5},{7,6},{9,8},{10,9},{11,10},{12... | collective-permute-start | bytes 442376 | tf_op jit(solution)/shard_map/ppermute | solution.py:671
  415.9 13.0 %collective-permute-start.50 = (bf16[4,64,768]{2,1,0:T(8,128)(2,1)}, bf16[4,64,768]{2,1,0:T(8,128)(2,1)S(1)}, u32[]{:S(2)}, u32[]{:S(2)}) collective-permute-start(bf16[4,64,768]{2,1,0:T(8,128)(2,1)} %get-tuple-element.224), channel_id=1, source_target_pairs={{0,8},{8,0},{16,24},{24,16},{1,9},{9,1},{17,25},{25,17},{2,10},{10... | collective-permute-start | bytes 1179656 | tf_op jit(solution)/shard_map/ppermute | solution.py:780
  418.5 21.4 %collective-permute-start.51 = (bf16[4,64,768]{2,1,0:T(8,128)(2,1)}, bf16[4,64,768]{2,1,0:T(8,128)(2,1)}, u32[]{:S(2)}, u32[]{:S(2)}) collective-permute-start(bf16[4,64,768]{2,1,0:T(8,128)(2,1)} %get-tuple-element.230), channel_id=1, source_target_pairs={{0,16},{8,24},{16,0},{24,8},{1,17},{9,25},{17,1},{25,9},{2,18},{10... | collective-permute-start | bytes 1179656 | tf_op jit(solution)/shard_map/ppermute | solution.py:780
  421.7 18.4 %collective-permute-start.52 = (bf16[4,64,768]{2,1,0:T(8,128)(2,1)}, bf16[4,64,768]{2,1,0:T(8,128)(2,1)}, u32[]{:S(2)}, u32[]{:S(2)}) collective-permute-start(bf16[4,64,768]{2,1,0:T(8,128)(2,1)} %get-tuple-element.232), channel_id=1, source_target_pairs={{0,24},{8,16},{16,8},{24,0},{1,25},{9,17},{17,9},{25,1},{2,26},{10... | collective-permute-start | bytes 1179656 | tf_op jit(solution)/shard_map/ppermute | solution.py:780
  442.6 10.9 %collective-permute-start.53 = (bf16[160,768]{1,0:T(8,128)(2,1)}, bf16[160,768]{1,0:T(8,128)(2,1)S(1)}, u32[]{:S(2)}, u32[]{:S(2)}) collective-permute-start(bf16[160,768]{1,0:T(8,128)(2,1)} %get-tuple-element.286), channel_id=1, source_target_pairs={{0,2},{1,3},{2,4},{3,5},{4,6},{5,7},{6,0},{7,1},{8,10},{9,11},{10,... | collective-permute-start | bytes 737288 | tf_op jit(solution)/shard_map/ppermute | solution.py:785
  444.5 23.8 %collective-permute-start.59 = (bf16[384,768]{1,0:T(8,128)(2,1)S(1)}, bf16[384,768]{1,0:T(8,128)(2,1)}, u32[]{:S(2)}, u32[]{:S(2)}) collective-permute-start(bf16[384,768]{1,0:T(8,128)(2,1)S(1)} %constant_dynamic-update-slice_fusion.7), channel_id=1, source_target_pairs={{0,8},{8,0},{16,24},{24,16},{1,9},{9,1},{17,25},{25,17},{2,10},{10... | collective-permute-start | bytes 1769480 | tf_op jit(solution)/shard_map/ppermute | solution.py:780
  445.9 23.5 %collective-permute-start.60 = (bf16[384,768]{1,0:T(8,128)(2,1)S(1)}, bf16[384,768]{1,0:T(8,128)(2,1)}, u32[]{:S(2)}, u32[]{:S(2)}) collective-permute-start(bf16[384,768]{1,0:T(8,128)(2,1)S(1)} %constant_dynamic-update-slice_fusion.7), channel_id=1, source_target_pairs={{0,16},{8,24},{16,0},{24,8},{1,17},{9,25},{17,1},{25,9},{2,18},{10... | collective-permute-start | bytes 1769480 | tf_op jit(solution)/shard_map/ppermute | solution.py:780
  446.9 27.8 %collective-permute-start.61 = (bf16[384,768]{1,0:T(8,128)(2,1)S(1)}, bf16[384,768]{1,0:T(8,128)(2,1)}, u32[]{:S(2)}, u32[]{:S(2)}) collective-permute-start(bf16[384,768]{1,0:T(8,128)(2,1)S(1)} %constant_dynamic-update-slice_fusion.7), channel_id=1, source_target_pairs={{0,24},{8,16},{16,8},{24,0},{1,25},{9,17},{17,9},{25,1},{2,26},{10... | collective-permute-start | bytes 1769480 | tf_op jit(solution)/shard_map/ppermute | solution.py:780
  448.1 15.3 %collective-permute-start.54 = (bf16[160,768]{1,0:T(8,128)(2,1)}, bf16[160,768]{1,0:T(8,128)(2,1)S(1)}, u32[]{:S(2)}, u32[]{:S(2)}) collective-permute-start(bf16[160,768]{1,0:T(8,128)(2,1)} %get-tuple-element.288), channel_id=1, source_target_pairs={{0,4},{1,5},{2,6},{3,7},{4,0},{5,1},{6,2},{7,3},{8,12},{9,13},{10,... | collective-permute-start | bytes 737288 | tf_op jit(solution)/shard_map/ppermute | solution.py:785
  453.5 12.0 %collective-permute-start.55 = (bf16[160,768]{1,0:T(8,128)(2,1)}, bf16[160,768]{1,0:T(8,128)(2,1)S(1)}, u32[]{:S(2)}, u32[]{:S(2)}) collective-permute-start(bf16[160,768]{1,0:T(8,128)(2,1)} %get-tuple-element.289), channel_id=1, source_target_pairs={{0,6},{1,7},{2,0},{3,1},{4,2},{5,3},{6,4},{7,5},{8,14},{9,15},{10,... | collective-permute-start | bytes 737288 | tf_op jit(solution)/shard_map/ppermute | solution.py:785
  465.7 17.4 %collective-permute-start.56 = (bf16[160,768]{1,0:T(8,128)(2,1)S(1)}, bf16[160,768]{1,0:T(8,128)(2,1)S(1)}, u32[]{:S(2)}, u32[]{:S(2)}) collective-permute-start(bf16[160,768]{1,0:T(8,128)(2,1)S(1)} %add_convert_fusion.11), channel_id=1, source_target_pairs={{0,8},{8,0},{16,24},{24,16},{1,9},{9,1},{17,25},{25,17},{2,10},{10... | collective-permute-start | bytes 737288 | tf_op jit(solution)/shard_map/ppermute | solution.py:780
  467.2 15.9 %collective-permute-start.57 = (bf16[160,768]{1,0:T(8,128)(2,1)S(1)}, bf16[160,768]{1,0:T(8,128)(2,1)S(1)}, u32[]{:S(2)}, u32[]{:S(2)}) collective-permute-start(bf16[160,768]{1,0:T(8,128)(2,1)S(1)} %add_convert_fusion.11), channel_id=1, source_target_pairs={{0,16},{8,24},{16,0},{24,8},{1,17},{9,25},{17,1},{25,9},{2,18},{10... | collective-permute-start | bytes 737288 | tf_op jit(solution)/shard_map/ppermute | solution.py:780
  468.3 14.7 %collective-permute-start.58 = (bf16[160,768]{1,0:T(8,128)(2,1)S(1)}, bf16[160,768]{1,0:T(8,128)(2,1)S(1)}, u32[]{:S(2)}, u32[]{:S(2)}) collective-permute-start(bf16[160,768]{1,0:T(8,128)(2,1)S(1)} %add_convert_fusion.11), channel_id=1, source_target_pairs={{0,24},{8,16},{16,8},{24,0},{1,25},{9,17},{17,9},{25,1},{2,26},{10... | collective-permute-start | bytes 737288 | tf_op jit(solution)/shard_map/ppermute | solution.py:780
  (69 other events, 768.4 us)
Sparse Core Ops, SparseCore 0:
  28.2 33.9 all-gather.4
  92.9 37.3 all-gather.6
  283.2 33.9 reduce-scatter.5
  333.1 34.4 reduce-scatter.7
  377.4 28.6 reduce-scatter.3

commit v4 on v3

--- a/solution.py
+++ b/solution.py
@@ -323,16 +323,8 @@
     width = value.shape[1]
     value = value.astype(bf16).reshape(chips, 2, value.shape[0] // chips // 2, width)
     even, odd = value[:, 0], value[:, 1]
-
-    @pl.when(core == 0)
-    def _():
-        keep_ref[...] = even
-        send_ref[...] = odd
-
-    @pl.when(core == 1)
-    def _():
-        keep_ref[...] = odd
-        send_ref[...] = even
+    keep_ref[...] = jnp.where(core == 0, even, odd)
+    send_ref[...] = jnp.where(core == 0, odd, even)
 
 
 def mlp_bwd_kernel(pos_ref, dm_ref, c_ref, u_ref, g_ref, fc1_ref, fc2_ref, dc_ref, gb_ref, k1_ref, s1_ref, k2_ref, s2_ref, *, chips):
@@ -359,15 +351,8 @@
 
 
 def split_two(pair, core, keep_ref, send_ref):
-    @pl.when(core == 0)
-    def _():
-        keep_ref[:, 0] = pair[0]
-        send_ref[:, 0] = pair[1]
-
-    @pl.when(core == 1)
-    def _():
-        keep_ref[:, 0] = pair[1]
-        send_ref[:, 0] = pair[0]
+    keep_ref[:, 0] = jnp.where(core == 0, pair[0], pair[1])
+    send_ref[:, 0] = jnp.where(core == 0, pair[1], pair[0])
 
 
 def mlp_bwd(pos, dm, c, u, g, gathered, chips):
@@ -451,15 +436,8 @@
         for part in range(parts):
             ref[part, 0, depth:, :] = block
 
-    @pl.when(core == 0)
-    def _():
-        put(keep_ref, grad[0])
-        put(send_ref, grad[1])
-
-    @pl.when(core == 1)
-    def _():
-        put(keep_ref, grad[1])
-        put(send_ref, grad[0])
+    put(keep_ref, jnp.where(core == 0, grad[0], grad[1]))
+    put(send_ref, jnp.where(core == 0, grad[1], grad[0]))
 
 
 def patch_grad(pos, ext, demb, bias, vectors, parts, chips):
@@ -575,7 +553,7 @@
 
 def norm2_back(dc, h1, dh2, gain, proj_w):
     tokens, width = dc.shape
-    tb = token_block(tokens)
+    tb = tokens // 2 if tokens % 32 == 0 else token_block(tokens)
     blk = rows(tb, width)
     vec = whole((1, width))
     return pl.pallas_call(
@@ -933,9 +911,6 @@
         front_a = parts_of(jnp.concatenate([gather(qkv_w), gather(proj_w)], axis=1))
         quarters_of = lambda m: m.reshape(8, 4, -1, model_width)
         full_mlp = jnp.concatenate([parts_of(gather(fc1_w)), quarters_of(gather(fc2_w))], axis=2)
-    tops = gather_apart(share_d)
-    full_dec = tops[:, :dec_rows].reshape(-1, dec_width)
-    full_head = tops[:, dec_rows:].reshape(-1, slabs, head_rows, dec_width).transpose(0, 2, 1, 3).reshape(-1, pixel_width)
     small = front_p[:, patch_w.shape[0] :]
     own_dates = scene_dates[own_scene]
     stamps = timestamps[own_scene]
@@ -959,6 +934,10 @@
     ratio = valid / denom
     gr = (cotangent.reshape(own, pixel_width).astype(f32) * ratio).astype(bf16)
     ext, h0, a = embed(strips, front_p, hot, table, vec)
+    share_d = after(share_d, a)
+    tops = gather_apart(share_d)
+    full_dec = tops[:, :dec_rows].reshape(-1, dec_width)
+    full_head = tops[:, dec_rows:].reshape(-1, slabs, head_rows, dec_width).transpose(0, 2, 1, 3).reshape(-1, pixel_width)
     if split:
         front_a = place(pos, pieces_a, (*others_a[:-1], after(others_a[-1], a)), ("wide",))
         a, got_b = tied(a, got_b)

time: 502 us -> 494 us (0.984)
  Pallas kernels: 179 us -> 172 us
    ppermute x9, waiting for transfers between devices: 25.7 us -> 19.4 us  [turn(): lax.ppermute(value, 'gx', [(i, (i + 2 * step) % count) for i in range(cou...]
    pallas_call x1, Pallas kernels: 31.8 us -> 26.2 us  [mlp_bwd(): pl.pallas_call(functools.partial(mlp_bwd_kernel, chips=chips), grid_spec=...]
  transfers between devices with their start and end apart: 67 -> 67, of which waited for: 22 -> 23; matrix products, arithmetic and copies ran while one was open for 18% -> 19% of each run, Pallas kernels for 26% -> 26%
where the time goes in v4:
time: 494 us; the launch traced here: 486 us
  Pallas kernels  172 us (35%)
  starting transfers between devices  98.9 us (20%)
  waiting for transfers between devices  81.6 us (17%)
  other arithmetic  50.7 us (10%)
  local copies, waits for them, and re-layouts  37.8 us (8%)
  matrix products  28.2 us (6%)
  between operations  17.5 us (4%)
    ppermute x37, waiting for transfers between devices, swap(): lax.ppermute(value, axis, [(i, i ^ bit) for i in range(lax.axis_size(axis...  45.6 us
    ppermute x37, starting transfers between devices, swap(): lax.ppermute(value, axis, [(i, i ^ bit) for i in range(lax.axis_size(axis...  43.7 us
    pallas_call x1, Pallas kernels, attn_bwd(): pl.pallas_call(functools.partial(attn_bwd_kernel, block=token_block(token...  33.6 us
    ppermute x8, starting transfers between devices, to_neighbours(): lax.ppermute(high, axis, chain(axis, 1))  31.4 us
    pallas_call x1, Pallas kernels, mlp_bwd(): pl.pallas_call(functools.partial(mlp_bwd_kernel, chips=chips), grid_spec=...  26.2 us
    convert_element_type x11, other arithmetic, added(): return sum((v.astype(f32) for v in values)).astype(bf16)  21.9 us
    ppermute x9, waiting for transfers between devices, turn(): lax.ppermute(value, 'gx', [(i, (i + 2 * step) % count) for i in range(cou...  19.4 us
    pallas_call x1, Pallas kernels, attn_fwd(): pl.pallas_call(functools.partial(attn_fwd_kernel, block=token_block(token...  18.4 us
  transfers between devices with their start and end apart: 67, of which 23 were waited for; matrix products, arithmetic and copies ran while one was open for 19% of the time, Pallas kernels for 26%

profile of v4, /device:TPU:0, one launch (start us, length us, event | category | flops | bytes accessed | tf_op | source)
XLA Modules:
  0.0 486.3 jit_solution(18092651531655450130)
XLA Ops:
  10.1 3.0 collective-permute-start.2
  13.1 2.6 collective-permute-start.3
  23.0 2.0 collective-permute-start.1
  33.7 1.9 pad_maximum_fusion.4.refs_1_
  42.8 5.5 %collective-permute-start.5 = (bf16[160,1536]{1,0:T(8,128)(2,1)}, bf16[160,1536]{1,0:T(8,128)(2,1)}, u32[]{:S(2)}, u32[]{:S(2)}) collective-permute-start(bf16[160,1536]{1,0:T(8,128)(2,1)} %fusion.40), channel_id=1, source_target_pairs={{0,8},{8,16},{16,24},{1,9},{9,17},{17,25},{2,10},{10,18},{18,26},{... | collective-permute-start | bytes 1474568 | tf_op jit(solution)/shard_map/ppermute | solution.py:649
  50.0 6.3 %collective-permute-done.6.lower_ref = bf16[160,1536]{1,0:T(8,128)(2,1)} collective-permute-done((bf16[160,1536]{1,0:T(8,128)(2,1)S(1)}, bf16[160,1536]{1,0:T(8,128)(2,1)}, u32[]{:S(2)}, u32[]{:S(2)}) %collective-permute-start.6) | collective-permute-done | bytes 491552 | tf_op jit(solution)/shard_map/ppermute | solution.py:649
  56.3 3.0 collective-permute-done.5.upper_ref
  59.3 2.9 all-gather.5.cloned.1.call-done
  64.6 4.4 collective-permute-start.10
  69.0 3.4 collective-permute-start.11
  74.2 1.8 collective-permute-start.9
  76.7 7.7 %embed.1 = (bf16[864,1536]{1,0:T(8,128)(2,1)}, f32[864,768]{1,0:T(8,128)}, bf16[864,768]{1,0:T(8,128)(2,1)}) custom-call(bf16[384,1536]{1,0:T(8,128)(2,1)} %bitcast.229, bf16[112,1536]{1,0:T(8,128)(2,1)} %collective-permute-done.1.left_ref, bf16[112,1536]{1,0:T(8,128)(2,1)} %collective-permute-done.right_ref, ...), custom_call_target="tpu_custom_call" | custom-call | flops 2038431744 | bytes 11649024 | tf_op jit(solution)/shard_map/embed/pallas_call | solution.py:97
  84.3 3.9 collective-permute-done.8
  105.5 5.4 %place.2.w_ref = bf16[8,4,96,768]{3,2,1,0:T(8,128)(2,1)} custom-call(s32[3]{0:T(128)} %pad_add_fusion.pos_ref, bf16[96,3072]{1,0:T(8,128)(2,1)} %copy-done.3, bf16[3,96,768]{2,1,0:T(8,128)(2,1)} %pad_maximum_fusion.4.refs_1_, bf16[3,96,768]{2,1,0:T(8,128)(2,1)} %collective-permute-done.10.refs_2_, bf16[3,96,768]{2,1,0:T(8,128)(2,1)} %collective-permute-done.11.refs_3_, ...), custom_call_target="tpu_custom_call" | custom-call | bytes 9437184 | tf_op jit(solution)/shard_map/place/pallas_call | solution.py:508
  110.9 2.9 collective-permute-start.18
  113.8 2.8 collective-permute-start.19
  116.6 8.6 %project.1.q_ref.k_ref.v_ref = bf16[864,2304]{1,0:T(8,128)(2,1)} custom-call(bf16[864,768]{1,0:T(8,128)(2,1)} %get-tuple-element.138.a_ref, bf16[8,4,96,768]{3,2,1,0:T(8,128)(2,1)} %place.2.w_ref), custom_call_target="tpu_custom_call" | custom-call | flops 3057647616 | bytes 8847360 | tf_op jit(solution)/shard_map/project/pallas_call | solution.py:118
  125.2 18.4 %attn_fwd.1 = (bf16[864,768]{1,0:T(8,128)(2,1)}, bf16[12,864,128]{2,1,0:T(8,128)(2,1)}) custom-call(bf16[864,2304]{1,0:T(8,128)(2,1)} %project.1.q_ref.k_ref.v_ref, bf16[864,2304]{1,0:T(8,128)(2,1)} %project.1.q_ref.k_ref.v_ref, bf16[864,2304]{1,0:T(8,128)(2,1)} %project.1.q_ref.k_ref.v_ref, bf16[864,128]{1,0:T(8,128)(2,1)} %select_convert_fusion.kx_ref), custom_call_target="tpu_custom_call" | custom-call | flops 18345885696 | bytes 5308416 | tf_op jit(solution)/shard_map/attn_fwd/pallas_call | solution.py:177
  143.6 10.7 %collective-permute-done.19.refs_4_ = bf16[3,192,768]{2,1,0:T(8,128)(2,1)} collective-permute-done((bf16[3,192,768]{2,1,0:T(8,128)(2,1)S(1)}, bf16[3,192,768]{2,1,0:T(8,128)(2,1)}, u32[]{:S(2)}, u32[]{:S(2)}) %collective-permute-start.19) | collective-permute-done | bytes 884768 | tf_op jit(solution)/shard_map/ppermute | solution.py:758
  156.7 5.8 %proj_norm.1 = (f32[864,768]{1,0:T(8,128)}, bf16[864,768]{1,0:T(8,128)(2,1)}) custom-call(bf16[864,768]{1,0:T(8,128)(2,1)} %get-tuple-element.142.o_ref, bf16[8,4,96,768]{3,2,1,0:T(8,128)(2,1)} %place.2.w_ref, f32[864,768]{1,0:T(8,128)} %get-tuple-element.143.h0_ref, f32[4,768]{1,0:T(4,128)} %reshape.344.vec_ref.gain_ref), custom_call_target="tpu_custom_call" | custom-call | flops 1019215872 | bytes 9142272 | tf_op jit(solution)/shard_map/proj_norm/pallas_call | solution.py:260
  170.3 3.3 collective-permute-start.28
  175.2 8.8 %place.3.fc1_ref.fc2_ref = bf16[8,4,192,768]{3,2,1,0:T(8,128)(2,1)} custom-call(s32[3]{0:T(128)} %pad_add_fusion.pos_ref, bf16[96,3072]{1,0:T(8,128)(2,1)} %refs_0_, bf16[384,768]{1,0:T(8,128)(2,1)} %refs_1_, bf16[3,192,768]{2,1,0:T(8,128)(2,1)} %copy-done.1, bf16[3,192,768]{2,1,0:T(8,128)(2,1)} %collective-permute-done.18.refs_3_, ...), custom_call_target="tpu_custom_call" | custom-call | bytes 18874368 | tf_op jit(solution)/shard_map/place/pallas_call | solution.py:508
  185.1 17.5 %mlp_fwd.1 = (bf16[864,3072]{1,0:T(8,128)(2,1)}, bf16[864,3072]{1,0:T(8,128)(2,1)}, bf16[864,768]{1,0:T(8,128)(2,1)}) custom-call(bf16[864,768]{1,0:T(8,128)(2,1)} %get-tuple-element.148.c_ref, bf16[8,4,192,768]{3,2,1,0:T(8,128)(2,1)} %place.3.fc1_ref.fc2_ref, f32[1,3072]{1,0:T(1,128)} %reshape.349.b_ref, bf16[8,4,192,768]{3,2,1,0:T(8,128)(2,1)} %place.3.fc1_ref.fc2_ref, ...), custom_call_target="tpu_custom_call" | custom-call | flops 8153726976 | bytes 25362432 | tf_op jit(solution)/shard_map/mlp_fwd/pallas_call | solution.py:308
  202.6 2.2 multiply_convert_fusion.1
  206.9 4.6 collective-permute-start.32
  214.2 2.8 fusion.97
  217.0 26.2 %mlp_bwd.1 = (f32[864,768]{1,0:T(8,128)}, f32[1,3072]{1,0:T(1,128)}, bf16[4,4,96,768]{3,2,1,0:T(8,128)(2,1)}, bf16[4,4,96,768]{3,2,1,0:T(8,128)(2,1)}, bf16[4,4,...) custom-call(s32[3]{0:T(128)} %pad_add_fusion.pos_ref, bf16[864,768]{1,0:T(8,128)(2,1)} %get-tuple-element.330.dm_ref, ...), custom_call_target="tpu_custom_call" | custom-call | flops 16307453952 | bytes 34799616 | tf_op jit(solution)/shard_map/mlp_bwd/pallas_call | solution.py:368
  243.3 3.6 collective-permute-start.35
  248.3 6.0 %collective-permute-start.30 = (bf16[144,512]{1,0:T(8,128)(2,1)}, bf16[144,512]{1,0:T(8,128)(2,1)}, u32[]{:S(2)}, u32[]{:S(2)}) collective-permute-start(bf16[144,512]{1,0:T(8,128)(2,1)} %get-tuple-element.294), channel_id=1, source_target_pairs={{0,8},{8,16},{16,24},{1,9},{9,17},{17,25},{2,10},{10,18},{18,26},{... | collective-permute-start | bytes 442376 | tf_op jit(solution)/shard_map/ppermute | solution.py:649
  254.3 3.5 convolution_convert_fusion.3
  257.8 7.1 %norm2_back.1 = (f32[864,768]{1,0:T(8,128)}, bf16[864,768]{1,0:T(8,128)(2,1)}, bf16[864,768]{1,0:T(8,128)(2,1)}, f32[1,768]{1,0:T(1,128)}, f32[1,768]{1,0:T(1,128)}) custom-call(f32[864,768]{1,0:T(8,128)} %get-tuple-element.171.dc_ref, f32[864,768]{1,0:T(8,128)} %get-tuple-element.162.h1_ref, f32[864,768]{1,0:T(8,128)} %get-tuple-element.331.dh2_ref, ...), custom_call_target="tpu_custom_call" | custom-call | flops 1019215872 | bytes 14450688 | tf_op jit(solution)/shard_map/norm2_back/pallas_call | solution.py:559
  266.3 2.2 fusion.98
  270.5 3.7 collective-permute-start.36
  275.6 4.2 add_convert_fusion
  281.6 3.6 collective-permute-start.38
  285.2 33.6 %attn_bwd.1.d_ref = bf16[3,864,768]{2,1,0:T(8,128)(2,1)} custom-call(bf16[864,2304]{1,0:T(8,128)(2,1)} %project.1.q_ref.k_ref.v_ref, bf16[864,2304]{1,0:T(8,128)(2,1)} %project.1.q_ref.k_ref.v_ref, bf16[864,2304]{1,0:T(8,128)(2,1)} %project.1.q_ref.k_ref.v_ref, bf16[864,768]{1,0:T(8,128)(2,1)} %get-tuple-element.184.do_ref, ...), custom_call_target="tpu_custom_call" | custom-call | flops 22932357120 | bytes 10616832 | tf_op jit(solution)/shard_map/attn_bwd/pallas_call | solution.py:237
  321.9 2.2 convolution_convert_fusion
  324.3 2.0 fusion.39
  326.3 2.0 fusion.38
  328.4 10.5 %qkvo_grad.1 = (bf16[4,4,96,768]{3,2,1,0:T(8,128)(2,1)}, bf16[4,4,96,768]{3,2,1,0:T(8,128)(2,1)}) custom-call(s32[3]{0:T(128)} %pad_add_fusion.pos_ref, bf16[864,768]{1,0:T(8,128)(2,1)} %get-tuple-element.138.a_ref, bf16[3,864,768]{2,1,0:T(8,128)(2,1)} %attn_bwd.1.d_ref, bf16[864,768]{1,0:T(8,128)(2,1)} %get-tuple-element.142.o_ref, ...), custom_call_target="tpu_custom_call" | custom-call | flops 4076863488 | bytes 12681216 | tf_op jit(solution)/shard_map/qkvo_grad/pallas_call | solution.py:402
  338.9 2.3 collective-permute-start.39
  343.2 8.8 %norm1_back.1 = (bf16[864,768]{1,0:T(8,128)(2,1)}, f32[1,768]{1,0:T(1,128)}, f32[1,768]{1,0:T(1,128)}) custom-call(bf16[3,864,768]{2,1,0:T(8,128)(2,1)} %attn_bwd.1.d_ref, bf16[8,4,96,768]{3,2,1,0:T(8,128)(2,1)} %place.2.w_ref, f32[864,768]{1,0:T(8,128)} %get-tuple-element.143.h0_ref, f32[864,768]{1,0:T(8,128)} %get-tuple-element.198.dh1_ref, ...), custom_call_target="tpu_custom_call" | custom-call | flops 3057647616 | bytes 14155776 | tf_op jit(solution)/shard_map/norm1_back/pallas_call | solution.py:588
  352.1 1.8 fusion.84
  353.9 2.7 collective-permute-done.40
  361.6 2.9 fusion.37
  368.0 7.3 %patch_grad.1 = (bf16[4,4,64,768]{3,2,1,0:T(8,128)(2,1)}, bf16[4,4,64,768]{3,2,1,0:T(8,128)(2,1)}) custom-call(s32[3]{0:T(128)} %pad_add_fusion.pos_ref, bf16[864,1536]{1,0:T(8,128)(2,1)} %get-tuple-element.207.ext_ref, bf16[864,768]{1,0:T(8,128)(2,1)} %get-tuple-element.208.demb_ref, f32[1,3072]{1,0:T(1,128)} %get-tuple-element.209.bias_ref, ...), custom_call_target="tpu_custom_call" | custom-call | flops 2038431744 | bytes 6340608 | tf_op jit(solution)/shard_map/patch_grad/pallas_call | solution.py:449
  378.5 2.6 collective-permute-done.42
  381.1 3.4 collective-permute-start.47
  384.5 7.0 %collective-permute-done.43 = bf16[4,96,768]{2,1,0:T(8,128)(2,1)} collective-permute-done((bf16[4,96,768]{2,1,0:T(8,128)(2,1)}, bf16[4,96,768]{2,1,0:T(8,128)(2,1)}, u32[]{:S(2)}, u32[]{:S(2)}) %collective-permute-start.43) | collective-permute-done | bytes 589856 | tf_op jit(solution)/shard_map/ppermute | solution.py:758
  391.5 3.1 collective-permute-done.44
  394.6 2.0 fusion.23
  396.6 1.8 collective-permute-done.46
  400.5 3.0 collective-permute-start.49
  403.8 2.8 fusion.44
  406.6 2.6 collective-permute-start.50
  409.2 3.2 collective-permute-start.51
  413.9 5.7 %pixel_back.1 = f32[384,1536]{1,0:T(8,128)} custom-call(bf16[384,768]{1,0:T(8,128)(2,1)} %fusion.12.d_ref, bf16[8,208,768]{2,1,0:T(8,128)(2,1)} %bitcast.236, f32[384,1]{1,0:T(8,128)} %convert_element_type.689.shown_ref), custom_call_target="tpu_custom_call" | custom-call | flops 905969664 | bytes 4718592 | tf_op jit(solution)/shard_map/pixel_back/pallas_call | solution.py:472
  419.6 10.9 %collective-permute-done.51 = bf16[4,64,768]{2,1,0:T(8,128)(2,1)} collective-permute-done((bf16[4,64,768]{2,1,0:T(8,128)(2,1)}, bf16[4,64,768]{2,1,0:T(8,128)(2,1)}, u32[]{:S(2)}, u32[]{:S(2)}) %collective-permute-start.51) | collective-permute-done | bytes 393248 | tf_op jit(solution)/shard_map/ppermute | solution.py:758
  433.3 1.8 collective-permute-start.53
  438.8 5.4 %collective-permute-done.53 = bf16[160,768]{1,0:T(8,128)(2,1)S(1)} collective-permute-done((bf16[160,768]{1,0:T(8,128)(2,1)}, bf16[160,768]{1,0:T(8,128)(2,1)S(1)}, u32[]{:S(2)}, u32[]{:S(2)}) %collective-permute-start.53) | collective-permute-done | bytes 245792 | tf_op jit(solution)/shard_map/ppermute | solution.py:763
  444.4 1.8 fusion
  446.2 7.9 %collective-permute-done.54 = bf16[160,768]{1,0:T(8,128)(2,1)S(1)} collective-permute-done((bf16[160,768]{1,0:T(8,128)(2,1)}, bf16[160,768]{1,0:T(8,128)(2,1)S(1)}, u32[]{:S(2)}, u32[]{:S(2)}) %collective-permute-start.54) | collective-permute-done | bytes 245792 | tf_op jit(solution)/shard_map/ppermute | solution.py:763
  454.1 2.2 collective-permute-done.55
  460.0 5.4 %collective-permute-done.61 = bf16[384,768]{1,0:T(8,128)(2,1)} collective-permute-done((bf16[384,768]{1,0:T(8,128)(2,1)S(1)}, bf16[384,768]{1,0:T(8,128)(2,1)}, u32[]{:S(2)}, u32[]{:S(2)}) %collective-permute-start.61) | collective-permute-done | bytes 589856 | tf_op jit(solution)/shard_map/ppermute | solution.py:758
  (391 shorter events, 117.7 us)
Async XLA Ops:
  7.2 55.0 %all-gather.5.cloned.1.call-start = ((), (), s32[]{:S(2)}) async-start(), calls=%async_computation.6 | async-start | bytes 2875392 | tf_op jit(solution)/shard_map/all_gather | solution.py:848
  10.1 23.5 %collective-permute-start.2 = (bf16[96,768]{1,0:T(8,128)(2,1)}, bf16[96,768]{1,0:T(8,128)(2,1)}, u32[]{:S(2)}, u32[]{:S(2)}) collective-permute-start(bf16[96,768]{1,0:T(8,128)(2,1)} %constant_dynamic-slice_fusion.7), channel_id=1, source_target_pairs={{0,2},{1,3},{2,4},{3,5},{4,6},{5,7},{6,0},{7,1},{8,10},{9,11},{10,... | collective-permute-start | bytes 442376 | tf_op jit(solution)/shard_map/ppermute | solution.py:763
  13.1 20.5 %collective-permute-start.3 = (bf16[96,768]{1,0:T(8,128)(2,1)}, bf16[96,768]{1,0:T(8,128)(2,1)}, u32[]{:S(2)}, u32[]{:S(2)}) collective-permute-start(bf16[96,768]{1,0:T(8,128)(2,1)} %constant_dynamic-slice_fusion.7), channel_id=1, source_target_pairs={{0,4},{1,5},{2,6},{3,7},{4,0},{5,1},{6,2},{7,3},{8,12},{9,13},{10,... | collective-permute-start | bytes 442376 | tf_op jit(solution)/shard_map/ppermute | solution.py:763
  15.7 17.9 %collective-permute-start.4 = (bf16[96,768]{1,0:T(8,128)(2,1)}, bf16[96,768]{1,0:T(8,128)(2,1)}, u32[]{:S(2)}, u32[]{:S(2)}) collective-permute-start(bf16[96,768]{1,0:T(8,128)(2,1)} %constant_dynamic-slice_fusion.7), channel_id=1, source_target_pairs={{0,6},{1,7},{2,0},{3,1},{4,2},{5,3},{6,4},{7,5},{8,14},{9,15},{10,... | collective-permute-start | bytes 442376 | tf_op jit(solution)/shard_map/ppermute | solution.py:763
  23.0 12.6 %collective-permute-start.1 = (bf16[112,1536]{1,0:T(8,128)(2,1)}, bf16[112,1536]{1,0:T(8,128)(2,1)}, u32[]{:S(2)}, u32[]{:S(2)}) collective-permute-start(bf16[112,1536]{1,0:T(8,128)(2,1)} %fusion.50), channel_id=1, source_target_pairs={{0,1},{1,2},{2,3},{3,4},{4,5},{5,6},{6,7},{8,9},{9,10},{10,11},{11... | collective-permute-start | bytes 1032200 | tf_op jit(solution)/shard_map/ppermute | solution.py:649
  25.9 9.6 %collective-permute-start = (bf16[112,1536]{1,0:T(8,128)(2,1)}, bf16[112,1536]{1,0:T(8,128)(2,1)}, u32[]{:S(2)}, u32[]{:S(2)}) collective-permute-start(bf16[112,1536]{1,0:T(8,128)(2,1)} %fusion.49), channel_id=1, source_target_pairs={{1,0},{2,1},{3,2},{4,3},{5,4},{6,5},{7,6},{9,8},{10,9},{11,10},{12... | collective-permute-start | bytes 1032200 | tf_op jit(solution)/shard_map/ppermute | solution.py:649
  28.2 135.4 %all-gather.7.cloned.1.call-start = ((), (), s32[]{:S(2)}) async-start(), calls=%async_computation.7 | async-start | bytes 2654208 | tf_op jit(solution)/shard_map/all_gather | solution.py:848
  40.4 15.9 %collective-permute-start.6 = (bf16[160,1536]{1,0:T(8,128)(2,1)S(1)}, bf16[160,1536]{1,0:T(8,128)(2,1)}, u32[]{:S(2)}, u32[]{:S(2)}) collective-permute-start(bf16[160,1536]{1,0:T(8,128)(2,1)S(1)} %fusion.41), channel_id=1, source_target_pairs={{8,0},{16,8},{24,16},{9,1},{17,9},{25,17},{10,2},{18,10},{26,18},{... | collective-permute-start | bytes 1474568 | tf_op jit(solution)/shard_map/ppermute | solution.py:649
  42.8 16.5 %collective-permute-start.5 = (bf16[160,1536]{1,0:T(8,128)(2,1)}, bf16[160,1536]{1,0:T(8,128)(2,1)}, u32[]{:S(2)}, u32[]{:S(2)}) collective-permute-start(bf16[160,1536]{1,0:T(8,128)(2,1)} %fusion.40), channel_id=1, source_target_pairs={{0,8},{8,16},{16,24},{1,9},{9,17},{17,25},{2,10},{10,18},{18,26},{... | collective-permute-start | bytes 1474568 | tf_op jit(solution)/shard_map/ppermute | solution.py:649
  62.2 12.0 %collective-permute-start.7 = (bf16[192,768]{1,0:T(8,128)(2,1)S(1)}, bf16[192,768]{1,0:T(8,128)(2,1)S(1)}, u32[]{:S(2)}, u32[]{:S(2)}) collective-permute-start(bf16[192,768]{1,0:T(8,128)(2,1)S(1)} %pad_maximum_fusion.5), channel_id=1, source_target_pairs={{0,2},{1,3},{2,4},{3,5},{4,6},{5,7},{6,0},{7,1},{8,10},{9,11},{10,... | collective-permute-start | bytes 884744 | tf_op jit(solution)/shard_map/ppermute | solution.py:763
  64.6 25.6 %collective-permute-start.10 = (bf16[3,96,768]{2,1,0:T(8,128)(2,1)}, bf16[3,96,768]{2,1,0:T(8,128)(2,1)}, u32[]{:S(2)}, u32[]{:S(2)}) collective-permute-start(bf16[3,96,768]{2,1,0:T(8,128)(2,1)} %pad_maximum_fusion.4.refs_1_), channel_id=1, source_target_pairs={{0,8},{8,0},{16,24},{24,16},{1,9},{9,1},{17,25},{25,17},{2,10},{10... | collective-permute-start | bytes 1327112 | tf_op jit(solution)/shard_map/ppermute | solution.py:758
  69.0 21.6 %collective-permute-start.11 = (bf16[3,96,768]{2,1,0:T(8,128)(2,1)}, bf16[3,96,768]{2,1,0:T(8,128)(2,1)}, u32[]{:S(2)}, u32[]{:S(2)}) collective-permute-start(bf16[3,96,768]{2,1,0:T(8,128)(2,1)} %pad_maximum_fusion.4.refs_1_), channel_id=1, source_target_pairs={{0,16},{8,24},{16,0},{24,8},{1,17},{9,25},{17,1},{25,9},{2,18},{10... | collective-permute-start | bytes 1327112 | tf_op jit(solution)/shard_map/ppermute | solution.py:758
  72.4 19.0 %collective-permute-start.12 = (bf16[3,96,768]{2,1,0:T(8,128)(2,1)}, bf16[3,96,768]{2,1,0:T(8,128)(2,1)}, u32[]{:S(2)}, u32[]{:S(2)}) collective-permute-start(bf16[3,96,768]{2,1,0:T(8,128)(2,1)} %pad_maximum_fusion.4.refs_1_), channel_id=1, source_target_pairs={{0,24},{8,16},{16,8},{24,0},{1,25},{9,17},{17,9},{25,1},{2,26},{10... | collective-permute-start | bytes 1327112 | tf_op jit(solution)/shard_map/ppermute | solution.py:758
  72.4 15.8 %collective-permute-start.8 = (bf16[192,768]{1,0:T(8,128)(2,1)S(1)}, bf16[192,768]{1,0:T(8,128)(2,1)S(1)}, u32[]{:S(2)}, u32[]{:S(2)}) collective-permute-start(bf16[192,768]{1,0:T(8,128)(2,1)S(1)} %pad_maximum_fusion.5), channel_id=1, source_target_pairs={{0,4},{1,5},{2,6},{3,7},{4,0},{5,1},{6,2},{7,3},{8,12},{9,13},{10,... | collective-permute-start | bytes 884744 | tf_op jit(solution)/shard_map/ppermute | solution.py:763
  74.2 14.0 %collective-permute-start.9 = (bf16[192,768]{1,0:T(8,128)(2,1)S(1)}, bf16[192,768]{1,0:T(8,128)(2,1)S(1)}, u32[]{:S(2)}, u32[]{:S(2)}) collective-permute-start(bf16[192,768]{1,0:T(8,128)(2,1)S(1)} %pad_maximum_fusion.5), channel_id=1, source_target_pairs={{0,6},{1,7},{2,0},{3,1},{4,2},{5,3},{6,4},{7,5},{8,14},{9,15},{10,... | collective-permute-start | bytes 884744 | tf_op jit(solution)/shard_map/ppermute | solution.py:763
  88.2 16.5 %collective-permute-start.13 = (bf16[96,3072]{1,0:T(8,128)(2,1)S(1)}, bf16[96,3072]{1,0:T(8,128)(2,1)S(1)}, u32[]{:S(2)}, u32[]{:S(2)}) collective-permute-start(bf16[96,3072]{1,0:T(8,128)(2,1)S(1)} %constant_dynamic-update-slice_fusion.refs_0_), channel_id=1, source_target_pairs={{0,1},{1,0},{2,3},{3,2},{4,5},{5,4},{6,7},{7,6},{8,9},{9,8},{10,11... | collective-permute-start | bytes 1769480 | tf_op jit(solution)/shard_map/ppermute | solution.py:758
  91.4 284.7 %reduce-scatter.6.cloned.1.call-start = ((), (), s32[]{:S(2)}) async-start(), calls=%async_computation.4 | async-start | bytes 884736 | tf_op jit(solution)/shard_map/reduce_scatter | solution.py:863
  100.1 4.5 collective-permute-start.14
  100.1 4.5 collective-permute-start.17
  110.9 32.7 %collective-permute-start.18 = (bf16[3,192,768]{2,1,0:T(8,128)(2,1)S(1)}, bf16[3,192,768]{2,1,0:T(8,128)(2,1)}, u32[]{:S(2)}, u32[]{:S(2)}) collective-permute-start(bf16[3,192,768]{2,1,0:T(8,128)(2,1)S(1)} %pad_maximum_fusion.3.refs_2_), channel_id=1, source_target_pairs={{0,8},{8,0},{16,24},{24,16},{1,9},{9,1},{17,25},{25,17},{2,10},{10... | collective-permute-start | bytes 2654216 | tf_op jit(solution)/shard_map/ppermute | solution.py:758
  113.8 40.6 %collective-permute-start.19 = (bf16[3,192,768]{2,1,0:T(8,128)(2,1)S(1)}, bf16[3,192,768]{2,1,0:T(8,128)(2,1)}, u32[]{:S(2)}, u32[]{:S(2)}) collective-permute-start(bf16[3,192,768]{2,1,0:T(8,128)(2,1)S(1)} %pad_maximum_fusion.3.refs_2_), channel_id=1, source_target_pairs={{0,16},{8,24},{16,0},{24,8},{1,17},{9,25},{17,1},{25,9},{2,18},{10... | collective-permute-start | bytes 2654216 | tf_op jit(solution)/shard_map/ppermute | solution.py:758
  116.6 38.5 %collective-permute-start.20 = (bf16[3,192,768]{2,1,0:T(8,128)(2,1)S(1)}, bf16[3,192,768]{2,1,0:T(8,128)(2,1)S(1)}, u32[]{:S(2)}, u32[]{:S(2)}) collective-permute-start(bf16[3,192,768]{2,1,0:T(8,128)(2,1)S(1)} %pad_maximum_fusion.3.refs_2_), channel_id=1, source_target_pairs={{0,24},{8,16},{16,8},{24,0},{1,25},{9,17},{17,9},{25,1},{2,26},{10... | collective-permute-start | bytes 2654216 | tf_op jit(solution)/shard_map/ppermute | solution.py:758
  155.1 11.8 %collective-permute-start.21 = (bf16[96,3072]{1,0:T(8,128)(2,1)S(1)}, bf16[96,3072]{1,0:T(8,128)(2,1)}, u32[]{:S(2)}, u32[]{:S(2)}) collective-permute-start(bf16[96,3072]{1,0:T(8,128)(2,1)S(1)} %copy-done.19), channel_id=1, source_target_pairs={{0,1},{1,0},{2,3},{3,2},{4,5},{5,4},{6,7},{7,6},{8,9},{9,8},{10,11... | collective-permute-start | bytes 1769480 | tf_op jit(solution)/shard_map/ppermute | solution.py:758
  156.7 13.6 %collective-permute-start.26 = (bf16[3,192,768]{2,1,0:T(8,128)(2,1)}, bf16[3,192,768]{2,1,0:T(8,128)(2,1)}, u32[]{:S(2)}, u32[]{:S(2)}) collective-permute-start(bf16[3,192,768]{2,1,0:T(8,128)(2,1)} %copy-done.25), channel_id=1, source_target_pairs={{0,1},{1,0},{2,3},{3,2},{4,5},{5,4},{6,7},{7,6},{8,9},{9,8},{10,11... | collective-permute-start | bytes 2654216 | tf_op jit(solution)/shard_map/ppermute | solution.py:758
  162.5 12.7 %collective-permute-start.23 = (bf16[3,192,768]{2,1,0:T(8,128)(2,1)S(1)}, bf16[3,192,768]{2,1,0:T(8,128)(2,1)}, u32[]{:S(2)}, u32[]{:S(2)}) collective-permute-start(bf16[3,192,768]{2,1,0:T(8,128)(2,1)S(1)} %pad_maximum_fusion.3.refs_2_), channel_id=1, source_target_pairs={{0,1},{1,0},{2,3},{3,2},{4,5},{5,4},{6,7},{7,6},{8,9},{9,8},{10,11... | collective-permute-start | bytes 2654216 | tf_op jit(solution)/shard_map/ppermute | solution.py:758
  163.0 12.2 %collective-permute-start.24 = (bf16[3,192,768]{2,1,0:T(8,128)(2,1)}, bf16[3,192,768]{2,1,0:T(8,128)(2,1)}, u32[]{:S(2)}, u32[]{:S(2)}) collective-permute-start(bf16[3,192,768]{2,1,0:T(8,128)(2,1)} %collective-permute-done.18.refs_3_), channel_id=1, source_target_pairs={{0,1},{1,0},{2,3},{3,2},{4,5},{5,4},{6,7},{7,6},{8,9},{9,8},{10,11... | collective-permute-start | bytes 2654216 | tf_op jit(solution)/shard_map/ppermute | solution.py:758
  163.1 12.1 %collective-permute-start.25 = (bf16[3,192,768]{2,1,0:T(8,128)(2,1)}, bf16[3,192,768]{2,1,0:T(8,128)(2,1)}, u32[]{:S(2)}, u32[]{:S(2)}) collective-permute-start(bf16[3,192,768]{2,1,0:T(8,128)(2,1)} %collective-permute-done.19.refs_4_), channel_id=1, source_target_pairs={{0,1},{1,0},{2,3},{3,2},{4,5},{5,4},{6,7},{7,6},{8,9},{9,8},{10,11... | collective-permute-start | bytes 2654216 | tf_op jit(solution)/shard_map/ppermute | solution.py:758
  169.0 15.0 %collective-permute-start.27 = (bf16[96,512]{1,0:T(8,128)(2,1)S(1)}, bf16[96,512]{1,0:T(8,128)(2,1)S(1)}, u32[]{:S(2)}, u32[]{:S(2)}) collective-permute-start(bf16[96,512]{1,0:T(8,128)(2,1)S(1)} %get-tuple-element.156), channel_id=1, source_target_pairs={{1,0},{2,1},{3,2},{4,3},{5,4},{6,5},{7,6},{9,8},{10,9},{11,10},{12... | collective-permute-start | bytes 294920 | tf_op jit(solution)/shard_map/ppermute | solution.py:649
  170.3 13.7 %collective-permute-start.28 = (bf16[96,512]{1,0:T(8,128)(2,1)S(1)}, bf16[96,512]{1,0:T(8,128)(2,1)S(1)}, u32[]{:S(2)}, u32[]{:S(2)}) collective-permute-start(bf16[96,512]{1,0:T(8,128)(2,1)S(1)} %get-tuple-element.157), channel_id=1, source_target_pairs={{0,1},{1,2},{2,3},{3,4},{4,5},{5,6},{6,7},{8,9},{9,10},{10,11},{11... | collective-permute-start | bytes 294920 | tf_op jit(solution)/shard_map/ppermute | solution.py:649
  205.6 7.0 %collective-permute-start.31 = (bf16[144,512]{1,0:T(8,128)(2,1)S(1)}, bf16[144,512]{1,0:T(8,128)(2,1)S(1)}, u32[]{:S(2)}, u32[]{:S(2)}) collective-permute-start(bf16[144,512]{1,0:T(8,128)(2,1)S(1)} %get-tuple-element.164), channel_id=1, source_target_pairs={{8,0},{16,8},{24,16},{9,1},{17,9},{25,17},{10,2},{18,10},{26,18},{... | collective-permute-start | bytes 442376 | tf_op jit(solution)/shard_map/ppermute | solution.py:649
  206.9 7.2 %collective-permute-start.32 = (bf16[144,512]{1,0:T(8,128)(2,1)S(1)}, bf16[144,512]{1,0:T(8,128)(2,1)S(1)}, u32[]{:S(2)}, u32[]{:S(2)}) collective-permute-start(bf16[144,512]{1,0:T(8,128)(2,1)S(1)} %get-tuple-element.165), channel_id=1, source_target_pairs={{0,8},{8,16},{16,24},{1,9},{9,17},{17,25},{2,10},{10,18},{18,26},{... | collective-permute-start | bytes 442376 | tf_op jit(solution)/shard_map/ppermute | solution.py:649
  243.3 30.9 %collective-permute-start.35 = (bf16[4,4,96,768]{3,2,1,0:T(8,128)(2,1)}, bf16[4,4,96,768]{3,2,1,0:T(8,128)(2,1)}, u32[]{:S(2)}, u32[]{:S(2)}) collective-permute-start(bf16[4,4,96,768]{3,2,1,0:T(8,128)(2,1)} %get-tuple-element.182), channel_id=1, source_target_pairs={{0,1},{1,0},{2,3},{3,2},{4,5},{5,4},{6,7},{7,6},{8,9},{9,8},{10,11... | collective-permute-start | bytes 7077896 | tf_op jit(solution)/shard_map/ppermute | solution.py:758
  246.9 27.3 %collective-permute-start.34 = (bf16[4,4,96,768]{3,2,1,0:T(8,128)(2,1)}, bf16[4,4,96,768]{3,2,1,0:T(8,128)(2,1)S(1)}, u32[]{:S(2)}, u32[]{:S(2)}) collective-permute-start(bf16[4,4,96,768]{3,2,1,0:T(8,128)(2,1)} %get-tuple-element.179), channel_id=1, source_target_pairs={{0,1},{1,0},{2,3},{3,2},{4,5},{5,4},{6,7},{7,6},{8,9},{9,8},{10,11... | collective-permute-start | bytes 7077896 | tf_op jit(solution)/shard_map/ppermute | solution.py:758
  247.0 17.9 %collective-permute-start.29 = (bf16[144,512]{1,0:T(8,128)(2,1)}, bf16[144,512]{1,0:T(8,128)(2,1)}, u32[]{:S(2)}, u32[]{:S(2)}) collective-permute-start(bf16[144,512]{1,0:T(8,128)(2,1)} %get-tuple-element.295), channel_id=1, source_target_pairs={{8,0},{16,8},{24,16},{9,1},{17,9},{25,17},{10,2},{18,10},{26,18},{... | collective-permute-start | bytes 442376 | tf_op jit(solution)/shard_map/ppermute | solution.py:649
  248.3 16.7 %collective-permute-start.30 = (bf16[144,512]{1,0:T(8,128)(2,1)}, bf16[144,512]{1,0:T(8,128)(2,1)}, u32[]{:S(2)}, u32[]{:S(2)}) collective-permute-start(bf16[144,512]{1,0:T(8,128)(2,1)} %get-tuple-element.294), channel_id=1, source_target_pairs={{0,8},{8,16},{16,24},{1,9},{9,17},{17,25},{2,10},{10,18},{18,26},{... | collective-permute-start | bytes 442376 | tf_op jit(solution)/shard_map/ppermute | solution.py:649
  269.2 49.6 %collective-permute-start.33 = (bf16[96,512]{1,0:T(8,128)(2,1)}, bf16[96,512]{1,0:T(8,128)(2,1)}, u32[]{:S(2)}, u32[]{:S(2)}) collective-permute-start(bf16[96,512]{1,0:T(8,128)(2,1)} %get-tuple-element.176), channel_id=1, source_target_pairs={{1,0},{2,1},{3,2},{4,3},{5,4},{6,5},{7,6},{9,8},{10,9},{11,10},{12... | collective-permute-start | bytes 294920 | tf_op jit(solution)/shard_map/ppermute | solution.py:649
  270.5 48.4 %collective-permute-start.36 = (bf16[96,512]{1,0:T(8,128)(2,1)}, bf16[96,512]{1,0:T(8,128)(2,1)}, u32[]{:S(2)}, u32[]{:S(2)}) collective-permute-start(bf16[96,512]{1,0:T(8,128)(2,1)} %get-tuple-element.187), channel_id=1, source_target_pairs={{0,1},{1,2},{2,3},{3,4},{4,5},{5,6},{6,7},{8,9},{9,10},{10,11},{11... | collective-permute-start | bytes 294920 | tf_op jit(solution)/shard_map/ppermute | solution.py:649
  274.2 102.0 %reduce-scatter.8.cloned.1.call-start = ((), (), s32[]{:S(2)}) async-start(), calls=%async_computation.5 | async-start | bytes 1769472 | tf_op jit(solution)/shard_map/reduce_scatter | solution.py:863
  281.6 42.8 %collective-permute-start.38 = (bf16[2,4,96,768]{3,2,1,0:T(8,128)(2,1)}, bf16[2,4,96,768]{3,2,1,0:T(8,128)(2,1)}, u32[]{:S(2)}, u32[]{:S(2)}) collective-permute-start(bf16[2,4,96,768]{3,2,1,0:T(8,128)(2,1)} %get-tuple-element.192), channel_id=1, source_target_pairs={{0,16},{8,24},{16,0},{24,8},{1,17},{9,25},{17,1},{25,9},{2,18},{10... | collective-permute-start | bytes 3538952 | tf_op jit(solution)/shard_map/ppermute | solution.py:758
  285.2 41.2 %collective-permute-start.37 = (bf16[2,4,96,768]{3,2,1,0:T(8,128)(2,1)}, bf16[2,4,96,768]{3,2,1,0:T(8,128)(2,1)}, u32[]{:S(2)}, u32[]{:S(2)}) collective-permute-start(bf16[2,4,96,768]{3,2,1,0:T(8,128)(2,1)} %get-tuple-element.190), channel_id=1, source_target_pairs={{0,8},{8,0},{16,24},{24,16},{1,9},{9,1},{17,25},{25,17},{2,10},{10... | collective-permute-start | bytes 3538952 | tf_op jit(solution)/shard_map/ppermute | solution.py:758
  324.1 89.8 %reduce-scatter.4.cloned.1.call-start = ((), (), s32[]{:S(2)}) async-start(), calls=%async_computation.3 | async-start | bytes 1474560 | tf_op jit(solution)/shard_map/reduce_scatter | solution.py:820
  338.9 21.7 %collective-permute-start.39 = (bf16[4,4,96,768]{3,2,1,0:T(8,128)(2,1)}, bf16[4,4,96,768]{3,2,1,0:T(8,128)(2,1)}, u32[]{:S(2)}, u32[]{:S(2)}) collective-permute-start(bf16[4,4,96,768]{3,2,1,0:T(8,128)(2,1)} %get-tuple-element.197), channel_id=1, source_target_pairs={{0,1},{1,0},{2,3},{3,2},{4,5},{5,4},{6,7},{7,6},{8,9},{9,8},{10,11... | collective-permute-start | bytes 7077896 | tf_op jit(solution)/shard_map/ppermute | solution.py:758
  341.2 15.4 %collective-permute-start.40 = (bf16[4,96,768]{2,1,0:T(8,128)(2,1)}, bf16[4,96,768]{2,1,0:T(8,128)(2,1)S(1)}, u32[]{:S(2)}, u32[]{:S(2)}) collective-permute-start(bf16[4,96,768]{2,1,0:T(8,128)(2,1)} %fusion.38), channel_id=1, source_target_pairs={{0,16},{8,24},{16,0},{24,8},{1,17},{9,25},{17,1},{25,9},{2,18},{10... | collective-permute-start | bytes 1769480 | tf_op jit(solution)/shard_map/ppermute | solution.py:758
  341.8 15.2 %collective-permute-start.41 = (bf16[4,96,768]{2,1,0:T(8,128)(2,1)}, bf16[4,96,768]{2,1,0:T(8,128)(2,1)S(1)}, u32[]{:S(2)}, u32[]{:S(2)}) collective-permute-start(bf16[4,96,768]{2,1,0:T(8,128)(2,1)} %fusion.39), channel_id=1, source_target_pairs={{0,8},{8,0},{16,24},{24,16},{1,9},{9,1},{17,25},{25,17},{2,10},{10... | collective-permute-start | bytes 1769480 | tf_op jit(solution)/shard_map/ppermute | solution.py:758
  364.5 16.6 %collective-permute-start.42 = (bf16[4,96,768]{2,1,0:T(8,128)(2,1)}, bf16[4,96,768]{2,1,0:T(8,128)(2,1)}, u32[]{:S(2)}, u32[]{:S(2)}) collective-permute-start(bf16[4,96,768]{2,1,0:T(8,128)(2,1)} %get-tuple-element.206), channel_id=1, source_target_pairs={{0,8},{8,0},{16,24},{24,16},{1,9},{9,1},{17,25},{25,17},{2,10},{10... | collective-permute-start | bytes 1769480 | tf_op jit(solution)/shard_map/ppermute | solution.py:758
  366.0 25.5 %collective-permute-start.43 = (bf16[4,96,768]{2,1,0:T(8,128)(2,1)}, bf16[4,96,768]{2,1,0:T(8,128)(2,1)}, u32[]{:S(2)}, u32[]{:S(2)}) collective-permute-start(bf16[4,96,768]{2,1,0:T(8,128)(2,1)} %get-tuple-element.216), channel_id=1, source_target_pairs={{0,16},{8,24},{16,0},{24,8},{1,17},{9,25},{17,1},{25,9},{2,18},{10... | collective-permute-start | bytes 1769480 | tf_op jit(solution)/shard_map/ppermute | solution.py:758
  367.7 27.0 %collective-permute-start.44 = (bf16[4,96,768]{2,1,0:T(8,128)(2,1)S(1)}, bf16[4,96,768]{2,1,0:T(8,128)(2,1)}, u32[]{:S(2)}, u32[]{:S(2)}) collective-permute-start(bf16[4,96,768]{2,1,0:T(8,128)(2,1)S(1)} %get-tuple-element.218), channel_id=1, source_target_pairs={{0,24},{8,16},{16,8},{24,0},{1,25},{9,17},{17,9},{25,1},{2,26},{10... | collective-permute-start | bytes 1769480 | tf_op jit(solution)/shard_map/ppermute | solution.py:758
  375.3 28.5 %collective-permute-start.45 = (bf16[4,4,64,768]{3,2,1,0:T(8,128)(2,1)}, bf16[4,4,64,768]{3,2,1,0:T(8,128)(2,1)}, u32[]{:S(2)}, u32[]{:S(2)}) collective-permute-start(bf16[4,4,64,768]{3,2,1,0:T(8,128)(2,1)} %get-tuple-element.220), channel_id=1, source_target_pairs={{0,1},{1,0},{2,3},{3,2},{4,5},{5,4},{6,7},{7,6},{8,9},{9,8},{10,11... | collective-permute-start | bytes 4718600 | tf_op jit(solution)/shard_map/ppermute | solution.py:758
  377.2 21.2 %collective-permute-start.46 = (bf16[144,768]{1,0:T(8,128)(2,1)}, bf16[144,768]{1,0:T(8,128)(2,1)S(1)}, u32[]{:S(2)}, u32[]{:S(2)}) collective-permute-start(bf16[144,768]{1,0:T(8,128)(2,1)} %get-tuple-element.222), channel_id=1, source_target_pairs={{8,0},{16,8},{24,16},{9,1},{17,9},{25,17},{10,2},{18,10},{26,18},{... | collective-permute-start | bytes 663560 | tf_op jit(solution)/shard_map/ppermute | solution.py:649
  381.1 17.3 %collective-permute-start.47 = (bf16[144,768]{1,0:T(8,128)(2,1)S(1)}, bf16[144,768]{1,0:T(8,128)(2,1)S(1)}, u32[]{:S(2)}, u32[]{:S(2)}) collective-permute-start(bf16[144,768]{1,0:T(8,128)(2,1)S(1)} %copy-done.46), channel_id=1, source_target_pairs={{0,8},{8,16},{16,24},{1,9},{9,17},{17,25},{2,10},{10,18},{18,26},{... | collective-permute-start | bytes 663560 | tf_op jit(solution)/shard_map/ppermute | solution.py:649
  399.2 7.4 %collective-permute-start.48 = (bf16[96,768]{1,0:T(8,128)(2,1)S(1)}, bf16[96,768]{1,0:T(8,128)(2,1)S(1)}, u32[]{:S(2)}, u32[]{:S(2)}) collective-permute-start(bf16[96,768]{1,0:T(8,128)(2,1)S(1)} %get-tuple-element.293), channel_id=1, source_target_pairs={{1,0},{2,1},{3,2},{4,3},{5,4},{6,5},{7,6},{9,8},{10,9},{11,10},{12... | collective-permute-start | bytes 442376 | tf_op jit(solution)/shard_map/ppermute | solution.py:649
  400.5 6.1 %collective-permute-start.49 = (bf16[96,768]{1,0:T(8,128)(2,1)S(1)}, bf16[96,768]{1,0:T(8,128)(2,1)S(1)}, u32[]{:S(2)}, u32[]{:S(2)}) collective-permute-start(bf16[96,768]{1,0:T(8,128)(2,1)S(1)} %get-tuple-element.292), channel_id=1, source_target_pairs={{0,1},{1,2},{2,3},{3,4},{4,5},{5,6},{6,7},{8,9},{9,10},{10,11},{11... | collective-permute-start | bytes 442376 | tf_op jit(solution)/shard_map/ppermute | solution.py:649
  406.6 13.0 %collective-permute-start.50 = (bf16[4,64,768]{2,1,0:T(8,128)(2,1)}, bf16[4,64,768]{2,1,0:T(8,128)(2,1)S(1)}, u32[]{:S(2)}, u32[]{:S(2)}) collective-permute-start(bf16[4,64,768]{2,1,0:T(8,128)(2,1)} %get-tuple-element.226), channel_id=1, source_target_pairs={{0,8},{8,0},{16,24},{24,16},{1,9},{9,1},{17,25},{25,17},{2,10},{10... | collective-permute-start | bytes 1179656 | tf_op jit(solution)/shard_map/ppermute | solution.py:758
  409.2 21.3 %collective-permute-start.51 = (bf16[4,64,768]{2,1,0:T(8,128)(2,1)}, bf16[4,64,768]{2,1,0:T(8,128)(2,1)}, u32[]{:S(2)}, u32[]{:S(2)}) collective-permute-start(bf16[4,64,768]{2,1,0:T(8,128)(2,1)} %get-tuple-element.232), channel_id=1, source_target_pairs={{0,16},{8,24},{16,0},{24,8},{1,17},{9,25},{17,1},{25,9},{2,18},{10... | collective-permute-start | bytes 1179656 | tf_op jit(solution)/shard_map/ppermute | solution.py:758
  412.4 18.3 %collective-permute-start.52 = (bf16[4,64,768]{2,1,0:T(8,128)(2,1)}, bf16[4,64,768]{2,1,0:T(8,128)(2,1)}, u32[]{:S(2)}, u32[]{:S(2)}) collective-permute-start(bf16[4,64,768]{2,1,0:T(8,128)(2,1)} %get-tuple-element.234), channel_id=1, source_target_pairs={{0,24},{8,16},{16,8},{24,0},{1,25},{9,17},{17,9},{25,1},{2,26},{10... | collective-permute-start | bytes 1179656 | tf_op jit(solution)/shard_map/ppermute | solution.py:758
  433.3 10.9 %collective-permute-start.53 = (bf16[160,768]{1,0:T(8,128)(2,1)}, bf16[160,768]{1,0:T(8,128)(2,1)S(1)}, u32[]{:S(2)}, u32[]{:S(2)}) collective-permute-start(bf16[160,768]{1,0:T(8,128)(2,1)} %get-tuple-element.288), channel_id=1, source_target_pairs={{0,2},{1,3},{2,4},{3,5},{4,6},{5,7},{6,0},{7,1},{8,10},{9,11},{10,... | collective-permute-start | bytes 737288 | tf_op jit(solution)/shard_map/ppermute | solution.py:763
  435.2 23.7 %collective-permute-start.59 = (bf16[384,768]{1,0:T(8,128)(2,1)S(1)}, bf16[384,768]{1,0:T(8,128)(2,1)}, u32[]{:S(2)}, u32[]{:S(2)}) collective-permute-start(bf16[384,768]{1,0:T(8,128)(2,1)S(1)} %constant_dynamic-update-slice_fusion.7), channel_id=1, source_target_pairs={{0,8},{8,0},{16,24},{24,16},{1,9},{9,1},{17,25},{25,17},{2,10},{10... | collective-permute-start | bytes 1769480 | tf_op jit(solution)/shard_map/ppermute | solution.py:758
  436.6 23.4 %collective-permute-start.60 = (bf16[384,768]{1,0:T(8,128)(2,1)S(1)}, bf16[384,768]{1,0:T(8,128)(2,1)}, u32[]{:S(2)}, u32[]{:S(2)}) collective-permute-start(bf16[384,768]{1,0:T(8,128)(2,1)S(1)} %constant_dynamic-update-slice_fusion.7), channel_id=1, source_target_pairs={{0,16},{8,24},{16,0},{24,8},{1,17},{9,25},{17,1},{25,9},{2,18},{10... | collective-permute-start | bytes 1769480 | tf_op jit(solution)/shard_map/ppermute | solution.py:758
  437.6 27.8 %collective-permute-start.61 = (bf16[384,768]{1,0:T(8,128)(2,1)S(1)}, bf16[384,768]{1,0:T(8,128)(2,1)}, u32[]{:S(2)}, u32[]{:S(2)}) collective-permute-start(bf16[384,768]{1,0:T(8,128)(2,1)S(1)} %constant_dynamic-update-slice_fusion.7), channel_id=1, source_target_pairs={{0,24},{8,16},{16,8},{24,0},{1,25},{9,17},{17,9},{25,1},{2,26},{10... | collective-permute-start | bytes 1769480 | tf_op jit(solution)/shard_map/ppermute | solution.py:758
  438.8 15.3 %collective-permute-start.54 = (bf16[160,768]{1,0:T(8,128)(2,1)}, bf16[160,768]{1,0:T(8,128)(2,1)S(1)}, u32[]{:S(2)}, u32[]{:S(2)}) collective-permute-start(bf16[160,768]{1,0:T(8,128)(2,1)} %get-tuple-element.290), channel_id=1, source_target_pairs={{0,4},{1,5},{2,6},{3,7},{4,0},{5,1},{6,2},{7,3},{8,12},{9,13},{10,... | collective-permute-start | bytes 737288 | tf_op jit(solution)/shard_map/ppermute | solution.py:763
  444.2 12.1 %collective-permute-start.55 = (bf16[160,768]{1,0:T(8,128)(2,1)}, bf16[160,768]{1,0:T(8,128)(2,1)S(1)}, u32[]{:S(2)}, u32[]{:S(2)}) collective-permute-start(bf16[160,768]{1,0:T(8,128)(2,1)} %get-tuple-element.291), channel_id=1, source_target_pairs={{0,6},{1,7},{2,0},{3,1},{4,2},{5,3},{6,4},{7,5},{8,14},{9,15},{10,... | collective-permute-start | bytes 737288 | tf_op jit(solution)/shard_map/ppermute | solution.py:763
  456.4 17.3 %collective-permute-start.56 = (bf16[160,768]{1,0:T(8,128)(2,1)S(1)}, bf16[160,768]{1,0:T(8,128)(2,1)S(1)}, u32[]{:S(2)}, u32[]{:S(2)}) collective-permute-start(bf16[160,768]{1,0:T(8,128)(2,1)S(1)} %add_convert_fusion.11), channel_id=1, source_target_pairs={{0,8},{8,0},{16,24},{24,16},{1,9},{9,1},{17,25},{25,17},{2,10},{10... | collective-permute-start | bytes 737288 | tf_op jit(solution)/shard_map/ppermute | solution.py:758
  457.8 15.9 %collective-permute-start.57 = (bf16[160,768]{1,0:T(8,128)(2,1)S(1)}, bf16[160,768]{1,0:T(8,128)(2,1)S(1)}, u32[]{:S(2)}, u32[]{:S(2)}) collective-permute-start(bf16[160,768]{1,0:T(8,128)(2,1)S(1)} %add_convert_fusion.11), channel_id=1, source_target_pairs={{0,16},{8,24},{16,0},{24,8},{1,17},{9,25},{17,1},{25,9},{2,18},{10... | collective-permute-start | bytes 737288 | tf_op jit(solution)/shard_map/ppermute | solution.py:758
  458.9 14.8 %collective-permute-start.58 = (bf16[160,768]{1,0:T(8,128)(2,1)S(1)}, bf16[160,768]{1,0:T(8,128)(2,1)S(1)}, u32[]{:S(2)}, u32[]{:S(2)}) collective-permute-start(bf16[160,768]{1,0:T(8,128)(2,1)S(1)} %add_convert_fusion.11), channel_id=1, source_target_pairs={{0,24},{8,16},{16,8},{24,0},{1,25},{9,17},{17,9},{25,1},{2,26},{10... | collective-permute-start | bytes 737288 | tf_op jit(solution)/shard_map/ppermute | solution.py:758
  (70 other events, 837.6 us)
Sparse Core Ops, SparseCore 0:
  28.3 33.8 all-gather.4
  91.5 37.0 all-gather.6
  274.3 33.7 reduce-scatter.5
  324.2 34.3 reduce-scatter.7
  368.1 28.5 reduce-scatter.3

commit v5 on v4

--- a/solution.py
+++ b/solution.py
@@ -944,14 +944,14 @@
         pieces_b = (fc1_w, fc2_w, *along_gy(got_b))
     qkv = project(a, front_a, 3)
     o, qx = attn_fwd(qkv, kx, scale)
+    gz = dense(after(gr, o), full_head, 1, 1).astype(bf16)
+    west, east = margin_first(gz, dates, side)
+    o, west, east, full_dec = tied(o, west, east, full_dec)
+    right, left = to_neighbours(west, east, "gx")
     if split:
         o, *pieces_b = tied(o, *pieces_b)
         others_b = core_swap(pieces_b)
     h1, c = proj_norm(o, front_a, h0, vec)
-    gz = dense(after(gr, c), full_head, 1, 1).astype(bf16)
-    west, east = margin_first(gz, dates, side)
-    c, west, east = tied(c, west, east)
-    right, left = to_neighbours(west, east, "gx")
     if split:
         full_mlp = place(pos, pieces_b, (*others_b[:-1], after(others_b[-1], c)), ("wide", "tall"))
         full_mlp, right, left = tied(full_mlp, right, left)

time: 494 us -> 485 us (0.982)
  waiting for transfers between devices: 81.6 us -> 76.6 us
  transfers between devices with their start and end apart: 67 -> 67, of which waited for: 23 -> 24; matrix products, arithmetic and copies ran while one was open for 19% -> 19% of each run, Pallas kernels for 26% -> 27%
where the time goes in v5:
time: 485 us; the launch traced here: 478 us
  Pallas kernels  172 us (35%)
  starting transfers between devices  98.2 us (20%)
  waiting for transfers between devices  76.6 us (16%)
  other arithmetic  46.6 us (10%)
  local copies, waits for them, and re-layouts  39.2 us (8%)
  matrix products  27.9 us (6%)
  between operations  17.5 us (4%)
    ppermute x37, starting transfers between devices, swap(): lax.ppermute(value, axis, [(i, i ^ bit) for i in range(lax.axis_size(axis...  43.2 us
    ppermute x37, waiting for transfers between devices, swap(): lax.ppermute(value, axis, [(i, i ^ bit) for i in range(lax.axis_size(axis...  42.3 us
    pallas_call x1, Pallas kernels, attn_bwd(): pl.pallas_call(functools.partial(attn_bwd_kernel, block=token_block(token...  33.6 us
    ppermute x8, starting transfers between devices, to_neighbours(): lax.ppermute(high, axis, chain(axis, 1))  31.5 us
    pallas_call x1, Pallas kernels, mlp_bwd(): pl.pallas_call(functools.partial(mlp_bwd_kernel, chips=chips), grid_spec=...  26.1 us
    convert_element_type x11, other arithmetic, added(): return sum((v.astype(f32) for v in values)).astype(bf16)  21.9 us
    ppermute x9, waiting for transfers between devices, turn(): lax.ppermute(value, 'gx', [(i, (i + 2 * step) % count) for i in range(cou...  19.6 us
    pallas_call x1, Pallas kernels, attn_fwd(): pl.pallas_call(functools.partial(attn_fwd_kernel, block=token_block(token...  18.4 us
  transfers between devices with their start and end apart: 67, of which 24 were waited for; matrix products, arithmetic and copies ran while one was open for 19% of the time, Pallas kernels for 27%

profile of v5, /device:TPU:0, one launch (start us, length us, event | category | flops | bytes accessed | tf_op | source)
XLA Modules:
  0.0 477.8 jit_solution(4412160210606390387)
XLA Ops:
  10.1 3.0 collective-permute-start.2
  13.1 2.6 collective-permute-start.3
  22.9 2.0 collective-permute-start.1
  33.7 1.9 pad_maximum_fusion.4.refs_1_
  42.0 5.5 %collective-permute-start.5 = (bf16[160,1536]{1,0:T(8,128)(2,1)S(1)}, bf16[160,1536]{1,0:T(8,128)(2,1)}, u32[]{:S(2)}, u32[]{:S(2)}) collective-permute-start(bf16[160,1536]{1,0:T(8,128)(2,1)S(1)} %fusion.40), channel_id=1, source_target_pairs={{0,8},{8,16},{16,24},{1,9},{9,17},{17,25},{2,10},{10,18},{18,26},{... | collective-permute-start | bytes 1474568 | tf_op jit(solution)/shard_map/ppermute | solution.py:649
  51.9 4.4 collective-permute-done.6.lower_ref
  56.3 1.9 collective-permute-done.5.upper_ref
  58.2 4.0 all-gather.5.cloned.1.call-done
  63.8 4.5 collective-permute-start.10
  68.2 3.3 collective-permute-start.11
  73.4 1.8 collective-permute-start.9
  75.8 7.7 %embed.1 = (bf16[864,1536]{1,0:T(8,128)(2,1)}, f32[864,768]{1,0:T(8,128)}, bf16[864,768]{1,0:T(8,128)(2,1)}) custom-call(bf16[384,1536]{1,0:T(8,128)(2,1)} %bitcast.229, bf16[112,1536]{1,0:T(8,128)(2,1)} %collective-permute-done.1.left_ref, bf16[112,1536]{1,0:T(8,128)(2,1)} %collective-permute-done.right_ref, ...), custom_call_target="tpu_custom_call" | custom-call | flops 2038431744 | bytes 11649024 | tf_op jit(solution)/shard_map/embed/pallas_call | solution.py:97
  83.5 4.0 collective-permute-done.8
  101.0 5.8 %place.2.w_ref = bf16[8,4,96,768]{3,2,1,0:T(8,128)(2,1)} custom-call(s32[3]{0:T(128)} %pad_add_fusion.pos_ref, bf16[96,3072]{1,0:T(8,128)(2,1)} %copy-done.3, bf16[3,96,768]{2,1,0:T(8,128)(2,1)} %pad_maximum_fusion.4.refs_1_, bf16[3,96,768]{2,1,0:T(8,128)(2,1)} %collective-permute-done.10.refs_2_, bf16[3,96,768]{2,1,0:T(8,128)(2,1)} %collective-permute-done.11.refs_3_, ...), custom_call_target="tpu_custom_call" | custom-call | bytes 9437184 | tf_op jit(solution)/shard_map/place/pallas_call | solution.py:508
  106.7 2.5 collective-permute-start.18
  109.2 2.7 collective-permute-start.19
  111.9 8.7 %project.1.q_ref.k_ref.v_ref = bf16[864,2304]{1,0:T(8,128)(2,1)} custom-call(bf16[864,768]{1,0:T(8,128)(2,1)} %get-tuple-element.139.a_ref, bf16[8,4,96,768]{3,2,1,0:T(8,128)(2,1)} %place.2.w_ref), custom_call_target="tpu_custom_call" | custom-call | flops 3057647616 | bytes 8847360 | tf_op jit(solution)/shard_map/project/pallas_call | solution.py:118
  120.5 18.4 %attn_fwd.1 = (bf16[864,768]{1,0:T(8,128)(2,1)}, bf16[12,864,128]{2,1,0:T(8,128)(2,1)}) custom-call(bf16[864,2304]{1,0:T(8,128)(2,1)} %project.1.q_ref.k_ref.v_ref, bf16[864,2304]{1,0:T(8,128)(2,1)} %project.1.q_ref.k_ref.v_ref, bf16[864,2304]{1,0:T(8,128)(2,1)} %project.1.q_ref.k_ref.v_ref, bf16[864,128]{1,0:T(8,128)(2,1)} %select_convert_fusion.kx_ref), custom_call_target="tpu_custom_call" | custom-call | flops 18345885696 | bytes 5308416 | tf_op jit(solution)/shard_map/attn_fwd/pallas_call | solution.py:177
  146.1 3.5 collective-permute-done.19.refs_4_
  151.5 1.8 collective-permute-done.21.refs_6_
  157.5 3.3 collective-permute-start.28
  161.1 5.8 %proj_norm.1 = (f32[864,768]{1,0:T(8,128)}, bf16[864,768]{1,0:T(8,128)(2,1)}) custom-call(bf16[864,768]{1,0:T(8,128)(2,1)} %get-tuple-element.147.o_ref, bf16[8,4,96,768]{3,2,1,0:T(8,128)(2,1)} %place.2.w_ref, f32[864,768]{1,0:T(8,128)} %get-tuple-element.148.h0_ref, f32[4,768]{1,0:T(4,128)} %reshape.344.vec_ref.gain_ref), custom_call_target="tpu_custom_call" | custom-call | flops 1019215872 | bytes 9142272 | tf_op jit(solution)/shard_map/proj_norm/pallas_call | solution.py:260
  166.9 8.8 %place.3.fc1_ref.fc2_ref = bf16[8,4,192,768]{3,2,1,0:T(8,128)(2,1)} custom-call(s32[3]{0:T(128)} %pad_add_fusion.pos_ref, bf16[96,3072]{1,0:T(8,128)(2,1)} %refs_0_, bf16[384,768]{1,0:T(8,128)(2,1)} %refs_1_, bf16[3,192,768]{2,1,0:T(8,128)(2,1)} %copy-done.1, bf16[3,192,768]{2,1,0:T(8,128)(2,1)} %collective-permute-done.18.refs_3_, ...), custom_call_target="tpu_custom_call" | custom-call | bytes 18874368 | tf_op jit(solution)/shard_map/place/pallas_call | solution.py:508
  176.9 17.5 %mlp_fwd.1 = (bf16[864,3072]{1,0:T(8,128)(2,1)}, bf16[864,3072]{1,0:T(8,128)(2,1)}, bf16[864,768]{1,0:T(8,128)(2,1)}) custom-call(bf16[864,768]{1,0:T(8,128)(2,1)} %get-tuple-element.149.c_ref, bf16[8,4,192,768]{3,2,1,0:T(8,128)(2,1)} %place.3.fc1_ref.fc2_ref, f32[1,3072]{1,0:T(1,128)} %reshape.350.b_ref, bf16[8,4,192,768]{3,2,1,0:T(8,128)(2,1)} %place.3.fc1_ref.fc2_ref, ...), custom_call_target="tpu_custom_call" | custom-call | flops 8153726976 | bytes 25362432 | tf_op jit(solution)/shard_map/mlp_fwd/pallas_call | solution.py:308
  194.4 2.2 multiply_convert_fusion.1
  198.8 4.6 collective-permute-start.32
  206.0 2.8 fusion.97
  208.9 26.1 %mlp_bwd.1 = (f32[864,768]{1,0:T(8,128)}, f32[1,3072]{1,0:T(1,128)}, bf16[4,4,96,768]{3,2,1,0:T(8,128)(2,1)}, bf16[4,4,96,768]{3,2,1,0:T(8,128)(2,1)}, bf16[4,4,...) custom-call(s32[3]{0:T(128)} %pad_add_fusion.pos_ref, bf16[864,768]{1,0:T(8,128)(2,1)} %get-tuple-element.332.dm_ref, ...), custom_call_target="tpu_custom_call" | custom-call | flops 16307453952 | bytes 34799616 | tf_op jit(solution)/shard_map/mlp_bwd/pallas_call | solution.py:368
  235.0 3.4 collective-permute-start.35
  239.7 6.0 %collective-permute-start.30 = (bf16[144,512]{1,0:T(8,128)(2,1)}, bf16[144,512]{1,0:T(8,128)(2,1)}, u32[]{:S(2)}, u32[]{:S(2)}) collective-permute-start(bf16[144,512]{1,0:T(8,128)(2,1)} %get-tuple-element.296), channel_id=1, source_target_pairs={{0,8},{8,16},{16,24},{1,9},{9,17},{17,25},{2,10},{10,18},{18,26},{... | collective-permute-start | bytes 442376 | tf_op jit(solution)/shard_map/ppermute | solution.py:649
  245.8 3.5 convolution_convert_fusion.3
  249.3 7.1 %norm2_back.1 = (f32[864,768]{1,0:T(8,128)}, bf16[864,768]{1,0:T(8,128)(2,1)}, bf16[864,768]{1,0:T(8,128)(2,1)}, f32[1,768]{1,0:T(1,128)}, f32[1,768]{1,0:T(1,128)}) custom-call(f32[864,768]{1,0:T(8,128)} %get-tuple-element.173.dc_ref, f32[864,768]{1,0:T(8,128)} %get-tuple-element.163.h1_ref, f32[864,768]{1,0:T(8,128)} %get-tuple-element.333.dh2_ref, ...), custom_call_target="tpu_custom_call" | custom-call | flops 1019215872 | bytes 14450688 | tf_op jit(solution)/shard_map/norm2_back/pallas_call | solution.py:559
  257.7 2.2 fusion.98
  261.9 3.7 collective-permute-start.36
  267.1 4.2 add_convert_fusion
  273.0 3.6 collective-permute-start.38
  276.7 33.6 %attn_bwd.1.d_ref = bf16[3,864,768]{2,1,0:T(8,128)(2,1)} custom-call(bf16[864,2304]{1,0:T(8,128)(2,1)} %project.1.q_ref.k_ref.v_ref, bf16[864,2304]{1,0:T(8,128)(2,1)} %project.1.q_ref.k_ref.v_ref, bf16[864,2304]{1,0:T(8,128)(2,1)} %project.1.q_ref.k_ref.v_ref, bf16[864,768]{1,0:T(8,128)(2,1)} %get-tuple-element.186.do_ref, ...), custom_call_target="tpu_custom_call" | custom-call | flops 22932357120 | bytes 10616832 | tf_op jit(solution)/shard_map/attn_bwd/pallas_call | solution.py:237
  313.3 2.2 convolution_convert_fusion
  315.8 2.0 fusion.39
  317.8 2.0 fusion.38
  319.8 10.5 %qkvo_grad.1 = (bf16[4,4,96,768]{3,2,1,0:T(8,128)(2,1)}, bf16[4,4,96,768]{3,2,1,0:T(8,128)(2,1)}) custom-call(s32[3]{0:T(128)} %pad_add_fusion.pos_ref, bf16[864,768]{1,0:T(8,128)(2,1)} %get-tuple-element.139.a_ref, bf16[3,864,768]{2,1,0:T(8,128)(2,1)} %attn_bwd.1.d_ref, bf16[864,768]{1,0:T(8,128)(2,1)} %get-tuple-element.147.o_ref, ...), custom_call_target="tpu_custom_call" | custom-call | flops 4076863488 | bytes 12681216 | tf_op jit(solution)/shard_map/qkvo_grad/pallas_call | solution.py:402
  330.4 2.3 collective-permute-start.39
  334.7 8.8 %norm1_back.1 = (bf16[864,768]{1,0:T(8,128)(2,1)}, f32[1,768]{1,0:T(1,128)}, f32[1,768]{1,0:T(1,128)}) custom-call(bf16[3,864,768]{2,1,0:T(8,128)(2,1)} %attn_bwd.1.d_ref, bf16[8,4,96,768]{3,2,1,0:T(8,128)(2,1)} %place.2.w_ref, f32[864,768]{1,0:T(8,128)} %get-tuple-element.148.h0_ref, f32[864,768]{1,0:T(8,128)} %get-tuple-element.200.dh1_ref, ...), custom_call_target="tpu_custom_call" | custom-call | flops 3057647616 | bytes 14155776 | tf_op jit(solution)/shard_map/norm1_back/pallas_call | solution.py:588
  343.5 1.8 fusion.84
  345.4 2.7 collective-permute-done.40
  353.1 2.9 fusion.37
  359.5 7.3 %patch_grad.1 = (bf16[4,4,64,768]{3,2,1,0:T(8,128)(2,1)}, bf16[4,4,64,768]{3,2,1,0:T(8,128)(2,1)}) custom-call(s32[3]{0:T(128)} %pad_add_fusion.pos_ref, bf16[864,1536]{1,0:T(8,128)(2,1)} %get-tuple-element.209.ext_ref, bf16[864,768]{1,0:T(8,128)(2,1)} %get-tuple-element.210.demb_ref, f32[1,3072]{1,0:T(1,128)} %get-tuple-element.211.bias_ref, ...), custom_call_target="tpu_custom_call" | custom-call | flops 2038431744 | bytes 6340608 | tf_op jit(solution)/shard_map/patch_grad/pallas_call | solution.py:449
  369.9 2.6 collective-permute-done.42
  372.5 3.4 collective-permute-start.47
  376.0 7.0 %collective-permute-done.43 = bf16[4,96,768]{2,1,0:T(8,128)(2,1)} collective-permute-done((bf16[4,96,768]{2,1,0:T(8,128)(2,1)}, bf16[4,96,768]{2,1,0:T(8,128)(2,1)}, u32[]{:S(2)}, u32[]{:S(2)}) %collective-permute-start.43) | collective-permute-done | bytes 589856 | tf_op jit(solution)/shard_map/ppermute | solution.py:758
  383.0 3.1 collective-permute-done.44
  386.1 2.0 fusion.23
  392.0 3.0 collective-permute-start.49
  395.3 2.8 fusion.44
  398.1 2.6 collective-permute-start.50
  400.7 3.2 collective-permute-start.51
  405.3 5.7 %pixel_back.1 = f32[384,1536]{1,0:T(8,128)} custom-call(bf16[384,768]{1,0:T(8,128)(2,1)} %fusion.12.d_ref, bf16[8,208,768]{2,1,0:T(8,128)(2,1)} %bitcast.236, f32[384,1]{1,0:T(8,128)} %convert_element_type.689.shown_ref), custom_call_target="tpu_custom_call" | custom-call | flops 905969664 | bytes 4718592 | tf_op jit(solution)/shard_map/pixel_back/pallas_call | solution.py:472
  411.1 11.0 %collective-permute-done.51 = bf16[4,64,768]{2,1,0:T(8,128)(2,1)} collective-permute-done((bf16[4,64,768]{2,1,0:T(8,128)(2,1)}, bf16[4,64,768]{2,1,0:T(8,128)(2,1)}, u32[]{:S(2)}, u32[]{:S(2)}) %collective-permute-start.51) | collective-permute-done | bytes 393248 | tf_op jit(solution)/shard_map/ppermute | solution.py:758
  424.8 1.8 collective-permute-start.53
  430.2 5.5 %collective-permute-done.53 = bf16[160,768]{1,0:T(8,128)(2,1)S(1)} collective-permute-done((bf16[160,768]{1,0:T(8,128)(2,1)}, bf16[160,768]{1,0:T(8,128)(2,1)S(1)}, u32[]{:S(2)}, u32[]{:S(2)}) %collective-permute-start.53) | collective-permute-done | bytes 245792 | tf_op jit(solution)/shard_map/ppermute | solution.py:763
  435.9 1.8 fusion
  437.7 7.9 %collective-permute-done.54 = bf16[160,768]{1,0:T(8,128)(2,1)S(1)} collective-permute-done((bf16[160,768]{1,0:T(8,128)(2,1)}, bf16[160,768]{1,0:T(8,128)(2,1)S(1)}, u32[]{:S(2)}, u32[]{:S(2)}) %collective-permute-start.54) | collective-permute-done | bytes 245792 | tf_op jit(solution)/shard_map/ppermute | solution.py:763
  445.6 2.2 collective-permute-done.55
  451.5 5.3 %collective-permute-done.61 = bf16[384,768]{1,0:T(8,128)(2,1)} collective-permute-done((bf16[384,768]{1,0:T(8,128)(2,1)S(1)}, bf16[384,768]{1,0:T(8,128)(2,1)}, u32[]{:S(2)}, u32[]{:S(2)}) %collective-permute-start.61) | collective-permute-done | bytes 589856 | tf_op jit(solution)/shard_map/ppermute | solution.py:758
  (403 shorter events, 118.5 us)
Async XLA Ops:
  7.2 54.9 %all-gather.5.cloned.1.call-start = ((), (), s32[]{:S(2)}) async-start(), calls=%async_computation.6 | async-start | bytes 2875392 | tf_op jit(solution)/shard_map/all_gather | solution.py:848
  10.1 23.5 %collective-permute-start.2 = (bf16[96,768]{1,0:T(8,128)(2,1)}, bf16[96,768]{1,0:T(8,128)(2,1)}, u32[]{:S(2)}, u32[]{:S(2)}) collective-permute-start(bf16[96,768]{1,0:T(8,128)(2,1)} %constant_dynamic-slice_fusion.7), channel_id=1, source_target_pairs={{0,2},{1,3},{2,4},{3,5},{4,6},{5,7},{6,0},{7,1},{8,10},{9,11},{10,... | collective-permute-start | bytes 442376 | tf_op jit(solution)/shard_map/ppermute | solution.py:763
  13.1 20.5 %collective-permute-start.3 = (bf16[96,768]{1,0:T(8,128)(2,1)}, bf16[96,768]{1,0:T(8,128)(2,1)}, u32[]{:S(2)}, u32[]{:S(2)}) collective-permute-start(bf16[96,768]{1,0:T(8,128)(2,1)} %constant_dynamic-slice_fusion.7), channel_id=1, source_target_pairs={{0,4},{1,5},{2,6},{3,7},{4,0},{5,1},{6,2},{7,3},{8,12},{9,13},{10,... | collective-permute-start | bytes 442376 | tf_op jit(solution)/shard_map/ppermute | solution.py:763
  15.7 17.9 %collective-permute-start.4 = (bf16[96,768]{1,0:T(8,128)(2,1)}, bf16[96,768]{1,0:T(8,128)(2,1)}, u32[]{:S(2)}, u32[]{:S(2)}) collective-permute-start(bf16[96,768]{1,0:T(8,128)(2,1)} %constant_dynamic-slice_fusion.7), channel_id=1, source_target_pairs={{0,6},{1,7},{2,0},{3,1},{4,2},{5,3},{6,4},{7,5},{8,14},{9,15},{10,... | collective-permute-start | bytes 442376 | tf_op jit(solution)/shard_map/ppermute | solution.py:763
  22.9 12.6 %collective-permute-start.1 = (bf16[112,1536]{1,0:T(8,128)(2,1)}, bf16[112,1536]{1,0:T(8,128)(2,1)}, u32[]{:S(2)}, u32[]{:S(2)}) collective-permute-start(bf16[112,1536]{1,0:T(8,128)(2,1)} %fusion.50), channel_id=1, source_target_pairs={{0,1},{1,2},{2,3},{3,4},{4,5},{5,6},{6,7},{8,9},{9,10},{10,11},{11... | collective-permute-start | bytes 1032200 | tf_op jit(solution)/shard_map/ppermute | solution.py:649
  25.9 9.6 %collective-permute-start = (bf16[112,1536]{1,0:T(8,128)(2,1)}, bf16[112,1536]{1,0:T(8,128)(2,1)}, u32[]{:S(2)}, u32[]{:S(2)}) collective-permute-start(bf16[112,1536]{1,0:T(8,128)(2,1)} %fusion.49), channel_id=1, source_target_pairs={{1,0},{2,1},{3,2},{4,3},{5,4},{6,5},{7,6},{9,8},{10,9},{11,10},{12... | collective-permute-start | bytes 1032200 | tf_op jit(solution)/shard_map/ppermute | solution.py:649
  28.1 110.8 %all-gather.7.cloned.1.call-start = ((), (), s32[]{:S(2)}) async-start(), calls=%async_computation.7 | async-start | bytes 2654208 | tf_op jit(solution)/shard_map/all_gather | solution.py:848
  40.4 15.9 %collective-permute-start.6 = (bf16[160,1536]{1,0:T(8,128)(2,1)S(1)}, bf16[160,1536]{1,0:T(8,128)(2,1)}, u32[]{:S(2)}, u32[]{:S(2)}) collective-permute-start(bf16[160,1536]{1,0:T(8,128)(2,1)S(1)} %fusion.41), channel_id=1, source_target_pairs={{8,0},{16,8},{24,16},{9,1},{17,9},{25,17},{10,2},{18,10},{26,18},{... | collective-permute-start | bytes 1474568 | tf_op jit(solution)/shard_map/ppermute | solution.py:649
  42.0 16.2 %collective-permute-start.5 = (bf16[160,1536]{1,0:T(8,128)(2,1)S(1)}, bf16[160,1536]{1,0:T(8,128)(2,1)}, u32[]{:S(2)}, u32[]{:S(2)}) collective-permute-start(bf16[160,1536]{1,0:T(8,128)(2,1)S(1)} %fusion.40), channel_id=1, source_target_pairs={{0,8},{8,16},{16,24},{1,9},{9,17},{17,25},{2,10},{10,18},{18,26},{... | collective-permute-start | bytes 1474568 | tf_op jit(solution)/shard_map/ppermute | solution.py:649
  62.2 11.2 %collective-permute-start.7 = (bf16[192,768]{1,0:T(8,128)(2,1)}, bf16[192,768]{1,0:T(8,128)(2,1)S(1)}, u32[]{:S(2)}, u32[]{:S(2)}) collective-permute-start(bf16[192,768]{1,0:T(8,128)(2,1)} %pad_maximum_fusion.5), channel_id=1, source_target_pairs={{0,2},{1,3},{2,4},{3,5},{4,6},{5,7},{6,0},{7,1},{8,10},{9,11},{10,... | collective-permute-start | bytes 884744 | tf_op jit(solution)/shard_map/ppermute | solution.py:763
  63.8 24.0 %collective-permute-start.10 = (bf16[3,96,768]{2,1,0:T(8,128)(2,1)S(1)}, bf16[3,96,768]{2,1,0:T(8,128)(2,1)}, u32[]{:S(2)}, u32[]{:S(2)}) collective-permute-start(bf16[3,96,768]{2,1,0:T(8,128)(2,1)S(1)} %copy-done.8), channel_id=1, source_target_pairs={{0,8},{8,0},{16,24},{24,16},{1,9},{9,1},{17,25},{25,17},{2,10},{10... | collective-permute-start | bytes 1327112 | tf_op jit(solution)/shard_map/ppermute | solution.py:758
  68.2 21.2 %collective-permute-start.11 = (bf16[3,96,768]{2,1,0:T(8,128)(2,1)S(1)}, bf16[3,96,768]{2,1,0:T(8,128)(2,1)}, u32[]{:S(2)}, u32[]{:S(2)}) collective-permute-start(bf16[3,96,768]{2,1,0:T(8,128)(2,1)S(1)} %copy-done.8), channel_id=1, source_target_pairs={{0,16},{8,24},{16,0},{24,8},{1,17},{9,25},{17,1},{25,9},{2,18},{10... | collective-permute-start | bytes 1327112 | tf_op jit(solution)/shard_map/ppermute | solution.py:758
  71.6 18.7 %collective-permute-start.12 = (bf16[3,96,768]{2,1,0:T(8,128)(2,1)S(1)}, bf16[3,96,768]{2,1,0:T(8,128)(2,1)}, u32[]{:S(2)}, u32[]{:S(2)}) collective-permute-start(bf16[3,96,768]{2,1,0:T(8,128)(2,1)S(1)} %copy-done.8), channel_id=1, source_target_pairs={{0,24},{8,16},{16,8},{24,0},{1,25},{9,17},{17,9},{25,1},{2,26},{10... | collective-permute-start | bytes 1327112 | tf_op jit(solution)/shard_map/ppermute | solution.py:758
  71.7 15.8 %collective-permute-start.8 = (bf16[192,768]{1,0:T(8,128)(2,1)}, bf16[192,768]{1,0:T(8,128)(2,1)S(1)}, u32[]{:S(2)}, u32[]{:S(2)}) collective-permute-start(bf16[192,768]{1,0:T(8,128)(2,1)} %pad_maximum_fusion.5), channel_id=1, source_target_pairs={{0,4},{1,5},{2,6},{3,7},{4,0},{5,1},{6,2},{7,3},{8,12},{9,13},{10,... | collective-permute-start | bytes 884744 | tf_op jit(solution)/shard_map/ppermute | solution.py:763
  73.4 14.2 %collective-permute-start.9 = (bf16[192,768]{1,0:T(8,128)(2,1)}, bf16[192,768]{1,0:T(8,128)(2,1)S(1)}, u32[]{:S(2)}, u32[]{:S(2)}) collective-permute-start(bf16[192,768]{1,0:T(8,128)(2,1)} %pad_maximum_fusion.5), channel_id=1, source_target_pairs={{0,6},{1,7},{2,0},{3,1},{4,2},{5,3},{6,4},{7,5},{8,14},{9,15},{10,... | collective-permute-start | bytes 884744 | tf_op jit(solution)/shard_map/ppermute | solution.py:763
  87.5 12.7 %collective-permute-start.13 = (bf16[96,3072]{1,0:T(8,128)(2,1)S(1)}, bf16[96,3072]{1,0:T(8,128)(2,1)}, u32[]{:S(2)}, u32[]{:S(2)}) collective-permute-start(bf16[96,3072]{1,0:T(8,128)(2,1)S(1)} %constant_dynamic-update-slice_fusion.refs_0_), channel_id=1, source_target_pairs={{0,1},{1,0},{2,3},{3,2},{4,5},{5,4},{6,7},{7,6},{8,9},{9,8},{10,11... | collective-permute-start | bytes 1769480 | tf_op jit(solution)/shard_map/ppermute | solution.py:758
  90.3 277.3 %reduce-scatter.6.cloned.1.call-start = ((), (), s32[]{:S(2)}) async-start(), calls=%async_computation.4 | async-start | bytes 884736 | tf_op jit(solution)/shard_map/reduce_scatter | solution.py:863
  95.0 5.2 %collective-permute-start.14 = (bf16[3,96,768]{2,1,0:T(8,128)(2,1)S(1)}, bf16[3,96,768]{2,1,0:T(8,128)(2,1)S(1)}, u32[]{:S(2)}, u32[]{:S(2)}) collective-permute-start(bf16[3,96,768]{2,1,0:T(8,128)(2,1)S(1)} %copy-done.8), channel_id=1, source_target_pairs={{0,1},{1,0},{2,3},{3,2},{4,5},{5,4},{6,7},{7,6},{8,9},{9,8},{10,11... | collective-permute-start | bytes 1327112 | tf_op jit(solution)/shard_map/ppermute | solution.py:758
  95.0 5.2 %collective-permute-start.17 = (bf16[3,96,768]{2,1,0:T(8,128)(2,1)}, bf16[3,96,768]{2,1,0:T(8,128)(2,1)}, u32[]{:S(2)}, u32[]{:S(2)}) collective-permute-start(bf16[3,96,768]{2,1,0:T(8,128)(2,1)} %collective-permute-done.12.refs_4_), channel_id=1, source_target_pairs={{0,1},{1,0},{2,3},{3,2},{4,5},{5,4},{6,7},{7,6},{8,9},{9,8},{10,11... | collective-permute-start | bytes 1327112 | tf_op jit(solution)/shard_map/ppermute | solution.py:758
  106.7 39.3 %collective-permute-start.18 = (bf16[3,192,768]{2,1,0:T(8,128)(2,1)S(1)}, bf16[3,192,768]{2,1,0:T(8,128)(2,1)}, u32[]{:S(2)}, u32[]{:S(2)}) collective-permute-start(bf16[3,192,768]{2,1,0:T(8,128)(2,1)S(1)} %pad_maximum_fusion.3.refs_2_), channel_id=1, source_target_pairs={{0,8},{8,0},{16,24},{24,16},{1,9},{9,1},{17,25},{25,17},{2,10},{10... | collective-permute-start | bytes 2654216 | tf_op jit(solution)/shard_map/ppermute | solution.py:758
  109.2 40.4 %collective-permute-start.19 = (bf16[3,192,768]{2,1,0:T(8,128)(2,1)S(1)}, bf16[3,192,768]{2,1,0:T(8,128)(2,1)}, u32[]{:S(2)}, u32[]{:S(2)}) collective-permute-start(bf16[3,192,768]{2,1,0:T(8,128)(2,1)S(1)} %pad_maximum_fusion.3.refs_2_), channel_id=1, source_target_pairs={{0,16},{8,24},{16,0},{24,8},{1,17},{9,25},{17,1},{25,9},{2,18},{10... | collective-permute-start | bytes 2654216 | tf_op jit(solution)/shard_map/ppermute | solution.py:758
  111.9 38.6 %collective-permute-start.20 = (bf16[3,192,768]{2,1,0:T(8,128)(2,1)S(1)}, bf16[3,192,768]{2,1,0:T(8,128)(2,1)}, u32[]{:S(2)}, u32[]{:S(2)}) collective-permute-start(bf16[3,192,768]{2,1,0:T(8,128)(2,1)S(1)} %pad_maximum_fusion.3.refs_2_), channel_id=1, source_target_pairs={{0,24},{8,16},{16,8},{24,0},{1,25},{9,17},{17,9},{25,1},{2,26},{10... | collective-permute-start | bytes 2654216 | tf_op jit(solution)/shard_map/ppermute | solution.py:758
  150.5 7.0 %collective-permute-start.26 = (bf16[3,192,768]{2,1,0:T(8,128)(2,1)}, bf16[3,192,768]{2,1,0:T(8,128)(2,1)}, u32[]{:S(2)}, u32[]{:S(2)}) collective-permute-start(bf16[3,192,768]{2,1,0:T(8,128)(2,1)} %collective-permute-done.20.refs_5_), channel_id=1, source_target_pairs={{0,1},{1,0},{2,3},{3,2},{4,5},{5,4},{6,7},{7,6},{8,9},{9,8},{10,11... | collective-permute-start | bytes 2654216 | tf_op jit(solution)/shard_map/ppermute | solution.py:758
  151.0 5.2 %collective-permute-start.22 = (bf16[384,768]{1,0:T(8,128)(2,1)}, bf16[384,768]{1,0:T(8,128)(2,1)}, u32[]{:S(2)}, u32[]{:S(2)}) collective-permute-start(bf16[384,768]{1,0:T(8,128)(2,1)} %refs_1_), channel_id=1, source_target_pairs={{0,1},{1,0},{2,3},{3,2},{4,5},{5,4},{6,7},{7,6},{8,9},{9,8},{10,11... | collective-permute-start | bytes 1769480 | tf_op jit(solution)/shard_map/ppermute | solution.py:758
  151.0 15.9 %collective-permute-start.23 = (bf16[3,192,768]{2,1,0:T(8,128)(2,1)S(1)}, bf16[3,192,768]{2,1,0:T(8,128)(2,1)}, u32[]{:S(2)}, u32[]{:S(2)}) collective-permute-start(bf16[3,192,768]{2,1,0:T(8,128)(2,1)S(1)} %pad_maximum_fusion.3.refs_2_), channel_id=1, source_target_pairs={{0,1},{1,0},{2,3},{3,2},{4,5},{5,4},{6,7},{7,6},{8,9},{9,8},{10,11... | collective-permute-start | bytes 2654216 | tf_op jit(solution)/shard_map/ppermute | solution.py:758
  151.5 15.4 %collective-permute-start.24 = (bf16[3,192,768]{2,1,0:T(8,128)(2,1)}, bf16[3,192,768]{2,1,0:T(8,128)(2,1)}, u32[]{:S(2)}, u32[]{:S(2)}) collective-permute-start(bf16[3,192,768]{2,1,0:T(8,128)(2,1)} %collective-permute-done.18.refs_3_), channel_id=1, source_target_pairs={{0,1},{1,0},{2,3},{3,2},{4,5},{5,4},{6,7},{7,6},{8,9},{9,8},{10,11... | collective-permute-start | bytes 2654216 | tf_op jit(solution)/shard_map/ppermute | solution.py:758
  154.1 12.8 %collective-permute-start.25 = (bf16[3,192,768]{2,1,0:T(8,128)(2,1)}, bf16[3,192,768]{2,1,0:T(8,128)(2,1)}, u32[]{:S(2)}, u32[]{:S(2)}) collective-permute-start(bf16[3,192,768]{2,1,0:T(8,128)(2,1)} %collective-permute-done.19.refs_4_), channel_id=1, source_target_pairs={{0,1},{1,0},{2,3},{3,2},{4,5},{5,4},{6,7},{7,6},{8,9},{9,8},{10,11... | collective-permute-start | bytes 2654216 | tf_op jit(solution)/shard_map/ppermute | solution.py:758
  156.2 19.5 %collective-permute-start.27 = (bf16[96,512]{1,0:T(8,128)(2,1)}, bf16[96,512]{1,0:T(8,128)(2,1)S(1)}, u32[]{:S(2)}, u32[]{:S(2)}) collective-permute-start(bf16[96,512]{1,0:T(8,128)(2,1)} %get-tuple-element.157), channel_id=1, source_target_pairs={{1,0},{2,1},{3,2},{4,3},{5,4},{6,5},{7,6},{9,8},{10,9},{11,10},{12... | collective-permute-start | bytes 294920 | tf_op jit(solution)/shard_map/ppermute | solution.py:649
  157.5 18.2 %collective-permute-start.28 = (bf16[96,512]{1,0:T(8,128)(2,1)}, bf16[96,512]{1,0:T(8,128)(2,1)S(1)}, u32[]{:S(2)}, u32[]{:S(2)}) collective-permute-start(bf16[96,512]{1,0:T(8,128)(2,1)} %get-tuple-element.158), channel_id=1, source_target_pairs={{0,1},{1,2},{2,3},{3,4},{4,5},{5,6},{6,7},{8,9},{9,10},{10,11},{11... | collective-permute-start | bytes 294920 | tf_op jit(solution)/shard_map/ppermute | solution.py:649
  197.5 7.0 %collective-permute-start.31 = (bf16[144,512]{1,0:T(8,128)(2,1)S(1)}, bf16[144,512]{1,0:T(8,128)(2,1)S(1)}, u32[]{:S(2)}, u32[]{:S(2)}) collective-permute-start(bf16[144,512]{1,0:T(8,128)(2,1)S(1)} %get-tuple-element.166), channel_id=1, source_target_pairs={{8,0},{16,8},{24,16},{9,1},{17,9},{25,17},{10,2},{18,10},{26,18},{... | collective-permute-start | bytes 442376 | tf_op jit(solution)/shard_map/ppermute | solution.py:649
  198.8 7.2 %collective-permute-start.32 = (bf16[144,512]{1,0:T(8,128)(2,1)S(1)}, bf16[144,512]{1,0:T(8,128)(2,1)S(1)}, u32[]{:S(2)}, u32[]{:S(2)}) collective-permute-start(bf16[144,512]{1,0:T(8,128)(2,1)S(1)} %get-tuple-element.167), channel_id=1, source_target_pairs={{0,8},{8,16},{16,24},{1,9},{9,17},{17,25},{2,10},{10,18},{18,26},{... | collective-permute-start | bytes 442376 | tf_op jit(solution)/shard_map/ppermute | solution.py:649
  235.0 30.7 %collective-permute-start.35 = (bf16[4,4,96,768]{3,2,1,0:T(8,128)(2,1)}, bf16[4,4,96,768]{3,2,1,0:T(8,128)(2,1)}, u32[]{:S(2)}, u32[]{:S(2)}) collective-permute-start(bf16[4,4,96,768]{3,2,1,0:T(8,128)(2,1)} %get-tuple-element.184), channel_id=1, source_target_pairs={{0,1},{1,0},{2,3},{3,2},{4,5},{5,4},{6,7},{7,6},{8,9},{9,8},{10,11... | collective-permute-start | bytes 7077896 | tf_op jit(solution)/shard_map/ppermute | solution.py:758
  238.4 27.3 %collective-permute-start.34 = (bf16[4,4,96,768]{3,2,1,0:T(8,128)(2,1)}, bf16[4,4,96,768]{3,2,1,0:T(8,128)(2,1)S(1)}, u32[]{:S(2)}, u32[]{:S(2)}) collective-permute-start(bf16[4,4,96,768]{3,2,1,0:T(8,128)(2,1)} %get-tuple-element.181), channel_id=1, source_target_pairs={{0,1},{1,0},{2,3},{3,2},{4,5},{5,4},{6,7},{7,6},{8,9},{9,8},{10,11... | collective-permute-start | bytes 7077896 | tf_op jit(solution)/shard_map/ppermute | solution.py:758
  238.5 17.9 %collective-permute-start.29 = (bf16[144,512]{1,0:T(8,128)(2,1)}, bf16[144,512]{1,0:T(8,128)(2,1)}, u32[]{:S(2)}, u32[]{:S(2)}) collective-permute-start(bf16[144,512]{1,0:T(8,128)(2,1)} %get-tuple-element.297), channel_id=1, source_target_pairs={{8,0},{16,8},{24,16},{9,1},{17,9},{25,17},{10,2},{18,10},{26,18},{... | collective-permute-start | bytes 442376 | tf_op jit(solution)/shard_map/ppermute | solution.py:649
  239.7 16.7 %collective-permute-start.30 = (bf16[144,512]{1,0:T(8,128)(2,1)}, bf16[144,512]{1,0:T(8,128)(2,1)}, u32[]{:S(2)}, u32[]{:S(2)}) collective-permute-start(bf16[144,512]{1,0:T(8,128)(2,1)} %get-tuple-element.296), channel_id=1, source_target_pairs={{0,8},{8,16},{16,24},{1,9},{9,17},{17,25},{2,10},{10,18},{18,26},{... | collective-permute-start | bytes 442376 | tf_op jit(solution)/shard_map/ppermute | solution.py:649
  260.6 49.6 %collective-permute-start.33 = (bf16[96,512]{1,0:T(8,128)(2,1)}, bf16[96,512]{1,0:T(8,128)(2,1)}, u32[]{:S(2)}, u32[]{:S(2)}) collective-permute-start(bf16[96,512]{1,0:T(8,128)(2,1)} %get-tuple-element.178), channel_id=1, source_target_pairs={{1,0},{2,1},{3,2},{4,3},{5,4},{6,5},{7,6},{9,8},{10,9},{11,10},{12... | collective-permute-start | bytes 294920 | tf_op jit(solution)/shard_map/ppermute | solution.py:649
  261.9 48.4 %collective-permute-start.36 = (bf16[96,512]{1,0:T(8,128)(2,1)}, bf16[96,512]{1,0:T(8,128)(2,1)}, u32[]{:S(2)}, u32[]{:S(2)}) collective-permute-start(bf16[96,512]{1,0:T(8,128)(2,1)} %get-tuple-element.189), channel_id=1, source_target_pairs={{0,1},{1,2},{2,3},{3,4},{4,5},{5,6},{6,7},{8,9},{9,10},{10,11},{11... | collective-permute-start | bytes 294920 | tf_op jit(solution)/shard_map/ppermute | solution.py:649
  265.6 102.0 %reduce-scatter.8.cloned.1.call-start = ((), (), s32[]{:S(2)}) async-start(), calls=%async_computation.5 | async-start | bytes 1769472 | tf_op jit(solution)/shard_map/reduce_scatter | solution.py:863
  273.0 42.8 %collective-permute-start.38 = (bf16[2,4,96,768]{3,2,1,0:T(8,128)(2,1)}, bf16[2,4,96,768]{3,2,1,0:T(8,128)(2,1)}, u32[]{:S(2)}, u32[]{:S(2)}) collective-permute-start(bf16[2,4,96,768]{3,2,1,0:T(8,128)(2,1)} %get-tuple-element.194), channel_id=1, source_target_pairs={{0,16},{8,24},{16,0},{24,8},{1,17},{9,25},{17,1},{25,9},{2,18},{10... | collective-permute-start | bytes 3538952 | tf_op jit(solution)/shard_map/ppermute | solution.py:758
  276.6 41.1 %collective-permute-start.37 = (bf16[2,4,96,768]{3,2,1,0:T(8,128)(2,1)}, bf16[2,4,96,768]{3,2,1,0:T(8,128)(2,1)}, u32[]{:S(2)}, u32[]{:S(2)}) collective-permute-start(bf16[2,4,96,768]{3,2,1,0:T(8,128)(2,1)} %get-tuple-element.192), channel_id=1, source_target_pairs={{0,8},{8,0},{16,24},{24,16},{1,9},{9,1},{17,25},{25,17},{2,10},{10... | collective-permute-start | bytes 3538952 | tf_op jit(solution)/shard_map/ppermute | solution.py:758
  315.5 89.8 %reduce-scatter.4.cloned.1.call-start = ((), (), s32[]{:S(2)}) async-start(), calls=%async_computation.3 | async-start | bytes 1474560 | tf_op jit(solution)/shard_map/reduce_scatter | solution.py:820
  330.4 21.7 %collective-permute-start.39 = (bf16[4,4,96,768]{3,2,1,0:T(8,128)(2,1)}, bf16[4,4,96,768]{3,2,1,0:T(8,128)(2,1)}, u32[]{:S(2)}, u32[]{:S(2)}) collective-permute-start(bf16[4,4,96,768]{3,2,1,0:T(8,128)(2,1)} %get-tuple-element.199), channel_id=1, source_target_pairs={{0,1},{1,0},{2,3},{3,2},{4,5},{5,4},{6,7},{7,6},{8,9},{9,8},{10,11... | collective-permute-start | bytes 7077896 | tf_op jit(solution)/shard_map/ppermute | solution.py:758
  332.6 15.4 %collective-permute-start.40 = (bf16[4,96,768]{2,1,0:T(8,128)(2,1)}, bf16[4,96,768]{2,1,0:T(8,128)(2,1)S(1)}, u32[]{:S(2)}, u32[]{:S(2)}) collective-permute-start(bf16[4,96,768]{2,1,0:T(8,128)(2,1)} %fusion.38), channel_id=1, source_target_pairs={{0,16},{8,24},{16,0},{24,8},{1,17},{9,25},{17,1},{25,9},{2,18},{10... | collective-permute-start | bytes 1769480 | tf_op jit(solution)/shard_map/ppermute | solution.py:758
  333.2 15.2 %collective-permute-start.41 = (bf16[4,96,768]{2,1,0:T(8,128)(2,1)}, bf16[4,96,768]{2,1,0:T(8,128)(2,1)S(1)}, u32[]{:S(2)}, u32[]{:S(2)}) collective-permute-start(bf16[4,96,768]{2,1,0:T(8,128)(2,1)} %fusion.39), channel_id=1, source_target_pairs={{0,8},{8,0},{16,24},{24,16},{1,9},{9,1},{17,25},{25,17},{2,10},{10... | collective-permute-start | bytes 1769480 | tf_op jit(solution)/shard_map/ppermute | solution.py:758
  356.0 16.6 %collective-permute-start.42 = (bf16[4,96,768]{2,1,0:T(8,128)(2,1)}, bf16[4,96,768]{2,1,0:T(8,128)(2,1)}, u32[]{:S(2)}, u32[]{:S(2)}) collective-permute-start(bf16[4,96,768]{2,1,0:T(8,128)(2,1)} %get-tuple-element.208), channel_id=1, source_target_pairs={{0,8},{8,0},{16,24},{24,16},{1,9},{9,1},{17,25},{25,17},{2,10},{10... | collective-permute-start | bytes 1769480 | tf_op jit(solution)/shard_map/ppermute | solution.py:758
  357.5 25.5 %collective-permute-start.43 = (bf16[4,96,768]{2,1,0:T(8,128)(2,1)}, bf16[4,96,768]{2,1,0:T(8,128)(2,1)}, u32[]{:S(2)}, u32[]{:S(2)}) collective-permute-start(bf16[4,96,768]{2,1,0:T(8,128)(2,1)} %get-tuple-element.218), channel_id=1, source_target_pairs={{0,16},{8,24},{16,0},{24,8},{1,17},{9,25},{17,1},{25,9},{2,18},{10... | collective-permute-start | bytes 1769480 | tf_op jit(solution)/shard_map/ppermute | solution.py:758
  359.1 27.0 %collective-permute-start.44 = (bf16[4,96,768]{2,1,0:T(8,128)(2,1)S(1)}, bf16[4,96,768]{2,1,0:T(8,128)(2,1)}, u32[]{:S(2)}, u32[]{:S(2)}) collective-permute-start(bf16[4,96,768]{2,1,0:T(8,128)(2,1)S(1)} %get-tuple-element.220), channel_id=1, source_target_pairs={{0,24},{8,16},{16,8},{24,0},{1,25},{9,17},{17,9},{25,1},{2,26},{10... | collective-permute-start | bytes 1769480 | tf_op jit(solution)/shard_map/ppermute | solution.py:758
  366.8 28.5 %collective-permute-start.45 = (bf16[4,4,64,768]{3,2,1,0:T(8,128)(2,1)}, bf16[4,4,64,768]{3,2,1,0:T(8,128)(2,1)}, u32[]{:S(2)}, u32[]{:S(2)}) collective-permute-start(bf16[4,4,64,768]{3,2,1,0:T(8,128)(2,1)} %get-tuple-element.222), channel_id=1, source_target_pairs={{0,1},{1,0},{2,3},{3,2},{4,5},{5,4},{6,7},{7,6},{8,9},{9,8},{10,11... | collective-permute-start | bytes 4718600 | tf_op jit(solution)/shard_map/ppermute | solution.py:758
  368.6 21.2 %collective-permute-start.46 = (bf16[144,768]{1,0:T(8,128)(2,1)}, bf16[144,768]{1,0:T(8,128)(2,1)S(1)}, u32[]{:S(2)}, u32[]{:S(2)}) collective-permute-start(bf16[144,768]{1,0:T(8,128)(2,1)} %get-tuple-element.224), channel_id=1, source_target_pairs={{8,0},{16,8},{24,16},{9,1},{17,9},{25,17},{10,2},{18,10},{26,18},{... | collective-permute-start | bytes 663560 | tf_op jit(solution)/shard_map/ppermute | solution.py:649
  372.5 17.3 %collective-permute-start.47 = (bf16[144,768]{1,0:T(8,128)(2,1)S(1)}, bf16[144,768]{1,0:T(8,128)(2,1)S(1)}, u32[]{:S(2)}, u32[]{:S(2)}) collective-permute-start(bf16[144,768]{1,0:T(8,128)(2,1)S(1)} %copy-done.44), channel_id=1, source_target_pairs={{0,8},{8,16},{16,24},{1,9},{9,17},{17,25},{2,10},{10,18},{18,26},{... | collective-permute-start | bytes 663560 | tf_op jit(solution)/shard_map/ppermute | solution.py:649
  390.7 7.4 %collective-permute-start.48 = (bf16[96,768]{1,0:T(8,128)(2,1)S(1)}, bf16[96,768]{1,0:T(8,128)(2,1)S(1)}, u32[]{:S(2)}, u32[]{:S(2)}) collective-permute-start(bf16[96,768]{1,0:T(8,128)(2,1)S(1)} %get-tuple-element.295), channel_id=1, source_target_pairs={{1,0},{2,1},{3,2},{4,3},{5,4},{6,5},{7,6},{9,8},{10,9},{11,10},{12... | collective-permute-start | bytes 442376 | tf_op jit(solution)/shard_map/ppermute | solution.py:649
  392.0 6.1 %collective-permute-start.49 = (bf16[96,768]{1,0:T(8,128)(2,1)S(1)}, bf16[96,768]{1,0:T(8,128)(2,1)S(1)}, u32[]{:S(2)}, u32[]{:S(2)}) collective-permute-start(bf16[96,768]{1,0:T(8,128)(2,1)S(1)} %get-tuple-element.294), channel_id=1, source_target_pairs={{0,1},{1,2},{2,3},{3,4},{4,5},{5,6},{6,7},{8,9},{9,10},{10,11},{11... | collective-permute-start | bytes 442376 | tf_op jit(solution)/shard_map/ppermute | solution.py:649
  398.1 13.0 %collective-permute-start.50 = (bf16[4,64,768]{2,1,0:T(8,128)(2,1)}, bf16[4,64,768]{2,1,0:T(8,128)(2,1)S(1)}, u32[]{:S(2)}, u32[]{:S(2)}) collective-permute-start(bf16[4,64,768]{2,1,0:T(8,128)(2,1)} %get-tuple-element.228), channel_id=1, source_target_pairs={{0,8},{8,0},{16,24},{24,16},{1,9},{9,1},{17,25},{25,17},{2,10},{10... | collective-permute-start | bytes 1179656 | tf_op jit(solution)/shard_map/ppermute | solution.py:758
  400.7 21.3 %collective-permute-start.51 = (bf16[4,64,768]{2,1,0:T(8,128)(2,1)}, bf16[4,64,768]{2,1,0:T(8,128)(2,1)}, u32[]{:S(2)}, u32[]{:S(2)}) collective-permute-start(bf16[4,64,768]{2,1,0:T(8,128)(2,1)} %get-tuple-element.234), channel_id=1, source_target_pairs={{0,16},{8,24},{16,0},{24,8},{1,17},{9,25},{17,1},{25,9},{2,18},{10... | collective-permute-start | bytes 1179656 | tf_op jit(solution)/shard_map/ppermute | solution.py:758
  403.9 18.3 %collective-permute-start.52 = (bf16[4,64,768]{2,1,0:T(8,128)(2,1)}, bf16[4,64,768]{2,1,0:T(8,128)(2,1)}, u32[]{:S(2)}, u32[]{:S(2)}) collective-permute-start(bf16[4,64,768]{2,1,0:T(8,128)(2,1)} %get-tuple-element.236), channel_id=1, source_target_pairs={{0,24},{8,16},{16,8},{24,0},{1,25},{9,17},{17,9},{25,1},{2,26},{10... | collective-permute-start | bytes 1179656 | tf_op jit(solution)/shard_map/ppermute | solution.py:758
  424.8 10.9 %collective-permute-start.53 = (bf16[160,768]{1,0:T(8,128)(2,1)}, bf16[160,768]{1,0:T(8,128)(2,1)S(1)}, u32[]{:S(2)}, u32[]{:S(2)}) collective-permute-start(bf16[160,768]{1,0:T(8,128)(2,1)} %get-tuple-element.290), channel_id=1, source_target_pairs={{0,2},{1,3},{2,4},{3,5},{4,6},{5,7},{6,0},{7,1},{8,10},{9,11},{10,... | collective-permute-start | bytes 737288 | tf_op jit(solution)/shard_map/ppermute | solution.py:763
  426.7 23.7 %collective-permute-start.59 = (bf16[384,768]{1,0:T(8,128)(2,1)S(1)}, bf16[384,768]{1,0:T(8,128)(2,1)}, u32[]{:S(2)}, u32[]{:S(2)}) collective-permute-start(bf16[384,768]{1,0:T(8,128)(2,1)S(1)} %constant_dynamic-update-slice_fusion.7), channel_id=1, source_target_pairs={{0,8},{8,0},{16,24},{24,16},{1,9},{9,1},{17,25},{25,17},{2,10},{10... | collective-permute-start | bytes 1769480 | tf_op jit(solution)/shard_map/ppermute | solution.py:758
  428.1 23.4 %collective-permute-start.60 = (bf16[384,768]{1,0:T(8,128)(2,1)S(1)}, bf16[384,768]{1,0:T(8,128)(2,1)}, u32[]{:S(2)}, u32[]{:S(2)}) collective-permute-start(bf16[384,768]{1,0:T(8,128)(2,1)S(1)} %constant_dynamic-update-slice_fusion.7), channel_id=1, source_target_pairs={{0,16},{8,24},{16,0},{24,8},{1,17},{9,25},{17,1},{25,9},{2,18},{10... | collective-permute-start | bytes 1769480 | tf_op jit(solution)/shard_map/ppermute | solution.py:758
  429.0 27.8 %collective-permute-start.61 = (bf16[384,768]{1,0:T(8,128)(2,1)S(1)}, bf16[384,768]{1,0:T(8,128)(2,1)}, u32[]{:S(2)}, u32[]{:S(2)}) collective-permute-start(bf16[384,768]{1,0:T(8,128)(2,1)S(1)} %constant_dynamic-update-slice_fusion.7), channel_id=1, source_target_pairs={{0,24},{8,16},{16,8},{24,0},{1,25},{9,17},{17,9},{25,1},{2,26},{10... | collective-permute-start | bytes 1769480 | tf_op jit(solution)/shard_map/ppermute | solution.py:758
  430.2 15.4 %collective-permute-start.54 = (bf16[160,768]{1,0:T(8,128)(2,1)}, bf16[160,768]{1,0:T(8,128)(2,1)S(1)}, u32[]{:S(2)}, u32[]{:S(2)}) collective-permute-start(bf16[160,768]{1,0:T(8,128)(2,1)} %get-tuple-element.292), channel_id=1, source_target_pairs={{0,4},{1,5},{2,6},{3,7},{4,0},{5,1},{6,2},{7,3},{8,12},{9,13},{10,... | collective-permute-start | bytes 737288 | tf_op jit(solution)/shard_map/ppermute | solution.py:763
  435.7 12.1 %collective-permute-start.55 = (bf16[160,768]{1,0:T(8,128)(2,1)}, bf16[160,768]{1,0:T(8,128)(2,1)S(1)}, u32[]{:S(2)}, u32[]{:S(2)}) collective-permute-start(bf16[160,768]{1,0:T(8,128)(2,1)} %get-tuple-element.293), channel_id=1, source_target_pairs={{0,6},{1,7},{2,0},{3,1},{4,2},{5,3},{6,4},{7,5},{8,14},{9,15},{10,... | collective-permute-start | bytes 737288 | tf_op jit(solution)/shard_map/ppermute | solution.py:763
  447.9 17.3 %collective-permute-start.56 = (bf16[160,768]{1,0:T(8,128)(2,1)S(1)}, bf16[160,768]{1,0:T(8,128)(2,1)S(1)}, u32[]{:S(2)}, u32[]{:S(2)}) collective-permute-start(bf16[160,768]{1,0:T(8,128)(2,1)S(1)} %add_convert_fusion.11), channel_id=1, source_target_pairs={{0,8},{8,0},{16,24},{24,16},{1,9},{9,1},{17,25},{25,17},{2,10},{10... | collective-permute-start | bytes 737288 | tf_op jit(solution)/shard_map/ppermute | solution.py:758
  449.3 15.9 %collective-permute-start.57 = (bf16[160,768]{1,0:T(8,128)(2,1)S(1)}, bf16[160,768]{1,0:T(8,128)(2,1)S(1)}, u32[]{:S(2)}, u32[]{:S(2)}) collective-permute-start(bf16[160,768]{1,0:T(8,128)(2,1)S(1)} %add_convert_fusion.11), channel_id=1, source_target_pairs={{0,16},{8,24},{16,0},{24,8},{1,17},{9,25},{17,1},{25,9},{2,18},{10... | collective-permute-start | bytes 737288 | tf_op jit(solution)/shard_map/ppermute | solution.py:758
  450.4 14.8 %collective-permute-start.58 = (bf16[160,768]{1,0:T(8,128)(2,1)S(1)}, bf16[160,768]{1,0:T(8,128)(2,1)S(1)}, u32[]{:S(2)}, u32[]{:S(2)}) collective-permute-start(bf16[160,768]{1,0:T(8,128)(2,1)S(1)} %add_convert_fusion.11), channel_id=1, source_target_pairs={{0,24},{8,16},{16,8},{24,0},{1,25},{9,17},{17,9},{25,1},{2,26},{10... | collective-permute-start | bytes 737288 | tf_op jit(solution)/shard_map/ppermute | solution.py:758
  (76 other events, 729.0 us)
Sparse Core Ops, SparseCore 0:
  28.3 33.8 all-gather.4
  90.4 36.5 all-gather.6
  265.7 33.9 reduce-scatter.5
  315.7 34.2 reduce-scatter.7
  359.6 28.5 reduce-scatter.3

commit v6 on v5

--- a/solution.py
+++ b/solution.py
@@ -959,12 +959,12 @@
     full_mlp, north, south = tied(full_mlp, north, south)
     lower, upper = to_neighbours(north, south, "gy")
     u, slope, h2r = mlp_fwd(c, full_mlp, full_b, h1)
+    lower, upper, h2r = tied(lower, upper, h2r)
     z = dense(h2r, full_dec).astype(bf16)
     every = (z.astype(f32) * weight_tok).astype(bf16)
     north, south = fold_first(every, dates, side)
     below, above = to_neighbours(north, south, "gy")
 
-    lower, upper, north, south = tied(lower, upper, north, south)
     dz_every = jnp.concatenate([middle, upper, lower])
     dz = (dz_every.astype(f32) * weight_tok).astype(bf16)
     dh2 = dense(dz, full_dec, 1, 1)

time: 485 us -> 476 us (0.981)
  transfers between devices with their start and end apart: 67 -> 67, of which waited for: 24 -> 23; matrix products, arithmetic and copies ran while one was open for 19% -> 18% of each run, Pallas kernels for 27% -> 31%
where the time goes in v6:
time: 476 us; the launch traced here: 469 us
  Pallas kernels  172 us (36%)
  starting transfers between devices  94.2 us (20%)
  waiting for transfers between devices  75.9 us (16%)
  other arithmetic  45.9 us (10%)
  local copies, waits for them, and re-layouts  39.4 us (8%)
  matrix products  23.9 us (5%)
  between operations  17.5 us (4%)
    ppermute x37, waiting for transfers between devices, swap(): lax.ppermute(value, axis, [(i, i ^ bit) for i in range(lax.axis_size(axis...  43.2 us
    ppermute x37, starting transfers between devices, swap(): lax.ppermute(value, axis, [(i, i ^ bit) for i in range(lax.axis_size(axis...  41 us
    pallas_call x1, Pallas kernels, attn_bwd(): pl.pallas_call(functools.partial(attn_bwd_kernel, block=token_block(token...  33.6 us
    ppermute x8, starting transfers between devices, to_neighbours(): lax.ppermute(high, axis, chain(axis, 1))  29.8 us
    pallas_call x1, Pallas kernels, mlp_bwd(): pl.pallas_call(functools.partial(mlp_bwd_kernel, chips=chips), grid_spec=...  26.3 us
    convert_element_type x11, other arithmetic, added(): return sum((v.astype(f32) for v in values)).astype(bf16)  21.2 us
    ppermute x9, waiting for transfers between devices, turn(): lax.ppermute(value, 'gx', [(i, (i + 2 * step) % count) for i in range(cou...  19.4 us
    pallas_call x1, Pallas kernels, attn_fwd(): pl.pallas_call(functools.partial(attn_fwd_kernel, block=token_block(token...  18.3 us
  transfers between devices with their start and end apart: 67, of which 23 were waited for; matrix products, arithmetic and copies ran while one was open for 18% of the time, Pallas kernels for 31%

profile of v6, /device:TPU:0, one launch (start us, length us, event | category | flops | bytes accessed | tf_op | source)
XLA Modules:
  0.0 468.6 jit_solution(18140902119405617356)
XLA Ops:
  10.1 3.0 collective-permute-start.2
  13.1 2.6 collective-permute-start.3
  23.0 2.0 collective-permute-start.1
  33.7 1.9 pad_maximum_fusion.4.refs_1_
  42.1 5.5 %collective-permute-start.5 = (bf16[160,1536]{1,0:T(8,128)(2,1)S(1)}, bf16[160,1536]{1,0:T(8,128)(2,1)}, u32[]{:S(2)}, u32[]{:S(2)}) collective-permute-start(bf16[160,1536]{1,0:T(8,128)(2,1)S(1)} %fusion.40), channel_id=1, source_target_pairs={{0,8},{8,16},{16,24},{1,9},{9,17},{17,25},{2,10},{10,18},{18,26},{... | collective-permute-start | bytes 1474568 | tf_op jit(solution)/shard_map/ppermute | solution.py:649
  51.9 4.5 collective-permute-done.6.lower_ref
  56.4 1.9 collective-permute-done.5.upper_ref
  58.3 3.9 all-gather.5.cloned.1.call-done
  63.8 4.5 collective-permute-start.10
  68.3 3.3 collective-permute-start.11
  73.4 1.8 collective-permute-start.9
  75.8 7.7 %embed.1 = (bf16[864,1536]{1,0:T(8,128)(2,1)}, f32[864,768]{1,0:T(8,128)}, bf16[864,768]{1,0:T(8,128)(2,1)}) custom-call(bf16[384,1536]{1,0:T(8,128)(2,1)} %bitcast.229, bf16[112,1536]{1,0:T(8,128)(2,1)} %collective-permute-done.1.left_ref, bf16[112,1536]{1,0:T(8,128)(2,1)} %collective-permute-done.right_ref, ...), custom_call_target="tpu_custom_call" | custom-call | flops 2038431744 | bytes 11649024 | tf_op jit(solution)/shard_map/embed/pallas_call | solution.py:97
  83.5 4.0 collective-permute-done.8
  87.8 1.7 collective-permute-done.11.refs_3_
  101.1 5.8 %place.2.w_ref = bf16[8,4,96,768]{3,2,1,0:T(8,128)(2,1)} custom-call(s32[3]{0:T(128)} %pad_add_fusion.pos_ref, bf16[96,3072]{1,0:T(8,128)(2,1)} %copy-done.2, bf16[3,96,768]{2,1,0:T(8,128)(2,1)} %pad_maximum_fusion.4.refs_1_, bf16[3,96,768]{2,1,0:T(8,128)(2,1)} %collective-permute-done.10.refs_2_, bf16[3,96,768]{2,1,0:T(8,128)(2,1)} %collective-permute-done.11.refs_3_, ...), custom_call_target="tpu_custom_call" | custom-call | bytes 9437184 | tf_op jit(solution)/shard_map/place/pallas_call | solution.py:508
  106.8 2.4 collective-permute-start.18
  109.2 2.8 collective-permute-start.19
  112.0 8.7 %project.1.q_ref.k_ref.v_ref = bf16[864,2304]{1,0:T(8,128)(2,1)} custom-call(bf16[864,768]{1,0:T(8,128)(2,1)} %get-tuple-element.141.a_ref, bf16[8,4,96,768]{3,2,1,0:T(8,128)(2,1)} %place.2.w_ref), custom_call_target="tpu_custom_call" | custom-call | flops 3057647616 | bytes 8847360 | tf_op jit(solution)/shard_map/project/pallas_call | solution.py:118
  120.7 18.3 %attn_fwd.1 = (bf16[864,768]{1,0:T(8,128)(2,1)}, bf16[12,864,128]{2,1,0:T(8,128)(2,1)}) custom-call(bf16[864,2304]{1,0:T(8,128)(2,1)} %project.1.q_ref.k_ref.v_ref, bf16[864,2304]{1,0:T(8,128)(2,1)} %project.1.q_ref.k_ref.v_ref, bf16[864,2304]{1,0:T(8,128)(2,1)} %project.1.q_ref.k_ref.v_ref, bf16[864,128]{1,0:T(8,128)(2,1)} %select_convert_fusion.kx_ref), custom_call_target="tpu_custom_call" | custom-call | flops 18345885696 | bytes 5308416 | tf_op jit(solution)/shard_map/attn_fwd/pallas_call | solution.py:177
  146.2 3.5 collective-permute-done.19.refs_4_
  151.6 1.8 collective-permute-done.21.refs_6_
  157.6 3.0 collective-permute-start.28
  160.9 5.8 %proj_norm.1 = (f32[864,768]{1,0:T(8,128)}, bf16[864,768]{1,0:T(8,128)(2,1)}) custom-call(bf16[864,768]{1,0:T(8,128)(2,1)} %get-tuple-element.155.o_ref, bf16[8,4,96,768]{3,2,1,0:T(8,128)(2,1)} %place.2.w_ref, f32[864,768]{1,0:T(8,128)} %get-tuple-element.156.h0_ref, f32[4,768]{1,0:T(4,128)} %reshape.344.vec_ref.gain_ref), custom_call_target="tpu_custom_call" | custom-call | flops 1019215872 | bytes 9142272 | tf_op jit(solution)/shard_map/proj_norm/pallas_call | solution.py:260
  166.8 8.8 %place.3.fc1_ref.fc2_ref = bf16[8,4,192,768]{3,2,1,0:T(8,128)(2,1)} custom-call(s32[3]{0:T(128)} %pad_add_fusion.pos_ref, bf16[96,3072]{1,0:T(8,128)(2,1)} %refs_0_, bf16[384,768]{1,0:T(8,128)(2,1)} %refs_1_, bf16[3,192,768]{2,1,0:T(8,128)(2,1)} %copy-done.1, bf16[3,192,768]{2,1,0:T(8,128)(2,1)} %collective-permute-done.18.refs_3_, ...), custom_call_target="tpu_custom_call" | custom-call | bytes 18874368 | tf_op jit(solution)/shard_map/place/pallas_call | solution.py:508
  178.0 4.8 %collective-permute-start.30 = (bf16[144,512]{1,0:T(8,128)(2,1)S(1)}, bf16[144,512]{1,0:T(8,128)(2,1)S(1)}, u32[]{:S(2)}, u32[]{:S(2)}) collective-permute-start(bf16[144,512]{1,0:T(8,128)(2,1)S(1)} %get-tuple-element.165), channel_id=1, source_target_pairs={{0,8},{8,16},{16,24},{1,9},{9,17},{17,25},{2,10},{10,18},{18,26},{... | collective-permute-start | bytes 442376 | tf_op jit(solution)/shard_map/ppermute | solution.py:649
  182.8 17.5 %mlp_fwd.1 = (bf16[864,3072]{1,0:T(8,128)(2,1)}, bf16[864,3072]{1,0:T(8,128)(2,1)}, bf16[864,768]{1,0:T(8,128)(2,1)}) custom-call(bf16[864,768]{1,0:T(8,128)(2,1)} %get-tuple-element.157.c_ref, bf16[8,4,192,768]{3,2,1,0:T(8,128)(2,1)} %place.3.fc1_ref.fc2_ref, f32[1,3072]{1,0:T(1,128)} %reshape.350.b_ref, bf16[8,4,192,768]{3,2,1,0:T(8,128)(2,1)} %place.3.fc1_ref.fc2_ref, ...), custom_call_target="tpu_custom_call" | custom-call | flops 8153726976 | bytes 25362432 | tf_op jit(solution)/shard_map/mlp_fwd/pallas_call | solution.py:308
  200.5 2.8 fusion.97
  205.8 26.3 %mlp_bwd.1 = (f32[864,768]{1,0:T(8,128)}, f32[1,3072]{1,0:T(1,128)}, bf16[4,4,96,768]{3,2,1,0:T(8,128)(2,1)}, bf16[4,4,96,768]{3,2,1,0:T(8,128)(2,1)}, bf16[4,4,...) custom-call(s32[3]{0:T(128)} %pad_add_fusion.pos_ref, bf16[864,768]{1,0:T(8,128)(2,1)} %get-tuple-element.173.dm_ref, ...), custom_call_target="tpu_custom_call" | custom-call | flops 16307453952 | bytes 34799616 | tf_op jit(solution)/shard_map/mlp_bwd/pallas_call | solution.py:368
  232.1 3.9 collective-permute-start.35
  237.4 5.6 %collective-permute-start.32 = (bf16[144,512]{1,0:T(8,128)(2,1)}, bf16[144,512]{1,0:T(8,128)(2,1)}, u32[]{:S(2)}, u32[]{:S(2)}) collective-permute-start(bf16[144,512]{1,0:T(8,128)(2,1)} %get-tuple-element.300), channel_id=1, source_target_pairs={{0,8},{8,16},{16,24},{1,9},{9,17},{17,25},{2,10},{10,18},{18,26},{... | collective-permute-start | bytes 442376 | tf_op jit(solution)/shard_map/ppermute | solution.py:649
  243.0 3.5 convolution_convert_fusion.3
  246.6 7.1 %norm2_back.1 = (f32[864,768]{1,0:T(8,128)}, bf16[864,768]{1,0:T(8,128)(2,1)}, bf16[864,768]{1,0:T(8,128)(2,1)}, f32[1,768]{1,0:T(1,128)}, f32[1,768]{1,0:T(1,128)}) custom-call(f32[864,768]{1,0:T(8,128)} %get-tuple-element.177.dc_ref, f32[864,768]{1,0:T(8,128)} %get-tuple-element.167.h1_ref, f32[864,768]{1,0:T(8,128)} %get-tuple-element.337.dh2_ref, ...), custom_call_target="tpu_custom_call" | custom-call | flops 1019215872 | bytes 14450688 | tf_op jit(solution)/shard_map/norm2_back/pallas_call | solution.py:559
  257.7 3.5 collective-permute-start.36
  262.6 3.5 add_convert_fusion
  270.1 33.6 %attn_bwd.1.d_ref = bf16[3,864,768]{2,1,0:T(8,128)(2,1)} custom-call(bf16[864,2304]{1,0:T(8,128)(2,1)} %project.1.q_ref.k_ref.v_ref, bf16[864,2304]{1,0:T(8,128)(2,1)} %project.1.q_ref.k_ref.v_ref, bf16[864,2304]{1,0:T(8,128)(2,1)} %project.1.q_ref.k_ref.v_ref, bf16[864,768]{1,0:T(8,128)(2,1)} %get-tuple-element.190.do_ref, ...), custom_call_target="tpu_custom_call" | custom-call | flops 22932357120 | bytes 10616832 | tf_op jit(solution)/shard_map/attn_bwd/pallas_call | solution.py:237
  305.0 2.2 convolution_convert_fusion
  307.4 2.0 fusion.39
  309.4 2.0 fusion.38
  311.4 10.5 %qkvo_grad.1 = (bf16[4,4,96,768]{3,2,1,0:T(8,128)(2,1)}, bf16[4,4,96,768]{3,2,1,0:T(8,128)(2,1)}) custom-call(s32[3]{0:T(128)} %pad_add_fusion.pos_ref, bf16[864,768]{1,0:T(8,128)(2,1)} %get-tuple-element.141.a_ref, bf16[3,864,768]{2,1,0:T(8,128)(2,1)} %attn_bwd.1.d_ref, bf16[864,768]{1,0:T(8,128)(2,1)} %get-tuple-element.155.o_ref, ...), custom_call_target="tpu_custom_call" | custom-call | flops 4076863488 | bytes 12681216 | tf_op jit(solution)/shard_map/qkvo_grad/pallas_call | solution.py:402
  323.0 1.7 collective-permute-start.40
  325.1 8.8 %norm1_back.1 = (bf16[864,768]{1,0:T(8,128)(2,1)}, f32[1,768]{1,0:T(1,128)}, f32[1,768]{1,0:T(1,128)}) custom-call(bf16[3,864,768]{2,1,0:T(8,128)(2,1)} %attn_bwd.1.d_ref, bf16[8,4,96,768]{3,2,1,0:T(8,128)(2,1)} %place.2.w_ref, f32[864,768]{1,0:T(8,128)} %get-tuple-element.156.h0_ref, f32[864,768]{1,0:T(8,128)} %get-tuple-element.204.dh1_ref, ...), custom_call_target="tpu_custom_call" | custom-call | flops 3057647616 | bytes 14155776 | tf_op jit(solution)/shard_map/norm1_back/pallas_call | solution.py:588
  334.0 1.8 fusion.84
  335.8 2.6 collective-permute-done.40
  344.5 2.9 fusion.37
  348.6 2.3 collective-permute-start.44
  351.0 7.3 %patch_grad.1 = (bf16[4,4,64,768]{3,2,1,0:T(8,128)(2,1)}, bf16[4,4,64,768]{3,2,1,0:T(8,128)(2,1)}) custom-call(s32[3]{0:T(128)} %pad_add_fusion.pos_ref, bf16[864,1536]{1,0:T(8,128)(2,1)} %get-tuple-element.213.ext_ref, bf16[864,768]{1,0:T(8,128)(2,1)} %get-tuple-element.214.demb_ref, f32[1,3072]{1,0:T(1,128)} %get-tuple-element.215.bias_ref, ...), custom_call_target="tpu_custom_call" | custom-call | flops 2038431744 | bytes 6340608 | tf_op jit(solution)/shard_map/patch_grad/pallas_call | solution.py:449
  361.4 2.6 collective-permute-done.42
  364.0 2.3 collective-permute-start.47
  366.4 10.1 %collective-permute-done.44 = bf16[4,96,768]{2,1,0:T(8,128)(2,1)} collective-permute-done((bf16[4,96,768]{2,1,0:T(8,128)(2,1)S(1)}, bf16[4,96,768]{2,1,0:T(8,128)(2,1)}, u32[]{:S(2)}, u32[]{:S(2)}) %collective-permute-start.44) | collective-permute-done | bytes 589856 | tf_op jit(solution)/shard_map/ppermute | solution.py:758
  376.5 2.0 fusion.23
  378.5 2.8 collective-permute-done.46
  383.4 3.0 collective-permute-start.49
  386.7 2.8 fusion.44
  389.5 2.2 collective-permute-start.50
  391.7 2.0 collective-permute-start.51
  396.5 5.7 %pixel_back.1 = f32[384,1536]{1,0:T(8,128)} custom-call(bf16[384,768]{1,0:T(8,128)(2,1)} %fusion.12.d_ref, bf16[8,208,768]{2,1,0:T(8,128)(2,1)} %bitcast.236, f32[384,1]{1,0:T(8,128)} %convert_element_type.689.shown_ref), custom_call_target="tpu_custom_call" | custom-call | flops 905969664 | bytes 4718592 | tf_op jit(solution)/shard_map/pixel_back/pallas_call | solution.py:472
  402.3 9.7 %collective-permute-done.51 = bf16[4,64,768]{2,1,0:T(8,128)(2,1)} collective-permute-done((bf16[4,64,768]{2,1,0:T(8,128)(2,1)}, bf16[4,64,768]{2,1,0:T(8,128)(2,1)}, u32[]{:S(2)}, u32[]{:S(2)}) %collective-permute-start.51) | collective-permute-done | bytes 393248 | tf_op jit(solution)/shard_map/ppermute | solution.py:758
  412.0 1.8 collective-permute-done.52
  418.6 1.7 collective-permute-start.60
  421.7 5.6 %collective-permute-done.53 = bf16[160,768]{1,0:T(8,128)(2,1)S(1)} collective-permute-done((bf16[160,768]{1,0:T(8,128)(2,1)}, bf16[160,768]{1,0:T(8,128)(2,1)S(1)}, u32[]{:S(2)}, u32[]{:S(2)}) %collective-permute-start.53) | collective-permute-done | bytes 245792 | tf_op jit(solution)/shard_map/ppermute | solution.py:763
  427.5 1.8 fusion
  429.3 7.7 %collective-permute-done.54 = bf16[160,768]{1,0:T(8,128)(2,1)S(1)} collective-permute-done((bf16[160,768]{1,0:T(8,128)(2,1)}, bf16[160,768]{1,0:T(8,128)(2,1)S(1)}, u32[]{:S(2)}, u32[]{:S(2)}) %collective-permute-start.54) | collective-permute-done | bytes 245792 | tf_op jit(solution)/shard_map/ppermute | solution.py:763
  437.0 2.1 collective-permute-done.55
  444.0 3.2 collective-permute-done.61
  (405 shorter events, 116.2 us)
Async XLA Ops:
  7.2 54.9 %all-gather.5.cloned.1.call-start = ((), (), s32[]{:S(2)}) async-start(), calls=%async_computation.6 | async-start | bytes 2875392 | tf_op jit(solution)/shard_map/all_gather | solution.py:848
  10.1 23.6 %collective-permute-start.2 = (bf16[96,768]{1,0:T(8,128)(2,1)}, bf16[96,768]{1,0:T(8,128)(2,1)}, u32[]{:S(2)}, u32[]{:S(2)}) collective-permute-start(bf16[96,768]{1,0:T(8,128)(2,1)} %constant_dynamic-slice_fusion.7), channel_id=1, source_target_pairs={{0,2},{1,3},{2,4},{3,5},{4,6},{5,7},{6,0},{7,1},{8,10},{9,11},{10,... | collective-permute-start | bytes 442376 | tf_op jit(solution)/shard_map/ppermute | solution.py:763
  13.1 20.5 %collective-permute-start.3 = (bf16[96,768]{1,0:T(8,128)(2,1)}, bf16[96,768]{1,0:T(8,128)(2,1)}, u32[]{:S(2)}, u32[]{:S(2)}) collective-permute-start(bf16[96,768]{1,0:T(8,128)(2,1)} %constant_dynamic-slice_fusion.7), channel_id=1, source_target_pairs={{0,4},{1,5},{2,6},{3,7},{4,0},{5,1},{6,2},{7,3},{8,12},{9,13},{10,... | collective-permute-start | bytes 442376 | tf_op jit(solution)/shard_map/ppermute | solution.py:763
  15.7 17.9 %collective-permute-start.4 = (bf16[96,768]{1,0:T(8,128)(2,1)}, bf16[96,768]{1,0:T(8,128)(2,1)}, u32[]{:S(2)}, u32[]{:S(2)}) collective-permute-start(bf16[96,768]{1,0:T(8,128)(2,1)} %constant_dynamic-slice_fusion.7), channel_id=1, source_target_pairs={{0,6},{1,7},{2,0},{3,1},{4,2},{5,3},{6,4},{7,5},{8,14},{9,15},{10,... | collective-permute-start | bytes 442376 | tf_op jit(solution)/shard_map/ppermute | solution.py:763
  23.0 12.6 %collective-permute-start.1 = (bf16[112,1536]{1,0:T(8,128)(2,1)}, bf16[112,1536]{1,0:T(8,128)(2,1)}, u32[]{:S(2)}, u32[]{:S(2)}) collective-permute-start(bf16[112,1536]{1,0:T(8,128)(2,1)} %fusion.50), channel_id=1, source_target_pairs={{0,1},{1,2},{2,3},{3,4},{4,5},{5,6},{6,7},{8,9},{9,10},{10,11},{11... | collective-permute-start | bytes 1032200 | tf_op jit(solution)/shard_map/ppermute | solution.py:649
  25.9 9.6 %collective-permute-start = (bf16[112,1536]{1,0:T(8,128)(2,1)}, bf16[112,1536]{1,0:T(8,128)(2,1)}, u32[]{:S(2)}, u32[]{:S(2)}) collective-permute-start(bf16[112,1536]{1,0:T(8,128)(2,1)} %fusion.49), channel_id=1, source_target_pairs={{1,0},{2,1},{3,2},{4,3},{5,4},{6,5},{7,6},{9,8},{10,9},{11,10},{12... | collective-permute-start | bytes 1032200 | tf_op jit(solution)/shard_map/ppermute | solution.py:649
  28.2 110.8 %all-gather.7.cloned.1.call-start = ((), (), s32[]{:S(2)}) async-start(), calls=%async_computation.7 | async-start | bytes 2654208 | tf_op jit(solution)/shard_map/all_gather | solution.py:848
  40.4 16.0 %collective-permute-start.6 = (bf16[160,1536]{1,0:T(8,128)(2,1)S(1)}, bf16[160,1536]{1,0:T(8,128)(2,1)}, u32[]{:S(2)}, u32[]{:S(2)}) collective-permute-start(bf16[160,1536]{1,0:T(8,128)(2,1)S(1)} %fusion.41), channel_id=1, source_target_pairs={{8,0},{16,8},{24,16},{9,1},{17,9},{25,17},{10,2},{18,10},{26,18},{... | collective-permute-start | bytes 1474568 | tf_op jit(solution)/shard_map/ppermute | solution.py:649
  42.1 16.2 %collective-permute-start.5 = (bf16[160,1536]{1,0:T(8,128)(2,1)S(1)}, bf16[160,1536]{1,0:T(8,128)(2,1)}, u32[]{:S(2)}, u32[]{:S(2)}) collective-permute-start(bf16[160,1536]{1,0:T(8,128)(2,1)S(1)} %fusion.40), channel_id=1, source_target_pairs={{0,8},{8,16},{16,24},{1,9},{9,17},{17,25},{2,10},{10,18},{18,26},{... | collective-permute-start | bytes 1474568 | tf_op jit(solution)/shard_map/ppermute | solution.py:649
  62.2 11.2 %collective-permute-start.7 = (bf16[192,768]{1,0:T(8,128)(2,1)}, bf16[192,768]{1,0:T(8,128)(2,1)S(1)}, u32[]{:S(2)}, u32[]{:S(2)}) collective-permute-start(bf16[192,768]{1,0:T(8,128)(2,1)} %pad_maximum_fusion.5), channel_id=1, source_target_pairs={{0,2},{1,3},{2,4},{3,5},{4,6},{5,7},{6,0},{7,1},{8,10},{9,11},{10,... | collective-permute-start | bytes 884744 | tf_op jit(solution)/shard_map/ppermute | solution.py:763
  63.8 24.0 %collective-permute-start.10 = (bf16[3,96,768]{2,1,0:T(8,128)(2,1)S(1)}, bf16[3,96,768]{2,1,0:T(8,128)(2,1)}, u32[]{:S(2)}, u32[]{:S(2)}) collective-permute-start(bf16[3,96,768]{2,1,0:T(8,128)(2,1)S(1)} %copy-done.8), channel_id=1, source_target_pairs={{0,8},{8,0},{16,24},{24,16},{1,9},{9,1},{17,25},{25,17},{2,10},{10... | collective-permute-start | bytes 1327112 | tf_op jit(solution)/shard_map/ppermute | solution.py:758
  68.3 21.2 %collective-permute-start.11 = (bf16[3,96,768]{2,1,0:T(8,128)(2,1)S(1)}, bf16[3,96,768]{2,1,0:T(8,128)(2,1)}, u32[]{:S(2)}, u32[]{:S(2)}) collective-permute-start(bf16[3,96,768]{2,1,0:T(8,128)(2,1)S(1)} %copy-done.8), channel_id=1, source_target_pairs={{0,16},{8,24},{16,0},{24,8},{1,17},{9,25},{17,1},{25,9},{2,18},{10... | collective-permute-start | bytes 1327112 | tf_op jit(solution)/shard_map/ppermute | solution.py:758
  71.6 18.8 %collective-permute-start.12 = (bf16[3,96,768]{2,1,0:T(8,128)(2,1)S(1)}, bf16[3,96,768]{2,1,0:T(8,128)(2,1)}, u32[]{:S(2)}, u32[]{:S(2)}) collective-permute-start(bf16[3,96,768]{2,1,0:T(8,128)(2,1)S(1)} %copy-done.8), channel_id=1, source_target_pairs={{0,24},{8,16},{16,8},{24,0},{1,25},{9,17},{17,9},{25,1},{2,26},{10... | collective-permute-start | bytes 1327112 | tf_op jit(solution)/shard_map/ppermute | solution.py:758
  71.8 15.8 %collective-permute-start.8 = (bf16[192,768]{1,0:T(8,128)(2,1)}, bf16[192,768]{1,0:T(8,128)(2,1)S(1)}, u32[]{:S(2)}, u32[]{:S(2)}) collective-permute-start(bf16[192,768]{1,0:T(8,128)(2,1)} %pad_maximum_fusion.5), channel_id=1, source_target_pairs={{0,4},{1,5},{2,6},{3,7},{4,0},{5,1},{6,2},{7,3},{8,12},{9,13},{10,... | collective-permute-start | bytes 884744 | tf_op jit(solution)/shard_map/ppermute | solution.py:763
  73.4 14.2 %collective-permute-start.9 = (bf16[192,768]{1,0:T(8,128)(2,1)}, bf16[192,768]{1,0:T(8,128)(2,1)S(1)}, u32[]{:S(2)}, u32[]{:S(2)}) collective-permute-start(bf16[192,768]{1,0:T(8,128)(2,1)} %pad_maximum_fusion.5), channel_id=1, source_target_pairs={{0,6},{1,7},{2,0},{3,1},{4,2},{5,3},{6,4},{7,5},{8,14},{9,15},{10,... | collective-permute-start | bytes 884744 | tf_op jit(solution)/shard_map/ppermute | solution.py:763
  87.6 12.7 %collective-permute-start.13 = (bf16[96,3072]{1,0:T(8,128)(2,1)S(1)}, bf16[96,3072]{1,0:T(8,128)(2,1)}, u32[]{:S(2)}, u32[]{:S(2)}) collective-permute-start(bf16[96,3072]{1,0:T(8,128)(2,1)S(1)} %constant_dynamic-update-slice_fusion.refs_0_), channel_id=1, source_target_pairs={{0,1},{1,0},{2,3},{3,2},{4,5},{5,4},{6,7},{7,6},{8,9},{9,8},{10,11... | collective-permute-start | bytes 1769480 | tf_op jit(solution)/shard_map/ppermute | solution.py:758
  90.3 268.7 %reduce-scatter.6.cloned.1.call-start = ((), (), s32[]{:S(2)}) async-start(), calls=%async_computation.4 | async-start | bytes 884736 | tf_op jit(solution)/shard_map/reduce_scatter | solution.py:863
  95.1 5.2 %collective-permute-start.14 = (bf16[3,96,768]{2,1,0:T(8,128)(2,1)S(1)}, bf16[3,96,768]{2,1,0:T(8,128)(2,1)S(1)}, u32[]{:S(2)}, u32[]{:S(2)}) collective-permute-start(bf16[3,96,768]{2,1,0:T(8,128)(2,1)S(1)} %copy-done.8), channel_id=1, source_target_pairs={{0,1},{1,0},{2,3},{3,2},{4,5},{5,4},{6,7},{7,6},{8,9},{9,8},{10,11... | collective-permute-start | bytes 1327112 | tf_op jit(solution)/shard_map/ppermute | solution.py:758
  95.1 5.2 %collective-permute-start.17 = (bf16[3,96,768]{2,1,0:T(8,128)(2,1)}, bf16[3,96,768]{2,1,0:T(8,128)(2,1)}, u32[]{:S(2)}, u32[]{:S(2)}) collective-permute-start(bf16[3,96,768]{2,1,0:T(8,128)(2,1)} %collective-permute-done.12.refs_4_), channel_id=1, source_target_pairs={{0,1},{1,0},{2,3},{3,2},{4,5},{5,4},{6,7},{7,6},{8,9},{9,8},{10,11... | collective-permute-start | bytes 1327112 | tf_op jit(solution)/shard_map/ppermute | solution.py:758
  106.8 39.4 %collective-permute-start.18 = (bf16[3,192,768]{2,1,0:T(8,128)(2,1)S(1)}, bf16[3,192,768]{2,1,0:T(8,128)(2,1)}, u32[]{:S(2)}, u32[]{:S(2)}) collective-permute-start(bf16[3,192,768]{2,1,0:T(8,128)(2,1)S(1)} %pad_maximum_fusion.3.refs_2_), channel_id=1, source_target_pairs={{0,8},{8,0},{16,24},{24,16},{1,9},{9,1},{17,25},{25,17},{2,10},{10... | collective-permute-start | bytes 2654216 | tf_op jit(solution)/shard_map/ppermute | solution.py:758
  109.2 40.5 %collective-permute-start.19 = (bf16[3,192,768]{2,1,0:T(8,128)(2,1)S(1)}, bf16[3,192,768]{2,1,0:T(8,128)(2,1)}, u32[]{:S(2)}, u32[]{:S(2)}) collective-permute-start(bf16[3,192,768]{2,1,0:T(8,128)(2,1)S(1)} %pad_maximum_fusion.3.refs_2_), channel_id=1, source_target_pairs={{0,16},{8,24},{16,0},{24,8},{1,17},{9,25},{17,1},{25,9},{2,18},{10... | collective-permute-start | bytes 2654216 | tf_op jit(solution)/shard_map/ppermute | solution.py:758
  112.0 38.6 %collective-permute-start.20 = (bf16[3,192,768]{2,1,0:T(8,128)(2,1)S(1)}, bf16[3,192,768]{2,1,0:T(8,128)(2,1)}, u32[]{:S(2)}, u32[]{:S(2)}) collective-permute-start(bf16[3,192,768]{2,1,0:T(8,128)(2,1)S(1)} %pad_maximum_fusion.3.refs_2_), channel_id=1, source_target_pairs={{0,24},{8,16},{16,8},{24,0},{1,25},{9,17},{17,9},{25,1},{2,26},{10... | collective-permute-start | bytes 2654216 | tf_op jit(solution)/shard_map/ppermute | solution.py:758
  150.5 7.0 %collective-permute-start.26 = (bf16[3,192,768]{2,1,0:T(8,128)(2,1)}, bf16[3,192,768]{2,1,0:T(8,128)(2,1)}, u32[]{:S(2)}, u32[]{:S(2)}) collective-permute-start(bf16[3,192,768]{2,1,0:T(8,128)(2,1)} %collective-permute-done.20.refs_5_), channel_id=1, source_target_pairs={{0,1},{1,0},{2,3},{3,2},{4,5},{5,4},{6,7},{7,6},{8,9},{9,8},{10,11... | collective-permute-start | bytes 2654216 | tf_op jit(solution)/shard_map/ppermute | solution.py:758
  151.1 5.2 %collective-permute-start.22 = (bf16[384,768]{1,0:T(8,128)(2,1)}, bf16[384,768]{1,0:T(8,128)(2,1)}, u32[]{:S(2)}, u32[]{:S(2)}) collective-permute-start(bf16[384,768]{1,0:T(8,128)(2,1)} %refs_1_), channel_id=1, source_target_pairs={{0,1},{1,0},{2,3},{3,2},{4,5},{5,4},{6,7},{7,6},{8,9},{9,8},{10,11... | collective-permute-start | bytes 1769480 | tf_op jit(solution)/shard_map/ppermute | solution.py:758
  151.1 15.7 %collective-permute-start.23 = (bf16[3,192,768]{2,1,0:T(8,128)(2,1)S(1)}, bf16[3,192,768]{2,1,0:T(8,128)(2,1)}, u32[]{:S(2)}, u32[]{:S(2)}) collective-permute-start(bf16[3,192,768]{2,1,0:T(8,128)(2,1)S(1)} %pad_maximum_fusion.3.refs_2_), channel_id=1, source_target_pairs={{0,1},{1,0},{2,3},{3,2},{4,5},{5,4},{6,7},{7,6},{8,9},{9,8},{10,11... | collective-permute-start | bytes 2654216 | tf_op jit(solution)/shard_map/ppermute | solution.py:758
  151.6 15.2 %collective-permute-start.24 = (bf16[3,192,768]{2,1,0:T(8,128)(2,1)}, bf16[3,192,768]{2,1,0:T(8,128)(2,1)}, u32[]{:S(2)}, u32[]{:S(2)}) collective-permute-start(bf16[3,192,768]{2,1,0:T(8,128)(2,1)} %collective-permute-done.18.refs_3_), channel_id=1, source_target_pairs={{0,1},{1,0},{2,3},{3,2},{4,5},{5,4},{6,7},{7,6},{8,9},{9,8},{10,11... | collective-permute-start | bytes 2654216 | tf_op jit(solution)/shard_map/ppermute | solution.py:758
  154.2 12.6 %collective-permute-start.25 = (bf16[3,192,768]{2,1,0:T(8,128)(2,1)}, bf16[3,192,768]{2,1,0:T(8,128)(2,1)}, u32[]{:S(2)}, u32[]{:S(2)}) collective-permute-start(bf16[3,192,768]{2,1,0:T(8,128)(2,1)} %collective-permute-done.19.refs_4_), channel_id=1, source_target_pairs={{0,1},{1,0},{2,3},{3,2},{4,5},{5,4},{6,7},{7,6},{8,9},{9,8},{10,11... | collective-permute-start | bytes 2654216 | tf_op jit(solution)/shard_map/ppermute | solution.py:758
  156.3 19.3 %collective-permute-start.27 = (bf16[96,512]{1,0:T(8,128)(2,1)}, bf16[96,512]{1,0:T(8,128)(2,1)S(1)}, u32[]{:S(2)}, u32[]{:S(2)}) collective-permute-start(bf16[96,512]{1,0:T(8,128)(2,1)} %get-tuple-element.159), channel_id=1, source_target_pairs={{1,0},{2,1},{3,2},{4,3},{5,4},{6,5},{7,6},{9,8},{10,9},{11,10},{12... | collective-permute-start | bytes 294920 | tf_op jit(solution)/shard_map/ppermute | solution.py:649
  157.6 18.0 %collective-permute-start.28 = (bf16[96,512]{1,0:T(8,128)(2,1)}, bf16[96,512]{1,0:T(8,128)(2,1)S(1)}, u32[]{:S(2)}, u32[]{:S(2)}) collective-permute-start(bf16[96,512]{1,0:T(8,128)(2,1)} %get-tuple-element.160), channel_id=1, source_target_pairs={{0,1},{1,2},{2,3},{3,4},{4,5},{5,6},{6,7},{8,9},{9,10},{10,11},{11... | collective-permute-start | bytes 294920 | tf_op jit(solution)/shard_map/ppermute | solution.py:649
  176.7 23.7 %collective-permute-start.29 = (bf16[144,512]{1,0:T(8,128)(2,1)S(1)}, bf16[144,512]{1,0:T(8,128)(2,1)S(1)}, u32[]{:S(2)}, u32[]{:S(2)}) collective-permute-start(bf16[144,512]{1,0:T(8,128)(2,1)S(1)} %get-tuple-element.164), channel_id=1, source_target_pairs={{8,0},{16,8},{24,16},{9,1},{17,9},{25,17},{10,2},{18,10},{26,18},{... | collective-permute-start | bytes 442376 | tf_op jit(solution)/shard_map/ppermute | solution.py:649
  178.0 22.4 %collective-permute-start.30 = (bf16[144,512]{1,0:T(8,128)(2,1)S(1)}, bf16[144,512]{1,0:T(8,128)(2,1)S(1)}, u32[]{:S(2)}, u32[]{:S(2)}) collective-permute-start(bf16[144,512]{1,0:T(8,128)(2,1)S(1)} %get-tuple-element.165), channel_id=1, source_target_pairs={{0,8},{8,16},{16,24},{1,9},{9,17},{17,25},{2,10},{10,18},{18,26},{... | collective-permute-start | bytes 442376 | tf_op jit(solution)/shard_map/ppermute | solution.py:649
  232.1 29.1 %collective-permute-start.35 = (bf16[4,4,96,768]{3,2,1,0:T(8,128)(2,1)}, bf16[4,4,96,768]{3,2,1,0:T(8,128)(2,1)}, u32[]{:S(2)}, u32[]{:S(2)}) collective-permute-start(bf16[4,4,96,768]{3,2,1,0:T(8,128)(2,1)} %get-tuple-element.188), channel_id=1, source_target_pairs={{0,1},{1,0},{2,3},{3,2},{4,5},{5,4},{6,7},{7,6},{8,9},{9,8},{10,11... | collective-permute-start | bytes 7077896 | tf_op jit(solution)/shard_map/ppermute | solution.py:758
  236.0 25.2 %collective-permute-start.34 = (bf16[4,4,96,768]{3,2,1,0:T(8,128)(2,1)}, bf16[4,4,96,768]{3,2,1,0:T(8,128)(2,1)S(1)}, u32[]{:S(2)}, u32[]{:S(2)}) collective-permute-start(bf16[4,4,96,768]{3,2,1,0:T(8,128)(2,1)} %get-tuple-element.185), channel_id=1, source_target_pairs={{0,1},{1,0},{2,3},{3,2},{4,5},{5,4},{6,7},{7,6},{8,9},{9,8},{10,11... | collective-permute-start | bytes 7077896 | tf_op jit(solution)/shard_map/ppermute | solution.py:758
  236.1 17.6 %collective-permute-start.31 = (bf16[144,512]{1,0:T(8,128)(2,1)}, bf16[144,512]{1,0:T(8,128)(2,1)}, u32[]{:S(2)}, u32[]{:S(2)}) collective-permute-start(bf16[144,512]{1,0:T(8,128)(2,1)} %get-tuple-element.301), channel_id=1, source_target_pairs={{8,0},{16,8},{24,16},{9,1},{17,9},{25,17},{10,2},{18,10},{26,18},{... | collective-permute-start | bytes 442376 | tf_op jit(solution)/shard_map/ppermute | solution.py:649
  237.4 16.3 %collective-permute-start.32 = (bf16[144,512]{1,0:T(8,128)(2,1)}, bf16[144,512]{1,0:T(8,128)(2,1)}, u32[]{:S(2)}, u32[]{:S(2)}) collective-permute-start(bf16[144,512]{1,0:T(8,128)(2,1)} %get-tuple-element.300), channel_id=1, source_target_pairs={{0,8},{8,16},{16,24},{1,9},{9,17},{17,25},{2,10},{10,18},{18,26},{... | collective-permute-start | bytes 442376 | tf_op jit(solution)/shard_map/ppermute | solution.py:649
  246.5 112.5 %reduce-scatter.8.cloned.1.call-start = ((), (), s32[]{:S(2)}) async-start(), calls=%async_computation.5 | async-start | bytes 1769472 | tf_op jit(solution)/shard_map/reduce_scatter | solution.py:863
  256.4 47.3 %collective-permute-start.33 = (bf16[96,512]{1,0:T(8,128)(2,1)S(1)}, bf16[96,512]{1,0:T(8,128)(2,1)S(1)}, u32[]{:S(2)}, u32[]{:S(2)}) collective-permute-start(bf16[96,512]{1,0:T(8,128)(2,1)S(1)} %get-tuple-element.182), channel_id=1, source_target_pairs={{1,0},{2,1},{3,2},{4,3},{5,4},{6,5},{7,6},{9,8},{10,9},{11,10},{12... | collective-permute-start | bytes 294920 | tf_op jit(solution)/shard_map/ppermute | solution.py:649
  257.7 46.0 %collective-permute-start.36 = (bf16[96,512]{1,0:T(8,128)(2,1)S(1)}, bf16[96,512]{1,0:T(8,128)(2,1)S(1)}, u32[]{:S(2)}, u32[]{:S(2)}) collective-permute-start(bf16[96,512]{1,0:T(8,128)(2,1)S(1)} %get-tuple-element.193), channel_id=1, source_target_pairs={{0,1},{1,2},{2,3},{3,4},{4,5},{5,6},{6,7},{8,9},{9,10},{10,11},{11... | collective-permute-start | bytes 294920 | tf_op jit(solution)/shard_map/ppermute | solution.py:649
  267.8 39.6 %collective-permute-start.38 = (bf16[2,4,96,768]{3,2,1,0:T(8,128)(2,1)}, bf16[2,4,96,768]{3,2,1,0:T(8,128)(2,1)}, u32[]{:S(2)}, u32[]{:S(2)}) collective-permute-start(bf16[2,4,96,768]{3,2,1,0:T(8,128)(2,1)} %get-tuple-element.198), channel_id=1, source_target_pairs={{0,16},{8,24},{16,0},{24,8},{1,17},{9,25},{17,1},{25,9},{2,18},{10... | collective-permute-start | bytes 3538952 | tf_op jit(solution)/shard_map/ppermute | solution.py:758
  269.2 40.2 %collective-permute-start.37 = (bf16[2,4,96,768]{3,2,1,0:T(8,128)(2,1)}, bf16[2,4,96,768]{3,2,1,0:T(8,128)(2,1)}, u32[]{:S(2)}, u32[]{:S(2)}) collective-permute-start(bf16[2,4,96,768]{3,2,1,0:T(8,128)(2,1)} %get-tuple-element.196), channel_id=1, source_target_pairs={{0,8},{8,0},{16,24},{24,16},{1,9},{9,1},{17,25},{25,17},{2,10},{10... | collective-permute-start | bytes 3538952 | tf_op jit(solution)/shard_map/ppermute | solution.py:758
  307.2 89.4 %reduce-scatter.4.cloned.1.call-start = ((), (), s32[]{:S(2)}) async-start(), calls=%async_computation.3 | async-start | bytes 1474560 | tf_op jit(solution)/shard_map/reduce_scatter | solution.py:820
  321.9 21.6 %collective-permute-start.39 = (bf16[4,4,96,768]{3,2,1,0:T(8,128)(2,1)}, bf16[4,4,96,768]{3,2,1,0:T(8,128)(2,1)}, u32[]{:S(2)}, u32[]{:S(2)}) collective-permute-start(bf16[4,4,96,768]{3,2,1,0:T(8,128)(2,1)} %get-tuple-element.203), channel_id=1, source_target_pairs={{0,1},{1,0},{2,3},{3,2},{4,5},{5,4},{6,7},{7,6},{8,9},{9,8},{10,11... | collective-permute-start | bytes 7077896 | tf_op jit(solution)/shard_map/ppermute | solution.py:758
  323.0 15.4 %collective-permute-start.40 = (bf16[4,96,768]{2,1,0:T(8,128)(2,1)}, bf16[4,96,768]{2,1,0:T(8,128)(2,1)S(1)}, u32[]{:S(2)}, u32[]{:S(2)}) collective-permute-start(bf16[4,96,768]{2,1,0:T(8,128)(2,1)} %fusion.38), channel_id=1, source_target_pairs={{0,16},{8,24},{16,0},{24,8},{1,17},{9,25},{17,1},{25,9},{2,18},{10... | collective-permute-start | bytes 1769480 | tf_op jit(solution)/shard_map/ppermute | solution.py:758
  324.7 15.2 %collective-permute-start.41 = (bf16[4,96,768]{2,1,0:T(8,128)(2,1)}, bf16[4,96,768]{2,1,0:T(8,128)(2,1)S(1)}, u32[]{:S(2)}, u32[]{:S(2)}) collective-permute-start(bf16[4,96,768]{2,1,0:T(8,128)(2,1)} %fusion.39), channel_id=1, source_target_pairs={{0,8},{8,0},{16,24},{24,16},{1,9},{9,1},{17,25},{25,17},{2,10},{10... | collective-permute-start | bytes 1769480 | tf_op jit(solution)/shard_map/ppermute | solution.py:758
  347.4 16.6 %collective-permute-start.42 = (bf16[4,96,768]{2,1,0:T(8,128)(2,1)}, bf16[4,96,768]{2,1,0:T(8,128)(2,1)}, u32[]{:S(2)}, u32[]{:S(2)}) collective-permute-start(bf16[4,96,768]{2,1,0:T(8,128)(2,1)} %get-tuple-element.212), channel_id=1, source_target_pairs={{0,8},{8,0},{16,24},{24,16},{1,9},{9,1},{17,25},{25,17},{2,10},{10... | collective-permute-start | bytes 1769480 | tf_op jit(solution)/shard_map/ppermute | solution.py:758
  347.8 18.5 %collective-permute-start.43 = (bf16[4,96,768]{2,1,0:T(8,128)(2,1)}, bf16[4,96,768]{2,1,0:T(8,128)(2,1)}, u32[]{:S(2)}, u32[]{:S(2)}) collective-permute-start(bf16[4,96,768]{2,1,0:T(8,128)(2,1)} %get-tuple-element.222), channel_id=1, source_target_pairs={{0,16},{8,24},{16,0},{24,8},{1,17},{9,25},{17,1},{25,9},{2,18},{10... | collective-permute-start | bytes 1769480 | tf_op jit(solution)/shard_map/ppermute | solution.py:758
  348.6 27.9 %collective-permute-start.44 = (bf16[4,96,768]{2,1,0:T(8,128)(2,1)S(1)}, bf16[4,96,768]{2,1,0:T(8,128)(2,1)}, u32[]{:S(2)}, u32[]{:S(2)}) collective-permute-start(bf16[4,96,768]{2,1,0:T(8,128)(2,1)S(1)} %get-tuple-element.224), channel_id=1, source_target_pairs={{0,24},{8,16},{16,8},{24,0},{1,25},{9,17},{17,9},{25,1},{2,26},{10... | collective-permute-start | bytes 1769480 | tf_op jit(solution)/shard_map/ppermute | solution.py:758
  358.2 28.5 %collective-permute-start.45 = (bf16[4,4,64,768]{3,2,1,0:T(8,128)(2,1)}, bf16[4,4,64,768]{3,2,1,0:T(8,128)(2,1)}, u32[]{:S(2)}, u32[]{:S(2)}) collective-permute-start(bf16[4,4,64,768]{3,2,1,0:T(8,128)(2,1)} %get-tuple-element.226), channel_id=1, source_target_pairs={{0,1},{1,0},{2,3},{3,2},{4,5},{5,4},{6,7},{7,6},{8,9},{9,8},{10,11... | collective-permute-start | bytes 4718600 | tf_op jit(solution)/shard_map/ppermute | solution.py:758
  360.1 21.2 %collective-permute-start.46 = (bf16[144,768]{1,0:T(8,128)(2,1)}, bf16[144,768]{1,0:T(8,128)(2,1)S(1)}, u32[]{:S(2)}, u32[]{:S(2)}) collective-permute-start(bf16[144,768]{1,0:T(8,128)(2,1)} %get-tuple-element.228), channel_id=1, source_target_pairs={{8,0},{16,8},{24,16},{9,1},{17,9},{25,17},{10,2},{18,10},{26,18},{... | collective-permute-start | bytes 663560 | tf_op jit(solution)/shard_map/ppermute | solution.py:649
  364.0 17.3 %collective-permute-start.47 = (bf16[144,768]{1,0:T(8,128)(2,1)S(1)}, bf16[144,768]{1,0:T(8,128)(2,1)S(1)}, u32[]{:S(2)}, u32[]{:S(2)}) collective-permute-start(bf16[144,768]{1,0:T(8,128)(2,1)S(1)} %copy-done.44), channel_id=1, source_target_pairs={{0,8},{8,16},{16,24},{1,9},{9,17},{17,25},{2,10},{10,18},{18,26},{... | collective-permute-start | bytes 663560 | tf_op jit(solution)/shard_map/ppermute | solution.py:649
  382.1 7.4 %collective-permute-start.48 = (bf16[96,768]{1,0:T(8,128)(2,1)S(1)}, bf16[96,768]{1,0:T(8,128)(2,1)S(1)}, u32[]{:S(2)}, u32[]{:S(2)}) collective-permute-start(bf16[96,768]{1,0:T(8,128)(2,1)S(1)} %get-tuple-element.299), channel_id=1, source_target_pairs={{1,0},{2,1},{3,2},{4,3},{5,4},{6,5},{7,6},{9,8},{10,9},{11,10},{12... | collective-permute-start | bytes 442376 | tf_op jit(solution)/shard_map/ppermute | solution.py:649
  383.4 6.1 %collective-permute-start.49 = (bf16[96,768]{1,0:T(8,128)(2,1)S(1)}, bf16[96,768]{1,0:T(8,128)(2,1)S(1)}, u32[]{:S(2)}, u32[]{:S(2)}) collective-permute-start(bf16[96,768]{1,0:T(8,128)(2,1)S(1)} %get-tuple-element.298), channel_id=1, source_target_pairs={{0,1},{1,2},{2,3},{3,4},{4,5},{5,6},{6,7},{8,9},{9,10},{10,11},{11... | collective-permute-start | bytes 442376 | tf_op jit(solution)/shard_map/ppermute | solution.py:649
  389.5 12.8 %collective-permute-start.50 = (bf16[4,64,768]{2,1,0:T(8,128)(2,1)}, bf16[4,64,768]{2,1,0:T(8,128)(2,1)S(1)}, u32[]{:S(2)}, u32[]{:S(2)}) collective-permute-start(bf16[4,64,768]{2,1,0:T(8,128)(2,1)} %get-tuple-element.232), channel_id=1, source_target_pairs={{0,8},{8,0},{16,24},{24,16},{1,9},{9,1},{17,25},{25,17},{2,10},{10... | collective-permute-start | bytes 1179656 | tf_op jit(solution)/shard_map/ppermute | solution.py:758
  391.7 20.2 %collective-permute-start.51 = (bf16[4,64,768]{2,1,0:T(8,128)(2,1)}, bf16[4,64,768]{2,1,0:T(8,128)(2,1)}, u32[]{:S(2)}, u32[]{:S(2)}) collective-permute-start(bf16[4,64,768]{2,1,0:T(8,128)(2,1)} %get-tuple-element.238), channel_id=1, source_target_pairs={{0,16},{8,24},{16,0},{24,8},{1,17},{9,25},{17,1},{25,9},{2,18},{10... | collective-permute-start | bytes 1179656 | tf_op jit(solution)/shard_map/ppermute | solution.py:758
  393.7 20.1 %collective-permute-start.52 = (bf16[4,64,768]{2,1,0:T(8,128)(2,1)}, bf16[4,64,768]{2,1,0:T(8,128)(2,1)}, u32[]{:S(2)}, u32[]{:S(2)}) collective-permute-start(bf16[4,64,768]{2,1,0:T(8,128)(2,1)} %get-tuple-element.240), channel_id=1, source_target_pairs={{0,24},{8,16},{16,8},{24,0},{1,25},{9,17},{17,9},{25,1},{2,26},{10... | collective-permute-start | bytes 1179656 | tf_op jit(solution)/shard_map/ppermute | solution.py:758
  416.4 10.9 %collective-permute-start.53 = (bf16[160,768]{1,0:T(8,128)(2,1)}, bf16[160,768]{1,0:T(8,128)(2,1)S(1)}, u32[]{:S(2)}, u32[]{:S(2)}) collective-permute-start(bf16[160,768]{1,0:T(8,128)(2,1)} %get-tuple-element.294), channel_id=1, source_target_pairs={{0,2},{1,3},{2,4},{3,5},{4,6},{5,7},{6,0},{7,1},{8,10},{9,11},{10,... | collective-permute-start | bytes 737288 | tf_op jit(solution)/shard_map/ppermute | solution.py:763
  418.0 23.1 %collective-permute-start.59 = (bf16[384,768]{1,0:T(8,128)(2,1)S(1)}, bf16[384,768]{1,0:T(8,128)(2,1)}, u32[]{:S(2)}, u32[]{:S(2)}) collective-permute-start(bf16[384,768]{1,0:T(8,128)(2,1)S(1)} %constant_dynamic-update-slice_fusion.7), channel_id=1, source_target_pairs={{0,8},{8,0},{16,24},{24,16},{1,9},{9,1},{17,25},{25,17},{2,10},{10... | collective-permute-start | bytes 1769480 | tf_op jit(solution)/shard_map/ppermute | solution.py:758
  418.6 25.3 %collective-permute-start.60 = (bf16[384,768]{1,0:T(8,128)(2,1)S(1)}, bf16[384,768]{1,0:T(8,128)(2,1)}, u32[]{:S(2)}, u32[]{:S(2)}) collective-permute-start(bf16[384,768]{1,0:T(8,128)(2,1)S(1)} %constant_dynamic-update-slice_fusion.7), channel_id=1, source_target_pairs={{0,16},{8,24},{16,0},{24,8},{1,17},{9,25},{17,1},{25,9},{2,18},{10... | collective-permute-start | bytes 1769480 | tf_op jit(solution)/shard_map/ppermute | solution.py:758
  420.4 26.8 %collective-permute-start.61 = (bf16[384,768]{1,0:T(8,128)(2,1)S(1)}, bf16[384,768]{1,0:T(8,128)(2,1)}, u32[]{:S(2)}, u32[]{:S(2)}) collective-permute-start(bf16[384,768]{1,0:T(8,128)(2,1)S(1)} %constant_dynamic-update-slice_fusion.7), channel_id=1, source_target_pairs={{0,24},{8,16},{16,8},{24,0},{1,25},{9,17},{17,9},{25,1},{2,26},{10... | collective-permute-start | bytes 1769480 | tf_op jit(solution)/shard_map/ppermute | solution.py:758
  421.6 15.5 %collective-permute-start.54 = (bf16[160,768]{1,0:T(8,128)(2,1)}, bf16[160,768]{1,0:T(8,128)(2,1)S(1)}, u32[]{:S(2)}, u32[]{:S(2)}) collective-permute-start(bf16[160,768]{1,0:T(8,128)(2,1)} %get-tuple-element.296), channel_id=1, source_target_pairs={{0,4},{1,5},{2,6},{3,7},{4,0},{5,1},{6,2},{7,3},{8,12},{9,13},{10,... | collective-permute-start | bytes 737288 | tf_op jit(solution)/shard_map/ppermute | solution.py:763
  427.3 11.8 %collective-permute-start.55 = (bf16[160,768]{1,0:T(8,128)(2,1)}, bf16[160,768]{1,0:T(8,128)(2,1)S(1)}, u32[]{:S(2)}, u32[]{:S(2)}) collective-permute-start(bf16[160,768]{1,0:T(8,128)(2,1)} %get-tuple-element.297), channel_id=1, source_target_pairs={{0,6},{1,7},{2,0},{3,1},{4,2},{5,3},{6,4},{7,5},{8,14},{9,15},{10,... | collective-permute-start | bytes 737288 | tf_op jit(solution)/shard_map/ppermute | solution.py:763
  439.2 16.3 %collective-permute-start.56 = (bf16[160,768]{1,0:T(8,128)(2,1)S(1)}, bf16[160,768]{1,0:T(8,128)(2,1)S(1)}, u32[]{:S(2)}, u32[]{:S(2)}) collective-permute-start(bf16[160,768]{1,0:T(8,128)(2,1)S(1)} %add_convert_fusion.11), channel_id=1, source_target_pairs={{0,8},{8,0},{16,24},{24,16},{1,9},{9,1},{17,25},{25,17},{2,10},{10... | collective-permute-start | bytes 737288 | tf_op jit(solution)/shard_map/ppermute | solution.py:758
  439.9 16.1 %collective-permute-start.57 = (bf16[160,768]{1,0:T(8,128)(2,1)S(1)}, bf16[160,768]{1,0:T(8,128)(2,1)S(1)}, u32[]{:S(2)}, u32[]{:S(2)}) collective-permute-start(bf16[160,768]{1,0:T(8,128)(2,1)S(1)} %add_convert_fusion.11), channel_id=1, source_target_pairs={{0,16},{8,24},{16,0},{24,8},{1,17},{9,25},{17,1},{25,9},{2,18},{10... | collective-permute-start | bytes 737288 | tf_op jit(solution)/shard_map/ppermute | solution.py:758
  441.2 14.8 %collective-permute-start.58 = (bf16[160,768]{1,0:T(8,128)(2,1)S(1)}, bf16[160,768]{1,0:T(8,128)(2,1)S(1)}, u32[]{:S(2)}, u32[]{:S(2)}) collective-permute-start(bf16[160,768]{1,0:T(8,128)(2,1)S(1)} %add_convert_fusion.11), channel_id=1, source_target_pairs={{0,24},{8,16},{16,8},{24,0},{1,25},{9,17},{17,9},{25,1},{2,26},{10... | collective-permute-start | bytes 737288 | tf_op jit(solution)/shard_map/ppermute | solution.py:758
  (77 other events, 705.0 us)
Sparse Core Ops, SparseCore 0:
  28.3 33.8 all-gather.4
  90.5 36.5 all-gather.6
  246.6 31.2 reduce-scatter.5
  307.3 33.3 reduce-scatter.7
  351.1 27.0 reduce-scatter.3
